TPU v7x, 32 devices: a whole 2x2x4 slice. The times are simulated.
32 devices in a mesh: rep: 8 (over y, x, core), shard: 4 (over z).
Axes of the slice: x: 2, y: 2, z: 4, core: 2. Of those that a mesh axis runs over, the one named last changes fastest.
Arguments:
- tokens: bfloat16 [4096, 768], P(('rep', 'shard')), may hold values from -6 to 6
- w_qkv: bfloat16 [768, 2304], P('shard'), may hold values from -0.21875 to 0.21875
- w_out: bfloat16 [768, 768], P('shard'), may hold values from -1.25 to 1.25
- w_up: bfloat16 [768, 3072], P('shard'), may hold values from -0.21875 to 0.21875
- w_down: bfloat16 [3072, 768], P('shard'), may hold values from -0.109375 to 0.109375
- vec_bias: bfloat16 [6, 768], P(None, 'shard'), may hold values from -1.796875 to 1.796875
- ln_gain: bfloat16 [2, 768], P(None, 'shard'), may hold values from 0.5 to 1.5
- hidden_bias: bfloat16 [3072], P('shard'), may hold values from -1.796875 to 1.796875
- seq_lengths: int32 [32, 3], P(('rep', 'shard')), may hold values from 0 to 128, as said below
- cotangent: bfloat16 [4096, 768], P(('rep', 'shard')), may hold values from -6 to 6
Outputs:
- activations: bfloat16 [4096, 768], P(('rep', 'shard'))
- grad_tokens: float32 [4096, 768], P(('rep', 'shard'))
- grad_w_qkv: float32 [768, 2304], P('shard')
- grad_w_out: float32 [768, 768], P('shard')
- grad_w_up: float32 [768, 3072], P('shard')
- grad_w_down: float32 [3072, 768], P('shard')
- grad_vec_bias: float32 [6, 768], P(None, 'shard')
- grad_ln_gain: float32 [2, 768], P(None, 'shard')
- grad_hidden_bias: float32 [3072], P('shard')
Inputs may be any that keep to these rules, and one draw needn't show every extreme that they name: `seq_lengths`: row r holds the lengths of the sequences packed into device r's rows, zeros last; each row sums to at most 128; at least two are nonzero except on one device, which holds a single sequence of exactly 128.
All inputs are finite; a program needn't handle non-finite values.
Results may differ from a plain program's by a relative error of at most 0.012.
Values may be sent and summed in bfloat16 or wider, within the bound.
No kernel may reach another device: no remote copies, remote signals or barrier semaphores. Data moves between devices by JAX's collectives and lax.ppermute only.
A program may use at most 128 MiB of HBM per device.

v0:
```python
import math

import jax
import jax.numpy as jnp
from jax import lax
from jax.sharding import PartitionSpec as P

HEADS = 12
HEAD_DIM = 64


layer_eps = 1e-12
masked_score = -1000000000.0


def norm_rows(hidden, scale_row, shift_row):
    centre = hidden - jnp.mean(hidden, axis=-1, keepdims=True)
    spread = jnp.mean(centre * centre, axis=-1, keepdims=True)
    return centre * lax.rsqrt(spread + layer_eps) * scale_row + shift_row


def segment_ids(lengths, row_count):
    seq_ends = jnp.cumsum(lengths)
    position = jnp.arange(row_count, dtype=jnp.int32)
    segment = jnp.sum((position[:, None] >= seq_ends[None, :]).astype(jnp.int32), axis=1)
    return (segment, position < seq_ends[-1])


def matmul_low(left_op, right_op):
    return jnp.dot(left_op, right_op, preferred_element_type=jnp.float32)


def matmul_left_t(left_op, right_op):
    return lax.dot_general(
        left_op, right_op, (((0,), (0,)), ((), ())), preferred_element_type=jnp.float32
    )


def matmul_right_t(left_op, right_op):
    return lax.dot_general(
        left_op, right_op, (((1,), (1,)), ((), ())), preferred_element_type=jnp.float32
    )


def gelu_exact(hidden):
    return jax.nn.gelu(hidden, approximate=False)


def attn_scores(queries, key_rows, same_seq):
    scores = jnp.einsum("qhd,khd->hqk", queries, key_rows, preferred_element_type=jnp.float32) * (
        1.0 / math.sqrt(HEAD_DIM)
    )
    return jnp.where(same_seq[None], scores, masked_score)


def body(
    tokens, w_qkv, w_out, w_up, w_down, vec_bias, ln_gain, hidden_bias, seq_lengths, cotangent
):
    row_count = tokens.shape[0]
    feat_width = tokens.shape[1]
    head_scale = 1.0 / math.sqrt(HEAD_DIM)
    segment, row_valid = segment_ids(seq_lengths[0], row_count)
    same_seq = segment[:, None] == segment[None, :]
    row_keep = row_valid.astype(jnp.float32)[:, None]
    full_qkv, full_out, full_vec, full_gain = (
        lax.all_gather(w_qkv, "shard", axis=0, tiled=True),
        lax.all_gather(w_out, "shard", axis=0, tiled=True),
        lax.all_gather(vec_bias, "shard", axis=1, tiled=True),
        lax.all_gather(ln_gain, "shard", axis=1, tiled=True),
    )
    full_up, full_down, full_hidden = (
        lax.all_gather(w_up, "shard", axis=0, tiled=True),
        lax.all_gather(w_down, "shard", axis=0, tiled=True),
        lax.all_gather(hidden_bias, "shard", axis=0, tiled=True),
    )
    vec_float = full_vec.astype(jnp.float32)
    gain_float = full_gain.astype(jnp.float32)
    zero_bias = jnp.zeros((feat_width,), jnp.float32)
    projected = matmul_low(tokens, full_qkv) + jnp.concatenate(
        [vec_float[0], zero_bias, vec_float[1]]
    )
    proj_low = projected.astype(jnp.bfloat16).reshape(row_count, 3, HEADS, HEAD_DIM)
    queries = proj_low[:, 0]
    key_rows = proj_low[:, 1]
    value_rows = proj_low[:, 2]
    scores = attn_scores(queries, key_rows, same_seq)
    row_top = jnp.max(scores, axis=-1, keepdims=True)
    exp_terms = jnp.exp(scores - row_top)
    exp_total = jnp.sum(exp_terms, axis=-1, keepdims=True)
    attn_probs = exp_terms / exp_total
    log_total = row_top + jnp.log(exp_total)
    attn_mix = jnp.einsum(
        "hqk,khd->qhd",
        attn_probs.astype(jnp.bfloat16),
        value_rows,
        preferred_element_type=jnp.float32,
    )
    attn_mix = attn_mix.reshape(row_count, feat_width).astype(jnp.bfloat16)
    attended = matmul_low(attn_mix, full_out) + vec_float[2]
    normed_one, norm_one_pull = jax.vjp(
        norm_rows, tokens.astype(jnp.float32) + attended, gain_float[0], vec_float[3]
    )
    normed_low = normed_one.astype(jnp.bfloat16)
    hidden_pre = matmul_low(normed_low, full_up) + full_hidden.astype(jnp.float32)
    active, gelu_pull = jax.vjp(gelu_exact, hidden_pre)
    active_low = active.astype(jnp.bfloat16)
    branch = matmul_low(active_low, full_down) + vec_float[4]
    result, norm_two_pull = jax.vjp(norm_rows, normed_one + branch, gain_float[1], vec_float[5])
    activations = (result * row_keep).astype(jnp.bfloat16)
    back_up, back_down = (full_up, full_down)
    grad_result = cotangent.astype(jnp.float32) * row_keep
    grad_sum_two, grad_gain_two, grad_shift_two = norm_two_pull(grad_result)
    branch_grad = grad_sum_two.astype(jnp.bfloat16)
    grad_branch_bias = jnp.sum(branch_grad.astype(jnp.float32), axis=0)
    grad_down = matmul_left_t(active_low, branch_grad)
    (hidden_grad,) = gelu_pull(matmul_right_t(branch_grad, back_down))
    hidden_low = hidden_grad.astype(jnp.bfloat16)
    grad_hidden = jnp.sum(hidden_low.astype(jnp.float32), axis=0)
    grad_up = matmul_left_t(normed_low, hidden_low)
    normed_grad = grad_sum_two + matmul_right_t(hidden_low, back_up)
    grad_sum_one, grad_gain_one, grad_shift_one = norm_one_pull(normed_grad)
    attended_grad = grad_sum_one.astype(jnp.bfloat16)
    grad_attn_bias = jnp.sum(attended_grad.astype(jnp.float32), axis=0)
    back_qkv, back_out = (full_qkv, full_out)
    grad_out = matmul_left_t(attn_mix, attended_grad)
    mix_grad = (
        matmul_right_t(attended_grad, back_out)
        .astype(jnp.bfloat16)
        .reshape(row_count, HEADS, HEAD_DIM)
    )
    again_scores = attn_scores(queries, key_rows, same_seq)
    again_probs = jnp.exp(again_scores - log_total)
    value_grad = jnp.einsum(
        "hqk,qhd->khd",
        again_probs.astype(jnp.bfloat16),
        mix_grad,
        preferred_element_type=jnp.float32,
    )
    prob_grad = jnp.einsum("qhd,khd->hqk", mix_grad, value_rows, preferred_element_type=jnp.float32)
    row_inner = jnp.sum(again_probs * prob_grad, axis=-1, keepdims=True)
    score_grad = (again_probs * (prob_grad - row_inner)).astype(jnp.bfloat16)
    query_grad = (
        jnp.einsum("hqk,khd->qhd", score_grad, key_rows, preferred_element_type=jnp.float32)
        * head_scale
    )
    key_grad = (
        jnp.einsum("hqk,qhd->khd", score_grad, queries, preferred_element_type=jnp.float32)
        * head_scale
    )
    proj_grad = (
        jnp.stack([query_grad, key_grad, value_grad], axis=1)
        .reshape(row_count, 3 * feat_width)
        .astype(jnp.bfloat16)
    )
    proj_float = proj_grad.astype(jnp.float32)
    grad_query_bias = jnp.sum(proj_float[:, :feat_width], axis=0)
    grad_value_bias = jnp.sum(proj_float[:, 2 * feat_width :], axis=0)
    grad_qkv = matmul_left_t(tokens, proj_grad)
    grad_tokens = grad_sum_one + matmul_right_t(proj_grad, back_qkv)
    grad_vec = jnp.stack(
        [
            grad_query_bias,
            grad_value_bias,
            grad_attn_bias,
            grad_shift_one,
            grad_branch_bias,
            grad_shift_two,
        ]
    )
    grad_gains = jnp.stack([grad_gain_one, grad_gain_two])
    share_qkv, share_out, share_up, share_down, share_vec, share_gain, share_hidden = (
        lax.psum_scatter(grad_qkv, "shard", scatter_dimension=0, tiled=True),
        lax.psum_scatter(grad_out, "shard", scatter_dimension=0, tiled=True),
        lax.psum_scatter(grad_up, "shard", scatter_dimension=0, tiled=True),
        lax.psum_scatter(grad_down, "shard", scatter_dimension=0, tiled=True),
        lax.psum_scatter(grad_vec, "shard", scatter_dimension=1, tiled=True),
        lax.psum_scatter(grad_gains, "shard", scatter_dimension=1, tiled=True),
        lax.psum_scatter(grad_hidden, "shard", scatter_dimension=0, tiled=True),
    )
    total_qkv, total_out, total_up, total_down, total_vec, total_gain, total_hidden = lax.psum(
        (share_qkv, share_out, share_up, share_down, share_vec, share_gain, share_hidden), "rep"
    )
    return (
        activations,
        grad_tokens,
        total_qkv,
        total_out,
        total_up,
        total_down,
        total_vec,
        total_gain,
        total_hidden,
    )


def solution(mesh):
    placed = (
        P(("rep", "shard"), None),
        P("shard", None),
        P("shard", None),
        P("shard", None),
        P("shard", None),
        P(None, "shard"),
        P(None, "shard"),
        P("shard"),
        P(("rep", "shard"), None),
        P(("rep", "shard"), None),
    )
    return jax.shard_map(
        body,
        mesh=mesh,
        in_specs=placed,
        out_specs=(
            P(("rep", "shard"), None),
            P(("rep", "shard"), None),
            P("shard", None),
            P("shard", None),
            P("shard", None),
            P("shard", None),
            P(None, "shard"),
            P(None, "shard"),
            P("shard"),
        ),
        check_vma=False,
    )
```

profile of v0, /device:TPU:0, one launch (start us, length us, event | category | flops | bytes accessed | tf_op | source)
XLA Modules:
  0.0 1008.5 jit_solution(5901143708368117234)
XLA Ops:
  7.3 0.7 all-gather.8.cloned.1.call-update
  8.0 0.7 all-gather.10.cloned.1.call-update
  8.8 0.7 all-gather.12.cloned.1.call-update
  9.5 0.5 all-gather.14.cloned.1.call-update
  10.3 0.6 slice.54
  10.9 12.6 %all-gather.1 = bf16[4,192,2]{1,2,0:T(2,128)(2,1)S(1)} all-gather(bf16[1,192,2]{1,2,0:T(2,128)(2,1)S(1)} %bitcast.110), channel_id=1, replica_groups=mesh['rep'=8,'shard'=4] {'shard'}, dimensions={0}, use_global_device_ids=true | all-gather | bytes 3840 | tf_op jit(solution)/shard_map/all_gather | solution.py:69
  23.6 13.3 %all-gather.2 = bf16[4,1,768]{2,1,0:T(2,128)(2,1)S(1)} all-gather(bf16[1,1,768]{2,1,0:T(2,128)(2,1)S(1)} %reshape.161), channel_id=1, replica_groups=mesh['rep'=8,'shard'=4] {'shard'}, dimensions={0}, use_global_device_ids=true | all-gather | bytes 7680 | tf_op jit(solution)/shard_map/all_gather | solution.py:74
  36.9 13.4 %all-gather = bf16[4,192,6]{1,2,0:T(8,128)(2,1)S(1)} all-gather(bf16[1,192,6]{1,2,0:T(8,128)(2,1)S(1)} %bitcast.109), channel_id=1, replica_groups=mesh['rep'=8,'shard'=4] {'shard'}, dimensions={0}, use_global_device_ids=true | all-gather | bytes 11520 | tf_op jit(solution)/shard_map/all_gather | solution.py:68
  50.4 0.6 compare_convert_fusion
  51.3 31.2 %all-gather.8.cloned.1.call-done = bf16[768,2304]{1,0:T(8,128)(2,1)} async-done(((bf16[192,2304]{1,0:T(8,128)(2,1)}), bf16[768,2304]{1,0:T(8,128)(2,1)}) %all-gather.8.cloned.1.call-update) | async-done | bytes 3538960 | tf_op jit(solution)/shard_map/all_gather | solution.py:66
  82.6 2.6 fusion
  85.2 0.3 copy.57
  85.5 0.3 fusion.31
  86.0 0.3 convolution_convert_fusion.2
  86.3 27.0 %all-gather.10.cloned.1.call-done = bf16[768,768]{1,0:T(8,128)(2,1)} async-done(((bf16[192,768]{1,0:T(8,128)(2,1)}), bf16[768,768]{1,0:T(8,128)(2,1)}) %all-gather.10.cloned.1.call-update) | async-done | bytes 1179664 | tf_op jit(solution)/shard_map/all_gather | solution.py:67
  113.3 1.7 fusion.32
  115.3 88.2 %all-gather.12.cloned.1.call-done = bf16[768,3072]{1,0:T(8,128)(2,1)} async-done(((bf16[192,3072]{1,0:T(8,128)(2,1)}), bf16[768,3072]{1,0:T(8,128)(2,1)}) %all-gather.12.cloned.1.call-update) | async-done | bytes 4718608 | tf_op jit(solution)/shard_map/all_gather | solution.py:72
  203.5 8.4 multiply_convert_fusion
  211.8 81.0 %all-gather.14.cloned.1.call-done = bf16[3072,768]{1,0:T(8,128)(2,1)} async-done(((bf16[768,768]{1,0:T(8,128)(2,1)}), bf16[3072,768]{1,0:T(8,128)(2,1)}) %all-gather.14.cloned.1.call-update) | async-done | bytes 4718608 | tf_op jit(solution)/shard_map/all_gather | solution.py:73
  292.8 3.4 fusion.33
  296.5 0.8 multiply_reduce_fusion.1
  297.3 0.9 fusion.29
  298.2 0.7 convert_reduce_fusion.1
  299.0 2.5 convert_reduce_fusion
  301.5 2.4 multiply_reduce_fusion.2
  304.2 0.7 copy-done.3
  304.9 0.7 convert_reduce_fusion.2
  305.6 0.7 copy-done.7
  306.3 1.2 convolution_convert_fusion.1
  307.5 1.7 copy.60
  309.3 1.3 fusion.14
  310.6 1.3 multiply_reduce_fusion
  312.0 0.4 fusion.12
  312.7 4.0 convolution_bitcast_fusion
  316.7 8.0 copy.69
  325.0 0.7 copy-done.8
  325.7 1.9 fusion.34
  327.7 0.5 copy-done.17
  328.2 5.1 fusion.25
  333.5 0.9 copy-done.13
  334.3 5.1 fusion.35
  339.6 0.5 copy-done.20
  340.1 0.9 copy.73
  341.1 0.3 slice_reduce_fusion
  341.6 0.9 copy.71
  342.6 104.2 %reduce-scatter.19.cloned.1.call-done = f32[192,2304]{1,0:T(8,128)} async-done(((f32[768,2304]{1,0:T(8,128)}), f32[192,2304]{1,0:T(8,128)}) %reduce-scatter.19.cloned.1.call-update) | async-done | bytes 1769488
  446.8 2.9 copy.70
  449.8 48.4 %reduce-scatter.13.cloned.1.call-done = f32[192,768]{1,0:T(8,128)} async-done(((f32[768,768]{1,0:T(8,128)}), f32[192,768]{1,0:T(8,128)}) %reduce-scatter.13.cloned.1.call-update) | async-done | bytes 589840 | tf_op jit(solution)/shard_map/reduce_scatter | solution.py:173
  498.2 163.2 %reduce-scatter.15.cloned.1.call-done = f32[192,3072]{1,0:T(8,128)} async-done(((f32[768,3072]{1,0:T(8,128)}), f32[192,3072]{1,0:T(8,128)}) %reduce-scatter.15.cloned.1.call-update) | async-done | bytes 2359312 | tf_op jit(solution)/shard_map/reduce_scatter | solution.py:174
  661.3 164.5 %reduce-scatter.17.cloned.1.call-done = f32[768,768]{1,0:T(8,128)} async-done(((f32[3072,768]{1,0:T(8,128)}), f32[768,768]{1,0:T(8,128)}) %reduce-scatter.17.cloned.1.call-update) | async-done | bytes 2359312 | tf_op jit(solution)/shard_map/reduce_scatter | solution.py:175
  825.9 0.6 copy-done.34
  826.5 0.6 dynamic-slice
  827.7 19.0 %all-reduce = f32[3072]{0:T(1024)S(1)} all-reduce(f32[3072]{0:T(1024)} %get-tuple-element.77), channel_id=8, replica_groups=mesh['rep'=8,'shard'=4] {'shard'}, use_global_device_ids=true, to_apply=%region_34.35.clone | all-reduce | flops 3072 | bytes 24576
  846.8 3.2 convolution_add_fusion.3
  850.0 1.0 copy.74
  851.0 20.4 %reduce-scatter.21.cloned.1.call-done = f32[192,6]{1,0:T(8,128)} async-done(((f32[768,6]{1,0:T(8,128)}), f32[192,6]{1,0:T(8,128)}) %reduce-scatter.21.cloned.1.call-update) | async-done | bytes 4624
  871.4 1.0 copy.72
  872.4 24.3 %all-reduce.1 = (f32[6,192]{1,0:T(8,128)}, f32[2,192]{1,0:T(2,128)}, f32[768]{0:T(1024)}) all-reduce(f32[6,192]{1,0:T(8,128)S(1)} %copy.72, f32[2,192]{1,0:T(2,128)S(1)} %copy.74, f32[768]{0:T(1024)S(1)} %dynamic-slice.1), channel_id=1, replica_groups=mesh['rep'=8,'shard'=4] {'rep'}, use_global_device_ids=true, to_apply=%region_28.29 | all-reduce | flops 2304 | bytes 18432 | tf_op jit(solution)/shard_map/psum | solution.py:180
  896.6 97.6 %all-reduce.5.cloned.1.call-done = (f32[192,2304]{0,1:T(8,128)}, f32[192,768]{1,0:T(8,128)}, f32[192,3072]{1,0:T(8,128)}, f32[768,768]{1,0:T(8,128)}) async-done(((f32[192,2304]{0,1:T(8,128)}, f32[192,768]{1,0:T(8,128)}, f32[192,3072]{1,0:T(8,128)}, f32[768,768]{1,0:T(8,128)}), (f32[192,2304]{0,1:T(8,128)}, f32[192,768]{1,0:T(8,128)}, f32[192,3072]{1,0:T(8,128)}, ...) | async-done | bytes 7077904 | tf_op jit(solution)/shard_map/psum | solution.py:180
  994.2 3.1 copy.64
  997.3 0.8 copy.80
  998.1 1.4 copy.81
  999.5 1.1 copy-done.4
  1000.6 1.4 copy.82
  (136 shorter events, 3.2 us)
Async XLA Ops:
  7.2 2.9 copy-start.33
  7.2 3.7 copy-start.28
  7.2 3.7 copy-start.30
  7.2 75.4 %all-gather.8.cloned.1.call-start = ((), (), s32[]{:S(2)}) async-start(), calls=%async_computation.6 | async-start | bytes 4423680 | tf_op jit(solution)/shard_map/all_gather | solution.py:66
  7.9 29.0 %copy-start.27 = (bf16[6,192]{1,0:T(8,128)(2,1)S(1)}, bf16[6,192]{1,0:T(8,128)(2,1)}, u32[]{:S(2)}) copy-start(bf16[6,192]{1,0:T(8,128)(2,1)} %param.15) | copy-start | bytes 6916
  8.0 74.6 %copy-start.6 = (bf16[128,768]{1,0:T(8,128)(2,1)S(1)}, bf16[128,768]{1,0:T(8,128)(2,1)}, u32[]{:S(2)}) copy-start(bf16[128,768]{1,0:T(8,128)(2,1)} %param.10) | copy-start | bytes 589828
  8.0 105.4 %all-gather.10.cloned.1.call-start = ((), (), s32[]{:S(2)}) async-start(), calls=%async_computation.7 | async-start | bytes 1474560 | tf_op jit(solution)/shard_map/all_gather | solution.py:67
  8.7 194.7 %all-gather.12.cloned.1.call-start = ((), (), s32[]{:S(2)}) async-start(), calls=%async_computation.8 | async-start | bytes 5898240 | tf_op jit(solution)/shard_map/all_gather | solution.py:72
  9.4 283.3 %all-gather.14.cloned.1.call-start = ((), (), s32[]{:S(2)}) async-start(), calls=%async_computation.9 | async-start | bytes 5898240 | tf_op jit(solution)/shard_map/all_gather | solution.py:73
  10.0 436.8 %reduce-scatter.19.cloned.1.call-start = ((), (), s32[]{:S(2)}) async-start(), calls=%async_computation.13 | async-start | bytes 8847360
  86.3 117.2 %copy-start.10 = (bf16[12,64,128]{2,1,0:T(8,128)(2,1)}, bf16[12,64,128]{2,1,0:T(8,128)(2,1)S(1)}, u32[]{:S(2)}) copy-start(bf16[12,64,128]{2,1,0:T(8,128)(2,1)S(1)} %convolution_convert_fusion.2) | copy-start | bytes 589828
  115.1 177.7 %copy-start.15 = (f32[128]{0:T(128)}, f32[128]{0:T(128)S(1)}, u32[]{:S(2)}) copy-start(f32[128]{0:T(128)S(1)} %broadcast_multiply_fusion.1) | copy-start | bytes 1540
  115.2 96.6 %copy-start.31 = (f32[128]{0:T(128)}, f32[128]{0:T(128)S(1)}, u32[]{:S(2)}) copy-start(f32[128]{0:T(128)S(1)} %multiply_reduce_fusion.6) | copy-start | bytes 1540
  115.3 177.5 %copy-start.24 = (f32[128]{0:T(128)}, f32[128]{0:T(128)S(1)}, u32[]{:S(2)}) copy-start(f32[128]{0:T(128)S(1)} %fusion.23) | copy-start | bytes 1540
  292.8 6.2 slice-start
  292.8 3.7 copy-start.9
  292.8 6.1 slice-start.1
  292.8 6.1 copy-start.36
  296.2 2.7 copy-start.35
  298.2 3.2 slice-start.2
  298.9 2.5 copy-start.12
  299.0 2.5 slice-start.3
  299.0 2.5 copy-start.16
  299.0 2.5 copy-start.25
  301.5 2.4 copy-start.32
  303.9 2.4 copy-start.2
  304.2 0.8 copy-start.3
  304.2 1.4 copy-start.29
  305.6 0.7 copy-start.7
  312.7 26.8 %copy-start.1 = (bf16[128,3,12,64]{0,3,2,1:T(8,128)(2,1)}, bf16[128,3,12,64]{0,3,2,1:T(8,128)(2,1)S(1)}, u32[]{:S(2)}) copy-start(bf16[128,3,12,64]{0,3,2,1:T(8,128)(2,1)S(1)} %pad_maximum_fusion) | copy-start | bytes 1769476
  324.7 0.9 copy-start.8
  324.7 1.0 copy-start.11
  324.7 173.4 %reduce-scatter.13.cloned.1.call-start = ((), (), s32[]{:S(2)}) async-start(), calls=%async_computation.10 | async-start | bytes 2949120 | tf_op jit(solution)/shard_map/reduce_scatter | solution.py:173
  327.6 0.6 copy-start.17
  327.6 0.7 copy-start.26
  327.6 333.7 %reduce-scatter.15.cloned.1.call-start = ((), (), s32[]{:S(2)}) async-start(), calls=%async_computation.11 | async-start | bytes 11796480 | tf_op jit(solution)/shard_map/reduce_scatter | solution.py:174
  333.4 0.9 copy-start.13
  333.4 492.4 %reduce-scatter.17.cloned.1.call-start = ((), (), s32[]{:S(2)}) async-start(), calls=%async_computation.12 | async-start | bytes 11796480 | tf_op jit(solution)/shard_map/reduce_scatter | solution.py:175
  339.4 0.7 copy-start.20
  339.4 0.7 copy-start.23
  339.4 2.0 copy-start.18
  339.4 2.0 copy-start.19
  339.5 2.0 copy-start.22
  339.5 2.0 copy-start.21
  339.5 510.5 %reduce-scatter.23.cloned.1.call-start = ((), (), s32[]{:S(2)}) async-start(), calls=%async_computation.15 | async-start | bytes 491520
  341.1 530.3 %reduce-scatter.21.cloned.1.call-start = ((), (), s32[]{:S(2)}) async-start(), calls=%async_computation.14 | async-start | bytes 491520
  342.5 651.7 %all-reduce.5.cloned.1.call-start = ((), (), s32[]{:S(2)}) async-start(), calls=%async_computation.16 | async-start | bytes 15335424 | tf_op jit(solution)/shard_map/psum | solution.py:180
  825.8 0.7 copy-start.34
  825.9 20.9 %copy-start = (bf16[768,2304]{1,0:T(8,128)(2,1)S(1)}, bf16[768,2304]{1,0:T(8,128)(2,1)}, u32[]{:S(2)}) copy-start(bf16[768,2304]{1,0:T(8,128)(2,1)} %all-gather.8.cloned.1.call-done) | copy-start | bytes 10616836
  994.2 3.1 copy-start.14
  994.2 3.9 copy-start.5
  998.1 2.5 copy-start.4
Sparse Core Ops, SparseCore 0:
  9.6 72.9 all-gather.7
  84.2 29.1 all-gather.9
  114.9 88.5 all-gather.11
  204.9 87.8 all-gather.13
  324.9 121.9 reduce-scatter.18
  449.6 48.5 reduce-scatter.12
  500.5 160.7 reduce-scatter.14
  663.7 162.1 reduce-scatter.16
  828.1 21.5 reduce-scatter.22
  852.6 18.8 reduce-scatter.20
  875.7 118.4 all-reduce.4
where the time goes:
time: 1010 us
  waiting for transfers between devices  828 us (82%)
  blocking collectives  82.6 us (8%)
  matrix products  45.3 us (4%)
  local copies, waits for them, and re-layouts  31 us (3%)
  between operations  15.1 us (1%)
    reduce_scatter x1, waiting for transfers between devices, body(): lax.psum_scatter(grad_down, 'shard', scatter_dimension=0, tiled=True)  165 us
    reduce_scatter x1, waiting for transfers between devices, body(): lax.psum_scatter(grad_up, 'shard', scatter_dimension=0, tiled=True)  163 us
    unnamed x14, waiting for transfers between devices  127 us
    psum x1, waiting for transfers between devices, body(): lax.psum((share_qkv, share_out, share_up, share_down, share_vec, share_ga...  97.6 us
    all_gather x1, waiting for transfers between devices, body(): lax.all_gather(w_up, 'shard', axis=0, tiled=True)  88.2 us
    all_gather x1, waiting for transfers between devices, body(): lax.all_gather(w_down, 'shard', axis=0, tiled=True)  81 us
    reduce_scatter x1, waiting for transfers between devices, body(): lax.psum_scatter(grad_out, 'shard', scatter_dimension=0, tiled=True)  48.4 us
    all_gather x1, waiting for transfers between devices, body(): lax.all_gather(w_qkv, 'shard', axis=0, tiled=True)  31.2 us
  transfers between devices with their start and end apart: 11, of which 10 were waited for; matrix products, arithmetic and copies ran while one was open for 4% of the time, Pallas kernels for 0%

commit v1 on v0

v1 whole, which is shorter than its diff:
```python
import math

import jax
import jax.numpy as jnp
from jax import lax
from jax.sharding import PartitionSpec as P

HEADS = 12
HEAD_DIM = 64
PARTS = 4
CORES = 2
layer_eps = 1e-12
masked_score = -1000000000.0
BF = jnp.bfloat16
F32 = jnp.float32


def mm(a, b):
    return jnp.dot(a, b, preferred_element_type=F32)


def mm_ta(a, b):
    return lax.dot_general(a, b, (((0,), (0,)), ((), ())), preferred_element_type=F32)


def mm_tb(a, b):
    return lax.dot_general(a, b, (((1,), (1,)), ((), ())), preferred_element_type=F32)


def norm_stats(h):
    centre = h - jnp.mean(h, axis=-1, keepdims=True)
    inv = lax.rsqrt(jnp.mean(centre * centre, axis=-1, keepdims=True) + layer_eps)
    return centre * inv, inv


def norm_back(g, unit, inv, gain):
    gg = g * gain
    m1 = jnp.mean(gg, axis=-1, keepdims=True)
    m2 = jnp.mean(gg * unit, axis=-1, keepdims=True)
    return inv * (gg - m1 - unit * m2)


def gelu_parts(u):
    phi = 0.5 * (1.0 + lax.erf(u * (1.0 / math.sqrt(2.0))))
    dens = jnp.exp(-0.5 * u * u) * (1.0 / math.sqrt(2.0 * math.pi))
    return phi, phi + u * dens


def rows_of(flat, start, size):
    return lax.dynamic_slice_in_dim(flat, start, size, 0)


def make_body(reps, shards):
    def xor_perm(n, k):
        return [(i, i ^ k) for i in range(n)]

    def swap_core(v):
        return lax.ppermute(v, "rep", xor_perm(reps, 1))

    def swap_part(v, k):
        return lax.ppermute(v, "rep", xor_perm(reps, CORES * k))

    def swap_shard(v, k):
        return lax.ppermute(v, "shard", xor_perm(shards, k))

    def spread_part(v):
        return [v] + [swap_part(v, k) for k in range(1, PARTS)]

    def spread_shard(v):
        return [v] + [swap_shard(v, k) for k in range(1, shards)]

    def in_order(slots, me):
        stacked = jnp.stack(slots)
        return jnp.stack(
            [lax.dynamic_index_in_dim(stacked, j ^ me, 0, False) for j in range(len(slots))]
        )

    def pick(stacked, index):
        return lax.dynamic_index_in_dim(stacked, index, 0, False)

    def pair(mine, other, core):
        first = core == 0
        return jnp.where(first, mine, other), jnp.where(first, other, mine)

    def sum_outer(v):
        step = CORES * PARTS
        while step < reps:
            got = lax.ppermute(v, "rep", xor_perm(reps, step))
            v = v + got
            step *= 2
        return v

    def body(
        tokens, w_qkv, w_out, w_up, w_down, vec_bias, ln_gain, hidden_bias, seq_lengths, cotangent
    ):
        rows, width = tokens.shape
        hidden = hidden_bias.shape[0] * shards
        wsh = width // shards
        half = wsh // CORES
        hcol = width // PARTS
        fcol = hidden // shards // PARTS
        heads = HEADS // PARTS
        oq = wsh // PARTS // CORES
        rep = lax.axis_index("rep")
        z = lax.axis_index("shard")
        core = rep % CORES
        c = (rep // CORES) % PARTS

        len_row = jnp.pad(seq_lengths.astype(BF), ((0, 15), (0, width - seq_lengths.shape[1])))
        tok_slots = spread_part(jnp.concatenate([tokens, len_row]))

        qkv_c = lax.dynamic_index_in_dim(
            w_qkv.reshape(wsh, 3, PARTS, hcol), c, 2, False
        ).reshape(wsh, 3 * hcol)
        extra = jnp.concatenate(
            [vec_bias, ln_gain, lax.dynamic_slice_in_dim(hidden_bias, c * fcol, fcol)[None]]
        ).reshape(3, 3 * hcol)
        extra = jnp.pad(extra, ((0, 13), (0, 0)))
        pay1 = jnp.concatenate([rows_of(qkv_c, core * half, half), extra])
        got1 = in_order(spread_shard(pay1), z)
        ext = got1[:, half : half + 3].reshape(shards, 9, hcol)
        q_lo, q_hi = pair(got1[:, :half], swap_core(got1[:, :half]), core)
        wq = jnp.concatenate([q_lo, q_hi], axis=1).reshape(width, 3 * hcol)
        vecs = ext[:, :6].transpose(1, 0, 2).reshape(6, width).astype(F32)
        gains = ext[:, 6:8].transpose(1, 0, 2).reshape(2, width).astype(F32)
        hid_b = ext[:, 8].reshape(1, shards * fcol).astype(F32)

        out_q = rows_of(w_out, c * (wsh // PARTS) + core * oq, oq)
        got_o = jnp.stack(spread_shard(out_q))
        up_c = lax.dynamic_index_in_dim(
            w_up.reshape(wsh, shards, PARTS, fcol), c, 2, False
        ).reshape(wsh, shards * fcol)
        down_c = rows_of(w_down, c * fcol, fcol)
        pay2 = jnp.concatenate(
            [rows_of(up_c, core * half, half), rows_of(down_c, core * (fcol // 2), fcol // 2)]
        )
        got2 = in_order(spread_shard(pay2), z)
        lo2, hi2 = pair(got2, swap_core(got2), core)
        wu = jnp.concatenate([lo2[:, :half], hi2[:, :half]], axis=1).reshape(width, -1)
        wd = jnp.concatenate([lo2[:, half:], hi2[:, half:]], axis=1).reshape(-1, width)
        part_o = in_order(spread_part(in_order(list(got_o), z)), c)
        o_lo, o_hi = pair(part_o, swap_core(part_o), core)
        wo = jnp.stack([o_lo, o_hi], axis=2).transpose(1, 0, 2, 3, 4).reshape(width, width)

        xg = jnp.stack([s[:rows] for s in tok_slots])
        lens = jnp.stack([s[rows, : seq_lengths.shape[1]] for s in tok_slots]).astype(jnp.int32)
        ends = jnp.cumsum(lens, axis=1)
        pos = jnp.arange(rows, dtype=jnp.int32)
        seg = jnp.sum((pos[None, :, None] >= ends[:, None, :]).astype(jnp.int32), axis=2)
        same = seg[:, :, None] == seg[:, None, :]
        keep = (pos < ends[0, -1]).astype(F32)[:, None]
        xf = xg.reshape(PARTS * rows, width)
        qb = jnp.concatenate(
            [
                lax.dynamic_slice_in_dim(vecs[0], c * hcol, hcol),
                jnp.zeros((hcol,), F32),
                lax.dynamic_slice_in_dim(vecs[1], c * hcol, hcol),
            ]
        )
        proj = (mm(xf, wq) + qb).astype(BF).reshape(PARTS, rows, 3, heads, HEAD_DIM)
        q, kk, v = proj[:, :, 0], proj[:, :, 1], proj[:, :, 2]
        scale = 1.0 / math.sqrt(HEAD_DIM)
        s = jnp.einsum("bqhd,bkhd->bhqk", q, kk, preferred_element_type=F32) * scale
        s = jnp.where(same[:, None], s, masked_score)
        top = jnp.max(s, axis=-1, keepdims=True)
        e = jnp.exp(s - top)
        probs = e / jnp.sum(e, axis=-1, keepdims=True)
        probs_low = probs.astype(BF)
        mix = jnp.einsum("bhqk,bkhd->bqhd", probs_low, v, preferred_element_type=F32)
        mix = mix.astype(BF).reshape(PARTS, rows, hcol)
        mix_slots = [mix[0]] + [swap_part(mix[k], k) for k in range(1, PARTS)]
        mix_full = in_order(mix_slots, c).transpose(1, 0, 2).reshape(rows, width)

        h1 = tokens.astype(F32) + (mm(mix_full, wo) + vecs[2])
        unit1, inv1 = norm_stats(h1)
        y1 = unit1 * gains[0] + vecs[3]
        y1_low = y1.astype(BF)
        yg = jnp.stack(spread_part(y1_low)).reshape(PARTS * rows, width)

        u = mm(yg, wu) + hid_b
        phi, slope = gelu_parts(u)
        act = (u * phi).astype(BF)
        zp = mm(act, wd).reshape(PARTS, rows, width)
        branch = zp[0] + vecs[4]
        for k in range(1, PARTS):
            branch = branch + swap_part(zp[k].astype(BF), k).astype(F32)

        unit2, inv2 = norm_stats(y1 + branch)
        activations = ((unit2 * gains[1] + vecs[5]) * keep).astype(BF)
        g_res = cotangent.astype(F32) * keep
        g_gain2 = jnp.sum(g_res * unit2, axis=0)
        g_shift2 = jnp.sum(g_res, axis=0)
        g_h2 = norm_back(g_res, unit2, inv2, gains[1])
        dz = g_h2.astype(BF)
        g_bias4 = jnp.sum(dz.astype(F32), axis=0)
        dzg = jnp.stack(spread_part(dz)).reshape(PARTS * rows, width)

        du = (mm_tb(dzg, wd) * slope).astype(BF)
        g_hid = jnp.sum(du.astype(F32), axis=0)
        dyp = mm_tb(du, wu).reshape(PARTS, rows, width)
        dy1 = g_h2 + dyp[0]
        for k in range(1, PARTS):
            dy1 = dy1 + swap_part(dyp[k].astype(BF), k).astype(F32)
        g_down = mm_ta(act, dzg).astype(BF)
        g_up = mm_ta(yg, du).astype(BF)

        hid_rows = jnp.pad(
            g_hid.astype(BF).reshape(shards, 1, 1, fcol), ((0, 0), (0, 1), (0, 15), (0, width - fcol))
        )
        hid_rows = jnp.concatenate([hid_rows[:, :1], hid_rows[:, :1]], axis=1)
        batch1 = jnp.concatenate(
            [
                g_up.reshape(shards, CORES, half, width),
                g_down.reshape(shards, CORES, fcol // 2, width),
                hid_rows,
            ],
            axis=2,
        )

        def reduce_batch(batch):
            b = batch.transpose(1, 0, 2, 3)
            mine, give = pick(b, core), pick(b, 1 - core)
            tot = mine.astype(F32) + swap_core(give).astype(F32)
            low = tot.astype(BF)
            own = pick(tot, z)
            for k in range(1, shards):
                own = own + swap_shard(pick(low, z ^ k), k).astype(F32)
            return sum_outer(own)

        def spread_batch(piece):
            full = in_order(spread_part(piece.astype(BF)), c)
            lo, hi = pair(full, swap_core(full), core)
            return jnp.stack([lo, hi], axis=1)

        done1 = spread_batch(reduce_batch(batch1))
        gw_up = (
            done1[:, :, :half]
            .reshape(PARTS, CORES, half, shards, fcol)
            .transpose(1, 2, 3, 0, 4)
            .reshape(wsh, hidden)
            .astype(F32)
        )
        gw_down = done1[:, :, half : half + fcol // 2].reshape(PARTS * fcol, width).astype(F32)
        g_hidden = done1[:, 0, half + fcol // 2, :fcol].reshape(-1).astype(F32)

        g_gain1 = jnp.sum(dy1 * unit1, axis=0)
        g_shift1 = jnp.sum(dy1, axis=0)
        g_h1 = norm_back(dy1, unit1, inv1, gains[0])
        da = g_h1.astype(BF)
        g_bias2 = jnp.sum(da.astype(F32), axis=0)
        dmix = mm_tb(da, wo).astype(BF).reshape(rows, PARTS, hcol).transpose(1, 0, 2)
        dm_slots = [pick(dmix, c)] + [swap_part(pick(dmix, c ^ k), k) for k in range(1, PARTS)]
        dm = jnp.stack(dm_slots).reshape(PARTS, rows, heads, HEAD_DIM)
        g_out = mm_ta(mix_full, da).astype(BF).reshape(shards, PARTS, CORES, oq, width)
        go = g_out.transpose(2, 1, 0, 3, 4)
        go = pick(go, core).astype(F32) + swap_core(pick(go, 1 - core)).astype(F32)
        go_low = go.astype(BF)
        go_sum = pick(go, c)
        for k in range(1, PARTS):
            go_sum = go_sum + swap_part(pick(go_low, c ^ k), k).astype(F32)

        dv = jnp.einsum("bhqk,bqhd->bkhd", probs_low, dm, preferred_element_type=F32)
        dpr = jnp.einsum("bqhd,bkhd->bhqk", dm, v, preferred_element_type=F32)
        inner = jnp.sum(probs * dpr, axis=-1, keepdims=True)
        ds = (probs * (dpr - inner)).astype(BF)
        dq = jnp.einsum("bhqk,bkhd->bqhd", ds, kk, preferred_element_type=F32) * scale
        dk = jnp.einsum("bhqk,bqhd->bkhd", ds, q, preferred_element_type=F32) * scale
        dp = (
            jnp.stack([dq, dk, dv], axis=2).astype(BF).reshape(PARTS * rows, 3 * hcol)
        )
        g_qkv = mm_ta(xf, dp).astype(BF)
        dxp = mm_tb(dp, wq).reshape(PARTS, rows, width)
        g_tok = g_h1 + dxp[0]
        for k in range(1, PARTS):
            g_tok = g_tok + swap_part(dxp[k].astype(BF), k).astype(F32)

        col = jnp.sum(dp.astype(F32), axis=0)
        qv = jnp.stack([col[:hcol], col[2 * hcol :]]).astype(BF)
        small = jnp.stack([g_bias2, g_shift1, g_bias4, g_shift2, g_gain1, g_gain2]).astype(BF)
        small = small.reshape(6, shards, wsh).transpose(1, 0, 2)
        at_c = (jnp.arange(shards) == c)[:, None, None]
        qv = jnp.where(at_c, qv[None], jnp.zeros((), BF))
        small = jnp.concatenate([qv, small], axis=1).reshape(shards, 1, -1)
        span = 3 * hcol
        extra_rows = -(-(8 * wsh) // span)
        small = jnp.pad(small, ((0, 0), (0, 0), (0, extra_rows * span - 8 * wsh)))
        small = small.reshape(shards, extra_rows, span)
        small = jnp.broadcast_to(small[:, None], (shards, CORES, extra_rows, span))
        batch2 = jnp.concatenate([g_qkv.reshape(shards, CORES, half, span), small], axis=2)
        piece2 = reduce_batch(batch2)
        own_o = pick(go_sum, z)
        go_sum_low = go_sum.astype(BF)
        for k in range(1, shards):
            own_o = own_o + swap_shard(pick(go_sum_low, z ^ k), k).astype(F32)
        own_o = sum_outer(own_o)
        done2 = spread_batch(piece2)
        done_o = spread_batch(own_o)
        gw_qkv = (
            done2[:, :, :half]
            .reshape(PARTS, CORES, half, 3, hcol)
            .transpose(1, 2, 3, 0, 4)
            .reshape(wsh, 3 * width)
            .astype(F32)
        )
        gw_out = done_o.reshape(wsh, width).astype(F32)
        tot_small = jnp.sum(done2[:, 0, half:].astype(F32), axis=0).reshape(-1)[: 8 * wsh]
        tot_small = tot_small.reshape(8, wsh)
        return (
            activations,
            g_tok,
            gw_qkv,
            gw_out,
            gw_up,
            gw_down,
            tot_small[:6],
            tot_small[6:],
            g_hidden,
        )

    return body


def solution(mesh):
    body = make_body(mesh.shape["rep"], mesh.shape["shard"])
    both = P(("rep", "shard"), None)
    first = P("shard", None)
    return jax.shard_map(
        body,
        mesh=mesh,
        in_specs=(
            both,
            first,
            first,
            first,
            first,
            P(None, "shard"),
            P(None, "shard"),
            P("shard"),
            both,
            both,
        ),
        out_specs=(
            both,
            both,
            first,
            first,
            first,
            first,
            P(None, "shard"),
            P(None, "shard"),
            P("shard"),
        ),
        check_vma=False,
    )
```

time: 1010 us -> 293 us (0.29)
  waiting for transfers between devices: 828 us -> 78.5 us
  starting transfers between devices: 0.62 us -> 84.2 us
  blocking collectives: 82.6 us -> 0 us
  local copies, waits for them, and re-layouts: 31 us -> 67.6 us
  other arithmetic: 5.56 us -> 33.8 us
  matrix products: 45.3 us -> 20.8 us
  between operations: 15.1 us -> 2.24 us
    reduce_scatter x3 -> x0, waiting for transfers between devices: 376 us -> none  [the longest x1 165 us: body(): lax.psum_scatter(grad_down, 'shard', scatter_dimension=0, tiled=True)]
    all_gather x4 -> x0, waiting for transfers between devices: 227 us -> none  [the longest x1 88.2 us: body(): lax.all_gather(w_up, 'shard', axis=0, tiled=True)]
    unnamed x14 -> x0, waiting for transfers between devices: 127 us -> none
    psum x1 -> x0, waiting for transfers between devices: 97.6 us -> none  [body(): lax.psum((share_qkv, share_out, share_up, share_down, share_vec, share_ga...]
    ppermute x0 -> x66, starting transfers between devices: none -> 84.2 us  [the longest x39 49.8 us: swap_part(): return lax.ppermute(v, 'rep', xor_perm(reps, CORES * k))]
    ppermute x0 -> x66, waiting for transfers between devices: none -> 78.5 us  [the longest x18 39.6 us: swap_shard(): return lax.ppermute(v, 'shard', xor_perm(shards, k))]
    all_gather x3 -> x0, blocking collectives: 39.3 us -> none  [the longest x1 13.4 us: body(): lax.all_gather(vec_bias, 'shard', axis=1, tiled=True)]
    dot_general x18 -> x17, matrix products: 45.3 us -> 19.4 us  [the longest x4 6.56 us: mm(): return jnp.dot(a, b, preferred_element_type=F32)]
  transfers between devices with their start and end apart: 11 -> 66, of which waited for: 10 -> 26; matrix products, arithmetic and copies ran while one was open for 4% -> 28% of each run, Pallas kernels for 0% -> 0%
where the time goes in v1:
time: 293 us; the launch traced here: 287 us
  starting transfers between devices  84.2 us (29%)
  waiting for transfers between devices  78.5 us (27%)
  local copies, waits for them, and re-layouts  67.6 us (23%)
  other arithmetic  33.8 us (12%)
  matrix products  20.8 us (7%)
    ppermute x39, starting transfers between devices, swap_part(): return lax.ppermute(v, 'rep', xor_perm(reps, CORES * k))  49.8 us
    ppermute x18, waiting for transfers between devices, swap_shard(): return lax.ppermute(v, 'shard', xor_perm(shards, k))  39.6 us
    ppermute x39, waiting for transfers between devices, swap_part(): return lax.ppermute(v, 'rep', xor_perm(reps, CORES * k))  37.1 us
    ppermute x18, starting transfers between devices, swap_shard(): return lax.ppermute(v, 'shard', xor_perm(shards, k))  33 us
    convert_element_type x3, local copies, waits for them, and re-layouts, body(): gw_up = done1[:, :, :half].reshape(PARTS, CORES, half, shards, fcol).tran...  12.2 us
    convert_element_type x3, local copies, waits for them, and re-layouts, body(): gw_qkv = done2[:, :, :half].reshape(PARTS, CORES, half, 3, hcol).transpos...  8.39 us
    dot_general x4, matrix products, mm(): return jnp.dot(a, b, preferred_element_type=F32)  6.56 us
    unnamed x126, local copies, waits for them, and re-layouts  6.04 us
  transfers between devices with their start and end apart: 66, of which 26 were waited for; matrix products, arithmetic and copies ran while one was open for 28% of the time, Pallas kernels for 0%

profile of v1, /device:TPU:0, one launch (start us, length us, event | category | flops | bytes accessed | tf_op | source)
XLA Modules:
  0.0 287.1 jit_solution(15380814936910687031)
XLA Ops:
  1.6 4.0 %collective-permute-start.11 = (bf16[24,768]{1,0:T(8,128)(2,1)S(1)}, bf16[24,768]{1,0:T(8,128)(2,1)S(1)}, u32[]{:S(2)}, u32[]{:S(2)}) collective-permute-start(bf16[24,768]{1,0:T(8,128)(2,1)S(1)} %constant_dynamic-slice_fusion.27), channel_id=1, source_target_pairs={{0,2},{1,3},{2,0},{3,1},{4,6},{5,7},{6,4},{7,5},{8,10},{9,11},{10,... | collective-permute-start | bytes 110600 | tf_op jit(solution)/shard_map/ppermute | solution.py:64
  5.6 1.6 collective-permute-start.10
  7.8 1.6 fusion.54
  9.5 2.7 collective-permute-start.2
  14.4 2.9 %reshape.327 = bf16[192,3,4,192]{3,2,1,0:T(4,128)(2,1)S(1)} reshape(bf16[192,2304]{1,0:T(8,128)(2,1)} %param.11) | data formatting | bytes 1769472 | tf_op jit(solution)/shard_map/reshape | solution.py:113
  19.8 3.9 %reshape.336 = bf16[192,4,4,192]{3,2,1,0:T(4,128)(2,1)S(1)} reshape(bf16[192,3072]{1,0:T(8,128)(2,1)} %param.13) | data formatting | bytes 2359296 | tf_op jit(solution)/shard_map/reshape | solution.py:131
  23.7 2.6 dynamic-slice_reduce_fusion
  28.4 1.7 collective-permute-start.4
  30.0 2.5 collective-permute-start.3
  32.8 6.7 %collective-permute-done.4 = bf16[112,576]{0,1:T(8,128)(2,1)S(1)} collective-permute-done((bf16[112,576]{0,1:T(8,128)(2,1)}, bf16[112,576]{0,1:T(8,128)(2,1)S(1)}, u32[]{:S(2)}, u32[]{:S(2)}) %collective-permute-start.4) | collective-permute-done | bytes 129056 | tf_op jit(solution)/shard_map/ppermute | solution.py:64
  39.5 1.5 collective-permute-start.14
  48.7 3.7 %collective-permute-start.21 = (bf16[192,768]{1,0:T(8,128)(2,1)}, bf16[192,768]{1,0:T(8,128)(2,1)S(1)}, u32[]{:S(2)}, u32[]{:S(2)}) collective-permute-start(bf16[192,768]{1,0:T(8,128)(2,1)} %get-tuple-element.104), channel_id=1, source_target_pairs={{0,2},{1,3},{2,0},{3,1},{4,6},{5,7},{6,4},{7,5},{8,10},{9,11},{10,... | collective-permute-start | bytes 884744 | tf_op jit(solution)/shard_map/ppermute | solution.py:64
  62.3 9.8 %collective-permute-done.21 = bf16[192,768]{1,0:T(8,128)(2,1)S(1)} collective-permute-done((bf16[192,768]{1,0:T(8,128)(2,1)}, bf16[192,768]{1,0:T(8,128)(2,1)S(1)}, u32[]{:S(2)}, u32[]{:S(2)}) %collective-permute-start.21) | collective-permute-done | bytes 294944 | tf_op jit(solution)/shard_map/ppermute | solution.py:64
  75.1 2.2 fusion.8
  92.2 4.1 %collective-permute-done.18 = bf16[128,768]{1,0:T(8,128)(2,1)S(1)} collective-permute-done((bf16[128,768]{1,0:T(8,128)(2,1)S(1)}, bf16[128,768]{1,0:T(8,128)(2,1)S(1)}, u32[]{:S(2)}, u32[]{:S(2)}) %collective-permute-start.18) | collective-permute-done | bytes 196640 | tf_op jit(solution)/shard_map/ppermute | solution.py:61
  96.4 2.6 collective-permute-done.19
  100.4 2.0 multiply_convert_fusion
  102.4 1.9 fusion.95
  113.2 1.8 collective-permute-done.25
  120.3 1.5 collective-permute-start.27
  128.6 1.8 convolution_convert_fusion
  131.6 1.8 convolution_convert_fusion.1
  133.4 2.3 fusion.96
  137.8 2.4 collective-permute-start.32
  144.0 2.0 collective-permute-done.32
  146.1 1.9 collective-permute-done.31
  148.0 2.2 multiply_reduce_fusion.2
  153.8 1.5 collective-permute-start.33
  155.4 1.5 collective-permute-done.35
  161.9 1.5 convolution_convert_fusion.3
  163.4 1.7 fusion.97
  165.7 1.5 copy.142
  168.4 1.6 collective-permute-start.36
  172.5 3.8 %collective-permute-done.36 = bf16[128,768]{1,0:T(8,128)(2,1)S(1)} collective-permute-done((bf16[128,768]{1,0:T(8,128)(2,1)S(1)}, bf16[128,768]{1,0:T(8,128)(2,1)S(1)}, u32[]{:S(2)}, u32[]{:S(2)}) %collective-permute-start.36) | collective-permute-done | bytes 196640 | tf_op jit(solution)/shard_map/ppermute | solution.py:61
  176.3 3.1 %collective-permute-done.38 = bf16[128,768]{1,0:T(8,128)(2,1)S(1)} collective-permute-done((bf16[128,768]{1,0:T(8,128)(2,1)S(1)}, bf16[128,768]{1,0:T(8,128)(2,1)S(1)}, u32[]{:S(2)}, u32[]{:S(2)}) %collective-permute-start.38) | collective-permute-done | bytes 196640 | tf_op jit(solution)/shard_map/ppermute | solution.py:61
  181.7 5.4 %collective-permute-start.40 = (bf16[99,576]{1,0:T(8,128)(2,1)S(1)}, bf16[99,576]{1,0:T(8,128)(2,1)S(1)}, u32[]{:S(2)}, u32[]{:S(2)}) collective-permute-start(bf16[99,576]{1,0:T(8,128)(2,1)S(1)} %get-tuple-element.97), channel_id=1, source_target_pairs={{0,1},{1,0},{2,3},{3,2},{4,5},{5,4},{6,7},{7,6},{8,9},{9,8},{10,11... | collective-permute-start | bytes 342152 | tf_op jit(solution)/shard_map/ppermute | solution.py:64
  187.2 1.7 collective-permute-start.42
  189.1 1.5 collective-permute-start.48
  192.0 2.3 collective-permute-start.50
  194.4 1.7 collective-permute-start.49
  196.1 2.6 collective-permute-done.41
  198.8 2.4 collective-permute-start.45
  202.4 3.5 %collective-permute-start.51 = (bf16[24,768]{1,0:T(8,128)(2,1)S(1)}, bf16[24,768]{1,0:T(8,128)(2,1)S(1)}, u32[]{:S(2)}, u32[]{:S(2)}) collective-permute-start(bf16[24,768]{1,0:T(8,128)(2,1)S(1)} %get-tuple-element.121), channel_id=1, source_target_pairs={{0,1},{1,0},{2,3},{3,2},{4,5},{5,4},{6,7},{7,6},{8,9},{9,8},{10,11... | collective-permute-start | bytes 110600 | tf_op jit(solution)/shard_map/ppermute | solution.py:64
  205.9 2.0 collective-permute-start.53
  208.0 1.6 fusion.75
  209.8 2.3 collective-permute-start.59
  212.1 2.0 collective-permute-start.61
  214.3 3.3 %collective-permute-done.52 = bf16[24,768]{1,0:T(8,128)(2,1)S(1)} collective-permute-done((bf16[24,768]{1,0:T(8,128)(2,1)S(1)}, bf16[24,768]{1,0:T(8,128)(2,1)S(1)}, u32[]{:S(2)}, u32[]{:S(2)}) %collective-permute-start.52) | collective-permute-done | bytes 36896 | tf_op jit(solution)/shard_map/ppermute | solution.py:64
  217.6 1.9 collective-permute-start.56
  222.9 3.8 %collective-permute-done.61 = bf16[208,768]{1,0:T(8,128)(2,1)S(1)} collective-permute-done((bf16[208,768]{1,0:T(8,128)(2,1)S(1)}, bf16[208,768]{1,0:T(8,128)(2,1)S(1)}, u32[]{:S(2)}, u32[]{:S(2)}) %collective-permute-start.61) | collective-permute-done | bytes 319520 | tf_op jit(solution)/shard_map/ppermute | solution.py:64
  226.7 10.8 %collective-permute-done.60 = bf16[208,768]{1,0:T(8,128)(2,1)S(1)} collective-permute-done((bf16[208,768]{1,0:T(8,128)(2,1)S(1)}, bf16[208,768]{1,0:T(8,128)(2,1)S(1)}, u32[]{:S(2)}, u32[]{:S(2)}) %collective-permute-start.60) | collective-permute-done | bytes 319520 | tf_op jit(solution)/shard_map/ppermute | solution.py:64
  237.7 2.3 collective-permute-start.64
  241.5 6.1 %collective-permute-done.64 = bf16[208,768]{1,0:T(8,128)(2,1)S(1)} collective-permute-done((bf16[208,768]{1,0:T(8,128)(2,1)S(1)}, bf16[208,768]{1,0:T(8,128)(2,1)S(1)}, u32[]{:S(2)}, u32[]{:S(2)}) %collective-permute-start.64) | collective-permute-done | bytes 319520 | tf_op jit(solution)/shard_map/ppermute | solution.py:61
  247.6 3.3 %collective-permute-done.63 = bf16[208,768]{1,0:T(8,128)(2,1)S(1)} collective-permute-done((bf16[208,768]{1,0:T(8,128)(2,1)S(1)}, bf16[208,768]{1,0:T(8,128)(2,1)S(1)}, u32[]{:S(2)}, u32[]{:S(2)}) %collective-permute-start.63) | collective-permute-done | bytes 319520 | tf_op jit(solution)/shard_map/ppermute | solution.py:61
  255.8 1.8 collective-permute-done.46
  260.6 2.0 copy.149
  262.6 2.5 copy.150
  265.2 3.8 %reshape.350 = f32[192,2304]{1,0:T(8,128)} reshape(f32[2,96,3,4,192]{4,3,2,1,0:T(4,128)} %copy.150) | data formatting | bytes 3538944 | tf_op jit(solution)/shard_map/convert_element_type | solution.py:303
  269.0 1.7 fusion.32
  271.3 1.7 pad_maximum_fusion.3
  273.1 1.7 bitcast_convert_fusion
  274.7 3.6 %reshape.358 = f32[4,2,96,4,192]{4,3,2,1,0:T(4,128)S(1)} reshape(f32[4,2,96,768]{3,2,1,0:T(8,128)} %get-tuple-element.44) | data formatting | bytes 4718592 | tf_op jit(solution)/shard_map/convert_element_type | solution.py:241
  278.4 3.7 %copy.206 = f32[4,2,96,4,192]{4,0,3,2,1:T(4,128)} copy(f32[4,2,96,4,192]{4,3,2,1,0:T(4,128)S(1)} %reshape.358) | data formatting | bytes 4718592 | tf_op jit(solution)/shard_map/convert_element_type | solution.py:241
  282.0 4.9 %reshape.354 = f32[192,3072]{1,0:T(8,128)} reshape(f32[2,96,4,4,192]{4,3,2,1,0:T(4,128)} %bitcast.294) | data formatting | bytes 4718592 | tf_op jit(solution)/shard_map/convert_element_type | solution.py:241
  (394 shorter events, 104.7 us)
Async XLA Ops:
  1.6 26.8 %collective-permute-start.11 = (bf16[24,768]{1,0:T(8,128)(2,1)S(1)}, bf16[24,768]{1,0:T(8,128)(2,1)S(1)}, u32[]{:S(2)}, u32[]{:S(2)}) collective-permute-start(bf16[24,768]{1,0:T(8,128)(2,1)S(1)} %constant_dynamic-slice_fusion.27), channel_id=1, source_target_pairs={{0,2},{1,3},{2,0},{3,1},{4,6},{5,7},{6,4},{7,5},{8,10},{9,11},{10,... | collective-permute-start | bytes 110600 | tf_op jit(solution)/shard_map/ppermute | solution.py:64
  5.6 24.4 %collective-permute-start.10 = (bf16[24,768]{1,0:T(8,128)(2,1)S(1)}, bf16[24,768]{1,0:T(8,128)(2,1)S(1)}, u32[]{:S(2)}, u32[]{:S(2)}) collective-permute-start(bf16[24,768]{1,0:T(8,128)(2,1)S(1)} %constant_dynamic-slice_fusion.27), channel_id=1, source_target_pairs={{0,1},{1,0},{2,3},{3,2},{4,5},{5,4},{6,7},{7,6},{8,9},{9,8},{10,11... | collective-permute-start | bytes 110600 | tf_op jit(solution)/shard_map/ppermute | solution.py:64
  7.2 25.4 %collective-permute-start.12 = (bf16[24,768]{1,0:T(8,128)(2,1)S(1)}, bf16[24,768]{1,0:T(8,128)(2,1)S(1)}, u32[]{:S(2)}, u32[]{:S(2)}) collective-permute-start(bf16[24,768]{1,0:T(8,128)(2,1)S(1)} %constant_dynamic-slice_fusion.27), channel_id=1, source_target_pairs={{0,3},{1,2},{2,1},{3,0},{4,7},{5,6},{6,5},{7,4},{8,11},{9,10},{10,... | collective-permute-start | bytes 110600 | tf_op jit(solution)/shard_map/ppermute | solution.py:64
  9.5 44.9 %collective-permute-start.2 = (bf16[144,768]{1,0:T(8,128)(2,1)}, bf16[144,768]{1,0:T(8,128)(2,1)}, u32[]{:S(2)}, u32[]{:S(2)}) collective-permute-start(bf16[144,768]{1,0:T(8,128)(2,1)} %fusion.54), channel_id=1, source_target_pairs={{0,24},{4,28},{8,16},{12,20},{16,8},{20,12},{24,0},{28,4},{1,25},{... | collective-permute-start | bytes 663560 | tf_op jit(solution)/shard_map/ppermute | solution.py:61
  12.1 44.3 %collective-permute-start.1 = (bf16[144,768]{1,0:T(8,128)(2,1)}, bf16[144,768]{1,0:T(8,128)(2,1)}, u32[]{:S(2)}, u32[]{:S(2)}) collective-permute-start(bf16[144,768]{1,0:T(8,128)(2,1)} %fusion.54), channel_id=1, source_target_pairs={{0,16},{4,20},{8,24},{12,28},{16,0},{20,4},{24,8},{28,12},{1,17},{... | collective-permute-start | bytes 663560 | tf_op jit(solution)/shard_map/ppermute | solution.py:61
  28.4 11.2 %collective-permute-start.4 = (bf16[112,576]{0,1:T(8,128)(2,1)}, bf16[112,576]{0,1:T(8,128)(2,1)S(1)}, u32[]{:S(2)}, u32[]{:S(2)}) collective-permute-start(bf16[112,576]{0,1:T(8,128)(2,1)} %fusion.58), channel_id=1, source_target_pairs={{0,2},{1,3},{2,0},{3,1},{4,6},{5,7},{6,4},{7,5},{8,10},{9,11},{10,... | collective-permute-start | bytes 387080 | tf_op jit(solution)/shard_map/ppermute | solution.py:64
  30.0 11.0 %collective-permute-start.3 = (bf16[112,576]{0,1:T(8,128)(2,1)}, bf16[112,576]{0,1:T(8,128)(2,1)S(1)}, u32[]{:S(2)}, u32[]{:S(2)}) collective-permute-start(bf16[112,576]{0,1:T(8,128)(2,1)} %fusion.58), channel_id=1, source_target_pairs={{0,1},{1,0},{2,3},{3,2},{4,5},{5,4},{6,7},{7,6},{8,9},{9,8},{10,11... | collective-permute-start | bytes 387080 | tf_op jit(solution)/shard_map/ppermute | solution.py:64
  32.5 9.1 %collective-permute-start.5 = (bf16[112,576]{0,1:T(8,128)(2,1)}, bf16[112,576]{0,1:T(8,128)(2,1)S(1)}, u32[]{:S(2)}, u32[]{:S(2)}) collective-permute-start(bf16[112,576]{0,1:T(8,128)(2,1)} %fusion.58), channel_id=1, source_target_pairs={{0,3},{1,2},{2,1},{3,0},{4,7},{5,6},{6,5},{7,4},{8,11},{9,10},{10,... | collective-permute-start | bytes 387080 | tf_op jit(solution)/shard_map/ppermute | solution.py:64
  39.5 8.0 %collective-permute-start.14 = (bf16[4,24,768]{2,1,0:T(8,128)(2,1)S(1)}, bf16[4,24,768]{2,1,0:T(8,128)(2,1)S(1)}, u32[]{:S(2)}, u32[]{:S(2)}) collective-permute-start(bf16[4,24,768]{2,1,0:T(8,128)(2,1)S(1)} %get-tuple-element.125), channel_id=1, source_target_pairs={{0,16},{4,20},{8,24},{12,28},{16,0},{20,4},{24,8},{28,12},{1,17},{... | collective-permute-start | bytes 442376 | tf_op jit(solution)/shard_map/ppermute | solution.py:61
  41.0 7.6 %collective-permute-start.13 = (bf16[4,24,768]{2,1,0:T(8,128)(2,1)S(1)}, bf16[4,24,768]{2,1,0:T(8,128)(2,1)S(1)}, u32[]{:S(2)}, u32[]{:S(2)}) collective-permute-start(bf16[4,24,768]{2,1,0:T(8,128)(2,1)S(1)} %get-tuple-element.125), channel_id=1, source_target_pairs={{0,8},{4,12},{8,0},{12,4},{16,24},{20,28},{24,16},{28,20},{1,9},{5... | collective-permute-start | bytes 442376 | tf_op jit(solution)/shard_map/ppermute | solution.py:61
  41.6 10.8 %collective-permute-start.15 = (bf16[4,24,768]{2,1,0:T(8,128)(2,1)S(1)}, bf16[4,24,768]{2,1,0:T(8,128)(2,1)S(1)}, u32[]{:S(2)}, u32[]{:S(2)}) collective-permute-start(bf16[4,24,768]{2,1,0:T(8,128)(2,1)S(1)} %get-tuple-element.125), channel_id=1, source_target_pairs={{0,24},{4,28},{8,16},{12,20},{16,8},{20,12},{24,0},{28,4},{1,25},{... | collective-permute-start | bytes 442376 | tf_op jit(solution)/shard_map/ppermute | solution.py:61
  47.6 9.6 %collective-permute-start = (bf16[144,768]{1,0:T(8,128)(2,1)}, bf16[144,768]{1,0:T(8,128)(2,1)S(1)}, u32[]{:S(2)}, u32[]{:S(2)}) collective-permute-start(bf16[144,768]{1,0:T(8,128)(2,1)} %fusion.54), channel_id=1, source_target_pairs={{0,8},{4,12},{8,0},{12,4},{16,24},{20,28},{24,16},{28,20},{1,9},{5... | collective-permute-start | bytes 663560 | tf_op jit(solution)/shard_map/ppermute | solution.py:61
  48.7 23.4 %collective-permute-start.21 = (bf16[192,768]{1,0:T(8,128)(2,1)}, bf16[192,768]{1,0:T(8,128)(2,1)S(1)}, u32[]{:S(2)}, u32[]{:S(2)}) collective-permute-start(bf16[192,768]{1,0:T(8,128)(2,1)} %get-tuple-element.104), channel_id=1, source_target_pairs={{0,2},{1,3},{2,0},{3,1},{4,6},{5,7},{6,4},{7,5},{8,10},{9,11},{10,... | collective-permute-start | bytes 884744 | tf_op jit(solution)/shard_map/ppermute | solution.py:64
  52.4 19.7 %collective-permute-start.20 = (bf16[192,768]{1,0:T(8,128)(2,1)}, bf16[192,768]{1,0:T(8,128)(2,1)S(1)}, u32[]{:S(2)}, u32[]{:S(2)}) collective-permute-start(bf16[192,768]{1,0:T(8,128)(2,1)} %get-tuple-element.104), channel_id=1, source_target_pairs={{0,1},{1,0},{2,3},{3,2},{4,5},{5,4},{6,7},{7,6},{8,9},{9,8},{10,11... | collective-permute-start | bytes 884744 | tf_op jit(solution)/shard_map/ppermute | solution.py:64
  54.4 17.7 %collective-permute-start.22 = (bf16[192,768]{1,0:T(8,128)(2,1)}, bf16[192,768]{1,0:T(8,128)(2,1)S(1)}, u32[]{:S(2)}, u32[]{:S(2)}) collective-permute-start(bf16[192,768]{1,0:T(8,128)(2,1)} %get-tuple-element.104), channel_id=1, source_target_pairs={{0,3},{1,2},{2,1},{3,0},{4,7},{5,6},{6,5},{7,4},{8,11},{9,10},{10,... | collective-permute-start | bytes 884744 | tf_op jit(solution)/shard_map/ppermute | solution.py:64
  56.5 15.9 %collective-permute-start.6 = (bf16[4,96,576]{2,1,0:T(8,128)(2,1)}, bf16[4,96,576]{2,1,0:T(8,128)(2,1)}, u32[]{:S(2)}, u32[]{:S(2)}) collective-permute-start(bf16[4,96,576]{2,1,0:T(8,128)(2,1)} %copy.122), channel_id=1, source_target_pairs={{0,4},{4,0},{8,12},{12,8},{16,20},{20,16},{24,28},{28,24},{1,5},{5... | collective-permute-start | bytes 1327112 | tf_op jit(solution)/shard_map/ppermute | solution.py:58
  57.1 29.1 %collective-permute-start.16 = (bf16[4,4,24,768]{3,2,0,1:T(8,128)(2,1)}, bf16[4,4,24,768]{3,2,0,1:T(8,128)(2,1)}, u32[]{:S(2)}, u32[]{:S(2)}) collective-permute-start(bf16[4,4,24,768]{3,2,0,1:T(8,128)(2,1)} %pad_maximum_fusion.17), channel_id=1, source_target_pairs={{0,4},{4,0},{8,12},{12,8},{16,20},{20,16},{24,28},{28,24},{1,5},{5... | collective-permute-start | bytes 1769480 | tf_op jit(solution)/shard_map/ppermute | solution.py:58
  80.0 5.2 %collective-permute-start.9 = (bf16[128,192]{0,1:T(8,128)(2,1)S(1)}, bf16[128,192]{0,1:T(8,128)(2,1)S(1)}, u32[]{:S(2)}, u32[]{:S(2)}) collective-permute-start(bf16[128,192]{0,1:T(8,128)(2,1)S(1)} %bitcast.353), channel_id=1, source_target_pairs={{0,24},{4,28},{8,16},{12,20},{16,8},{20,12},{24,0},{28,4},{1,25},{... | collective-permute-start | bytes 147464 | tf_op jit(solution)/shard_map/ppermute | solution.py:61
  80.6 4.6 %collective-permute-start.8 = (bf16[128,192]{0,1:T(8,128)(2,1)S(1)}, bf16[128,192]{0,1:T(8,128)(2,1)S(1)}, u32[]{:S(2)}, u32[]{:S(2)}) collective-permute-start(bf16[128,192]{0,1:T(8,128)(2,1)S(1)} %bitcast.351), channel_id=1, source_target_pairs={{0,16},{4,20},{8,24},{12,28},{16,0},{20,4},{24,8},{28,12},{1,17},{... | collective-permute-start | bytes 147464 | tf_op jit(solution)/shard_map/ppermute | solution.py:61
  82.1 4.1 %collective-permute-start.7 = (bf16[128,192]{0,1:T(8,128)(2,1)S(1)}, bf16[128,192]{0,1:T(8,128)(2,1)S(1)}, u32[]{:S(2)}, u32[]{:S(2)}) collective-permute-start(bf16[128,192]{0,1:T(8,128)(2,1)S(1)} %bitcast.349), channel_id=1, source_target_pairs={{0,8},{4,12},{8,0},{12,4},{16,24},{20,28},{24,16},{28,20},{1,9},{5... | collective-permute-start | bytes 147464 | tf_op jit(solution)/shard_map/ppermute | solution.py:61
  83.7 15.4 %collective-permute-start.23 = (bf16[4,192,768]{2,1,0:T(8,128)(2,1)S(1)}, bf16[4,192,768]{2,1,0:T(8,128)(2,1)S(1)}, u32[]{:S(2)}, u32[]{:S(2)}) collective-permute-start(bf16[4,192,768]{2,1,0:T(8,128)(2,1)S(1)} %pad_maximum_fusion.7), channel_id=1, source_target_pairs={{0,4},{4,0},{8,12},{12,8},{16,20},{20,16},{24,28},{28,24},{1,5},{5... | collective-permute-start | bytes 3538952 | tf_op jit(solution)/shard_map/ppermute | solution.py:58
  88.5 7.8 %collective-permute-start.18 = (bf16[128,768]{1,0:T(8,128)(2,1)S(1)}, bf16[128,768]{1,0:T(8,128)(2,1)S(1)}, u32[]{:S(2)}, u32[]{:S(2)}) collective-permute-start(bf16[128,768]{1,0:T(8,128)(2,1)S(1)} %fusion.47), channel_id=1, source_target_pairs={{0,16},{4,20},{8,24},{12,28},{16,0},{20,4},{24,8},{28,12},{1,17},{... | collective-permute-start | bytes 589832 | tf_op jit(solution)/shard_map/ppermute | solution.py:61
  89.1 7.3 %collective-permute-start.17 = (bf16[128,768]{1,0:T(8,128)(2,1)S(1)}, bf16[128,768]{1,0:T(8,128)(2,1)S(1)}, u32[]{:S(2)}, u32[]{:S(2)}) collective-permute-start(bf16[128,768]{1,0:T(8,128)(2,1)S(1)} %fusion.47), channel_id=1, source_target_pairs={{0,8},{4,12},{8,0},{12,4},{16,24},{20,28},{24,16},{28,20},{1,9},{5... | collective-permute-start | bytes 589832 | tf_op jit(solution)/shard_map/ppermute | solution.py:61
  90.6 8.4 %collective-permute-start.19 = (bf16[128,768]{1,0:T(8,128)(2,1)S(1)}, bf16[128,768]{1,0:T(8,128)(2,1)S(1)}, u32[]{:S(2)}, u32[]{:S(2)}) collective-permute-start(bf16[128,768]{1,0:T(8,128)(2,1)S(1)} %fusion.47), channel_id=1, source_target_pairs={{0,24},{4,28},{8,16},{12,20},{16,8},{20,12},{24,0},{28,4},{1,25},{... | collective-permute-start | bytes 589832 | tf_op jit(solution)/shard_map/ppermute | solution.py:61
  105.1 7.4 %collective-permute-start.24 = (bf16[128,768]{1,0:T(8,128)(2,1)}, bf16[128,768]{1,0:T(8,128)(2,1)S(1)}, u32[]{:S(2)}, u32[]{:S(2)}) collective-permute-start(bf16[128,768]{1,0:T(8,128)(2,1)} %get-tuple-element.76), channel_id=1, source_target_pairs={{0,8},{4,12},{8,0},{12,4},{16,24},{20,28},{24,16},{28,20},{1,9},{5... | collective-permute-start | bytes 589832 | tf_op jit(solution)/shard_map/ppermute | solution.py:61
  105.6 7.5 %collective-permute-start.26 = (bf16[128,768]{1,0:T(8,128)(2,1)}, bf16[128,768]{1,0:T(8,128)(2,1)S(1)}, u32[]{:S(2)}, u32[]{:S(2)}) collective-permute-start(bf16[128,768]{1,0:T(8,128)(2,1)} %get-tuple-element.77), channel_id=1, source_target_pairs={{0,24},{4,28},{8,16},{12,20},{16,8},{20,12},{24,0},{28,4},{1,25},{... | collective-permute-start | bytes 589832 | tf_op jit(solution)/shard_map/ppermute | solution.py:61
  107.1 7.9 %collective-permute-start.25 = (bf16[128,768]{1,0:T(8,128)(2,1)S(1)}, bf16[128,768]{1,0:T(8,128)(2,1)}, u32[]{:S(2)}, u32[]{:S(2)}) collective-permute-start(bf16[128,768]{1,0:T(8,128)(2,1)S(1)} %get-tuple-element.78), channel_id=1, source_target_pairs={{0,16},{4,20},{8,24},{12,28},{16,0},{20,4},{24,8},{28,12},{1,17},{... | collective-permute-start | bytes 589832 | tf_op jit(solution)/shard_map/ppermute | solution.py:61
  118.2 8.9 %collective-permute-start.29 = (bf16[128,768]{1,0:T(8,128)(2,1)S(1)}, bf16[128,768]{1,0:T(8,128)(2,1)}, u32[]{:S(2)}, u32[]{:S(2)}) collective-permute-start(bf16[128,768]{1,0:T(8,128)(2,1)S(1)} %get-tuple-element.34), channel_id=1, source_target_pairs={{0,24},{4,28},{8,16},{12,20},{16,8},{20,12},{24,0},{28,4},{1,25},{... | collective-permute-start | bytes 589832 | tf_op jit(solution)/shard_map/ppermute | solution.py:61
  119.7 7.5 %collective-permute-start.28 = (bf16[128,768]{1,0:T(8,128)(2,1)S(1)}, bf16[128,768]{1,0:T(8,128)(2,1)}, u32[]{:S(2)}, u32[]{:S(2)}) collective-permute-start(bf16[128,768]{1,0:T(8,128)(2,1)S(1)} %get-tuple-element.34), channel_id=1, source_target_pairs={{0,16},{4,20},{8,24},{12,28},{16,0},{20,4},{24,8},{28,12},{1,17},{... | collective-permute-start | bytes 589832 | tf_op jit(solution)/shard_map/ppermute | solution.py:61
  120.3 6.9 %collective-permute-start.27 = (bf16[128,768]{1,0:T(8,128)(2,1)S(1)}, bf16[128,768]{1,0:T(8,128)(2,1)}, u32[]{:S(2)}, u32[]{:S(2)}) collective-permute-start(bf16[128,768]{1,0:T(8,128)(2,1)S(1)} %get-tuple-element.34), channel_id=1, source_target_pairs={{0,8},{4,12},{8,0},{12,4},{16,24},{20,28},{24,16},{28,20},{1,9},{5... | collective-permute-start | bytes 589832 | tf_op jit(solution)/shard_map/ppermute | solution.py:61
  137.2 6.9 %collective-permute-start.30 = (bf16[128,768]{1,0:T(8,128)(2,1)S(1)}, bf16[128,768]{1,0:T(8,128)(2,1)S(1)}, u32[]{:S(2)}, u32[]{:S(2)}) collective-permute-start(bf16[128,768]{1,0:T(8,128)(2,1)S(1)} %get-tuple-element.73), channel_id=1, source_target_pairs={{0,8},{4,12},{8,0},{12,4},{16,24},{20,28},{24,16},{28,20},{1,9},{5... | collective-permute-start | bytes 589832 | tf_op jit(solution)/shard_map/ppermute | solution.py:61
  137.8 8.3 %collective-permute-start.32 = (bf16[128,768]{1,0:T(8,128)(2,1)S(1)}, bf16[128,768]{1,0:T(8,128)(2,1)S(1)}, u32[]{:S(2)}, u32[]{:S(2)}) collective-permute-start(bf16[128,768]{1,0:T(8,128)(2,1)S(1)} %get-tuple-element.74), channel_id=1, source_target_pairs={{0,24},{4,28},{8,16},{12,20},{16,8},{20,12},{24,0},{28,4},{1,25},{... | collective-permute-start | bytes 589832 | tf_op jit(solution)/shard_map/ppermute | solution.py:61
  140.2 7.8 %collective-permute-start.31 = (bf16[128,768]{1,0:T(8,128)(2,1)S(1)}, bf16[128,768]{1,0:T(8,128)(2,1)S(1)}, u32[]{:S(2)}, u32[]{:S(2)}) collective-permute-start(bf16[128,768]{1,0:T(8,128)(2,1)S(1)} %get-tuple-element.75), channel_id=1, source_target_pairs={{0,16},{4,20},{8,24},{12,28},{16,0},{20,4},{24,8},{28,12},{1,17},{... | collective-permute-start | bytes 589832 | tf_op jit(solution)/shard_map/ppermute | solution.py:61
  144.0 61.9 %collective-permute-start.58 = (bf16[4,208,768]{2,1,0:T(8,128)(2,1)}, bf16[4,208,768]{2,1,0:T(8,128)(2,1)}, u32[]{:S(2)}, u32[]{:S(2)}) collective-permute-start(bf16[4,208,768]{2,1,0:T(8,128)(2,1)} %dynamic-slice_bitcast_fusion), channel_id=1, source_target_pairs={{0,4},{4,0},{8,12},{12,8},{16,20},{20,16},{24,28},{28,24},{1,5},{5... | collective-permute-start | bytes 3833864 | tf_op jit(solution)/shard_map/ppermute | solution.py:58
  151.5 5.5 %collective-permute-start.35 = (bf16[128,192]{0,1:T(8,128)(2,1)S(1)}, bf16[128,192]{0,1:T(8,128)(2,1)S(1)}, u32[]{:S(2)}, u32[]{:S(2)}) collective-permute-start(bf16[128,192]{0,1:T(8,128)(2,1)S(1)} %get-tuple-element.106), channel_id=1, source_target_pairs={{0,24},{4,28},{8,16},{12,20},{16,8},{20,12},{24,0},{28,4},{1,25},{... | collective-permute-start | bytes 147464 | tf_op jit(solution)/shard_map/ppermute | solution.py:61
  152.4 4.6 %collective-permute-start.34 = (bf16[128,192]{0,1:T(8,128)(2,1)S(1)}, bf16[128,192]{0,1:T(8,128)(2,1)S(1)}, u32[]{:S(2)}, u32[]{:S(2)}) collective-permute-start(bf16[128,192]{0,1:T(8,128)(2,1)S(1)} %get-tuple-element.107), channel_id=1, source_target_pairs={{0,16},{4,20},{8,24},{12,28},{16,0},{20,4},{24,8},{28,12},{1,17},{... | collective-permute-start | bytes 147464 | tf_op jit(solution)/shard_map/ppermute | solution.py:61
  167.5 14.0 %collective-permute-start.39 = (bf16[4,99,576]{2,0,1:T(4,128)(2,1)S(1)}, bf16[4,99,576]{2,0,1:T(4,128)(2,1)S(1)}, u32[]{:S(2)}, u32[]{:S(2)}) collective-permute-start(bf16[4,99,576]{2,0,1:T(4,128)(2,1)S(1)} %copy.144), channel_id=1, source_target_pairs={{0,4},{4,0},{8,12},{12,8},{16,20},{20,16},{24,28},{28,24},{1,5},{5... | collective-permute-start | bytes 1368584 | tf_op jit(solution)/shard_map/ppermute | solution.py:58
  168.4 7.9 %collective-permute-start.36 = (bf16[128,768]{1,0:T(8,128)(2,1)S(1)}, bf16[128,768]{1,0:T(8,128)(2,1)S(1)}, u32[]{:S(2)}, u32[]{:S(2)}) collective-permute-start(bf16[128,768]{1,0:T(8,128)(2,1)S(1)} %get-tuple-element.70), channel_id=1, source_target_pairs={{0,8},{4,12},{8,0},{12,4},{16,24},{20,28},{24,16},{28,20},{1,9},{5... | collective-permute-start | bytes 589832 | tf_op jit(solution)/shard_map/ppermute | solution.py:61
  170.0 9.3 %collective-permute-start.38 = (bf16[128,768]{1,0:T(8,128)(2,1)S(1)}, bf16[128,768]{1,0:T(8,128)(2,1)S(1)}, u32[]{:S(2)}, u32[]{:S(2)}) collective-permute-start(bf16[128,768]{1,0:T(8,128)(2,1)S(1)} %get-tuple-element.71), channel_id=1, source_target_pairs={{0,24},{4,28},{8,16},{12,20},{16,8},{20,12},{24,0},{28,4},{1,25},{... | collective-permute-start | bytes 589832 | tf_op jit(solution)/shard_map/ppermute | solution.py:61
  170.5 10.2 %collective-permute-start.37 = (bf16[128,768]{1,0:T(8,128)(2,1)S(1)}, bf16[128,768]{1,0:T(8,128)(2,1)S(1)}, u32[]{:S(2)}, u32[]{:S(2)}) collective-permute-start(bf16[128,768]{1,0:T(8,128)(2,1)S(1)} %get-tuple-element.72), channel_id=1, source_target_pairs={{0,16},{4,20},{8,24},{12,28},{16,0},{20,4},{24,8},{28,12},{1,17},{... | collective-permute-start | bytes 589832 | tf_op jit(solution)/shard_map/ppermute | solution.py:61
  176.3 12.6 %collective-permute-start.47 = (bf16[4,4,24,768]{3,2,0,1:T(8,128)(2,1)S(1)}, bf16[4,4,24,768]{3,2,0,1:T(8,128)(2,1)S(1)}, u32[]{:S(2)}, u32[]{:S(2)}) collective-permute-start(bf16[4,4,24,768]{3,2,0,1:T(8,128)(2,1)S(1)} %dynamic-slice_bitcast_fusion.1), channel_id=1, source_target_pairs={{0,4},{4,0},{8,12},{12,8},{16,20},{20,16},{24,28},{28,24},{1,5},{5... | collective-permute-start | bytes 1769480 | tf_op jit(solution)/shard_map/ppermute | solution.py:58
  181.7 10.3 %collective-permute-start.40 = (bf16[99,576]{1,0:T(8,128)(2,1)S(1)}, bf16[99,576]{1,0:T(8,128)(2,1)S(1)}, u32[]{:S(2)}, u32[]{:S(2)}) collective-permute-start(bf16[99,576]{1,0:T(8,128)(2,1)S(1)} %get-tuple-element.97), channel_id=1, source_target_pairs={{0,1},{1,0},{2,3},{3,2},{4,5},{5,4},{6,7},{7,6},{8,9},{9,8},{10,11... | collective-permute-start | bytes 342152 | tf_op jit(solution)/shard_map/ppermute | solution.py:64
  187.2 7.3 %collective-permute-start.42 = (bf16[99,576]{1,0:T(8,128)(2,1)S(1)}, bf16[99,576]{1,0:T(8,128)(2,1)S(1)}, u32[]{:S(2)}, u32[]{:S(2)}) collective-permute-start(bf16[99,576]{1,0:T(8,128)(2,1)S(1)} %get-tuple-element.98), channel_id=1, source_target_pairs={{0,3},{1,2},{2,1},{3,0},{4,7},{5,6},{6,5},{7,4},{8,11},{9,10},{10,... | collective-permute-start | bytes 342152 | tf_op jit(solution)/shard_map/ppermute | solution.py:64
  188.8 9.9 %collective-permute-start.41 = (bf16[99,576]{1,0:T(8,128)(2,1)S(1)}, bf16[99,576]{1,0:T(8,128)(2,1)S(1)}, u32[]{:S(2)}, u32[]{:S(2)}) collective-permute-start(bf16[99,576]{1,0:T(8,128)(2,1)S(1)} %get-tuple-element.99), channel_id=1, source_target_pairs={{0,2},{1,3},{2,0},{3,1},{4,6},{5,7},{6,4},{7,5},{8,10},{9,11},{10,... | collective-permute-start | bytes 342152 | tf_op jit(solution)/shard_map/ppermute | solution.py:64
  189.1 12.1 %collective-permute-start.48 = (bf16[4,24,768]{2,1,0:T(8,128)(2,1)S(1)}, bf16[4,24,768]{2,1,0:T(8,128)(2,1)S(1)}, u32[]{:S(2)}, u32[]{:S(2)}) collective-permute-start(bf16[4,24,768]{2,1,0:T(8,128)(2,1)S(1)} %get-tuple-element.79), channel_id=1, source_target_pairs={{0,8},{4,12},{8,0},{12,4},{16,24},{20,28},{24,16},{28,20},{1,9},{5... | collective-permute-start | bytes 442376 | tf_op jit(solution)/shard_map/ppermute | solution.py:61
  192.0 9.7 %collective-permute-start.50 = (bf16[4,24,768]{2,1,0:T(8,128)(2,1)S(1)}, bf16[4,24,768]{2,1,0:T(8,128)(2,1)S(1)}, u32[]{:S(2)}, u32[]{:S(2)}) collective-permute-start(bf16[4,24,768]{2,1,0:T(8,128)(2,1)S(1)} %get-tuple-element.80), channel_id=1, source_target_pairs={{0,24},{4,28},{8,16},{12,20},{16,8},{20,12},{24,0},{28,4},{1,25},{... | collective-permute-start | bytes 442376 | tf_op jit(solution)/shard_map/ppermute | solution.py:61
  194.4 7.9 %collective-permute-start.49 = (bf16[4,24,768]{2,1,0:T(8,128)(2,1)S(1)}, bf16[4,24,768]{2,1,0:T(8,128)(2,1)S(1)}, u32[]{:S(2)}, u32[]{:S(2)}) collective-permute-start(bf16[4,24,768]{2,1,0:T(8,128)(2,1)S(1)} %get-tuple-element.81), channel_id=1, source_target_pairs={{0,16},{4,20},{8,24},{12,28},{16,0},{20,4},{24,8},{28,12},{1,17},{... | collective-permute-start | bytes 442376 | tf_op jit(solution)/shard_map/ppermute | solution.py:61
  198.8 10.9 %collective-permute-start.45 = (bf16[99,576]{1,0:T(8,128)(2,1)S(1)}, bf16[99,576]{1,0:T(8,128)(2,1)S(1)}, u32[]{:S(2)}, u32[]{:S(2)}) collective-permute-start(bf16[99,576]{1,0:T(8,128)(2,1)S(1)} %fusion.53), channel_id=1, source_target_pairs={{0,24},{4,28},{8,16},{12,20},{16,8},{20,12},{24,0},{28,4},{1,25},{... | collective-permute-start | bytes 342152 | tf_op jit(solution)/shard_map/ppermute | solution.py:61
  201.2 8.6 %collective-permute-start.44 = (bf16[99,576]{1,0:T(8,128)(2,1)S(1)}, bf16[99,576]{1,0:T(8,128)(2,1)S(1)}, u32[]{:S(2)}, u32[]{:S(2)}) collective-permute-start(bf16[99,576]{1,0:T(8,128)(2,1)S(1)} %fusion.53), channel_id=1, source_target_pairs={{0,16},{4,20},{8,24},{12,28},{16,0},{20,4},{24,8},{28,12},{1,17},{... | collective-permute-start | bytes 342152 | tf_op jit(solution)/shard_map/ppermute | solution.py:61
  201.7 10.4 %collective-permute-start.43 = (bf16[99,576]{1,0:T(8,128)(2,1)S(1)}, bf16[99,576]{1,0:T(8,128)(2,1)S(1)}, u32[]{:S(2)}, u32[]{:S(2)}) collective-permute-start(bf16[99,576]{1,0:T(8,128)(2,1)S(1)} %fusion.53), channel_id=1, source_target_pairs={{0,8},{4,12},{8,0},{12,4},{16,24},{20,28},{24,16},{28,20},{1,9},{5... | collective-permute-start | bytes 342152 | tf_op jit(solution)/shard_map/ppermute | solution.py:61
  202.4 11.7 %collective-permute-start.51 = (bf16[24,768]{1,0:T(8,128)(2,1)S(1)}, bf16[24,768]{1,0:T(8,128)(2,1)S(1)}, u32[]{:S(2)}, u32[]{:S(2)}) collective-permute-start(bf16[24,768]{1,0:T(8,128)(2,1)S(1)} %get-tuple-element.121), channel_id=1, source_target_pairs={{0,1},{1,0},{2,3},{3,2},{4,5},{5,4},{6,7},{7,6},{8,9},{9,8},{10,11... | collective-permute-start | bytes 110600 | tf_op jit(solution)/shard_map/ppermute | solution.py:64
  205.9 8.3 %collective-permute-start.53 = (bf16[24,768]{1,0:T(8,128)(2,1)S(1)}, bf16[24,768]{1,0:T(8,128)(2,1)S(1)}, u32[]{:S(2)}, u32[]{:S(2)}) collective-permute-start(bf16[24,768]{1,0:T(8,128)(2,1)S(1)} %get-tuple-element.122), channel_id=1, source_target_pairs={{0,3},{1,2},{2,1},{3,0},{4,7},{5,6},{6,5},{7,4},{8,11},{9,10},{10,... | collective-permute-start | bytes 110600 | tf_op jit(solution)/shard_map/ppermute | solution.py:64
  209.7 7.9 %collective-permute-start.52 = (bf16[24,768]{1,0:T(8,128)(2,1)S(1)}, bf16[24,768]{1,0:T(8,128)(2,1)S(1)}, u32[]{:S(2)}, u32[]{:S(2)}) collective-permute-start(bf16[24,768]{1,0:T(8,128)(2,1)S(1)} %get-tuple-element.123), channel_id=1, source_target_pairs={{0,2},{1,3},{2,0},{3,1},{4,6},{5,7},{6,4},{7,5},{8,10},{9,11},{10,... | collective-permute-start | bytes 110600 | tf_op jit(solution)/shard_map/ppermute | solution.py:64
  209.8 11.8 %collective-permute-start.59 = (bf16[208,768]{1,0:T(8,128)(2,1)S(1)}, bf16[208,768]{1,0:T(8,128)(2,1)S(1)}, u32[]{:S(2)}, u32[]{:S(2)}) collective-permute-start(bf16[208,768]{1,0:T(8,128)(2,1)S(1)} %get-tuple-element.53), channel_id=1, source_target_pairs={{0,1},{1,0},{2,3},{3,2},{4,5},{5,4},{6,7},{7,6},{8,9},{9,8},{10,11... | collective-permute-start | bytes 958472 | tf_op jit(solution)/shard_map/ppermute | solution.py:64
  212.1 14.6 %collective-permute-start.61 = (bf16[208,768]{1,0:T(8,128)(2,1)S(1)}, bf16[208,768]{1,0:T(8,128)(2,1)S(1)}, u32[]{:S(2)}, u32[]{:S(2)}) collective-permute-start(bf16[208,768]{1,0:T(8,128)(2,1)S(1)} %get-tuple-element.54), channel_id=1, source_target_pairs={{0,3},{1,2},{2,1},{3,0},{4,7},{5,6},{6,5},{7,4},{8,11},{9,10},{10,... | collective-permute-start | bytes 958472 | tf_op jit(solution)/shard_map/ppermute | solution.py:64
  214.1 23.4 %collective-permute-start.60 = (bf16[208,768]{1,0:T(8,128)(2,1)S(1)}, bf16[208,768]{1,0:T(8,128)(2,1)S(1)}, u32[]{:S(2)}, u32[]{:S(2)}) collective-permute-start(bf16[208,768]{1,0:T(8,128)(2,1)S(1)} %get-tuple-element.55), channel_id=1, source_target_pairs={{0,2},{1,3},{2,0},{3,1},{4,6},{5,7},{6,4},{7,5},{8,10},{9,11},{10,... | collective-permute-start | bytes 958472 | tf_op jit(solution)/shard_map/ppermute | solution.py:64
  217.6 23.0 %collective-permute-start.56 = (bf16[24,768]{1,0:T(8,128)(2,1)S(1)}, bf16[24,768]{1,0:T(8,128)(2,1)S(1)}, u32[]{:S(2)}, u32[]{:S(2)}) collective-permute-start(bf16[24,768]{1,0:T(8,128)(2,1)S(1)} %fusion.61), channel_id=1, source_target_pairs={{0,24},{4,28},{8,16},{12,20},{16,8},{20,12},{24,0},{28,4},{1,25},{... | collective-permute-start | bytes 110600 | tf_op jit(solution)/shard_map/ppermute | solution.py:61
  219.5 21.8 %collective-permute-start.55 = (bf16[24,768]{1,0:T(8,128)(2,1)S(1)}, bf16[24,768]{1,0:T(8,128)(2,1)S(1)}, u32[]{:S(2)}, u32[]{:S(2)}) collective-permute-start(bf16[24,768]{1,0:T(8,128)(2,1)S(1)} %fusion.61), channel_id=1, source_target_pairs={{0,16},{4,20},{8,24},{12,28},{16,0},{20,4},{24,8},{28,12},{1,17},{... | collective-permute-start | bytes 110600 | tf_op jit(solution)/shard_map/ppermute | solution.py:61
  221.6 19.8 %collective-permute-start.54 = (bf16[24,768]{1,0:T(8,128)(2,1)S(1)}, bf16[24,768]{1,0:T(8,128)(2,1)S(1)}, u32[]{:S(2)}, u32[]{:S(2)}) collective-permute-start(bf16[24,768]{1,0:T(8,128)(2,1)S(1)} %fusion.61), channel_id=1, source_target_pairs={{0,8},{4,12},{8,0},{12,4},{16,24},{20,28},{24,16},{28,20},{1,9},{5... | collective-permute-start | bytes 110600 | tf_op jit(solution)/shard_map/ppermute | solution.py:61
  237.7 9.9 %collective-permute-start.64 = (bf16[208,768]{1,0:T(8,128)(2,1)S(1)}, bf16[208,768]{1,0:T(8,128)(2,1)S(1)}, u32[]{:S(2)}, u32[]{:S(2)}) collective-permute-start(bf16[208,768]{1,0:T(8,128)(2,1)S(1)} %fusion.21), channel_id=1, source_target_pairs={{0,24},{4,28},{8,16},{12,20},{16,8},{20,12},{24,0},{28,4},{1,25},{... | collective-permute-start | bytes 958472 | tf_op jit(solution)/shard_map/ppermute | solution.py:61
  240.0 10.9 %collective-permute-start.63 = (bf16[208,768]{1,0:T(8,128)(2,1)S(1)}, bf16[208,768]{1,0:T(8,128)(2,1)S(1)}, u32[]{:S(2)}, u32[]{:S(2)}) collective-permute-start(bf16[208,768]{1,0:T(8,128)(2,1)S(1)} %fusion.21), channel_id=1, source_target_pairs={{0,16},{4,20},{8,24},{12,28},{16,0},{20,4},{24,8},{28,12},{1,17},{... | collective-permute-start | bytes 958472 | tf_op jit(solution)/shard_map/ppermute | solution.py:61
  240.6 11.8 %collective-permute-start.62 = (bf16[208,768]{1,0:T(8,128)(2,1)S(1)}, bf16[208,768]{1,0:T(8,128)(2,1)S(1)}, u32[]{:S(2)}, u32[]{:S(2)}) collective-permute-start(bf16[208,768]{1,0:T(8,128)(2,1)S(1)} %fusion.21), channel_id=1, source_target_pairs={{0,8},{4,12},{8,0},{12,4},{16,24},{20,28},{24,16},{28,20},{1,9},{5... | collective-permute-start | bytes 958472 | tf_op jit(solution)/shard_map/ppermute | solution.py:61
  241.4 13.4 %collective-permute-start.57 = (bf16[4,24,768]{2,1,0:T(8,128)(2,1)S(1)}, bf16[4,24,768]{2,1,0:T(8,128)(2,1)S(1)}, u32[]{:S(2)}, u32[]{:S(2)}) collective-permute-start(bf16[4,24,768]{2,1,0:T(8,128)(2,1)S(1)} %pad_maximum_fusion.30), channel_id=1, source_target_pairs={{0,4},{4,0},{8,12},{12,8},{16,20},{20,16},{24,28},{28,24},{1,5},{5... | collective-permute-start | bytes 442376 | tf_op jit(solution)/shard_map/ppermute | solution.py:58
  253.9 15.1 %collective-permute-start.65 = (bf16[4,208,768]{2,1,0:T(8,128)(2,1)}, bf16[4,208,768]{2,1,0:T(8,128)(2,1)}, u32[]{:S(2)}, u32[]{:S(2)}) collective-permute-start(bf16[4,208,768]{2,1,0:T(8,128)(2,1)} %pad_maximum_fusion.2), channel_id=1, source_target_pairs={{0,4},{4,0},{8,12},{12,8},{16,20},{20,16},{24,28},{28,24},{1,5},{5... | collective-permute-start | bytes 3833864 | tf_op jit(solution)/shard_map/ppermute | solution.py:58
  (62 other events, 279.5 us)

commit v2 on v1

v2 whole, which is shorter than its diff:
```python
import functools
import math

import jax
import jax.numpy as jnp
from jax import lax
from jax.experimental import pallas as pl
from jax.experimental.pallas import tpu as pltpu
from jax.sharding import PartitionSpec as P

HEADS = 12
HEAD_DIM = 64
PARTS = 4
CORES = 2
layer_eps = 1e-12
masked_score = -1000000000.0
BF = jnp.bfloat16
F32 = jnp.float32
VMEM_BYTES = 48 * 1024 * 1024
PACK_BYTES = 62 * 1024 * 1024
COST = 11 * 10**9


def mm(a, b):
    return jnp.dot(a, b, preferred_element_type=F32)


def mm_ta(a, b):
    return lax.dot_general(a, b, (((0,), (0,)), ((), ())), preferred_element_type=F32)


def mm_tb(a, b):
    return lax.dot_general(a, b, (((1,), (1,)), ((), ())), preferred_element_type=F32)


def at(start, size, unit):
    return pl.ds(pl.multiple_of(start, unit), size)


def norm_stats(h):
    centre = h - jnp.mean(h, axis=-1, keepdims=True)
    inv = lax.rsqrt(jnp.mean(centre * centre, axis=-1, keepdims=True) + layer_eps)
    return centre * inv, inv


def norm_back(g, unit, inv, gain):
    gg = g * gain
    m1 = jnp.mean(gg, axis=-1, keepdims=True)
    m2 = jnp.mean(gg * unit, axis=-1, keepdims=True)
    return inv * (gg - m1 - unit * m2)


def gelu_parts(u):
    phi = 0.5 * (1.0 + lax.erf(u * (1.0 / math.sqrt(2.0))))
    dens = jnp.exp(-0.5 * u * u) * (1.0 / math.sqrt(2.0 * math.pi))
    return phi, phi + u * dens


def col_sum(v):
    return jnp.sum(v, axis=0, keepdims=True)


def fold_piece(put, get, cols):
    put(0, 0, get(0, 0, cols))
    put(1, 0, get(1, 0, cols))
    put(0, cols, get(2, 0, cols // 2))
    put(1, cols, get(2, cols // 2, cols // 2))


def pack_kernel(idx, tok, wqkv, wout, vec_in, gain_in, hid_in, lens_in, xp, pay, bq, bo, vec, gain, hid, lens, sem):
    rows, width = tok.shape
    half = bq.shape[0]
    piece, ocol = bo.shape
    hc = width // PARTS
    fc = hid.shape[1] // PARTS
    load_q = pltpu.make_async_copy(wqkv.at[at(idx[1] * half, half, 32)], bq, sem.at[0])
    load_o = pltpu.make_async_copy(
        wout.at[at(idx[0] * piece, piece, 16), at(idx[1] * ocol, ocol, 128)], bo, sem.at[1]
    )
    load_x = pltpu.make_async_copy(tok, xp.at[:rows], sem.at[2])
    small = [
        pltpu.make_async_copy(a, b, sem.at[3 + n])
        for n, (a, b) in enumerate(
            ((vec_in, vec), (gain_in, gain), (hid_in, hid), (lens_in, lens))
        )
    ]
    load_q.start()
    load_x.start()
    load_o.start()
    for load in small:
        load.start()
    base = half + 16
    pay[half:base] = jnp.zeros((16, 3 * hc), BF)
    xp[rows:] = jnp.zeros((16, width), BF)
    for load in small:
        load.wait()
    xp[rows : rows + 1, : lens.shape[1]] = lens[...].astype(BF)
    for n in range(8):
        src = vec[n : n + 1, :] if n < 6 else gain[n - 6 : n - 5, :]
        pay[half + n // 3 : half + n // 3 + 1, (n % 3) * hc : (n % 3 + 1) * hc] = src
    load_o.wait()
    third = piece // 3

    def put(row, col, v):
        pay[base + row * third : base + (row + 1) * third, col : col + v.shape[1]] = v

    fold_piece(put, lambda g, col, n: bo[g * third : (g + 1) * third, col : col + n], ocol)
    load_q.wait()
    for j in range(PARTS):

        @pl.when(idx[0] == j)
        def _(j=j):
            pay[half + 2 : half + 3, 2 * hc :] = hid[:, j * fc : (j + 1) * fc]
            for s in range(3):
                pay[:half, s * hc : (s + 1) * hc] = bq[
                    :, s * width + j * hc : s * width + (j + 1) * hc
                ]

    load_x.wait()


def pack2_kernel(idx, wup, wdown, pay, bu, sem):
    half = bu.shape[0]
    fc = pay.shape[0] - half
    units = wdown.shape[0]
    shards = wup.shape[1] // units
    fpart = units // PARTS
    load_u = pltpu.make_async_copy(wup.at[at(idx[1] * half, half, 32)], bu, sem.at[0])
    load_d = pltpu.make_async_copy(
        wdown.at[at(idx[0] * fpart + idx[1] * fc, fc, 32)], pay.at[half:], sem.at[1]
    )
    load_u.start()
    load_d.start()
    load_u.wait()
    for j in range(PARTS):

        @pl.when(idx[0] == j)
        def _(j=j):
            for s in range(shards):
                base = (s * PARTS + j) * fpart
                pay[:half, s * fpart : (s + 1) * fpart] = bu[:, base : base + fpart]

    load_d.wait()


def split_kernel(g0, g1, g2, g3, first, second):
    base = first.shape[1]
    for k, g in enumerate((g0, g1, g2, g3)):
        first[k] = g[:base, :]
        cols = second.shape[2]
        third = second.shape[1] // 3
        top, low = g[base : base + third, :], g[base + third :, :]
        second[k, :third] = top[:, :cols]
        second[k, third : 2 * third] = low[:, :cols]
        second[k, 2 * third :, : cols // 2] = top[:, cols:]
        second[k, 2 * third :, cols // 2 :] = low[:, cols:]


def sum_kernel(own, got, out):
    out[...] = (own[...] + got[...].astype(F32)).astype(out.dtype)


def wq_kernel(idx, mine, other, wq, small, bias):
    c, core, z = idx[0], idx[1], idx[2]
    shards, _, span = mine.shape
    hc = span // 3
    half = wq.shape[0] // shards // CORES
    for m in range(shards):
        base = (z ^ m) * (CORES * half)
        wq[at(base + core * half, half, 32), :] = mine[m, :half, :]
        wq[at(base + (1 - core) * half, half, 32), :] = other[m, :half, :]
    small[...] = jnp.zeros_like(small)
    for j in range(shards):
        e = mine[j ^ z, half:, :].astype(F32)
        for n in range(9):
            small[n : n + 1, j * hc : (j + 1) * hc] = e[
                n // 3 : n // 3 + 1, (n % 3) * hc : (n % 3 + 1) * hc
            ]
    e = mine[c ^ z, half:, :].astype(F32)[:1]
    row = jnp.concatenate([e[:, :hc], jnp.zeros((1, hc), F32), e[:, hc : 2 * hc]], axis=1)
    bias[...] = jnp.broadcast_to(row, bias.shape)


def attn_kernel(x, wq, bias, pj, probs, out):
    rows, span = pj.shape
    hc = span // 3
    heads = hc // HEAD_DIM
    scale = 1.0 / math.sqrt(HEAD_DIM)
    pj[...] = (mm(x[:rows, :], wq[...]) + bias[:1, :]).astype(BF)
    pos_r = lax.broadcasted_iota(jnp.int32, (rows, 1), 0).astype(F32)
    pos_c = lax.broadcasted_iota(jnp.int32, (1, rows), 1).astype(F32)
    lens = x[rows : rows + 16, :128].astype(F32)[:1]
    end = jnp.zeros((1, 1), F32)
    seg_r = jnp.zeros((rows, 1), F32)
    seg_c = jnp.zeros((1, rows), F32)
    for n in range(3):
        end = end + lens[:, n : n + 1]
        seg_r = seg_r + (pos_r >= end).astype(F32)
        seg_c = seg_c + (pos_c >= end).astype(F32)
    same = seg_r == seg_c
    pb = pj[...]
    mixes = []
    for h in range(heads):
        q = pb[:, h * HEAD_DIM : (h + 1) * HEAD_DIM]
        k = pb[:, hc + h * HEAD_DIM : hc + (h + 1) * HEAD_DIM]
        v = pb[:, 2 * hc + h * HEAD_DIM : 2 * hc + (h + 1) * HEAD_DIM]
        s = jnp.where(same, mm_tb(q, k) * scale, masked_score)
        e = jnp.exp(s - jnp.max(s, axis=-1, keepdims=True))
        p = e / jnp.sum(e, axis=-1, keepdims=True)
        probs[h] = p
        mixes.append(mm(p.astype(BF), v))
    out[...] = jnp.concatenate(mixes, axis=1).astype(BF)


def wo_kernel(idx, mine, other, wo):
    c, core, z = idx[0], idx[1], idx[2]
    parts, shards, piece, cols = mine.shape
    for k in range(parts):
        for m in range(shards):
            base = at((z ^ m) * (parts * piece) + (c ^ k) * piece, piece, 16)
            wo[base, at(core * cols, cols, 128)] = mine[k, m]
            wo[base, at((1 - core) * cols, cols, 128)] = other[k, m]


def out_kernel(idx, tok, m0, m1, m2, m3, wo, small, y1, y1low, unit, inv):
    c = idx[0]
    hc = m0.shape[1]
    acc = small[2:3, :]
    for k, m in enumerate((m0, m1, m2, m3)):
        acc = acc + mm(m[...], wo[at((c ^ k) * hc, hc, 64), :])
    u, r = norm_stats(tok[...].astype(F32) + acc)
    unit[...] = u
    inv[...] = jnp.broadcast_to(r, inv.shape)
    y = u * small[6:7, :] + small[3:4, :]
    y1[...] = y
    y1low[...] = y.astype(BF)


def join_kernel(g0, g1, g2, g3, out):
    for k, g in enumerate((g0, g1, g2, g3)):
        out[k] = g[...]


def w2_kernel(idx, mine, other, wu, wd):
    core, z = idx[1], idx[2]
    half = mine.shape[1] // 2
    for m in range(mine.shape[0]):
        base = (z ^ m) * (2 * half)
        lo = at(base + core * half, half, 32)
        hi = at(base + (1 - core) * half, half, 32)
        wu[lo, :] = mine[m, :half, :]
        wu[hi, :] = other[m, :half, :]
        wd[lo, :] = mine[m, half:, :]
        wd[hi, :] = other[m, half:, :]


def ffn_kernel(y, wu, wd, small, act, slope, out):
    u = mm(y[...], wu[...]) + small[8:9, :]
    phi, slp = gelu_parts(u)
    a = (u * phi).astype(BF)
    act[...] = a
    slope[...] = slp
    out[...] = mm(a, wd[...]).astype(out.dtype)


def ln2_kernel(y1, z0, r1, r2, r3, small, cot, x0, actv, dz, gh2, sm):
    rows = y1.shape[0]
    branch = z0[...] + r1[...].astype(F32) + r2[...].astype(F32) + r3[...].astype(F32)
    u, r = norm_stats(y1[...] + (branch + small[4:5, :]))
    lens = x0[rows : rows + 16, :128].astype(F32)[:1]
    total = lens[:, 0:1] + lens[:, 1:2] + lens[:, 2:3]
    keep = (lax.broadcasted_iota(jnp.int32, (rows, 1), 0).astype(F32) < total).astype(F32)
    actv[...] = ((u * small[7:8, :] + small[5:6, :]) * keep).astype(BF)
    g = cot[...].astype(F32) * keep
    gh = norm_back(g, u, r, small[7:8, :])
    gh2[...] = gh
    low = gh.astype(BF)
    dz[...] = low
    sm[...] = jnp.zeros_like(sm)
    sm[0:1, :] = col_sum(low.astype(F32))
    sm[1:2, :] = col_sum(g)
    sm[2:3, :] = col_sum(g * u)


def ffb_kernel(d, wu, wd, slope, du, out):
    t = (mm_tb(d[...], wd[...]) * slope[...]).astype(BF)
    du[...] = t
    out[...] = mm_tb(t, wu[...]).astype(out.dtype)


def ffw_kernel(idx, *refs):
    core = idx[1]
    groups = [refs[n * PARTS : (n + 1) * PARTS] for n in range(4)]
    give, mine, hid, left, right, full = refs[4 * PARTS :]
    rows, width = groups[0][0].shape
    shards = give.shape[0]
    half = width // shards // CORES
    acts, dzs, ys, dus = groups
    h = None
    for base, lefts, rights in ((0, ys, dus), (half, acts, dzs)):
        for k in range(PARTS):
            left[k * rows : (k + 1) * rows, :] = lefts[k][...]
            right[k * rows : (k + 1) * rows, :] = rights[k][...]
        if base == 0:
            h = col_sum(right[...].astype(F32))
        full[...] = mm_ta(left[...], right[...]).astype(BF)
        for j in range(shards):
            mine[j, base : base + half, :] = full[at(j * 2 * half + core * half, half, 32), :]
            give[j, base : base + half, :] = full[
                at(j * 2 * half + (1 - core) * half, half, 32), :
            ]
    hid[...] = jnp.broadcast_to(h, hid.shape)


def add_kernel(idx, mine, got, keep, send):
    z = idx[2]
    for n in range(4):
        out, m, j = (keep, send)[n % 2], n // 2, z ^ n
        out[m] = (mine[j].astype(F32) + got[j].astype(F32)).astype(out.dtype)


def add_far_kernel(keep, got, own, send):
    own[...] = keep[0] + got[0].astype(F32)
    send[...] = (keep[1] + got[1].astype(F32)).astype(BF)


def fin1_kernel(idx, mine, other, gup, gdown):
    c, core = idx[0], idx[1]
    parts, _, width = mine.shape
    half = gup.shape[0] // 2
    fc = gdown.shape[0] // parts
    shards = gup.shape[1] // (parts * fc)
    for j in range(parts):
        k = j ^ c
        for src, row in ((mine, core * half), (other, (1 - core) * half)):
            v = src[k, :half, :].astype(F32)
            for s in range(shards):
                base = (s * parts + j) * fc
                gup[at(row, half, 32), base : base + fc] = v[:, s * fc : (s + 1) * fc]
            gdown[at(j * fc + row, half, 32), :] = src[k, half : 2 * half, :].astype(F32)


def ln1b_kernel(idx, gh2, o0, r1, r2, r3, unit, inv, small, wo, gh1, da, m0, m1, m2, m3, sm):
    c = idx[0]
    hc = m0.shape[1]
    dy = gh2[...] + o0[...] + r1[...].astype(F32) + r2[...].astype(F32) + r3[...].astype(F32)
    u = unit[...]
    gh = norm_back(dy, u, inv[:, :1], small[6:7, :])
    gh1[...] = gh
    low = gh.astype(BF)
    da[...] = low
    for k, m in enumerate((m0, m1, m2, m3)):
        m[...] = mm_tb(low, wo[at((c ^ k) * hc, hc, 64), :]).astype(BF)
    sm[...] = jnp.zeros_like(sm)
    sm[0:1, :] = col_sum(low.astype(F32))
    sm[1:2, :] = col_sum(dy)
    sm[2:3, :] = col_sum(dy * u)


def outw_kernel(idx, m0, m1, m2, m3, da, give, mine):
    c, core = idx[0], idx[1]
    cols = give.shape[2]
    lo, hi = da[:, :cols], da[:, cols:]
    first = core == 0
    keep = jnp.where(first, lo.astype(F32), hi.astype(F32)).astype(BF)
    pass_on = jnp.where(first, hi.astype(F32), lo.astype(F32)).astype(BF)
    for k, m in enumerate((m0, m1, m2, m3)):
        mine[c ^ k] = mm_ta(m[...], keep).astype(BF)
        give[c ^ k] = mm_ta(m[...], pass_on).astype(BF)


def oadd_kernel(idx, mine, got, own, s1, s2, s3):
    c = idx[0]
    shards, piece = own.shape[0], own.shape[1]
    for k, out in enumerate((own, s1, s2, s3)):
        rng = at((c ^ k) * piece, piece, 16)
        for j in range(shards):
            v = mine[j, rng, :].astype(F32) + got[j, rng, :].astype(F32)
            out[j] = v.astype(out.dtype)


def attb_kernel(d, pj, probs, dp):
    rows, hc = d.shape
    heads = hc // HEAD_DIM
    scale = 1.0 / math.sqrt(HEAD_DIM)
    pb = pj[...]
    db = d[...]
    dqs, dks, dvs = [], [], []
    for h in range(heads):
        q = pb[:, h * HEAD_DIM : (h + 1) * HEAD_DIM]
        k = pb[:, hc + h * HEAD_DIM : hc + (h + 1) * HEAD_DIM]
        v = pb[:, 2 * hc + h * HEAD_DIM : 2 * hc + (h + 1) * HEAD_DIM]
        g = db[:, h * HEAD_DIM : (h + 1) * HEAD_DIM]
        p = probs[h]
        dvs.append(mm_ta(p.astype(BF), g))
        dpr = mm_tb(g, v)
        inner = jnp.sum(p * dpr, axis=-1, keepdims=True)
        ds = (p * (dpr - inner)).astype(BF)
        dqs.append(mm(ds, k) * scale)
        dks.append(mm_ta(ds, q) * scale)
    dp[...] = jnp.concatenate(dqs + dks + dvs, axis=1).astype(BF)


def dx_kernel(d0, d1, d2, d3, wq, o0, o1, o2, o3):
    for d, out in ((d0, o0), (d1, o1), (d2, o2), (d3, o3)):
        out[...] = mm_tb(d[...], wq[...]).astype(out.dtype)


def qw_kernel(idx, x0, x1, x2, x3, d0, d1, d2, d3, sm1, sm2, hid, give, mine, xg, dp, full):
    c, core = idx[0], idx[1]
    shards, _, span = give.shape
    rows = d0.shape[0]
    hc = span // 3
    half = xg.shape[1] // shards // CORES
    for k, (x, d) in enumerate(((x0, d0), (x1, d1), (x2, d2), (x3, d3))):
        xg[k * rows : (k + 1) * rows, :] = x[:rows, :]
        dp[k * rows : (k + 1) * rows, :] = d[...]
    full[...] = mm_ta(xg[...], dp[...]).astype(BF)
    cols = col_sum(dp[...].astype(F32))
    vecs = (sm1[0:1], sm1[1:2], sm2[0:1], sm2[1:2], sm1[2:3], sm2[2:3])
    for j in range(shards):
        mine[j, :half, :] = full[at(j * 2 * half + core * half, half, 32), :]
        give[j, :half, :] = full[at(j * 2 * half + (1 - core) * half, half, 32), :]
        part = [v[:, j * hc : (j + 1) * hc] for v in vecs]
        own = jnp.where(c == j, 1.0, 0.0)
        rows = jnp.concatenate(
            [
                jnp.concatenate([cols[:, :hc] * own, cols[:, 2 * hc :] * own, part[0]], axis=1),
                jnp.concatenate(part[1:4], axis=1),
                jnp.concatenate(part[4:6] + [hid[:1, j * hc : (j + 1) * hc]], axis=1),
                jnp.zeros((13, span), F32),
            ],
            axis=0,
        ).astype(BF)
        mine[j, half:, :] = rows
        give[j, half:, :] = rows


def add2_kernel(idx, mine, got, osum, keep, send):
    z = idx[2]
    base, _ = mine.shape[1:]
    piece, cols = osum.shape[1:]
    third = piece // 3
    for n in range(4):
        out, m, j = (keep, send)[n % 2], n // 2, z ^ n
        out[m, :base, :] = (mine[j].astype(F32) + got[j].astype(F32)).astype(out.dtype)
        w = osum[j]

        def put(row, col, v, out=out, m=m):
            rng = slice(base + row * third, base + (row + 1) * third)
            out[m, rng, col : col + v.shape[1]] = v.astype(out.dtype)

        fold_piece(put, lambda g, col, k, w=w: w[g * third : (g + 1) * third, col : col + k], cols)


def fin2_kernel(idx, mine, other, gqkv, gout, gvec, ggain, ghid):
    c, core = idx[0], idx[1]
    parts, _, span = mine.shape
    hc = span // 3
    half = gqkv.shape[0] // 2
    width = gout.shape[1]
    piece = gout.shape[0] // parts
    cols = width // 2
    base = half + 16
    tot = mine[0, half:base, :].astype(F32)
    for k in range(1, parts):
        tot = tot + mine[k, half:base, :].astype(F32)
    for n in range(8):
        v = tot[n // 3 : n // 3 + 1, (n % 3) * hc : (n % 3 + 1) * hc]
        if n < 6:
            gvec[n : n + 1, :] = v
        else:
            ggain[n - 6 : n - 5, :] = v
    for j in range(parts):
        k = j ^ c
        ghid[:, j * hc : (j + 1) * hc] = mine[k, half:base, :].astype(F32)[2:3, 2 * hc :]
        for src, who in ((mine, core), (other, 1 - core)):
            v = src[k, :half, :].astype(F32)
            for s in range(3):
                gqkv[at(who * half, half, 32), s * width + j * hc : s * width + (j + 1) * hc] = v[
                    :, s * hc : (s + 1) * hc
                ]
            w = src[k, base:, :].astype(F32)
            third = piece // 3
            last = jnp.concatenate([w[:third, cols:], w[third:, cols:]], axis=1)
            for g, v in enumerate((w[:third, :cols], w[third:, :cols], last)):
                row = j * piece + g * third
                gout[row : row + third, at(who * cols, cols, 128)] = v


def call(kernel, out, *args, idx=None, scratch=(), hbm=(), after=(), limit=VMEM_BYTES):
    shapes = [jax.ShapeDtypeStruct(s, d) for s, d in out]
    specs = [
        pl.BlockSpec(memory_space=pltpu.HBM if n in hbm else pltpu.VMEM) for n in range(len(args))
    ]
    args = args + tuple(after)
    specs = specs + [pl.BlockSpec(memory_space=pl.ANY) for _ in after]
    skip = len(args) + (idx is not None)
    drop = len(after)

    def run(*refs):
        kernel(*refs[: skip - drop], *refs[skip:])

    if idx is not None:
        specs = [pl.BlockSpec(memory_space=pltpu.SMEM)] + specs
        args = (idx,) + args
    return pl.pallas_call(
        run if drop else kernel,
        out_shape=shapes,
        in_specs=specs,
        out_specs=[pl.BlockSpec(memory_space=pltpu.VMEM) for _ in shapes],
        scratch_shapes=[pltpu.VMEM(*s) if isinstance(s, tuple) else s for s in scratch],
        compiler_params=pltpu.CompilerParams(vmem_limit_bytes=limit),
        name=kernel.__name__,
        cost_estimate=pl.CostEstimate(flops=COST, bytes_accessed=100000, transcendentals=0),
    )(*args)


def gate(x, after):
    n = len(after)
    return pl.pallas_call(
        lambda *refs: None,
        out_shape=jax.ShapeDtypeStruct(x.shape, x.dtype),
        in_specs=[pl.BlockSpec(memory_space=pl.ANY)] * (n + 1),
        out_specs=pl.BlockSpec(memory_space=pl.ANY),
        input_output_aliases={0: 0},
        compiler_params=pltpu.CompilerParams(vmem_limit_bytes=VMEM_BYTES),
        name="gate_kernel",
    )(x, *after)


def make_body(reps, shards):
    def xor_perm(n, k):
        return [(i, i ^ k) for i in range(n)]

    def swap_core(v):
        return lax.ppermute(v, "rep", xor_perm(reps, 1))

    def swap_part(v, k):
        return lax.ppermute(v, "rep", xor_perm(reps, CORES * k))

    def swap_shard(v, k):
        return lax.ppermute(v, "shard", xor_perm(shards, k))

    def spread_part(v):
        return [v] + [swap_part(v, k) for k in range(1, PARTS)]

    def spread_shard(v):
        return [v] + [swap_shard(v, k) for k in range(1, shards)]

    def relay_shard(v):
        near, far = swap_shard(v, 1), swap_shard(v, 2)
        return [v, near, far, swap_shard(far, 1)]

    def trade_part(slots):
        return [slots[0]] + [swap_part(slots[k], k) for k in range(1, PARTS)]

    def trade_shard(slots):
        return [slots[0]] + [swap_shard(slots[k], k) for k in range(1, shards)]

    def total(slots):
        acc = slots[0]
        for s in slots[1:]:
            acc = acc + s.astype(F32)
        return acc

    def sum_outer(v):
        step = CORES * PARTS
        while step < reps:
            v = v + lax.ppermute(v, "rep", xor_perm(reps, step))
            step *= 2
        return v

    def body(
        tokens, w_qkv, w_out, w_up, w_down, vec_bias, ln_gain, hidden_bias, seq_lengths, cotangent
    ):
        rows, width = tokens.shape
        hid_own = hidden_bias.shape[0]
        wsh = width // shards
        half = wsh // CORES
        hc = width // PARTS
        fc = hid_own // PARTS
        span = 3 * hc
        piece = wsh // PARTS
        ocol = width // CORES
        rep = lax.axis_index("rep")
        z = lax.axis_index("shard")
        core = rep % CORES
        c = (rep // CORES) % PARTS
        idx = jnp.stack([c, core, z]).astype(jnp.int32)
        mats = [((rows, width), BF)]

        xp, pay1 = call(
            pack_kernel,
            [((rows + 16, width), BF), ((half + 16 + 2 * piece // 3, span), BF)],
            tokens,
            w_qkv,
            w_out,
            vec_bias,
            ln_gain,
            hidden_bias.reshape(1, hid_own),
            seq_lengths,
            idx=idx,
            hbm=range(7),
            limit=PACK_BYTES,
            scratch=[
                ((half, 3 * width), BF),
                ((piece, ocol), BF),
                (vec_bias.shape, BF),
                (ln_gain.shape, BF),
                ((1, hid_own), BF),
                (seq_lengths.shape, jnp.int32),
                pltpu.SemaphoreType.DMA((7,)),
            ],
        )
        got1 = relay_shard(pay1)
        xs = spread_part(xp)
        (pay2,) = call(
            pack2_kernel,
            [((half + fc // CORES, width), BF)],
            w_up,
            w_down,
            idx=idx,
            hbm=(0, 1),
            after=[xp],
            scratch=[((half, w_up.shape[1]), BF), pltpu.SemaphoreType.DMA((2,))],
        )
        pay2 = gate(pay2, [got1[3]] + xs[1:])
        got2 = relay_shard(pay2)
        mine1, pay_o = call(
            split_kernel,
            [((shards, half + 16, span), BF), ((shards, piece, ocol), BF)],
            *got1,
            after=[pay2],
        )
        other1 = swap_core(mine1)
        mine_o = jnp.stack(spread_part(pay_o))
        other_o = swap_core(mine_o)

        wq, small, bias = call(
            wq_kernel,
            [((width, span), BF), ((16, width), F32), ((8, span), F32)],
            mine1,
            other1,
            idx=idx,
            after=[pay2],
        )
        att = [
            call(
                attn_kernel,
                [((rows, span), BF), ((HEADS // PARTS, rows, rows), F32), ((rows, hc), BF)],
                x,
                wq,
                bias,
                after=[] if k else [mine_o],
            )
            for k, x in enumerate(xs)
        ]
        mix = trade_part([a[2] for a in att])
        (wo,) = call(wo_kernel, [((width, width), BF)], mine_o, other_o, idx=idx)
        y1, y1low, unit1, inv1 = call(
            out_kernel,
            [((rows, width), F32), ((rows, width), BF), ((rows, width), F32), ((rows, 128), F32)],
            tokens,
            *mix,
            wo,
            small,
            idx=idx,
            after=[got2[2]],
        )
        ys = spread_part(y1low)
        (mine2,) = call(
            join_kernel, [((shards,) + pay2.shape, BF)], *got2, after=ys[1:]
        )
        wu, wd = call(
            w2_kernel,
            [((width, shards * fc), BF), ((shards * fc, width), BF)],
            mine2,
            swap_core(mine2),
            idx=idx,
        )
        part_type = [F32] + [BF] * (PARTS - 1)
        ffn = [
            call(
                ffn_kernel,
                [((rows, shards * fc), BF), ((rows, shards * fc), F32), ((rows, width), t)],
                y,
                wu,
                wd,
                small,
            )
            for y, t in zip(ys, part_type)
        ]
        activations, dz, gh2, sm2 = call(
            ln2_kernel,
            mats * 2 + [((rows, width), F32), ((8, width), F32)],
            y1,
            *trade_part([f[2] for f in ffn]),
            small,
            cotangent,
            xp,
        )
        dzs = spread_part(dz)
        ffb = [
            call(
                ffb_kernel, [((rows, shards * fc), BF), ((rows, width), t)], d, wu, wd, f[1]
            )
            for d, f, t in zip(dzs, ffn, part_type)
        ]
        dyp = trade_part([f[1] for f in ffb])
        rows1 = half + fc // CORES
        give1, keep1, sm3 = call(
            ffw_kernel,
            [((shards, rows1, width), BF)] * 2 + [((8, shards * fc), F32)],
            *[f[0] for f in ffn],
            *dzs,
            *ys,
            *[f[0] for f in ffb],
            idx=idx,
            after=[dyp[3]],
            scratch=[((PARTS * rows, width), BF)] * 2 + [((width, width), BF)],
        )
        gh1, da, *rest = call(
            ln1b_kernel,
            [((rows, width), F32)] + mats + [((rows, hc), BF)] * PARTS + [((8, width), F32)],
            gh2,
            *dyp,
            unit1,
            inv1,
            small,
            wo,
            idx=idx,
            after=[give1],
        )
        dm, sm1 = trade_part(rest[:PARTS]), rest[PARTS]
        give_o, keep_o = call(
            outw_kernel,
            [((shards, wsh, ocol), BF)] * 2,
            *mix,
            da,
            idx=idx,
            after=[sm1],
        )
        out_send = call(
            oadd_kernel,
            [((shards, piece, ocol), F32)] + [((shards, piece, ocol), BF)] * 3,
            keep_o,
            swap_core(give_o),
            idx=idx,
        )
        osum = total(trade_part(out_send))

        def halve(keep, send, after):
            n, w = keep.shape[1:]
            own, far = call(
                add_far_kernel,
                [((n, w), F32), ((n, w), BF)],
                keep,
                swap_shard(send, 1),
                after=after,
            )
            return own, far

        def join(own, far, after):
            got = swap_shard(far, 2)
            if reps > CORES * PARTS:
                return sum_outer(own + got.astype(F32)).astype(BF)
            return call(sum_kernel, [(own.shape, BF)], own, got, after=after)[0]

        def spread_piece(v):
            done = jnp.stack(spread_part(v))
            return done, swap_core(done)

        def pair_shapes(n, w):
            return [((2, n, w), F32), ((2, n, w), BF)]

        keep_a, send_a = call(
            add_kernel,
            pair_shapes(rows1, width),
            keep1,
            swap_core(give1),
            idx=idx,
            after=[sm1],
        )
        dps = [
            call(
                attb_kernel,
                [((rows, span), BF)],
                d,
                a[0],
                a[1],
                after=[] if k else [send_a, give_o],
            )[0]
            for k, (d, a) in enumerate(zip(dm, att))
        ]
        rows2 = half + 16
        give2, keep2 = call(
            qw_kernel,
            [((shards, rows2, span), BF)] * 2,
            *xs,
            *dps,
            sm1,
            sm2,
            sm3,
            idx=idx,
            after=[out_send[0]],
            scratch=[
                ((PARTS * rows, width), BF),
                ((PARTS * rows, span), BF),
                ((width, span), BF),
            ],
        )
        keep_b, send_b = call(
            add2_kernel,
            pair_shapes(rows2 + 2 * piece // 3, span),
            keep2,
            swap_core(give2),
            osum,
            idx=idx,
        )
        dxp = call(
            dx_kernel, [((rows, width), t) for t in part_type], *dps, wq, after=[send_b]
        )
        dxp_got = trade_part(dxp)
        own_a, far_a = halve(keep_a, send_a, [send_b])
        own_b, far_b = halve(keep_b, send_b, [far_a])
        piece1 = join(own_a, far_a, dxp_got[1:] + [far_b])
        piece2 = join(own_b, far_b, [piece1])
        done1 = spread_piece(piece1)
        done2 = spread_piece(piece2)
        g_tok = gh1 + total(dxp_got)
        gw_up, gw_down = call(
            fin1_kernel, [(w_up.shape, F32), (w_down.shape, F32)], *done1, idx=idx, after=[piece2]
        )
        gw_qkv, gw_out, g_vec, g_gain, g_hidden = call(
            fin2_kernel,
            [
                (w_qkv.shape, F32),
                (w_out.shape, F32),
                ((6, wsh), F32),
                ((2, wsh), F32),
                ((1, hid_own), F32),
            ],
            *done2,
            idx=idx,
            after=[gw_up, g_tok],
        )
        return (
            activations,
            g_tok,
            gw_qkv,
            gw_out,
            gw_up,
            gw_down,
            g_vec,
            g_gain,
            g_hidden.reshape(hid_own),
        )

    return body


def solution(mesh):
    body = make_body(mesh.shape["rep"], mesh.shape["shard"])
    both = P(("rep", "shard"), None)
    first = P("shard", None)
    last = P(None, "shard")
    return jax.shard_map(
        body,
        mesh=mesh,
        in_specs=(both, first, first, first, first, last, last, P("shard"), both, both),
        out_specs=(both, both, first, first, first, first, last, last, P("shard")),
        check_vma=False,
    )
```

time: 293 us -> 193 us (0.66); the launches traced: 287 us -> 193 us
  local copies, waits for them, and re-layouts: 67.6 us -> 5.22 us
  Pallas kernels: 0 us -> 38.2 us
  other arithmetic: 33.8 us -> 1.75 us
  starting transfers between devices: 84.2 us -> 62.4 us
  matrix products: 20.8 us -> 0 us
  waiting for transfers between devices: 78.5 us -> 83.8 us
    pallas_call x0 -> x40, Pallas kernels: none -> 38.2 us  [the longest x39 38.2 us: call(): pl.pallas_call(run if drop else kernel, out_shape=shapes, in_specs=specs,...]
    convert_element_type x10 -> x0, local copies, waits for them, and re-layouts: 23.6 us -> none  [the longest x3 12.2 us: body(): gw_up = done1[:, :, :half].reshape(PARTS, CORES, half, shards, fcol).tran...]
    dot_general x17 -> x0, matrix products: 19.4 us -> none  [the longest x4 6.56 us: mm(): return jnp.dot(a, b, preferred_element_type=F32)]
    ppermute x39 -> x36, waiting for transfers between devices: 37.1 us -> 55.6 us  [swap_part(): return lax.ppermute(v, 'rep', xor_perm(reps, CORES * k))]
    ppermute x18 -> x10, waiting for transfers between devices: 39.6 us -> 25.4 us  [swap_shard(): return lax.ppermute(v, 'shard', xor_perm(shards, k))]
    ppermute x18 -> x10, starting transfers between devices: 33 us -> 19 us  [swap_shard(): return lax.ppermute(v, 'shard', xor_perm(shards, k))]
    another operation x31 -> x4, other arithmetic: 11.9 us -> 0.98 us  [the longest x1 0.59 us: body(): idx = jnp.stack([c, core, z]).astype(jnp.int32)]
    slice x23 -> x0, local copies, waits for them, and re-layouts: 9.4 us -> none  [the longest x3 1.36 us: body(): s[rows, :seq_lengths.shape[1]]]
  transfers between devices with their start and end apart: 66 -> 54, of which waited for: 26 -> 29; matrix products, arithmetic and copies ran while one was open for 28% -> 0% of each run, Pallas kernels for 0% -> 14%
where the time goes in v2:
time: 193 us
  waiting for transfers between devices  83.8 us (43%)
  starting transfers between devices  62.4 us (32%)
  Pallas kernels  38.2 us (20%)
  local copies, waits for them, and re-layouts  5.22 us (3%)
    ppermute x36, waiting for transfers between devices, swap_part(): return lax.ppermute(v, 'rep', xor_perm(reps, CORES * k))  55.6 us
    ppermute x36, starting transfers between devices, swap_part(): return lax.ppermute(v, 'rep', xor_perm(reps, CORES * k))  42.6 us
    pallas_call x39, Pallas kernels, call(): pl.pallas_call(run if drop else kernel, out_shape=shapes, in_specs=specs,...  38.2 us
    ppermute x10, waiting for transfers between devices, swap_shard(): return lax.ppermute(v, 'shard', xor_perm(shards, k))  25.4 us
    ppermute x10, starting transfers between devices, swap_shard(): return lax.ppermute(v, 'shard', xor_perm(shards, k))  19 us
    unnamed x36, local copies, waits for them, and re-layouts  3.96 us
  transfers between devices with their start and end apart: 54, of which 29 were waited for; matrix products, arithmetic and copies ran while one was open for 0% of the time, Pallas kernels for 14%

profile of v2, /device:TPU:0, one launch (start us, length us, event | category | flops | bytes accessed | tf_op | source)
XLA Modules:
  0.0 192.7 jit_solution(11688003263762343353)
XLA Ops:
  0.7 1.3 reshape.24.hid_in
  2.5 2.8 %pack_kernel.1 = (bf16[144,768]{1,0:T(8,128)(2,1)}, bf16[144,576]{1,0:T(8,128)(2,1)}) custom-call(s32[3]{0:T(128)} %pad_add_fusion.idx.refs_0_, bf16[128,768]{1,0:T(8,128)(2,1)} %refs_1_.3, bf16[192,2304]{1,0:T(8,128)(2,1)} %wqkv.1, bf16[192,768]{1,0:T(8,128)(2,1)} %wout.1, bf16[6,192]{1,0:T(8,128)(2,1)} %vec_in.1, bf16[2,192]{1,0:T(2,128)(2,1)} %gain_in.1, ...), custom_call_target="tpu_custom_call" | custom-call | flops 11000000512 | bytes 100000 | tf_op jit(solution)/shard_map/pack_kernel/pallas_call | solution.py:507
  5.3 4.1 %collective-permute-start.1 = (bf16[144,576]{1,0:T(8,128)(2,1)}, bf16[144,576]{1,0:T(8,128)(2,1)S(1)}, u32[]{:S(2)}, u32[]{:S(2)}) collective-permute-start(bf16[144,576]{1,0:T(8,128)(2,1)} %get-tuple-element.96.refs_0_), channel_id=1, source_target_pairs={{0,2},{1,3},{2,0},{3,1},{4,6},{5,7},{6,4},{7,5},{8,10},{9,11},{10,... | collective-permute-start | bytes 497672 | tf_op jit(solution)/shard_map/ppermute | solution.py:543
  9.4 1.6 collective-permute-start
  11.0 2.5 %collective-permute-start.5 = (bf16[144,768]{1,0:T(8,128)(2,1)}, bf16[144,768]{1,0:T(8,128)(2,1)S(1)}, u32[]{:S(2)}, u32[]{:S(2)}) collective-permute-start(bf16[144,768]{1,0:T(8,128)(2,1)} %get-tuple-element.95.refs_3_.refs_0_.x0.refs_1_), channel_id=1, source_target_pairs={{0,24},{4,28},{8,16},{12,20},{16,8},{20,12},{24,0},{28,4},{1,25},{... | collective-permute-start | bytes 663560 | tf_op jit(solution)/shard_map/ppermute | solution.py:540
  14.5 3.8 %collective-permute-done.1.refs_2_ = bf16[144,576]{1,0:T(8,128)(2,1)S(1)} collective-permute-done((bf16[144,576]{1,0:T(8,128)(2,1)}, bf16[144,576]{1,0:T(8,128)(2,1)S(1)}, u32[]{:S(2)}, u32[]{:S(2)}) %collective-permute-start.1) | collective-permute-done | bytes 165920 | tf_op jit(solution)/shard_map/ppermute | solution.py:543
  19.1 1.3 copy-done.9
  22.3 1.2 collective-permute-done.4.refs_3_.x
  24.3 3.2 %collective-permute-start.14 = (bf16[192,768]{1,0:T(8,128)(2,1)S(1)}, bf16[192,768]{1,0:T(8,128)(2,1)S(1)}, u32[]{:S(2)}, u32[]{:S(2)}) collective-permute-start(bf16[192,768]{1,0:T(8,128)(2,1)S(1)} %gate_kernel.1.refs_4_.refs_3_.refs_0_), channel_id=1, source_target_pairs={{0,2},{1,3},{2,0},{3,1},{4,6},{5,7},{6,4},{7,5},{8,10},{9,11},{10,... | collective-permute-start | bytes 884744 | tf_op jit(solution)/shard_map/ppermute | solution.py:543
  27.4 2.5 %collective-permute-start.9 = (bf16[4,48,384]{2,1,0:T(8,128)(2,1)S(1)}, bf16[4,48,384]{2,1,0:T(8,128)(2,1)S(1)}, u32[]{:S(2)}, u32[]{:S(2)}) collective-permute-start(bf16[4,48,384]{2,1,0:T(8,128)(2,1)S(1)} %get-tuple-element.100), channel_id=1, source_target_pairs={{0,24},{4,28},{8,16},{12,20},{16,8},{20,12},{24,0},{28,4},{1,25},{... | collective-permute-start | bytes 442376 | tf_op jit(solution)/shard_map/ppermute | solution.py:540
  30.9 4.0 %collective-permute-done.9 = bf16[4,48,384]{2,1,0:T(8,128)(2,1)S(1)} collective-permute-done((bf16[4,48,384]{2,1,0:T(8,128)(2,1)S(1)}, bf16[4,48,384]{2,1,0:T(8,128)(2,1)S(1)}, u32[]{:S(2)}, u32[]{:S(2)}) %collective-permute-start.9) | collective-permute-done | bytes 147488 | tf_op jit(solution)/shard_map/ppermute | solution.py:540
  34.9 1.7 collective-permute-start.15
  37.7 3.8 %collective-permute-done.14.refs_8_.refs_2_ = bf16[192,768]{1,0:T(8,128)(2,1)S(1)} collective-permute-done((bf16[192,768]{1,0:T(8,128)(2,1)S(1)}, bf16[192,768]{1,0:T(8,128)(2,1)S(1)}, u32[]{:S(2)}, u32[]{:S(2)}) %collective-permute-start.14) | collective-permute-done | bytes 294944 | tf_op jit(solution)/shard_map/ppermute | solution.py:543
  44.7 2.5 %collective-permute-start.12 = (bf16[128,192]{1,0:T(8,128)(2,1)S(1)}, bf16[128,192]{1,0:T(8,128)(2,1)S(1)}, u32[]{:S(2)}, u32[]{:S(2)}) collective-permute-start(bf16[128,192]{1,0:T(8,128)(2,1)S(1)} %get-tuple-element.104), channel_id=1, source_target_pairs={{0,24},{4,28},{8,16},{12,20},{16,8},{20,12},{24,0},{28,4},{1,25},{... | collective-permute-start | bytes 147464 | tf_op jit(solution)/shard_map/ppermute | solution.py:540
  51.0 1.6 collective-permute-done.11.refs_4_.refs_3_
  52.5 1.6 collective-permute-done.10.refs_3_.refs_2_
  54.1 1.1 out_kernel.1
  55.2 1.5 collective-permute-start.19
  57.2 1.5 collective-permute-start.17
  58.8 4.8 %collective-permute-done.19.refs_6_.y.refs_12_ = bf16[128,768]{1,0:T(8,128)(2,1)S(1)} collective-permute-done((bf16[128,768]{1,0:T(8,128)(2,1)S(1)}, bf16[128,768]{1,0:T(8,128)(2,1)S(1)}, u32[]{:S(2)}, u32[]{:S(2)}) %collective-permute-start.19) | collective-permute-done | bytes 196640 | tf_op jit(solution)/shard_map/ppermute | solution.py:540
  63.6 2.0 %collective-permute-done.18.refs_5_.y.refs_11_ = bf16[128,768]{1,0:T(8,128)(2,1)S(1)} collective-permute-done((bf16[128,768]{1,0:T(8,128)(2,1)S(1)}, bf16[128,768]{1,0:T(8,128)(2,1)S(1)}, u32[]{:S(2)}, u32[]{:S(2)}) %collective-permute-start.18) | collective-permute-done | bytes 196640 | tf_op jit(solution)/shard_map/ppermute | solution.py:540
  65.8 2.8 %collective-permute-done.20.other = bf16[4,192,768]{2,1,0:T(8,128)(2,1)S(1)} collective-permute-done((bf16[4,192,768]{2,1,0:T(8,128)(2,1)S(1)}, bf16[4,192,768]{2,1,0:T(8,128)(2,1)S(1)}, u32[]{:S(2)}, u32[]{:S(2)}) %collective-permute-start.20) | collective-permute-done | bytes 1179680 | tf_op jit(solution)/shard_map/ppermute | solution.py:537
  70.0 1.4 collective-permute-start.23
  73.5 1.6 collective-permute-start.21
  75.8 3.0 %collective-permute-done.23.r3 = bf16[128,768]{1,0:T(8,128)(2,1)S(1)} collective-permute-done((bf16[128,768]{1,0:T(8,128)(2,1)S(1)}, bf16[128,768]{1,0:T(8,128)(2,1)S(1)}, u32[]{:S(2)}, u32[]{:S(2)}) %collective-permute-start.23) | collective-permute-done | bytes 196640 | tf_op jit(solution)/shard_map/ppermute | solution.py:540
  78.8 3.4 %collective-permute-done.22.r2 = bf16[128,768]{1,0:T(8,128)(2,1)S(1)} collective-permute-done((bf16[128,768]{1,0:T(8,128)(2,1)S(1)}, bf16[128,768]{1,0:T(8,128)(2,1)S(1)}, u32[]{:S(2)}, u32[]{:S(2)}) %collective-permute-start.22) | collective-permute-done | bytes 196640 | tf_op jit(solution)/shard_map/ppermute | solution.py:540
  82.1 1.2 ln2_kernel.1
  83.3 1.4 collective-permute-start.28
  85.3 1.5 collective-permute-start.24
  87.8 4.3 %collective-permute-done.28.d.refs_8_ = bf16[128,768]{1,0:T(8,128)(2,1)S(1)} collective-permute-done((bf16[128,768]{1,0:T(8,128)(2,1)S(1)}, bf16[128,768]{1,0:T(8,128)(2,1)S(1)}, u32[]{:S(2)}, u32[]{:S(2)}) %collective-permute-start.28) | collective-permute-done | bytes 196640 | tf_op jit(solution)/shard_map/ppermute | solution.py:540
  93.0 1.4 collective-permute-start.29
  94.4 1.3 collective-permute-done.26.d.refs_7_
  98.4 1.3 collective-permute-start.25
  99.6 2.1 %ffw_kernel.1 = (bf16[4,192,768]{2,1,0:T(8,128)(2,1)S(1)}, bf16[4,192,768]{2,1,0:T(8,128)(2,1)S(1)}, f32[8,768]{1,0:T(8,128)S(1)}) custom-call(s32[3]{0:T(128)S(1)} %copy-done.7, bf16[128,768]{1,0:T(8,128)(2,1)S(1)} %get-tuple-element.127.refs_1_, bf16[128,768]{1,0:T(8,128)(2,1)S(1)} %get-tuple-element.128.refs_2_, ...), custom_call_target="tpu_custom_call" | custom-call | flops 11000000512 | bytes 100000 | tf_op jit(solution)/shard_map/ffw_kernel/pallas_call | solution.py:507
  101.9 1.9 %collective-permute-done.27.refs_4_ = bf16[128,768]{1,0:T(8,128)(2,1)S(1)} collective-permute-done((bf16[128,768]{1,0:T(8,128)(2,1)S(1)}, bf16[128,768]{1,0:T(8,128)(2,1)S(1)}, u32[]{:S(2)}, u32[]{:S(2)}) %collective-permute-start.27) | collective-permute-done | bytes 196640 | tf_op jit(solution)/shard_map/ppermute | solution.py:540
  104.9 1.3 ln1b_kernel.1
  106.2 1.3 collective-permute-start.31
  108.1 1.6 collective-permute-start.33
  111.1 1.1 attb_kernel.5.refs_6_.refs_1_
  112.3 1.1 attb_kernel.6.refs_7_.refs_2_
  113.4 1.1 attb_kernel.7.refs_8_.refs_3_
  116.1 1.1 attb_kernel.4.refs_5_.refs_0_
  117.3 1.5 qw_kernel.1
  119.0 1.3 collective-permute-start.36
  120.9 1.6 collective-permute-start.38
  122.5 3.2 %collective-permute-done.36 = bf16[4,48,384]{2,1,0:T(8,128)(2,1)S(1)} collective-permute-done((bf16[4,48,384]{2,1,0:T(8,128)(2,1)S(1)}, bf16[4,48,384]{2,1,0:T(8,128)(2,1)S(1)}, u32[]{:S(2)}, u32[]{:S(2)}) %collective-permute-start.36) | collective-permute-done | bytes 147488 | tf_op jit(solution)/shard_map/ppermute | solution.py:540
  125.7 3.6 %collective-permute-done.37 = bf16[4,48,384]{2,1,0:T(8,128)(2,1)S(1)} collective-permute-done((bf16[4,48,384]{2,1,0:T(8,128)(2,1)S(1)}, bf16[4,48,384]{2,1,0:T(8,128)(2,1)S(1)}, u32[]{:S(2)}, u32[]{:S(2)}) %collective-permute-start.37) | collective-permute-done | bytes 147488 | tf_op jit(solution)/shard_map/ppermute | solution.py:540
  131.2 1.1 collective-permute-start.42
  132.3 1.4 dx_kernel.1
  134.4 1.3 collective-permute-start.40
  135.7 1.5 collective-permute-start.41
  137.2 8.5 %collective-permute-done.43.refs_1_ = bf16[2,192,768]{2,1,0:T(8,128)(2,1)S(1)} collective-permute-done((bf16[2,192,768]{2,1,0:T(8,128)(2,1)S(1)}, bf16[2,192,768]{2,1,0:T(8,128)(2,1)S(1)}, u32[]{:S(2)}, u32[]{:S(2)}) %collective-permute-start.43) | collective-permute-done | bytes 589856 | tf_op jit(solution)/shard_map/ppermute | solution.py:543
  145.8 3.4 %collective-permute-start.45 = (bf16[192,768]{1,0:T(8,128)(2,1)S(1)}, bf16[192,768]{1,0:T(8,128)(2,1)S(1)}, u32[]{:S(2)}, u32[]{:S(2)}) collective-permute-start(bf16[192,768]{1,0:T(8,128)(2,1)S(1)} %get-tuple-element.170.refs_2_), channel_id=1, source_target_pairs={{0,2},{1,3},{2,0},{3,1},{4,6},{5,7},{6,4},{7,5},{8,10},{9,11},{10,... | collective-permute-start | bytes 884744 | tf_op jit(solution)/shard_map/ppermute | solution.py:543
  149.2 8.8 %collective-permute-done.42.refs_1_ = bf16[2,144,576]{2,1,0:T(8,128)(2,1)S(1)} collective-permute-done((bf16[2,144,576]{2,1,0:T(8,128)(2,1)S(1)}, bf16[2,144,576]{2,1,0:T(8,128)(2,1)S(1)}, u32[]{:S(2)}, u32[]{:S(2)}) %collective-permute-start.42) | collective-permute-done | bytes 331808 | tf_op jit(solution)/shard_map/ppermute | solution.py:543
  158.2 1.7 collective-permute-start.52
  161.7 1.5 collective-permute-start.44
  163.2 5.9 %collective-permute-done.52 = bf16[192,768]{1,0:T(8,128)(2,1)S(1)} collective-permute-done((bf16[192,768]{1,0:T(8,128)(2,1)S(1)}, bf16[192,768]{1,0:T(8,128)(2,1)S(1)}, u32[]{:S(2)}, u32[]{:S(2)}) %collective-permute-start.52) | collective-permute-done | bytes 294944 | tf_op jit(solution)/shard_map/ppermute | solution.py:540
  169.1 3.4 %collective-permute-done.51 = bf16[192,768]{1,0:T(8,128)(2,1)S(1)} collective-permute-done((bf16[192,768]{1,0:T(8,128)(2,1)S(1)}, bf16[192,768]{1,0:T(8,128)(2,1)S(1)}, u32[]{:S(2)}, u32[]{:S(2)}) %collective-permute-start.51) | collective-permute-done | bytes 294944 | tf_op jit(solution)/shard_map/ppermute | solution.py:540
  172.8 1.8 collective-permute-start.48
  176.5 4.8 %collective-permute-done.48 = bf16[144,576]{1,0:T(8,128)(2,1)S(1)} collective-permute-done((bf16[144,576]{1,0:T(8,128)(2,1)S(1)}, bf16[144,576]{1,0:T(8,128)(2,1)S(1)}, u32[]{:S(2)}, u32[]{:S(2)}) %collective-permute-start.48) | collective-permute-done | bytes 165920 | tf_op jit(solution)/shard_map/ppermute | solution.py:540
  181.2 3.5 %collective-permute-done.47 = bf16[144,576]{1,0:T(8,128)(2,1)S(1)} collective-permute-done((bf16[144,576]{1,0:T(8,128)(2,1)S(1)}, bf16[144,576]{1,0:T(8,128)(2,1)S(1)}, u32[]{:S(2)}, u32[]{:S(2)}) %collective-permute-start.47) | collective-permute-done | bytes 165920 | tf_op jit(solution)/shard_map/ppermute | solution.py:540
  185.0 3.1 %fin1_kernel.1 = (f32[192,3072]{1,0:T(8,128)}, f32[768,768]{1,0:T(8,128)}) custom-call(s32[3]{0:T(128)S(1)} %copy-done.7, bf16[4,192,768]{2,1,0:T(8,128)(2,1)S(1)} %pad_maximum_fusion.refs_1_, bf16[4,192,768]{2,1,0:T(8,128)(2,1)S(1)} %collective-permute-done.53.refs_2_, bf16[144,576]{1,0:T(8,128)(2,1)S(1)} %sum_kernel.3.refs_3_), custom_call_target="tpu_custom_call" | custom-call | flops 11000000512 | bytes 100000 | tf_op jit(solution)/shard_map/fin1_kernel/pallas_call | solution.py:507
  188.2 1.7 copy-done.15
  189.8 2.2 %fin2_kernel.1 = (f32[192,2304]{1,0:T(8,128)}, f32[192,768]{1,0:T(8,128)}, f32[6,192]{1,0:T(8,128)}, f32[2,192]{1,0:T(2,128)}, f32[1,768]{1,0:T(1,128)S(1)}) custom-call(s32[3]{0:T(128)S(1)} %copy-done.7, bf16[4,144,576]{2,1,0:T(8,128)(2,1)S(1)} %pad_maximum_fusion.1.refs_1_, bf16[4,144,576]{2,1,0:T(8,128)(2,1)S(1)} %collective-permute-done.49.refs_2_, ...), custom_call_target="tpu_custom_call" | custom-call | flops 11000000512 | bytes 100000 | tf_op jit(solution)/shard_map/fin2_kernel/pallas_call | solution.py:507
  (128 shorter events, 37.3 us)
Async XLA Ops:
  2.5 16.6 %copy-start.7 = (s32[3]{0:T(128)S(1)}, s32[3]{0:T(128)}, u32[]{:S(2)}) copy-start(s32[3]{0:T(128)} %pad_add_fusion.idx.refs_0_) | copy-start | bytes 40
  2.5 16.6 %copy-start.8 = (bf16[192,3072]{1,0:T(8,128)(2,1)S(1)}, bf16[192,3072]{1,0:T(8,128)(2,1)}, u32[]{:S(2)}) copy-start(bf16[192,3072]{1,0:T(8,128)(2,1)} %refs_1_.2) | copy-start | bytes 3538948
  5.3 13.0 %collective-permute-start.1 = (bf16[144,576]{1,0:T(8,128)(2,1)}, bf16[144,576]{1,0:T(8,128)(2,1)S(1)}, u32[]{:S(2)}, u32[]{:S(2)}) collective-permute-start(bf16[144,576]{1,0:T(8,128)(2,1)} %get-tuple-element.96.refs_0_), channel_id=1, source_target_pairs={{0,2},{1,3},{2,0},{3,1},{4,6},{5,7},{6,4},{7,5},{8,10},{9,11},{10,... | collective-permute-start | bytes 497672 | tf_op jit(solution)/shard_map/ppermute | solution.py:543
  9.4 14.6 %collective-permute-start = (bf16[144,576]{1,0:T(8,128)(2,1)}, bf16[144,576]{1,0:T(8,128)(2,1)S(1)}, u32[]{:S(2)}, u32[]{:S(2)}) collective-permute-start(bf16[144,576]{1,0:T(8,128)(2,1)} %get-tuple-element.96.refs_0_), channel_id=1, source_target_pairs={{0,1},{1,0},{2,3},{3,2},{4,5},{5,4},{6,7},{7,6},{8,9},{9,8},{10,11... | collective-permute-start | bytes 497672 | tf_op jit(solution)/shard_map/ppermute | solution.py:543
  11.0 11.3 %collective-permute-start.5 = (bf16[144,768]{1,0:T(8,128)(2,1)}, bf16[144,768]{1,0:T(8,128)(2,1)S(1)}, u32[]{:S(2)}, u32[]{:S(2)}) collective-permute-start(bf16[144,768]{1,0:T(8,128)(2,1)} %get-tuple-element.95.refs_3_.refs_0_.x0.refs_1_), channel_id=1, source_target_pairs={{0,24},{4,28},{8,16},{12,20},{16,8},{20,12},{24,0},{28,4},{1,25},{... | collective-permute-start | bytes 663560 | tf_op jit(solution)/shard_map/ppermute | solution.py:540
  13.5 10.0 %collective-permute-start.4 = (bf16[144,768]{1,0:T(8,128)(2,1)}, bf16[144,768]{1,0:T(8,128)(2,1)S(1)}, u32[]{:S(2)}, u32[]{:S(2)}) collective-permute-start(bf16[144,768]{1,0:T(8,128)(2,1)} %get-tuple-element.95.refs_3_.refs_0_.x0.refs_1_), channel_id=1, source_target_pairs={{0,16},{4,20},{8,24},{12,28},{16,0},{20,4},{24,8},{28,12},{1,17},{... | collective-permute-start | bytes 663560 | tf_op jit(solution)/shard_map/ppermute | solution.py:540
  14.0 9.6 %collective-permute-start.3 = (bf16[144,768]{1,0:T(8,128)(2,1)}, bf16[144,768]{1,0:T(8,128)(2,1)S(1)}, u32[]{:S(2)}, u32[]{:S(2)}) collective-permute-start(bf16[144,768]{1,0:T(8,128)(2,1)} %get-tuple-element.95.refs_3_.refs_0_.x0.refs_1_), channel_id=1, source_target_pairs={{0,8},{4,12},{8,0},{12,4},{16,24},{20,28},{24,16},{28,20},{1,9},{5... | collective-permute-start | bytes 663560 | tf_op jit(solution)/shard_map/ppermute | solution.py:540
  18.4 5.7 %collective-permute-start.2 = (bf16[144,576]{1,0:T(8,128)(2,1)S(1)}, bf16[144,576]{1,0:T(8,128)(2,1)S(1)}, u32[]{:S(2)}, u32[]{:S(2)}) collective-permute-start(bf16[144,576]{1,0:T(8,128)(2,1)S(1)} %collective-permute-done.1.refs_2_), channel_id=1, source_target_pairs={{0,1},{1,0},{2,3},{3,2},{4,5},{5,4},{6,7},{7,6},{8,9},{9,8},{10,11... | collective-permute-start | bytes 497672 | tf_op jit(solution)/shard_map/ppermute | solution.py:543
  22.3 21.5 %copy-start.1 = (bf16[144,768]{1,0:T(8,128)(2,1)}, bf16[144,768]{1,0:T(8,128)(2,1)S(1)}, u32[]{:S(2)}) copy-start(bf16[144,768]{1,0:T(8,128)(2,1)S(1)} %collective-permute-done.5.refs_4_.x) | copy-start | bytes 663556
  23.5 23.8 %copy-start.3 = (bf16[144,768]{1,0:T(8,128)(2,1)}, bf16[144,768]{1,0:T(8,128)(2,1)S(1)}, u32[]{:S(2)}) copy-start(bf16[144,768]{1,0:T(8,128)(2,1)S(1)} %collective-permute-done.4.refs_3_.x) | copy-start | bytes 663556
  23.6 25.2 %copy-start.5 = (bf16[144,768]{1,0:T(8,128)(2,1)}, bf16[144,768]{1,0:T(8,128)(2,1)S(1)}, u32[]{:S(2)}) copy-start(bf16[144,768]{1,0:T(8,128)(2,1)S(1)} %collective-permute-done.3.refs_2_.x) | copy-start | bytes 663556
  24.2 18.0 %collective-permute-start.6 = (bf16[4,112,576]{2,1,0:T(8,128)(2,1)S(1)}, bf16[4,112,576]{2,1,0:T(8,128)(2,1)S(1)}, u32[]{:S(2)}, u32[]{:S(2)}) collective-permute-start(bf16[4,112,576]{2,1,0:T(8,128)(2,1)S(1)} %get-tuple-element.97.refs_1_), channel_id=1, source_target_pairs={{0,4},{4,0},{8,12},{12,8},{16,20},{20,16},{24,28},{28,24},{1,5},{5... | collective-permute-start | bytes 1548296 | tf_op jit(solution)/shard_map/ppermute | solution.py:537
  24.3 17.2 %collective-permute-start.14 = (bf16[192,768]{1,0:T(8,128)(2,1)S(1)}, bf16[192,768]{1,0:T(8,128)(2,1)S(1)}, u32[]{:S(2)}, u32[]{:S(2)}) collective-permute-start(bf16[192,768]{1,0:T(8,128)(2,1)S(1)} %gate_kernel.1.refs_4_.refs_3_.refs_0_), channel_id=1, source_target_pairs={{0,2},{1,3},{2,0},{3,1},{4,6},{5,7},{6,4},{7,5},{8,10},{9,11},{10,... | collective-permute-start | bytes 884744 | tf_op jit(solution)/shard_map/ppermute | solution.py:543
  27.4 7.4 %collective-permute-start.9 = (bf16[4,48,384]{2,1,0:T(8,128)(2,1)S(1)}, bf16[4,48,384]{2,1,0:T(8,128)(2,1)S(1)}, u32[]{:S(2)}, u32[]{:S(2)}) collective-permute-start(bf16[4,48,384]{2,1,0:T(8,128)(2,1)S(1)} %get-tuple-element.100), channel_id=1, source_target_pairs={{0,24},{4,28},{8,16},{12,20},{16,8},{20,12},{24,0},{28,4},{1,25},{... | collective-permute-start | bytes 442376 | tf_op jit(solution)/shard_map/ppermute | solution.py:540
  29.9 7.5 %collective-permute-start.8 = (bf16[4,48,384]{2,1,0:T(8,128)(2,1)S(1)}, bf16[4,48,384]{2,1,0:T(8,128)(2,1)S(1)}, u32[]{:S(2)}, u32[]{:S(2)}) collective-permute-start(bf16[4,48,384]{2,1,0:T(8,128)(2,1)S(1)} %get-tuple-element.100), channel_id=1, source_target_pairs={{0,16},{4,20},{8,24},{12,28},{16,0},{20,4},{24,8},{28,12},{1,17},{... | collective-permute-start | bytes 442376 | tf_op jit(solution)/shard_map/ppermute | solution.py:540
  30.4 7.1 %collective-permute-start.7 = (bf16[4,48,384]{2,1,0:T(8,128)(2,1)S(1)}, bf16[4,48,384]{2,1,0:T(8,128)(2,1)S(1)}, u32[]{:S(2)}, u32[]{:S(2)}) collective-permute-start(bf16[4,48,384]{2,1,0:T(8,128)(2,1)S(1)} %get-tuple-element.100), channel_id=1, source_target_pairs={{0,8},{4,12},{8,0},{12,4},{16,24},{20,28},{24,16},{28,20},{1,9},{5... | collective-permute-start | bytes 442376 | tf_op jit(solution)/shard_map/ppermute | solution.py:540
  34.9 23.9 %collective-permute-start.15 = (bf16[192,768]{1,0:T(8,128)(2,1)S(1)}, bf16[192,768]{1,0:T(8,128)(2,1)S(1)}, u32[]{:S(2)}, u32[]{:S(2)}) collective-permute-start(bf16[192,768]{1,0:T(8,128)(2,1)S(1)} %gate_kernel.1.refs_4_.refs_3_.refs_0_), channel_id=1, source_target_pairs={{0,1},{1,0},{2,3},{3,2},{4,5},{5,4},{6,7},{7,6},{8,9},{9,8},{10,11... | collective-permute-start | bytes 884744 | tf_op jit(solution)/shard_map/ppermute | solution.py:543
  37.6 5.3 %copy-start.11 = (bf16[144,768]{1,0:T(8,128)(2,1)S(1)}, bf16[144,768]{1,0:T(8,128)(2,1)}, u32[]{:S(2)}) copy-start(bf16[144,768]{1,0:T(8,128)(2,1)} %get-tuple-element.95.refs_3_.refs_0_.x0.refs_1_) | copy-start | bytes 663556
  37.6 12.1 %collective-permute-start.13 = (bf16[4,4,48,384]{3,2,1,0:T(8,128)(2,1)S(1)}, bf16[4,4,48,384]{3,2,1,0:T(8,128)(2,1)S(1)}, u32[]{:S(2)}, u32[]{:S(2)}) collective-permute-start(bf16[4,4,48,384]{3,2,1,0:T(8,128)(2,1)S(1)} %pad_maximum_fusion.2.refs_3_.mine), channel_id=1, source_target_pairs={{0,4},{4,0},{8,12},{12,8},{16,20},{20,16},{24,28},{28,24},{1,5},{5... | collective-permute-start | bytes 1769480 | tf_op jit(solution)/shard_map/ppermute | solution.py:537
  41.5 17.3 %collective-permute-start.16 = (bf16[192,768]{1,0:T(8,128)(2,1)S(1)}, bf16[192,768]{1,0:T(8,128)(2,1)S(1)}, u32[]{:S(2)}, u32[]{:S(2)}) collective-permute-start(bf16[192,768]{1,0:T(8,128)(2,1)S(1)} %collective-permute-done.14.refs_8_.refs_2_), channel_id=1, source_target_pairs={{0,1},{1,0},{2,3},{3,2},{4,5},{5,4},{6,7},{7,6},{8,9},{9,8},{10,11... | collective-permute-start | bytes 884744 | tf_op jit(solution)/shard_map/ppermute | solution.py:543
  42.9 5.9 %copy-start.16 = (bf16[768,576]{1,0:T(8,128)(2,1)}, bf16[768,576]{1,0:T(8,128)(2,1)S(1)}, u32[]{:S(2)}) copy-start(bf16[768,576]{1,0:T(8,128)(2,1)S(1)} %get-tuple-element.98.refs_1_.wq.refs_4_) | copy-start | bytes 2654212
  44.7 6.2 %collective-permute-start.12 = (bf16[128,192]{1,0:T(8,128)(2,1)S(1)}, bf16[128,192]{1,0:T(8,128)(2,1)S(1)}, u32[]{:S(2)}, u32[]{:S(2)}) collective-permute-start(bf16[128,192]{1,0:T(8,128)(2,1)S(1)} %get-tuple-element.104), channel_id=1, source_target_pairs={{0,24},{4,28},{8,16},{12,20},{16,8},{20,12},{24,0},{28,4},{1,25},{... | collective-permute-start | bytes 147464 | tf_op jit(solution)/shard_map/ppermute | solution.py:540
  48.2 4.3 %collective-permute-start.11 = (bf16[128,192]{1,0:T(8,128)(2,1)S(1)}, bf16[128,192]{1,0:T(8,128)(2,1)S(1)}, u32[]{:S(2)}, u32[]{:S(2)}) collective-permute-start(bf16[128,192]{1,0:T(8,128)(2,1)S(1)} %get-tuple-element.103), channel_id=1, source_target_pairs={{0,16},{4,20},{8,24},{12,28},{16,0},{20,4},{24,8},{28,12},{1,17},{... | collective-permute-start | bytes 147464 | tf_op jit(solution)/shard_map/ppermute | solution.py:540
  49.7 4.3 %copy-start.12 = (bf16[128,768]{1,0:T(8,128)(2,1)S(1)}, bf16[128,768]{1,0:T(8,128)(2,1)}, u32[]{:S(2)}) copy-start(bf16[128,768]{1,0:T(8,128)(2,1)} %refs_1_.3) | copy-start | bytes 589828
  49.8 4.3 %collective-permute-start.10 = (bf16[128,192]{1,0:T(8,128)(2,1)S(1)}, bf16[128,192]{1,0:T(8,128)(2,1)S(1)}, u32[]{:S(2)}, u32[]{:S(2)}) collective-permute-start(bf16[128,192]{1,0:T(8,128)(2,1)S(1)} %get-tuple-element.102), channel_id=1, source_target_pairs={{0,8},{4,12},{8,0},{12,4},{16,24},{20,28},{24,16},{28,20},{1,9},{5... | collective-permute-start | bytes 147464 | tf_op jit(solution)/shard_map/ppermute | solution.py:540
  55.2 8.4 %collective-permute-start.19 = (bf16[128,768]{1,0:T(8,128)(2,1)S(1)}, bf16[128,768]{1,0:T(8,128)(2,1)S(1)}, u32[]{:S(2)}, u32[]{:S(2)}) collective-permute-start(bf16[128,768]{1,0:T(8,128)(2,1)S(1)} %get-tuple-element.107.y.refs_9_), channel_id=1, source_target_pairs={{0,24},{4,28},{8,16},{12,20},{16,8},{20,12},{24,0},{28,4},{1,25},{... | collective-permute-start | bytes 589832 | tf_op jit(solution)/shard_map/ppermute | solution.py:540
  56.7 8.8 %collective-permute-start.18 = (bf16[128,768]{1,0:T(8,128)(2,1)S(1)}, bf16[128,768]{1,0:T(8,128)(2,1)S(1)}, u32[]{:S(2)}, u32[]{:S(2)}) collective-permute-start(bf16[128,768]{1,0:T(8,128)(2,1)S(1)} %get-tuple-element.107.y.refs_9_), channel_id=1, source_target_pairs={{0,16},{4,20},{8,24},{12,28},{16,0},{20,4},{24,8},{28,12},{1,17},{... | collective-permute-start | bytes 589832 | tf_op jit(solution)/shard_map/ppermute | solution.py:540
  57.2 8.4 %collective-permute-start.17 = (bf16[128,768]{1,0:T(8,128)(2,1)S(1)}, bf16[128,768]{1,0:T(8,128)(2,1)S(1)}, u32[]{:S(2)}, u32[]{:S(2)}) collective-permute-start(bf16[128,768]{1,0:T(8,128)(2,1)S(1)} %get-tuple-element.107.y.refs_9_), channel_id=1, source_target_pairs={{0,8},{4,12},{8,0},{12,4},{16,24},{20,28},{24,16},{28,20},{1,9},{5... | collective-permute-start | bytes 589832 | tf_op jit(solution)/shard_map/ppermute | solution.py:540
  65.7 2.9 %collective-permute-start.20 = (bf16[4,192,768]{2,1,0:T(8,128)(2,1)S(1)}, bf16[4,192,768]{2,1,0:T(8,128)(2,1)S(1)}, u32[]{:S(2)}, u32[]{:S(2)}) collective-permute-start(bf16[4,192,768]{2,1,0:T(8,128)(2,1)S(1)} %join_kernel.1.mine), channel_id=1, source_target_pairs={{0,4},{4,0},{8,12},{12,8},{16,20},{20,16},{24,28},{28,24},{1,5},{5... | collective-permute-start | bytes 3538952 | tf_op jit(solution)/shard_map/ppermute | solution.py:537
  70.0 8.8 %collective-permute-start.23 = (bf16[128,768]{1,0:T(8,128)(2,1)S(1)}, bf16[128,768]{1,0:T(8,128)(2,1)S(1)}, u32[]{:S(2)}, u32[]{:S(2)}) collective-permute-start(bf16[128,768]{1,0:T(8,128)(2,1)S(1)} %get-tuple-element.113), channel_id=1, source_target_pairs={{0,24},{4,28},{8,16},{12,20},{16,8},{20,12},{24,0},{28,4},{1,25},{... | collective-permute-start | bytes 589832 | tf_op jit(solution)/shard_map/ppermute | solution.py:540
  72.2 10.0 %collective-permute-start.22 = (bf16[128,768]{1,0:T(8,128)(2,1)S(1)}, bf16[128,768]{1,0:T(8,128)(2,1)S(1)}, u32[]{:S(2)}, u32[]{:S(2)}) collective-permute-start(bf16[128,768]{1,0:T(8,128)(2,1)S(1)} %get-tuple-element.112), channel_id=1, source_target_pairs={{0,16},{4,20},{8,24},{12,28},{16,0},{20,4},{24,8},{28,12},{1,17},{... | collective-permute-start | bytes 589832 | tf_op jit(solution)/shard_map/ppermute | solution.py:540
  73.5 8.6 %copy-start.13 = (bf16[128,768]{1,0:T(8,128)(2,1)S(1)}, bf16[128,768]{1,0:T(8,128)(2,1)}, u32[]{:S(2)}) copy-start(bf16[128,768]{1,0:T(8,128)(2,1)} %cot.1) | copy-start | bytes 589828
  73.5 8.6 %collective-permute-start.21 = (bf16[128,768]{1,0:T(8,128)(2,1)S(1)}, bf16[128,768]{1,0:T(8,128)(2,1)S(1)}, u32[]{:S(2)}, u32[]{:S(2)}) collective-permute-start(bf16[128,768]{1,0:T(8,128)(2,1)S(1)} %get-tuple-element.111), channel_id=1, source_target_pairs={{0,8},{4,12},{8,0},{12,4},{16,24},{20,28},{24,16},{28,20},{1,9},{5... | collective-permute-start | bytes 589832 | tf_op jit(solution)/shard_map/ppermute | solution.py:540
  83.3 8.7 %collective-permute-start.28 = (bf16[128,768]{1,0:T(8,128)(2,1)S(1)}, bf16[128,768]{1,0:T(8,128)(2,1)S(1)}, u32[]{:S(2)}, u32[]{:S(2)}) collective-permute-start(bf16[128,768]{1,0:T(8,128)(2,1)S(1)} %get-tuple-element.116.d.refs_5_), channel_id=1, source_target_pairs={{0,24},{4,28},{8,16},{12,20},{16,8},{20,12},{24,0},{28,4},{1,25},{... | collective-permute-start | bytes 589832 | tf_op jit(solution)/shard_map/ppermute | solution.py:540
  84.7 11.0 %collective-permute-start.26 = (bf16[128,768]{1,0:T(8,128)(2,1)S(1)}, bf16[128,768]{1,0:T(8,128)(2,1)S(1)}, u32[]{:S(2)}, u32[]{:S(2)}) collective-permute-start(bf16[128,768]{1,0:T(8,128)(2,1)S(1)} %get-tuple-element.116.d.refs_5_), channel_id=1, source_target_pairs={{0,16},{4,20},{8,24},{12,28},{16,0},{20,4},{24,8},{28,12},{1,17},{... | collective-permute-start | bytes 589832 | tf_op jit(solution)/shard_map/ppermute | solution.py:540
  85.3 12.1 %collective-permute-start.24 = (bf16[128,768]{1,0:T(8,128)(2,1)S(1)}, bf16[128,768]{1,0:T(8,128)(2,1)S(1)}, u32[]{:S(2)}, u32[]{:S(2)}) collective-permute-start(bf16[128,768]{1,0:T(8,128)(2,1)S(1)} %get-tuple-element.116.d.refs_5_), channel_id=1, source_target_pairs={{0,8},{4,12},{8,0},{12,4},{16,24},{20,28},{24,16},{28,20},{1,9},{5... | collective-permute-start | bytes 589832 | tf_op jit(solution)/shard_map/ppermute | solution.py:540
  93.0 6.7 %collective-permute-start.29 = (bf16[128,768]{1,0:T(8,128)(2,1)S(1)}, bf16[128,768]{1,0:T(8,128)(2,1)S(1)}, u32[]{:S(2)}, u32[]{:S(2)}) collective-permute-start(bf16[128,768]{1,0:T(8,128)(2,1)S(1)} %get-tuple-element.124), channel_id=1, source_target_pairs={{0,24},{4,28},{8,16},{12,20},{16,8},{20,12},{24,0},{28,4},{1,25},{... | collective-permute-start | bytes 589832 | tf_op jit(solution)/shard_map/ppermute | solution.py:540
  96.6 7.2 %collective-permute-start.27 = (bf16[128,768]{1,0:T(8,128)(2,1)S(1)}, bf16[128,768]{1,0:T(8,128)(2,1)S(1)}, u32[]{:S(2)}, u32[]{:S(2)}) collective-permute-start(bf16[128,768]{1,0:T(8,128)(2,1)S(1)} %get-tuple-element.122), channel_id=1, source_target_pairs={{0,16},{4,20},{8,24},{12,28},{16,0},{20,4},{24,8},{28,12},{1,17},{... | collective-permute-start | bytes 589832 | tf_op jit(solution)/shard_map/ppermute | solution.py:540
  98.4 6.5 %collective-permute-start.25 = (bf16[128,768]{1,0:T(8,128)(2,1)S(1)}, bf16[128,768]{1,0:T(8,128)(2,1)S(1)}, u32[]{:S(2)}, u32[]{:S(2)}) collective-permute-start(bf16[128,768]{1,0:T(8,128)(2,1)S(1)} %get-tuple-element.120), channel_id=1, source_target_pairs={{0,8},{4,12},{8,0},{12,4},{16,24},{20,28},{24,16},{28,20},{1,9},{5... | collective-permute-start | bytes 589832 | tf_op jit(solution)/shard_map/ppermute | solution.py:540
  101.8 13.5 %collective-permute-start.30 = (bf16[4,192,768]{2,1,0:T(8,128)(2,1)S(1)}, bf16[4,192,768]{2,1,0:T(8,128)(2,1)S(1)}, u32[]{:S(2)}, u32[]{:S(2)}) collective-permute-start(bf16[4,192,768]{2,1,0:T(8,128)(2,1)S(1)} %get-tuple-element.135.refs_10_), channel_id=1, source_target_pairs={{0,4},{4,0},{8,12},{12,8},{16,20},{20,16},{24,28},{28,24},{1,5},{5... | collective-permute-start | bytes 3538952 | tf_op jit(solution)/shard_map/ppermute | solution.py:537
  106.2 5.0 %collective-permute-start.31 = (bf16[128,192]{1,0:T(8,128)(2,1)S(1)}, bf16[128,192]{1,0:T(8,128)(2,1)S(1)}, u32[]{:S(2)}, u32[]{:S(2)}) collective-permute-start(bf16[128,192]{1,0:T(8,128)(2,1)S(1)} %get-tuple-element.145), channel_id=1, source_target_pairs={{0,8},{4,12},{8,0},{12,4},{16,24},{20,28},{24,16},{28,20},{1,9},{5... | collective-permute-start | bytes 147464 | tf_op jit(solution)/shard_map/ppermute | solution.py:540
  107.5 4.8 %collective-permute-start.32 = (bf16[128,192]{1,0:T(8,128)(2,1)S(1)}, bf16[128,192]{1,0:T(8,128)(2,1)S(1)}, u32[]{:S(2)}, u32[]{:S(2)}) collective-permute-start(bf16[128,192]{1,0:T(8,128)(2,1)S(1)} %get-tuple-element.148), channel_id=1, source_target_pairs={{0,16},{4,20},{8,24},{12,28},{16,0},{20,4},{24,8},{28,12},{1,17},{... | collective-permute-start | bytes 147464 | tf_op jit(solution)/shard_map/ppermute | solution.py:540
  108.1 5.3 %collective-permute-start.33 = (bf16[128,192]{1,0:T(8,128)(2,1)S(1)}, bf16[128,192]{1,0:T(8,128)(2,1)S(1)}, u32[]{:S(2)}, u32[]{:S(2)}) collective-permute-start(bf16[128,192]{1,0:T(8,128)(2,1)S(1)} %get-tuple-element.151), channel_id=1, source_target_pairs={{0,24},{4,28},{8,16},{12,20},{16,8},{20,12},{24,0},{28,4},{1,25},{... | collective-permute-start | bytes 147464 | tf_op jit(solution)/shard_map/ppermute | solution.py:540
  110.8 3.8 %collective-permute-start.34 = (bf16[4,192,384]{2,1,0:T(8,128)(2,1)S(1)}, bf16[4,192,384]{2,1,0:T(8,128)(2,1)S(1)}, u32[]{:S(2)}, u32[]{:S(2)}) collective-permute-start(bf16[4,192,384]{2,1,0:T(8,128)(2,1)S(1)} %get-tuple-element.144.refs_4_), channel_id=1, source_target_pairs={{0,4},{4,0},{8,12},{12,8},{16,20},{20,16},{24,28},{28,24},{1,5},{5... | collective-permute-start | bytes 1769480 | tf_op jit(solution)/shard_map/ppermute | solution.py:537
  118.7 11.7 %collective-permute-start.35 = (bf16[4,112,576]{2,1,0:T(8,128)(2,1)S(1)}, bf16[4,112,576]{2,1,0:T(8,128)(2,1)S(1)}, u32[]{:S(2)}, u32[]{:S(2)}) collective-permute-start(bf16[4,112,576]{2,1,0:T(8,128)(2,1)S(1)} %get-tuple-element.159), channel_id=1, source_target_pairs={{0,4},{4,0},{8,12},{12,8},{16,20},{20,16},{24,28},{28,24},{1,5},{5... | collective-permute-start | bytes 1548296 | tf_op jit(solution)/shard_map/ppermute | solution.py:537
  119.0 6.7 %collective-permute-start.36 = (bf16[4,48,384]{2,1,0:T(8,128)(2,1)S(1)}, bf16[4,48,384]{2,1,0:T(8,128)(2,1)S(1)}, u32[]{:S(2)}, u32[]{:S(2)}) collective-permute-start(bf16[4,48,384]{2,1,0:T(8,128)(2,1)S(1)} %get-tuple-element.160), channel_id=1, source_target_pairs={{0,8},{4,12},{8,0},{12,4},{16,24},{20,28},{24,16},{28,20},{1,9},{5... | collective-permute-start | bytes 442376 | tf_op jit(solution)/shard_map/ppermute | solution.py:540
  120.3 9.0 %collective-permute-start.37 = (bf16[4,48,384]{2,1,0:T(8,128)(2,1)S(1)}, bf16[4,48,384]{2,1,0:T(8,128)(2,1)S(1)}, u32[]{:S(2)}, u32[]{:S(2)}) collective-permute-start(bf16[4,48,384]{2,1,0:T(8,128)(2,1)S(1)} %get-tuple-element.161), channel_id=1, source_target_pairs={{0,16},{4,20},{8,24},{12,28},{16,0},{20,4},{24,8},{28,12},{1,17},{... | collective-permute-start | bytes 442376 | tf_op jit(solution)/shard_map/ppermute | solution.py:540
  120.9 8.4 %collective-permute-start.38 = (bf16[4,48,384]{2,1,0:T(8,128)(2,1)S(1)}, bf16[4,48,384]{2,1,0:T(8,128)(2,1)S(1)}, u32[]{:S(2)}, u32[]{:S(2)}) collective-permute-start(bf16[4,48,384]{2,1,0:T(8,128)(2,1)S(1)} %get-tuple-element.162), channel_id=1, source_target_pairs={{0,24},{4,28},{8,16},{12,20},{16,8},{20,12},{24,0},{28,4},{1,25},{... | collective-permute-start | bytes 442376 | tf_op jit(solution)/shard_map/ppermute | solution.py:540
  129.4 16.3 %collective-permute-start.43 = (bf16[2,192,768]{2,1,0:T(8,128)(2,1)S(1)}, bf16[2,192,768]{2,1,0:T(8,128)(2,1)S(1)}, u32[]{:S(2)}, u32[]{:S(2)}) collective-permute-start(bf16[2,192,768]{2,1,0:T(8,128)(2,1)S(1)} %get-tuple-element.142.refs_3_), channel_id=1, source_target_pairs={{0,1},{1,0},{2,3},{3,2},{4,5},{5,4},{6,7},{7,6},{8,9},{9,8},{10,11... | collective-permute-start | bytes 1769480 | tf_op jit(solution)/shard_map/ppermute | solution.py:543
  131.2 26.8 %collective-permute-start.42 = (bf16[2,144,576]{2,1,0:T(8,128)(2,1)S(1)}, bf16[2,144,576]{2,1,0:T(8,128)(2,1)S(1)}, u32[]{:S(2)}, u32[]{:S(2)}) collective-permute-start(bf16[2,144,576]{2,1,0:T(8,128)(2,1)S(1)} %get-tuple-element.163.refs_5_.refs_2_), channel_id=1, source_target_pairs={{0,1},{1,0},{2,3},{3,2},{4,5},{5,4},{6,7},{7,6},{8,9},{9,8},{10,11... | collective-permute-start | bytes 995336 | tf_op jit(solution)/shard_map/ppermute | solution.py:543
  133.6 24.4 %collective-permute-start.39 = (bf16[128,768]{1,0:T(8,128)(2,1)S(1)}, bf16[128,768]{1,0:T(8,128)(2,1)S(1)}, u32[]{:S(2)}, u32[]{:S(2)}) collective-permute-start(bf16[128,768]{1,0:T(8,128)(2,1)S(1)} %get-tuple-element.165), channel_id=1, source_target_pairs={{0,8},{4,12},{8,0},{12,4},{16,24},{20,28},{24,16},{28,20},{1,9},{5... | collective-permute-start | bytes 589832 | tf_op jit(solution)/shard_map/ppermute | solution.py:540
  134.4 23.7 %collective-permute-start.40 = (bf16[128,768]{1,0:T(8,128)(2,1)S(1)}, bf16[128,768]{1,0:T(8,128)(2,1)S(1)}, u32[]{:S(2)}, u32[]{:S(2)}) collective-permute-start(bf16[128,768]{1,0:T(8,128)(2,1)S(1)} %get-tuple-element.166), channel_id=1, source_target_pairs={{0,16},{4,20},{8,24},{12,28},{16,0},{20,4},{24,8},{28,12},{1,17},{... | collective-permute-start | bytes 589832 | tf_op jit(solution)/shard_map/ppermute | solution.py:540
  135.7 22.4 %collective-permute-start.41 = (bf16[128,768]{1,0:T(8,128)(2,1)S(1)}, bf16[128,768]{1,0:T(8,128)(2,1)S(1)}, u32[]{:S(2)}, u32[]{:S(2)}) collective-permute-start(bf16[128,768]{1,0:T(8,128)(2,1)S(1)} %get-tuple-element.167), channel_id=1, source_target_pairs={{0,24},{4,28},{8,16},{12,20},{16,8},{20,12},{24,0},{28,4},{1,25},{... | collective-permute-start | bytes 589832 | tf_op jit(solution)/shard_map/ppermute | solution.py:540
  145.8 12.3 %collective-permute-start.45 = (bf16[192,768]{1,0:T(8,128)(2,1)S(1)}, bf16[192,768]{1,0:T(8,128)(2,1)S(1)}, u32[]{:S(2)}, u32[]{:S(2)}) collective-permute-start(bf16[192,768]{1,0:T(8,128)(2,1)S(1)} %get-tuple-element.170.refs_2_), channel_id=1, source_target_pairs={{0,2},{1,3},{2,0},{3,1},{4,6},{5,7},{6,4},{7,5},{8,10},{9,11},{10,... | collective-permute-start | bytes 884744 | tf_op jit(solution)/shard_map/ppermute | solution.py:543
  158.2 10.9 %collective-permute-start.52 = (bf16[192,768]{1,0:T(8,128)(2,1)S(1)}, bf16[192,768]{1,0:T(8,128)(2,1)S(1)}, u32[]{:S(2)}, u32[]{:S(2)}) collective-permute-start(bf16[192,768]{1,0:T(8,128)(2,1)S(1)} %sum_kernel.2.refs_2_), channel_id=1, source_target_pairs={{0,24},{4,28},{8,16},{12,20},{16,8},{20,12},{24,0},{28,4},{1,25},{... | collective-permute-start | bytes 884744 | tf_op jit(solution)/shard_map/ppermute | solution.py:540
  159.9 12.6 %collective-permute-start.51 = (bf16[192,768]{1,0:T(8,128)(2,1)S(1)}, bf16[192,768]{1,0:T(8,128)(2,1)S(1)}, u32[]{:S(2)}, u32[]{:S(2)}) collective-permute-start(bf16[192,768]{1,0:T(8,128)(2,1)S(1)} %sum_kernel.2.refs_2_), channel_id=1, source_target_pairs={{0,16},{4,20},{8,24},{12,28},{16,0},{20,4},{24,8},{28,12},{1,17},{... | collective-permute-start | bytes 884744 | tf_op jit(solution)/shard_map/ppermute | solution.py:540
  160.7 11.8 %collective-permute-start.50 = (bf16[192,768]{1,0:T(8,128)(2,1)S(1)}, bf16[192,768]{1,0:T(8,128)(2,1)S(1)}, u32[]{:S(2)}, u32[]{:S(2)}) collective-permute-start(bf16[192,768]{1,0:T(8,128)(2,1)S(1)} %sum_kernel.2.refs_2_), channel_id=1, source_target_pairs={{0,8},{4,12},{8,0},{12,4},{16,24},{20,28},{24,16},{28,20},{1,9},{5... | collective-permute-start | bytes 884744 | tf_op jit(solution)/shard_map/ppermute | solution.py:540
  161.7 11.0 %collective-permute-start.44 = (bf16[144,576]{1,0:T(8,128)(2,1)S(1)}, bf16[144,576]{1,0:T(8,128)(2,1)S(1)}, u32[]{:S(2)}, u32[]{:S(2)}) collective-permute-start(bf16[144,576]{1,0:T(8,128)(2,1)S(1)} %get-tuple-element.172.refs_5_), channel_id=1, source_target_pairs={{0,2},{1,3},{2,0},{3,1},{4,6},{5,7},{6,4},{7,5},{8,10},{9,11},{10,... | collective-permute-start | bytes 497672 | tf_op jit(solution)/shard_map/ppermute | solution.py:543
  172.7 12.4 %collective-permute-start.53 = (bf16[4,192,768]{2,1,0:T(8,128)(2,1)S(1)}, bf16[4,192,768]{2,1,0:T(8,128)(2,1)S(1)}, u32[]{:S(2)}, u32[]{:S(2)}) collective-permute-start(bf16[4,192,768]{2,1,0:T(8,128)(2,1)S(1)} %pad_maximum_fusion.refs_1_), channel_id=1, source_target_pairs={{0,4},{4,0},{8,12},{12,8},{16,20},{20,16},{24,28},{28,24},{1,5},{5... | collective-permute-start | bytes 3538952 | tf_op jit(solution)/shard_map/ppermute | solution.py:537
  172.8 8.4 %collective-permute-start.48 = (bf16[144,576]{1,0:T(8,128)(2,1)S(1)}, bf16[144,576]{1,0:T(8,128)(2,1)S(1)}, u32[]{:S(2)}, u32[]{:S(2)}) collective-permute-start(bf16[144,576]{1,0:T(8,128)(2,1)S(1)} %sum_kernel.3.refs_3_), channel_id=1, source_target_pairs={{0,24},{4,28},{8,16},{12,20},{16,8},{20,12},{24,0},{28,4},{1,25},{... | collective-permute-start | bytes 497672 | tf_op jit(solution)/shard_map/ppermute | solution.py:540
  174.6 10.1 %collective-permute-start.47 = (bf16[144,576]{1,0:T(8,128)(2,1)S(1)}, bf16[144,576]{1,0:T(8,128)(2,1)S(1)}, u32[]{:S(2)}, u32[]{:S(2)}) collective-permute-start(bf16[144,576]{1,0:T(8,128)(2,1)S(1)} %sum_kernel.3.refs_3_), channel_id=1, source_target_pairs={{0,16},{4,20},{8,24},{12,28},{16,0},{20,4},{24,8},{28,12},{1,17},{... | collective-permute-start | bytes 497672 | tf_op jit(solution)/shard_map/ppermute | solution.py:540
  175.6 9.2 %collective-permute-start.46 = (bf16[144,576]{1,0:T(8,128)(2,1)S(1)}, bf16[144,576]{1,0:T(8,128)(2,1)S(1)}, u32[]{:S(2)}, u32[]{:S(2)}) collective-permute-start(bf16[144,576]{1,0:T(8,128)(2,1)S(1)} %sum_kernel.3.refs_3_), channel_id=1, source_target_pairs={{0,8},{4,12},{8,0},{12,4},{16,24},{20,28},{24,16},{28,20},{1,9},{5... | collective-permute-start | bytes 497672 | tf_op jit(solution)/shard_map/ppermute | solution.py:540
  176.5 11.7 %copy-start = (f32[128,768]{1,0:T(8,128)}, f32[128,768]{1,0:T(8,128)S(1)}, u32[]{:S(2)}) copy-start(f32[128,768]{1,0:T(8,128)S(1)} %add_add_fusion.refs_4_) | copy-start | bytes 1179652
  184.9 3.3 %collective-permute-start.49 = (bf16[4,144,576]{2,1,0:T(8,128)(2,1)S(1)}, bf16[4,144,576]{2,1,0:T(8,128)(2,1)S(1)}, u32[]{:S(2)}, u32[]{:S(2)}) collective-permute-start(bf16[4,144,576]{2,1,0:T(8,128)(2,1)S(1)} %pad_maximum_fusion.1.refs_1_), channel_id=1, source_target_pairs={{0,4},{4,0},{8,12},{12,8},{16,20},{20,16},{24,28},{28,24},{1,5},{5... | collective-permute-start | bytes 1990664 | tf_op jit(solution)/shard_map/ppermute | solution.py:537
  (8 other events, 11.0 us)

commit v3 on v2

--- a/solution.py
+++ b/solution.py
@@ -145,10 +145,10 @@
 
 def split_kernel(g0, g1, g2, g3, first, second):
     base = first.shape[1]
+    cols = second.shape[2]
+    third = second.shape[1] // 3
     for k, g in enumerate((g0, g1, g2, g3)):
         first[k] = g[:base, :]
-        cols = second.shape[2]
-        third = second.shape[1] // 3
         top, low = g[base : base + third, :], g[base + third :, :]
         second[k, :third] = top[:, :cols]
         second[k, third : 2 * third] = low[:, :cols]
@@ -156,8 +156,12 @@
         second[k, 2 * third :, cols // 2 :] = low[:, cols:]
 
 
-def sum_kernel(own, got, out):
-    out[...] = (own[...] + got[...].astype(F32)).astype(out.dtype)
+def sum_kernel(*refs):
+    out = refs[-1]
+    v = refs[0][...].astype(F32)
+    for r in refs[1:-1]:
+        v = v + r[...].astype(F32)
+    out[...] = v.astype(out.dtype)
 
 
 def wq_kernel(idx, mine, other, wq, small, bias):
@@ -236,7 +240,12 @@
     y1low[...] = y.astype(BF)
 
 
-def join_kernel(g0, g1, g2, g3, out):
+def join_kernel(near, far, out):
+    out[:2] = near[...]
+    out[2:] = far[...]
+
+
+def stack_kernel(g0, g1, g2, g3, out):
     for k, g in enumerate((g0, g1, g2, g3)):
         out[k] = g[...]
 
@@ -312,19 +321,13 @@
     hid[...] = jnp.broadcast_to(h, hid.shape)
 
 
-def add_kernel(idx, mine, got, keep, send):
+def add_kernel(idx, mine, got, own, near, far, send):
     z = idx[2]
-    for n in range(4):
-        out, m, j = (keep, send)[n % 2], n // 2, z ^ n
-        out[m] = (mine[j].astype(F32) + got[j].astype(F32)).astype(out.dtype)
-
-
-def add_far_kernel(keep, got, own, send):
-    own[...] = keep[0] + got[0].astype(F32)
-    send[...] = (keep[1] + got[1].astype(F32)).astype(BF)
-
-
-def fin1_kernel(idx, mine, other, gup, gdown):
+    for k, out in enumerate((own, near, far, send)):
+        out[...] = (mine[z ^ k].astype(F32) + got[z ^ k].astype(F32)).astype(out.dtype)
+
+
+def fin1_kernel(idx, mine, other, gup, gdown, token):
     c, core = idx[0], idx[1]
     parts, _, width = mine.shape
     half = gup.shape[0] // 2
@@ -332,6 +335,7 @@
     shards = gup.shape[1] // (parts * fc)
     for j in range(parts):
         k = j ^ c
+        token[...] = jnp.zeros_like(token)
         for src, row in ((mine, core * half), (other, (1 - core) * half)):
             v = src[k, :half, :].astype(F32)
             for s in range(shards):
@@ -436,19 +440,19 @@
         give[j, half:, :] = rows
 
 
-def add2_kernel(idx, mine, got, osum, keep, send):
+def add2_kernel(idx, mine, got, osum, own, near, far, send):
     z = idx[2]
     base, _ = mine.shape[1:]
     piece, cols = osum.shape[1:]
     third = piece // 3
-    for n in range(4):
-        out, m, j = (keep, send)[n % 2], n // 2, z ^ n
-        out[m, :base, :] = (mine[j].astype(F32) + got[j].astype(F32)).astype(out.dtype)
+    for n, out in enumerate((own, near, far, send)):
+        j = z ^ n
+        out[:base, :] = (mine[j].astype(F32) + got[j].astype(F32)).astype(out.dtype)
         w = osum[j]
 
-        def put(row, col, v, out=out, m=m):
+        def put(row, col, v, out=out):
             rng = slice(base + row * third, base + (row + 1) * third)
-            out[m, rng, col : col + v.shape[1]] = v.astype(out.dtype)
+            out[rng, col : col + v.shape[1]] = v.astype(out.dtype)
 
         fold_piece(put, lambda g, col, k, w=w: w[g * third : (g + 1) * third, col : col + k], cols)
 
@@ -548,8 +552,10 @@
     def spread_shard(v):
         return [v] + [swap_shard(v, k) for k in range(1, shards)]
 
-    def relay_shard(v):
+    def relay_shard(v, after=None):
         near, far = swap_shard(v, 1), swap_shard(v, 2)
+        if after is not None:
+            far = gate(far, after())
         return [v, near, far, swap_shard(far, 1)]
 
     def trade_part(slots):
@@ -613,8 +619,8 @@
                 pltpu.SemaphoreType.DMA((7,)),
             ],
         )
-        got1 = relay_shard(pay1)
         xs = spread_part(xp)
+        got1 = relay_shard(pay1, lambda: [xs[3]])
         (pay2,) = call(
             pack2_kernel,
             [((half + fc // CORES, width), BF)],
@@ -626,16 +632,14 @@
             scratch=[((half, w_up.shape[1]), BF), pltpu.SemaphoreType.DMA((2,))],
         )
         pay2 = gate(pay2, [got1[3]] + xs[1:])
-        got2 = relay_shard(pay2)
         mine1, pay_o = call(
             split_kernel,
             [((shards, half + 16, span), BF), ((shards, piece, ocol), BF)],
             *got1,
-            after=[pay2],
         )
         other1 = swap_core(mine1)
-        mine_o = jnp.stack(spread_part(pay_o))
-        other_o = swap_core(mine_o)
+        pair_o = jnp.stack([pay_o, swap_part(pay_o, 1)])
+        far_o = swap_part(pair_o, 2)
 
         wq, small, bias = call(
             wq_kernel,
@@ -652,11 +656,15 @@
                 x,
                 wq,
                 bias,
-                after=[] if k else [mine_o],
             )
             for k, x in enumerate(xs)
         ]
         mix = trade_part([a[2] for a in att])
+        got2 = relay_shard(pay2, lambda: mix[1:])
+        (mine_o,) = call(
+            join_kernel, [((PARTS,) + pay_o.shape, BF)], pair_o, far_o, after=[att[3][2]]
+        )
+        other_o = swap_core(mine_o)
         (wo,) = call(wo_kernel, [((width, width), BF)], mine_o, other_o, idx=idx)
         y1, y1low, unit1, inv1 = call(
             out_kernel,
@@ -666,11 +674,10 @@
             wo,
             small,
             idx=idx,
-            after=[got2[2]],
         )
         ys = spread_part(y1low)
         (mine2,) = call(
-            join_kernel, [((shards,) + pay2.shape, BF)], *got2, after=ys[1:]
+            stack_kernel, [((shards,) + pay2.shape, BF)], *got2, after=ys[1:]
         )
         wu, wd = call(
             w2_kernel,
@@ -705,8 +712,19 @@
             call(
                 ffb_kernel, [((rows, shards * fc), BF), ((rows, width), t)], d, wu, wd, f[1]
             )
-            for d, f, t in zip(dzs, ffn, part_type)
+            for d, f, t in list(zip(dzs, ffn, part_type))[1:]
         ]
+        ffb = [
+            call(
+                ffb_kernel,
+                [((rows, shards * fc), BF), ((rows, width), F32)],
+                dz,
+                wu,
+                wd,
+                ffn[0][1],
+                after=[f[0] for f in ffb],
+            )
+        ] + ffb
         dyp = trade_part([f[1] for f in ffb])
         rows1 = half + fc // CORES
         give1, keep1, sm3 = call(
@@ -720,6 +738,33 @@
             after=[dyp[3]],
             scratch=[((PARTS * rows, width), BF)] * 2 + [((width, width), BF)],
         )
+        def relay_sum(far, send, after):
+            got = swap_shard(send, 1)
+            (low,) = call(sum_kernel, [(far.shape, BF)], far, got, after=after)
+            return low, swap_shard(low, 2)
+
+        def join(own, near, far, after):
+            if reps > CORES * PARTS:
+                return sum_outer(own + near.astype(F32) + far.astype(F32)).astype(BF)
+            return call(sum_kernel, [(own.shape, BF)], own, near, far, after=after)[0]
+
+        def spread_piece(v, after):
+            (done,) = call(
+                stack_kernel, [((PARTS,) + v.shape, BF)], *spread_part(v), after=after
+            )
+            return done, swap_core(done)
+
+        def pair_shapes(n, w):
+            return [((n, w), F32), ((n, w), BF), ((n, w), F32), ((n, w), BF)]
+
+        own_a, near_a, far_a, send_a = call(
+            add_kernel,
+            pair_shapes(rows1, width),
+            keep1,
+            swap_core(give1),
+            idx=idx,
+            after=[dyp[3]],
+        )
         gh1, da, *rest = call(
             ln1b_kernel,
             [((rows, width), F32)] + mats + [((rows, hc), BF)] * PARTS + [((8, width), F32)],
@@ -730,7 +775,7 @@
             small,
             wo,
             idx=idx,
-            after=[give1],
+            after=[send_a],
         )
         dm, sm1 = trade_part(rest[:PARTS]), rest[PARTS]
         give_o, keep_o = call(
@@ -748,40 +793,9 @@
             swap_core(give_o),
             idx=idx,
         )
-        osum = total(trade_part(out_send))
-
-        def halve(keep, send, after):
-            n, w = keep.shape[1:]
-            own, far = call(
-                add_far_kernel,
-                [((n, w), F32), ((n, w), BF)],
-                keep,
-                swap_shard(send, 1),
-                after=after,
-            )
-            return own, far
-
-        def join(own, far, after):
-            got = swap_shard(far, 2)
-            if reps > CORES * PARTS:
-                return sum_outer(own + got.astype(F32)).astype(BF)
-            return call(sum_kernel, [(own.shape, BF)], own, got, after=after)[0]
-
-        def spread_piece(v):
-            done = jnp.stack(spread_part(v))
-            return done, swap_core(done)
-
-        def pair_shapes(n, w):
-            return [((2, n, w), F32), ((2, n, w), BF)]
-
-        keep_a, send_a = call(
-            add_kernel,
-            pair_shapes(rows1, width),
-            keep1,
-            swap_core(give1),
-            idx=idx,
-            after=[sm1],
-        )
+        out_got = trade_part(out_send)
+        osum = total(out_got)
+
         dps = [
             call(
                 attb_kernel,
@@ -789,10 +803,12 @@
                 d,
                 a[0],
                 a[1],
-                after=[] if k else [send_a, give_o],
+                after=[out_send[0]] if k < 2 else [],
             )[0]
             for k, (d, a) in enumerate(zip(dm, att))
         ]
+        low_a, got_a = relay_sum(far_a, send_a, [dps[3]])
+        near_a = swap_shard(gate(near_a, [low_a]), 1)
         rows2 = half + 16
         give2, keep2 = call(
             qw_kernel,
@@ -803,34 +819,35 @@
             sm2,
             sm3,
             idx=idx,
-            after=[out_send[0]],
+            after=[out_got[1], low_a],
             scratch=[
                 ((PARTS * rows, width), BF),
                 ((PARTS * rows, span), BF),
                 ((width, span), BF),
             ],
         )
-        keep_b, send_b = call(
+        dxp = call(
+            dx_kernel, [((rows, width), t) for t in part_type], *dps, wq, after=[give2] + out_got[2:]
+        )
+        dxp_got = trade_part(dxp)
+        own_b, near_b, far_b, send_b = call(
             add2_kernel,
             pair_shapes(rows2 + 2 * piece // 3, span),
             keep2,
             swap_core(give2),
             osum,
             idx=idx,
-        )
-        dxp = call(
-            dx_kernel, [((rows, width), t) for t in part_type], *dps, wq, after=[send_b]
-        )
-        dxp_got = trade_part(dxp)
-        own_a, far_a = halve(keep_a, send_a, [send_b])
-        own_b, far_b = halve(keep_b, send_b, [far_a])
-        piece1 = join(own_a, far_a, dxp_got[1:] + [far_b])
-        piece2 = join(own_b, far_b, [piece1])
-        done1 = spread_piece(piece1)
-        done2 = spread_piece(piece2)
+            after=[got_a, dxp[0]],
+        )
+        low_b, got_b = relay_sum(far_b, send_b, dxp_got[1:])
+        near_b = swap_shard(gate(near_b, [low_b]), 1)
+        piece1 = join(own_a, near_a, got_a, [low_b])
+        done1 = spread_piece(piece1, [got_b, near_b])
+        piece2 = join(own_b, near_b, got_b, [])
+        done2 = spread_piece(piece2, [])
         g_tok = gh1 + total(dxp_got)
-        gw_up, gw_down = call(
-            fin1_kernel, [(w_up.shape, F32), (w_down.shape, F32)], *done1, idx=idx, after=[piece2]
+        gw_up, gw_down, token = call(
+            fin1_kernel, [(w_up.shape, F32), (w_down.shape, F32), ((8, 128), F32)], *done1, idx=idx, after=[piece2]
         )
         gw_qkv, gw_out, g_vec, g_gain, g_hidden = call(
             fin2_kernel,
@@ -843,7 +860,7 @@
             ],
             *done2,
             idx=idx,
-            after=[gw_up, g_tok],
+            after=[token, g_tok],
         )
         return (
             activations,

time: 193 us -> 177 us (0.917)
  waiting for transfers between devices: 83.8 us -> 71.9 us
  local copies, waits for them, and re-layouts: 5.22 us -> 2.32 us
    ppermute x36 -> x35, waiting for transfers between devices: 55.6 us -> 40 us  [swap_part(): return lax.ppermute(v, 'rep', xor_perm(reps, CORES * k))]
    ppermute x10 -> x12, waiting for transfers between devices: 25.4 us -> 28.5 us  [swap_shard(): return lax.ppermute(v, 'shard', xor_perm(shards, k))]
    unnamed x36 -> x50, local copies, waits for them, and re-layouts: 3.96 us -> 1.05 us
    ppermute x10 -> x12, starting transfers between devices: 19 us -> 17.5 us  [swap_shard(): return lax.ppermute(v, 'shard', xor_perm(shards, k))]
    ppermute x36 -> x35, starting transfers between devices: 42.6 us -> 43.2 us  [swap_part(): return lax.ppermute(v, 'rep', xor_perm(reps, CORES * k))]
    pallas_call x39 -> x42, Pallas kernels: 38.2 us -> 38.3 us  [call(): pl.pallas_call(run if drop else kernel, out_shape=shapes, in_specs=specs,...]
  transfers between devices with their start and end apart: 54 -> 55, of which waited for: 29 -> 32; matrix products, arithmetic and copies ran while one was open for 0% -> 0% of each run, Pallas kernels for 14% -> 16%
where the time goes in v3:
time: 177 us; the launch traced here: 176 us
  waiting for transfers between devices  71.9 us (41%)
  starting transfers between devices  61.1 us (35%)
  Pallas kernels  38.3 us (22%)
  local copies, waits for them, and re-layouts  2.32 us (1%)
    ppermute x35, starting transfers between devices, swap_part(): return lax.ppermute(v, 'rep', xor_perm(reps, CORES * k))  43.2 us
    ppermute x35, waiting for transfers between devices, swap_part(): return lax.ppermute(v, 'rep', xor_perm(reps, CORES * k))  40 us
    pallas_call x42, Pallas kernels, call(): pl.pallas_call(run if drop else kernel, out_shape=shapes, in_specs=specs,...  38.3 us
    ppermute x12, waiting for transfers between devices, swap_shard(): return lax.ppermute(v, 'shard', xor_perm(shards, k))  28.5 us
    ppermute x12, starting transfers between devices, swap_shard(): return lax.ppermute(v, 'shard', xor_perm(shards, k))  17.5 us
  transfers between devices with their start and end apart: 55, of which 32 were waited for; matrix products, arithmetic and copies ran while one was open for 0% of the time, Pallas kernels for 16%

profile of v3, /device:TPU:0, one launch (start us, length us, event | category | flops | bytes accessed | tf_op | source)
XLA Modules:
  0.0 176.4 jit_solution(10094246981467179919)
XLA Ops:
  0.7 1.3 reshape.24.hid_in
  2.5 2.7 %pack_kernel.1 = (bf16[144,768]{1,0:T(8,128)(2,1)}, bf16[144,576]{1,0:T(8,128)(2,1)}) custom-call(s32[3]{0:T(128)} %pad_add_fusion.idx.refs_0_, bf16[128,768]{1,0:T(8,128)(2,1)} %tok.3, bf16[192,2304]{1,0:T(8,128)(2,1)} %wqkv.1, bf16[192,768]{1,0:T(8,128)(2,1)} %wout.1, bf16[6,192]{1,0:T(8,128)(2,1)} %vec_in.1, bf16[2,192]{1,0:T(2,128)(2,1)} %gain_in.1, ...), custom_call_target="tpu_custom_call" | custom-call | flops 11000000512 | bytes 100000 | tf_op jit(solution)/shard_map/pack_kernel/pallas_call | solution.py:511
  5.2 4.0 %collective-permute-start.2 = (bf16[144,768]{1,0:T(8,128)(2,1)}, bf16[144,768]{1,0:T(8,128)(2,1)S(1)}, u32[]{:S(2)}, u32[]{:S(2)}) collective-permute-start(bf16[144,768]{1,0:T(8,128)(2,1)} %get-tuple-element.96.refs_3_.x.x0.refs_1_), channel_id=1, source_target_pairs={{0,24},{4,28},{8,16},{12,20},{16,8},{20,12},{24,0},{28,4},{1,25},{... | collective-permute-start | bytes 663560 | tf_op jit(solution)/shard_map/ppermute | solution.py:544
  9.2 2.6 %collective-permute-start.1 = (bf16[144,576]{1,0:T(8,128)(2,1)}, bf16[144,576]{1,0:T(8,128)(2,1)S(1)}, u32[]{:S(2)}, u32[]{:S(2)}) collective-permute-start(bf16[144,576]{1,0:T(8,128)(2,1)} %get-tuple-element.97.g0), channel_id=1, source_target_pairs={{0,2},{1,3},{2,0},{3,1},{4,6},{5,7},{6,4},{7,5},{8,10},{9,11},{10,... | collective-permute-start | bytes 497672 | tf_op jit(solution)/shard_map/ppermute | solution.py:547
  11.8 1.6 collective-permute-start
  13.4 7.1 %collective-permute-done.1.refs_0_ = bf16[144,576]{1,0:T(8,128)(2,1)S(1)} collective-permute-done((bf16[144,576]{1,0:T(8,128)(2,1)}, bf16[144,576]{1,0:T(8,128)(2,1)S(1)}, u32[]{:S(2)}, u32[]{:S(2)}) %collective-permute-start.1) | collective-permute-done | bytes 165920 | tf_op jit(solution)/shard_map/ppermute | solution.py:547
  22.3 3.8 %collective-permute-done.3.g3.refs_1_ = bf16[144,576]{1,0:T(8,128)(2,1)S(1)} collective-permute-done((bf16[144,576]{1,0:T(8,128)(2,1)S(1)}, bf16[144,576]{1,0:T(8,128)(2,1)S(1)}, u32[]{:S(2)}, u32[]{:S(2)}) %collective-permute-start.3) | collective-permute-done | bytes 165920 | tf_op jit(solution)/shard_map/ppermute | solution.py:547
  29.3 2.8 %collective-permute-start.14 = (bf16[192,768]{1,0:T(8,128)(2,1)S(1)}, bf16[192,768]{1,0:T(8,128)(2,1)S(1)}, u32[]{:S(2)}, u32[]{:S(2)}) collective-permute-start(bf16[192,768]{1,0:T(8,128)(2,1)S(1)} %gate_kernel.6.refs_3_.refs_0_), channel_id=1, source_target_pairs={{0,2},{1,3},{2,0},{3,1},{4,6},{5,7},{6,4},{7,5},{8,10},{9,11},{10,... | collective-permute-start | bytes 884744 | tf_op jit(solution)/shard_map/ppermute | solution.py:547
  32.4 1.7 collective-permute-start.11
  35.7 1.2 collective-permute-start.9
  39.7 1.6 collective-permute-start.7
  41.3 2.2 %collective-permute-done.11.refs_1_ = bf16[2,4,48,384]{3,2,1,0:T(8,128)(2,1)S(1)} collective-permute-done((bf16[2,4,48,384]{3,2,1,0:T(8,128)(2,1)S(1)}, bf16[2,4,48,384]{3,2,1,0:T(8,128)(2,1)S(1)}, u32[]{:S(2)}, u32[]{:S(2)}) %collective-permute-start.11) | collective-permute-done | bytes 294944 | tf_op jit(solution)/shard_map/ppermute | solution.py:544
  44.5 1.6 collective-permute-done.14.refs_0_
  46.9 1.3 collective-permute-start.15
  49.0 1.1 out_kernel.1
  50.1 1.5 collective-permute-start.18
  51.6 1.5 collective-permute-start.17
  53.6 2.3 %collective-permute-done.13.refs_1_ = bf16[192,768]{1,0:T(8,128)(2,1)S(1)} collective-permute-done((bf16[192,768]{1,0:T(8,128)(2,1)S(1)}, bf16[192,768]{1,0:T(8,128)(2,1)S(1)}, u32[]{:S(2)}, u32[]{:S(2)}) %collective-permute-start.13) | collective-permute-done | bytes 294944 | tf_op jit(solution)/shard_map/ppermute | solution.py:547
  56.0 5.2 %collective-permute-done.15.refs_3_ = bf16[192,768]{1,0:T(8,128)(2,1)S(1)} collective-permute-done((bf16[192,768]{1,0:T(8,128)(2,1)S(1)}, bf16[192,768]{1,0:T(8,128)(2,1)S(1)}, u32[]{:S(2)}, u32[]{:S(2)}) %collective-permute-start.15) | collective-permute-done | bytes 294944 | tf_op jit(solution)/shard_map/ppermute | solution.py:547
  61.5 2.8 %collective-permute-done.19.other = bf16[4,192,768]{2,1,0:T(8,128)(2,1)S(1)} collective-permute-done((bf16[4,192,768]{2,1,0:T(8,128)(2,1)S(1)}, bf16[4,192,768]{2,1,0:T(8,128)(2,1)S(1)}, u32[]{:S(2)}, u32[]{:S(2)}) %collective-permute-start.19) | collective-permute-done | bytes 1179680 | tf_op jit(solution)/shard_map/ppermute | solution.py:541
  65.8 1.7 collective-permute-start.22
  68.1 1.3 collective-permute-start.21
  71.5 3.0 %collective-permute-done.22.r3 = bf16[128,768]{1,0:T(8,128)(2,1)S(1)} collective-permute-done((bf16[128,768]{1,0:T(8,128)(2,1)S(1)}, bf16[128,768]{1,0:T(8,128)(2,1)S(1)}, u32[]{:S(2)}, u32[]{:S(2)}) %collective-permute-start.22) | collective-permute-done | bytes 196640 | tf_op jit(solution)/shard_map/ppermute | solution.py:544
  74.5 3.4 %collective-permute-done.21.r2 = bf16[128,768]{1,0:T(8,128)(2,1)S(1)} collective-permute-done((bf16[128,768]{1,0:T(8,128)(2,1)S(1)}, bf16[128,768]{1,0:T(8,128)(2,1)S(1)}, u32[]{:S(2)}, u32[]{:S(2)}) %collective-permute-start.21) | collective-permute-done | bytes 196640 | tf_op jit(solution)/shard_map/ppermute | solution.py:544
  77.9 1.2 ln2_kernel.1
  79.0 1.6 collective-permute-start.25
  80.7 1.2 collective-permute-start.24
  82.5 5.2 %collective-permute-done.25.d.refs_8_ = bf16[128,768]{1,0:T(8,128)(2,1)S(1)} collective-permute-done((bf16[128,768]{1,0:T(8,128)(2,1)S(1)}, bf16[128,768]{1,0:T(8,128)(2,1)S(1)}, u32[]{:S(2)}, u32[]{:S(2)}) %collective-permute-start.25) | collective-permute-done | bytes 196640 | tf_op jit(solution)/shard_map/ppermute | solution.py:544
  88.7 1.7 collective-permute-start.28
  90.4 1.0 collective-permute-done.24.d.refs_7_
  94.3 1.1 collective-permute-done.28.refs_17_.refs_3_.refs_5_
  95.3 2.1 %ffw_kernel.1 = (bf16[4,192,768]{2,1,0:T(8,128)(2,1)S(1)}, bf16[4,192,768]{2,1,0:T(8,128)(2,1)S(1)}, f32[8,768]{1,0:T(8,128)S(1)}) custom-call(s32[3]{0:T(128)S(1)} %copy-done.13, bf16[128,768]{1,0:T(8,128)(2,1)S(1)} %get-tuple-element.131.refs_1_, bf16[128,768]{1,0:T(8,128)(2,1)S(1)} %get-tuple-element.132.refs_2_, ...), custom_call_target="tpu_custom_call" | custom-call | flops 11000000512 | bytes 100000 | tf_op jit(solution)/shard_map/ffw_kernel/pallas_call | solution.py:511
  98.2 1.6 collective-permute-start.26
  102.2 2.7 %collective-permute-done.27.refs_4_ = bf16[128,768]{1,0:T(8,128)(2,1)S(1)} collective-permute-done((bf16[128,768]{1,0:T(8,128)(2,1)S(1)}, bf16[128,768]{1,0:T(8,128)(2,1)S(1)}, u32[]{:S(2)}, u32[]{:S(2)}) %collective-permute-start.27) | collective-permute-done | bytes 196640 | tf_op jit(solution)/shard_map/ppermute | solution.py:544
  105.2 1.3 ln1b_kernel.1
  106.5 1.8 %collective-permute-start.31 = (bf16[128,192]{1,0:T(8,128)(2,1)S(1)}, bf16[128,192]{1,0:T(8,128)(2,1)S(1)}, u32[]{:S(2)}, u32[]{:S(2)}) collective-permute-start(bf16[128,192]{1,0:T(8,128)(2,1)S(1)} %get-tuple-element.148), channel_id=1, source_target_pairs={{0,8},{4,12},{8,0},{12,4},{16,24},{20,28},{24,16},{28,20},{1,9},{5... | collective-permute-start | bytes 147464 | tf_op jit(solution)/shard_map/ppermute | solution.py:544
  108.4 1.2 collective-permute-start.32
  110.3 1.1 outw_kernel.1
  111.4 1.9 %collective-permute-done.32.d = bf16[128,192]{1,0:T(8,128)(2,1)S(1)} collective-permute-done((bf16[128,192]{1,0:T(8,128)(2,1)S(1)}, bf16[128,192]{1,0:T(8,128)(2,1)S(1)}, u32[]{:S(2)}, u32[]{:S(2)}) %collective-permute-start.32) | collective-permute-done | bytes 49184 | tf_op jit(solution)/shard_map/ppermute | solution.py:544
  113.3 1.1 attb_kernel.6.refs_7_.refs_2_
  114.8 1.1 attb_kernel.7.refs_2_.refs_8_.refs_3_
  116.0 2.6 %collective-permute-start.42 = (bf16[192,768]{1,0:T(8,128)(2,1)S(1)}, bf16[192,768]{1,0:T(8,128)(2,1)S(1)}, u32[]{:S(2)}, u32[]{:S(2)}) collective-permute-start(bf16[192,768]{1,0:T(8,128)(2,1)S(1)} %sum_kernel.4.refs_13_.refs_1_), channel_id=1, source_target_pairs={{0,2},{1,3},{2,0},{3,1},{4,6},{5,7},{6,4},{7,5},{8,10},{9,11},{10,... | collective-permute-start | bytes 884744 | tf_op jit(solution)/shard_map/ppermute | solution.py:547
  120.8 2.0 %collective-permute-start.37 = (bf16[4,48,384]{2,1,0:T(8,128)(2,1)S(1)}, bf16[4,48,384]{2,1,0:T(8,128)(2,1)S(1)}, u32[]{:S(2)}, u32[]{:S(2)}) collective-permute-start(bf16[4,48,384]{2,1,0:T(8,128)(2,1)S(1)} %get-tuple-element.163), channel_id=1, source_target_pairs={{0,24},{4,28},{8,16},{12,20},{16,8},{20,12},{24,0},{28,4},{1,25},{... | collective-permute-start | bytes 442376 | tf_op jit(solution)/shard_map/ppermute | solution.py:544
  122.8 1.1 attb_kernel.4.refs_5_.refs_0_
  124.0 1.1 attb_kernel.5.refs_6_.refs_1_
  125.8 1.5 qw_kernel.1
  128.1 1.4 dx_kernel.1
  129.5 1.2 collective-permute-start.38
  131.2 1.8 %collective-permute-start.40 = (bf16[128,768]{1,0:T(8,128)(2,1)S(1)}, bf16[128,768]{1,0:T(8,128)(2,1)S(1)}, u32[]{:S(2)}, u32[]{:S(2)}) collective-permute-start(bf16[128,768]{1,0:T(8,128)(2,1)S(1)} %get-tuple-element.167), channel_id=1, source_target_pairs={{0,24},{4,28},{8,16},{12,20},{16,8},{20,12},{24,0},{28,4},{1,25},{... | collective-permute-start | bytes 589832 | tf_op jit(solution)/shard_map/ppermute | solution.py:544
  133.9 1.8 %collective-permute-start.43 = (bf16[144,576]{1,0:T(8,128)(2,1)S(1)}, bf16[144,576]{1,0:T(8,128)(2,1)S(1)}, u32[]{:S(2)}, u32[]{:S(2)}) collective-permute-start(bf16[144,576]{1,0:T(8,128)(2,1)S(1)} %get-tuple-element.172), channel_id=1, source_target_pairs={{0,1},{1,0},{2,3},{3,2},{4,5},{5,4},{6,7},{7,6},{8,9},{9,8},{10,11... | collective-permute-start | bytes 497672 | tf_op jit(solution)/shard_map/ppermute | solution.py:547
  136.0 1.4 collective-permute-done.38.refs_2_
  137.3 3.5 %collective-permute-done.40.refs_4_ = bf16[128,768]{1,0:T(8,128)(2,1)S(1)} collective-permute-done((bf16[128,768]{1,0:T(8,128)(2,1)S(1)}, bf16[128,768]{1,0:T(8,128)(2,1)S(1)}, u32[]{:S(2)}, u32[]{:S(2)}) %collective-permute-start.40) | collective-permute-done | bytes 196640 | tf_op jit(solution)/shard_map/ppermute | solution.py:544
  142.0 1.5 collective-permute-start.44
  143.5 7.7 %collective-permute-done.50.refs_1_ = bf16[192,768]{1,0:T(8,128)(2,1)S(1)} collective-permute-done((bf16[192,768]{1,0:T(8,128)(2,1)S(1)}, bf16[192,768]{1,0:T(8,128)(2,1)S(1)}, u32[]{:S(2)}, u32[]{:S(2)}) %collective-permute-start.50) | collective-permute-done | bytes 294944 | tf_op jit(solution)/shard_map/ppermute | solution.py:547
  152.1 1.4 collective-permute-start.52
  153.5 1.4 collective-permute-start.51
  155.7 1.4 collective-permute-start.47
  157.1 4.8 %collective-permute-done.53.refs_3_ = bf16[192,768]{1,0:T(8,128)(2,1)S(1)} collective-permute-done((bf16[192,768]{1,0:T(8,128)(2,1)S(1)}, bf16[192,768]{1,0:T(8,128)(2,1)S(1)}, u32[]{:S(2)}, u32[]{:S(2)}) %collective-permute-start.53) | collective-permute-done | bytes 294944 | tf_op jit(solution)/shard_map/ppermute | solution.py:544
  162.9 1.9 %collective-permute-done.52.refs_2_ = bf16[192,768]{1,0:T(8,128)(2,1)S(1)} collective-permute-done((bf16[192,768]{1,0:T(8,128)(2,1)S(1)}, bf16[192,768]{1,0:T(8,128)(2,1)S(1)}, u32[]{:S(2)}, u32[]{:S(2)}) %collective-permute-start.52) | collective-permute-done | bytes 294944 | tf_op jit(solution)/shard_map/ppermute | solution.py:544
  164.9 1.4 collective-permute-done.51.refs_1_
  167.1 1.7 collective-permute-done.47.g2
  168.8 1.4 collective-permute-done.46.g1
  170.4 3.1 %fin1_kernel.1 = (f32[192,3072]{1,0:T(8,128)}, f32[768,768]{1,0:T(8,128)}, f32[8,128]{1,0:T(8,128)S(1)}) custom-call(s32[3]{0:T(128)S(1)} %copy-done.13, bf16[4,192,768]{2,1,0:T(8,128)(2,1)S(1)} %stack_kernel.5.refs_1_, bf16[4,192,768]{2,1,0:T(8,128)(2,1)S(1)} %collective-permute-done.54.refs_2_, bf16[144,576]{1,0:T(8,128)(2,1)S(1)} %sum_kernel.6.g0.refs_3_), custom_call_target="tpu_custom_call" | custom-call | flops 11000000512 | bytes 100000 | tf_op jit(solution)/shard_map/fin1_kernel/pallas_call | solution.py:511
  173.5 2.3 %fin2_kernel.1 = (f32[192,2304]{1,0:T(8,128)}, f32[192,768]{1,0:T(8,128)}, f32[6,192]{1,0:T(8,128)}, f32[2,192]{1,0:T(2,128)}, f32[1,768]{1,0:T(1,128)S(1)}) custom-call(s32[3]{0:T(128)S(1)} %copy-done.13, bf16[4,144,576]{2,1,0:T(8,128)(2,1)S(1)} %stack_kernel.4.refs_1_, bf16[4,144,576]{2,1,0:T(8,128)(2,1)S(1)} %collective-permute-done.49.refs_2_, ...), custom_call_target="tpu_custom_call" | custom-call | flops 11000000512 | bytes 100000 | tf_op jit(solution)/shard_map/fin2_kernel/pallas_call | solution.py:511
  (149 shorter events, 37.4 us)
Async XLA Ops:
  5.2 15.2 %collective-permute-start.2 = (bf16[144,768]{1,0:T(8,128)(2,1)}, bf16[144,768]{1,0:T(8,128)(2,1)S(1)}, u32[]{:S(2)}, u32[]{:S(2)}) collective-permute-start(bf16[144,768]{1,0:T(8,128)(2,1)} %get-tuple-element.96.refs_3_.x.x0.refs_1_), channel_id=1, source_target_pairs={{0,24},{4,28},{8,16},{12,20},{16,8},{20,12},{24,0},{28,4},{1,25},{... | collective-permute-start | bytes 663560 | tf_op jit(solution)/shard_map/ppermute | solution.py:544
  9.2 11.3 %collective-permute-start.1 = (bf16[144,576]{1,0:T(8,128)(2,1)}, bf16[144,576]{1,0:T(8,128)(2,1)S(1)}, u32[]{:S(2)}, u32[]{:S(2)}) collective-permute-start(bf16[144,576]{1,0:T(8,128)(2,1)} %get-tuple-element.97.g0), channel_id=1, source_target_pairs={{0,2},{1,3},{2,0},{3,1},{4,6},{5,7},{6,4},{7,5},{8,10},{9,11},{10,... | collective-permute-start | bytes 497672 | tf_op jit(solution)/shard_map/ppermute | solution.py:547
  11.8 10.5 %collective-permute-start = (bf16[144,576]{1,0:T(8,128)(2,1)}, bf16[144,576]{1,0:T(8,128)(2,1)S(1)}, u32[]{:S(2)}, u32[]{:S(2)}) collective-permute-start(bf16[144,576]{1,0:T(8,128)(2,1)} %get-tuple-element.97.g0), channel_id=1, source_target_pairs={{0,1},{1,0},{2,3},{3,2},{4,5},{5,4},{6,7},{7,6},{8,9},{9,8},{10,11... | collective-permute-start | bytes 497672 | tf_op jit(solution)/shard_map/ppermute | solution.py:547
  20.5 14.4 %copy-start = (bf16[144,768]{1,0:T(8,128)(2,1)}, bf16[144,768]{1,0:T(8,128)(2,1)S(1)}, u32[]{:S(2)}) copy-start(bf16[144,768]{1,0:T(8,128)(2,1)S(1)} %collective-permute-done.2.refs_1_.refs_4_.x) | copy-start | bytes 663556
  20.5 7.3 %copy-start.13 = (s32[3]{0:T(128)S(1)}, s32[3]{0:T(128)}, u32[]{:S(2)}) copy-start(s32[3]{0:T(128)} %pad_add_fusion.idx.refs_0_) | copy-start | bytes 40
  20.5 7.3 %copy-start.14 = (bf16[192,3072]{1,0:T(8,128)(2,1)S(1)}, bf16[192,3072]{1,0:T(8,128)(2,1)}, u32[]{:S(2)}) copy-start(bf16[192,3072]{1,0:T(8,128)(2,1)} %refs_1_.1) | copy-start | bytes 3538948
  20.5 7.3 %copy-start.15 = (bf16[768,768]{1,0:T(8,128)(2,1)S(1)}, bf16[768,768]{1,0:T(8,128)(2,1)}, u32[]{:S(2)}) copy-start(bf16[768,768]{1,0:T(8,128)(2,1)} %refs_2_.1) | copy-start | bytes 3538948
  20.5 7.3 %copy-start.16 = (bf16[144,768]{1,0:T(8,128)(2,1)S(1)}, bf16[144,768]{1,0:T(8,128)(2,1)}, u32[]{:S(2)}) copy-start(bf16[144,768]{1,0:T(8,128)(2,1)} %get-tuple-element.96.refs_3_.x.x0.refs_1_) | copy-start | bytes 663556
  20.5 5.6 %collective-permute-start.3 = (bf16[144,576]{1,0:T(8,128)(2,1)S(1)}, bf16[144,576]{1,0:T(8,128)(2,1)S(1)}, u32[]{:S(2)}, u32[]{:S(2)}) collective-permute-start(bf16[144,576]{1,0:T(8,128)(2,1)S(1)} %gate_kernel.5.g2), channel_id=1, source_target_pairs={{0,1},{1,0},{2,3},{3,2},{4,5},{5,4},{6,7},{7,6},{8,9},{9,8},{10,11... | collective-permute-start | bytes 497672 | tf_op jit(solution)/shard_map/ppermute | solution.py:547
  21.2 7.5 %collective-permute-start.6 = (bf16[144,768]{1,0:T(8,128)(2,1)}, bf16[144,768]{1,0:T(8,128)(2,1)S(1)}, u32[]{:S(2)}, u32[]{:S(2)}) collective-permute-start(bf16[144,768]{1,0:T(8,128)(2,1)} %get-tuple-element.96.refs_3_.x.x0.refs_1_), channel_id=1, source_target_pairs={{0,16},{4,20},{8,24},{12,28},{16,0},{20,4},{24,8},{28,12},{1,17},{... | collective-permute-start | bytes 663560 | tf_op jit(solution)/shard_map/ppermute | solution.py:544
  21.7 7.5 %collective-permute-start.5 = (bf16[144,768]{1,0:T(8,128)(2,1)}, bf16[144,768]{1,0:T(8,128)(2,1)S(1)}, u32[]{:S(2)}, u32[]{:S(2)}) collective-permute-start(bf16[144,768]{1,0:T(8,128)(2,1)} %get-tuple-element.96.refs_3_.x.x0.refs_1_), channel_id=1, source_target_pairs={{0,8},{4,12},{8,0},{12,4},{16,24},{20,28},{24,16},{28,20},{1,9},{5... | collective-permute-start | bytes 663560 | tf_op jit(solution)/shard_map/ppermute | solution.py:544
  27.1 5.2 %collective-permute-start.10 = (bf16[4,48,384]{2,1,0:T(8,128)(2,1)S(1)}, bf16[4,48,384]{2,1,0:T(8,128)(2,1)S(1)}, u32[]{:S(2)}, u32[]{:S(2)}) collective-permute-start(bf16[4,48,384]{2,1,0:T(8,128)(2,1)S(1)} %get-tuple-element.105), channel_id=1, source_target_pairs={{0,8},{4,12},{8,0},{12,4},{16,24},{20,28},{24,16},{28,20},{1,9},{5... | collective-permute-start | bytes 442376 | tf_op jit(solution)/shard_map/ppermute | solution.py:544
  27.7 6.4 %collective-permute-start.4 = (bf16[4,112,576]{2,1,0:T(8,128)(2,1)S(1)}, bf16[4,112,576]{2,1,0:T(8,128)(2,1)S(1)}, u32[]{:S(2)}, u32[]{:S(2)}) collective-permute-start(bf16[4,112,576]{2,1,0:T(8,128)(2,1)S(1)} %get-tuple-element.98.refs_1_), channel_id=1, source_target_pairs={{0,4},{4,0},{8,12},{12,8},{16,20},{20,16},{24,28},{28,24},{1,5},{5... | collective-permute-start | bytes 1548296 | tf_op jit(solution)/shard_map/ppermute | solution.py:541
  28.8 8.1 %copy-start.3 = (bf16[144,768]{1,0:T(8,128)(2,1)}, bf16[144,768]{1,0:T(8,128)(2,1)S(1)}, u32[]{:S(2)}) copy-start(bf16[144,768]{1,0:T(8,128)(2,1)S(1)} %collective-permute-done.6.refs_3_.x) | copy-start | bytes 663556
  29.3 9.5 %copy-start.5 = (bf16[144,768]{1,0:T(8,128)(2,1)}, bf16[144,768]{1,0:T(8,128)(2,1)S(1)}, u32[]{:S(2)}) copy-start(bf16[144,768]{1,0:T(8,128)(2,1)S(1)} %collective-permute-done.5.refs_2_.x) | copy-start | bytes 663556
  29.3 16.8 %collective-permute-start.14 = (bf16[192,768]{1,0:T(8,128)(2,1)S(1)}, bf16[192,768]{1,0:T(8,128)(2,1)S(1)}, u32[]{:S(2)}, u32[]{:S(2)}) collective-permute-start(bf16[192,768]{1,0:T(8,128)(2,1)S(1)} %gate_kernel.6.refs_3_.refs_0_), channel_id=1, source_target_pairs={{0,2},{1,3},{2,0},{3,1},{4,6},{5,7},{6,4},{7,5},{8,10},{9,11},{10,... | collective-permute-start | bytes 884744 | tf_op jit(solution)/shard_map/ppermute | solution.py:547
  32.4 11.1 %collective-permute-start.11 = (bf16[2,4,48,384]{3,2,1,0:T(8,128)(2,1)S(1)}, bf16[2,4,48,384]{3,2,1,0:T(8,128)(2,1)S(1)}, u32[]{:S(2)}, u32[]{:S(2)}) collective-permute-start(bf16[2,4,48,384]{3,2,1,0:T(8,128)(2,1)S(1)} %pad_maximum_fusion.refs_0_), channel_id=1, source_target_pairs={{0,16},{4,20},{8,24},{12,28},{16,0},{20,4},{24,8},{28,12},{1,17},{... | collective-permute-start | bytes 884744 | tf_op jit(solution)/shard_map/ppermute | solution.py:544
  34.8 8.8 %copy-start.21 = (bf16[768,576]{1,0:T(8,128)(2,1)}, bf16[768,576]{1,0:T(8,128)(2,1)S(1)}, u32[]{:S(2)}) copy-start(bf16[768,576]{1,0:T(8,128)(2,1)S(1)} %get-tuple-element.99.wq.refs_4_) | copy-start | bytes 2654212
  35.7 11.1 %collective-permute-start.9 = (bf16[128,192]{1,0:T(8,128)(2,1)S(1)}, bf16[128,192]{1,0:T(8,128)(2,1)S(1)}, u32[]{:S(2)}, u32[]{:S(2)}) collective-permute-start(bf16[128,192]{1,0:T(8,128)(2,1)S(1)} %get-tuple-element.104.refs_2_), channel_id=1, source_target_pairs={{0,24},{4,28},{8,16},{12,20},{16,8},{20,12},{24,0},{28,4},{1,25},{... | collective-permute-start | bytes 147464 | tf_op jit(solution)/shard_map/ppermute | solution.py:544
  37.8 9.0 %collective-permute-start.8 = (bf16[128,192]{1,0:T(8,128)(2,1)S(1)}, bf16[128,192]{1,0:T(8,128)(2,1)S(1)}, u32[]{:S(2)}, u32[]{:S(2)}) collective-permute-start(bf16[128,192]{1,0:T(8,128)(2,1)S(1)} %get-tuple-element.103), channel_id=1, source_target_pairs={{0,16},{4,20},{8,24},{12,28},{16,0},{20,4},{24,8},{28,12},{1,17},{... | collective-permute-start | bytes 147464 | tf_op jit(solution)/shard_map/ppermute | solution.py:544
  39.7 7.2 %collective-permute-start.7 = (bf16[128,192]{1,0:T(8,128)(2,1)S(1)}, bf16[128,192]{1,0:T(8,128)(2,1)S(1)}, u32[]{:S(2)}, u32[]{:S(2)}) collective-permute-start(bf16[128,192]{1,0:T(8,128)(2,1)S(1)} %get-tuple-element.102), channel_id=1, source_target_pairs={{0,8},{4,12},{8,0},{12,4},{16,24},{20,28},{24,16},{28,20},{1,9},{5... | collective-permute-start | bytes 147464 | tf_op jit(solution)/shard_map/ppermute | solution.py:544
  43.5 4.7 %collective-permute-start.12 = (bf16[4,4,48,384]{3,2,1,0:T(8,128)(2,1)S(1)}, bf16[4,4,48,384]{3,2,1,0:T(8,128)(2,1)S(1)}, u32[]{:S(2)}, u32[]{:S(2)}) collective-permute-start(bf16[4,4,48,384]{3,2,1,0:T(8,128)(2,1)S(1)} %join_kernel.1.mine), channel_id=1, source_target_pairs={{0,4},{4,0},{8,12},{12,8},{16,20},{20,16},{24,28},{28,24},{1,5},{5... | collective-permute-start | bytes 1769480 | tf_op jit(solution)/shard_map/ppermute | solution.py:541
  46.1 9.9 %collective-permute-start.13 = (bf16[192,768]{1,0:T(8,128)(2,1)S(1)}, bf16[192,768]{1,0:T(8,128)(2,1)S(1)}, u32[]{:S(2)}, u32[]{:S(2)}) collective-permute-start(bf16[192,768]{1,0:T(8,128)(2,1)S(1)} %gate_kernel.6.refs_3_.refs_0_), channel_id=1, source_target_pairs={{0,1},{1,0},{2,3},{3,2},{4,5},{5,4},{6,7},{7,6},{8,9},{9,8},{10,11... | collective-permute-start | bytes 884744 | tf_op jit(solution)/shard_map/ppermute | solution.py:547
  46.9 14.3 %collective-permute-start.15 = (bf16[192,768]{1,0:T(8,128)(2,1)S(1)}, bf16[192,768]{1,0:T(8,128)(2,1)S(1)}, u32[]{:S(2)}, u32[]{:S(2)}) collective-permute-start(bf16[192,768]{1,0:T(8,128)(2,1)S(1)} %gate_kernel.7.refs_2_), channel_id=1, source_target_pairs={{0,1},{1,0},{2,3},{3,2},{4,5},{5,4},{6,7},{7,6},{8,9},{9,8},{10,11... | collective-permute-start | bytes 884744 | tf_op jit(solution)/shard_map/ppermute | solution.py:547
  50.1 11.1 %collective-permute-start.18 = (bf16[128,768]{1,0:T(8,128)(2,1)S(1)}, bf16[128,768]{1,0:T(8,128)(2,1)S(1)}, u32[]{:S(2)}, u32[]{:S(2)}) collective-permute-start(bf16[128,768]{1,0:T(8,128)(2,1)S(1)} %get-tuple-element.108.y.refs_9_), channel_id=1, source_target_pairs={{0,24},{4,28},{8,16},{12,20},{16,8},{20,12},{24,0},{28,4},{1,25},{... | collective-permute-start | bytes 589832 | tf_op jit(solution)/shard_map/ppermute | solution.py:544
  51.6 9.7 %collective-permute-start.17 = (bf16[128,768]{1,0:T(8,128)(2,1)S(1)}, bf16[128,768]{1,0:T(8,128)(2,1)S(1)}, u32[]{:S(2)}, u32[]{:S(2)}) collective-permute-start(bf16[128,768]{1,0:T(8,128)(2,1)S(1)} %get-tuple-element.108.y.refs_9_), channel_id=1, source_target_pairs={{0,16},{4,20},{8,24},{12,28},{16,0},{20,4},{24,8},{28,12},{1,17},{... | collective-permute-start | bytes 589832 | tf_op jit(solution)/shard_map/ppermute | solution.py:544
  53.1 8.2 %collective-permute-start.16 = (bf16[128,768]{1,0:T(8,128)(2,1)S(1)}, bf16[128,768]{1,0:T(8,128)(2,1)S(1)}, u32[]{:S(2)}, u32[]{:S(2)}) collective-permute-start(bf16[128,768]{1,0:T(8,128)(2,1)S(1)} %get-tuple-element.108.y.refs_9_), channel_id=1, source_target_pairs={{0,8},{4,12},{8,0},{12,4},{16,24},{20,28},{24,16},{28,20},{1,9},{5... | collective-permute-start | bytes 589832 | tf_op jit(solution)/shard_map/ppermute | solution.py:544
  61.4 2.9 %collective-permute-start.19 = (bf16[4,192,768]{2,1,0:T(8,128)(2,1)S(1)}, bf16[4,192,768]{2,1,0:T(8,128)(2,1)S(1)}, u32[]{:S(2)}, u32[]{:S(2)}) collective-permute-start(bf16[4,192,768]{2,1,0:T(8,128)(2,1)S(1)} %stack_kernel.3.mine), channel_id=1, source_target_pairs={{0,4},{4,0},{8,12},{12,8},{16,20},{20,16},{24,28},{28,24},{1,5},{5... | collective-permute-start | bytes 3538952 | tf_op jit(solution)/shard_map/ppermute | solution.py:541
  65.8 8.8 %collective-permute-start.22 = (bf16[128,768]{1,0:T(8,128)(2,1)S(1)}, bf16[128,768]{1,0:T(8,128)(2,1)S(1)}, u32[]{:S(2)}, u32[]{:S(2)}) collective-permute-start(bf16[128,768]{1,0:T(8,128)(2,1)S(1)} %get-tuple-element.114), channel_id=1, source_target_pairs={{0,24},{4,28},{8,16},{12,20},{16,8},{20,12},{24,0},{28,4},{1,25},{... | collective-permute-start | bytes 589832 | tf_op jit(solution)/shard_map/ppermute | solution.py:544
  68.1 9.7 %collective-permute-start.21 = (bf16[128,768]{1,0:T(8,128)(2,1)S(1)}, bf16[128,768]{1,0:T(8,128)(2,1)S(1)}, u32[]{:S(2)}, u32[]{:S(2)}) collective-permute-start(bf16[128,768]{1,0:T(8,128)(2,1)S(1)} %get-tuple-element.113), channel_id=1, source_target_pairs={{0,16},{4,20},{8,24},{12,28},{16,0},{20,4},{24,8},{28,12},{1,17},{... | collective-permute-start | bytes 589832 | tf_op jit(solution)/shard_map/ppermute | solution.py:544
  70.2 7.7 %copy-start.19 = (bf16[128,768]{1,0:T(8,128)(2,1)S(1)}, bf16[128,768]{1,0:T(8,128)(2,1)}, u32[]{:S(2)}) copy-start(bf16[128,768]{1,0:T(8,128)(2,1)} %cot.1) | copy-start | bytes 589828
  70.2 7.7 %collective-permute-start.20 = (bf16[128,768]{1,0:T(8,128)(2,1)S(1)}, bf16[128,768]{1,0:T(8,128)(2,1)S(1)}, u32[]{:S(2)}, u32[]{:S(2)}) collective-permute-start(bf16[128,768]{1,0:T(8,128)(2,1)S(1)} %get-tuple-element.112), channel_id=1, source_target_pairs={{0,8},{4,12},{8,0},{12,4},{16,24},{20,28},{24,16},{28,20},{1,9},{5... | collective-permute-start | bytes 589832 | tf_op jit(solution)/shard_map/ppermute | solution.py:544
  79.0 8.7 %collective-permute-start.25 = (bf16[128,768]{1,0:T(8,128)(2,1)S(1)}, bf16[128,768]{1,0:T(8,128)(2,1)S(1)}, u32[]{:S(2)}, u32[]{:S(2)}) collective-permute-start(bf16[128,768]{1,0:T(8,128)(2,1)S(1)} %get-tuple-element.117.refs_0_.refs_5_), channel_id=1, source_target_pairs={{0,24},{4,28},{8,16},{12,20},{16,8},{20,12},{24,0},{28,4},{1,25},{... | collective-permute-start | bytes 589832 | tf_op jit(solution)/shard_map/ppermute | solution.py:544
  80.7 10.7 %collective-permute-start.24 = (bf16[128,768]{1,0:T(8,128)(2,1)S(1)}, bf16[128,768]{1,0:T(8,128)(2,1)S(1)}, u32[]{:S(2)}, u32[]{:S(2)}) collective-permute-start(bf16[128,768]{1,0:T(8,128)(2,1)S(1)} %get-tuple-element.117.refs_0_.refs_5_), channel_id=1, source_target_pairs={{0,16},{4,20},{8,24},{12,28},{16,0},{20,4},{24,8},{28,12},{1,17},{... | collective-permute-start | bytes 589832 | tf_op jit(solution)/shard_map/ppermute | solution.py:544
  81.9 10.4 %collective-permute-start.23 = (bf16[128,768]{1,0:T(8,128)(2,1)S(1)}, bf16[128,768]{1,0:T(8,128)(2,1)S(1)}, u32[]{:S(2)}, u32[]{:S(2)}) collective-permute-start(bf16[128,768]{1,0:T(8,128)(2,1)S(1)} %get-tuple-element.117.refs_0_.refs_5_), channel_id=1, source_target_pairs={{0,8},{4,12},{8,0},{12,4},{16,24},{20,28},{24,16},{28,20},{1,9},{5... | collective-permute-start | bytes 589832 | tf_op jit(solution)/shard_map/ppermute | solution.py:544
  88.7 6.6 %collective-permute-start.28 = (bf16[128,768]{1,0:T(8,128)(2,1)S(1)}, bf16[128,768]{1,0:T(8,128)(2,1)S(1)}, u32[]{:S(2)}, u32[]{:S(2)}) collective-permute-start(bf16[128,768]{1,0:T(8,128)(2,1)S(1)} %get-tuple-element.128), channel_id=1, source_target_pairs={{0,24},{4,28},{8,16},{12,20},{16,8},{20,12},{24,0},{28,4},{1,25},{... | collective-permute-start | bytes 589832 | tf_op jit(solution)/shard_map/ppermute | solution.py:544
  97.5 2.9 %collective-permute-start.29 = (bf16[4,192,768]{2,1,0:T(8,128)(2,1)S(1)}, bf16[4,192,768]{2,1,0:T(8,128)(2,1)S(1)}, u32[]{:S(2)}, u32[]{:S(2)}) collective-permute-start(bf16[4,192,768]{2,1,0:T(8,128)(2,1)S(1)} %get-tuple-element.137), channel_id=1, source_target_pairs={{0,4},{4,0},{8,12},{12,8},{16,20},{20,16},{24,28},{28,24},{1,5},{5... | collective-permute-start | bytes 3538952 | tf_op jit(solution)/shard_map/ppermute | solution.py:541
  97.5 7.3 %collective-permute-start.27 = (bf16[128,768]{1,0:T(8,128)(2,1)S(1)}, bf16[128,768]{1,0:T(8,128)(2,1)S(1)}, u32[]{:S(2)}, u32[]{:S(2)}) collective-permute-start(bf16[128,768]{1,0:T(8,128)(2,1)S(1)} %get-tuple-element.127), channel_id=1, source_target_pairs={{0,16},{4,20},{8,24},{12,28},{16,0},{20,4},{24,8},{28,12},{1,17},{... | collective-permute-start | bytes 589832 | tf_op jit(solution)/shard_map/ppermute | solution.py:544
  98.2 7.0 %collective-permute-start.26 = (bf16[128,768]{1,0:T(8,128)(2,1)S(1)}, bf16[128,768]{1,0:T(8,128)(2,1)S(1)}, u32[]{:S(2)}, u32[]{:S(2)}) collective-permute-start(bf16[128,768]{1,0:T(8,128)(2,1)S(1)} %get-tuple-element.126), channel_id=1, source_target_pairs={{0,8},{4,12},{8,0},{12,4},{16,24},{20,28},{24,16},{28,20},{1,9},{5... | collective-permute-start | bytes 589832 | tf_op jit(solution)/shard_map/ppermute | solution.py:544
  101.2 14.7 %collective-permute-start.35 = (bf16[192,768]{1,0:T(8,128)(2,1)S(1)}, bf16[192,768]{1,0:T(8,128)(2,1)S(1)}, u32[]{:S(2)}, u32[]{:S(2)}) collective-permute-start(bf16[192,768]{1,0:T(8,128)(2,1)S(1)} %get-tuple-element.138.refs_10_), channel_id=1, source_target_pairs={{0,1},{1,0},{2,3},{3,2},{4,5},{5,4},{6,7},{7,6},{8,9},{9,8},{10,11... | collective-permute-start | bytes 884744 | tf_op jit(solution)/shard_map/ppermute | solution.py:547
  106.5 17.4 %collective-permute-start.31 = (bf16[128,192]{1,0:T(8,128)(2,1)S(1)}, bf16[128,192]{1,0:T(8,128)(2,1)S(1)}, u32[]{:S(2)}, u32[]{:S(2)}) collective-permute-start(bf16[128,192]{1,0:T(8,128)(2,1)S(1)} %get-tuple-element.148), channel_id=1, source_target_pairs={{0,8},{4,12},{8,0},{12,4},{16,24},{20,28},{24,16},{28,20},{1,9},{5... | collective-permute-start | bytes 147464 | tf_op jit(solution)/shard_map/ppermute | solution.py:544
  108.4 4.9 %collective-permute-start.32 = (bf16[128,192]{1,0:T(8,128)(2,1)S(1)}, bf16[128,192]{1,0:T(8,128)(2,1)S(1)}, u32[]{:S(2)}, u32[]{:S(2)}) collective-permute-start(bf16[128,192]{1,0:T(8,128)(2,1)S(1)} %get-tuple-element.151), channel_id=1, source_target_pairs={{0,16},{4,20},{8,24},{12,28},{16,0},{20,4},{24,8},{28,12},{1,17},{... | collective-permute-start | bytes 147464 | tf_op jit(solution)/shard_map/ppermute | solution.py:544
  109.6 5.2 %collective-permute-start.33 = (bf16[128,192]{1,0:T(8,128)(2,1)S(1)}, bf16[128,192]{1,0:T(8,128)(2,1)S(1)}, u32[]{:S(2)}, u32[]{:S(2)}) collective-permute-start(bf16[128,192]{1,0:T(8,128)(2,1)S(1)} %get-tuple-element.154), channel_id=1, source_target_pairs={{0,24},{4,28},{8,16},{12,20},{16,8},{20,12},{24,0},{28,4},{1,25},{... | collective-permute-start | bytes 147464 | tf_op jit(solution)/shard_map/ppermute | solution.py:544
  111.4 7.2 %collective-permute-start.30 = (bf16[4,192,384]{2,1,0:T(8,128)(2,1)S(1)}, bf16[4,192,384]{2,1,0:T(8,128)(2,1)S(1)}, u32[]{:S(2)}, u32[]{:S(2)}) collective-permute-start(bf16[4,192,384]{2,1,0:T(8,128)(2,1)S(1)} %get-tuple-element.146), channel_id=1, source_target_pairs={{0,4},{4,0},{8,12},{12,8},{16,20},{20,16},{24,28},{28,24},{1,5},{5... | collective-permute-start | bytes 1769480 | tf_op jit(solution)/shard_map/ppermute | solution.py:541
  116.0 17.1 %collective-permute-start.42 = (bf16[192,768]{1,0:T(8,128)(2,1)S(1)}, bf16[192,768]{1,0:T(8,128)(2,1)S(1)}, u32[]{:S(2)}, u32[]{:S(2)}) collective-permute-start(bf16[192,768]{1,0:T(8,128)(2,1)S(1)} %sum_kernel.4.refs_13_.refs_1_), channel_id=1, source_target_pairs={{0,2},{1,3},{2,0},{3,1},{4,6},{5,7},{6,4},{7,5},{8,10},{9,11},{10,... | collective-permute-start | bytes 884744 | tf_op jit(solution)/shard_map/ppermute | solution.py:547
  119.3 6.5 %collective-permute-start.34 = (bf16[4,48,384]{2,1,0:T(8,128)(2,1)S(1)}, bf16[4,48,384]{2,1,0:T(8,128)(2,1)S(1)}, u32[]{:S(2)}, u32[]{:S(2)}) collective-permute-start(bf16[4,48,384]{2,1,0:T(8,128)(2,1)S(1)} %get-tuple-element.159), channel_id=1, source_target_pairs={{0,8},{4,12},{8,0},{12,4},{16,24},{20,28},{24,16},{28,20},{1,9},{5... | collective-permute-start | bytes 442376 | tf_op jit(solution)/shard_map/ppermute | solution.py:544
  120.2 7.9 %collective-permute-start.36 = (bf16[4,48,384]{2,1,0:T(8,128)(2,1)S(1)}, bf16[4,48,384]{2,1,0:T(8,128)(2,1)S(1)}, u32[]{:S(2)}, u32[]{:S(2)}) collective-permute-start(bf16[4,48,384]{2,1,0:T(8,128)(2,1)S(1)} %get-tuple-element.162), channel_id=1, source_target_pairs={{0,16},{4,20},{8,24},{12,28},{16,0},{20,4},{24,8},{28,12},{1,17},{... | collective-permute-start | bytes 442376 | tf_op jit(solution)/shard_map/ppermute | solution.py:544
  120.8 7.3 %collective-permute-start.37 = (bf16[4,48,384]{2,1,0:T(8,128)(2,1)S(1)}, bf16[4,48,384]{2,1,0:T(8,128)(2,1)S(1)}, u32[]{:S(2)}, u32[]{:S(2)}) collective-permute-start(bf16[4,48,384]{2,1,0:T(8,128)(2,1)S(1)} %get-tuple-element.163), channel_id=1, source_target_pairs={{0,24},{4,28},{8,16},{12,20},{16,8},{20,12},{24,0},{28,4},{1,25},{... | collective-permute-start | bytes 442376 | tf_op jit(solution)/shard_map/ppermute | solution.py:544
  127.3 5.8 %collective-permute-start.41 = (bf16[4,112,576]{2,1,0:T(8,128)(2,1)S(1)}, bf16[4,112,576]{2,1,0:T(8,128)(2,1)S(1)}, u32[]{:S(2)}, u32[]{:S(2)}) collective-permute-start(bf16[4,112,576]{2,1,0:T(8,128)(2,1)S(1)} %get-tuple-element.161.refs_5_), channel_id=1, source_target_pairs={{0,4},{4,0},{8,12},{12,8},{16,20},{20,16},{24,28},{28,24},{1,5},{5... | collective-permute-start | bytes 1548296 | tf_op jit(solution)/shard_map/ppermute | solution.py:541
  129.5 7.9 %collective-permute-start.38 = (bf16[128,768]{1,0:T(8,128)(2,1)S(1)}, bf16[128,768]{1,0:T(8,128)(2,1)S(1)}, u32[]{:S(2)}, u32[]{:S(2)}) collective-permute-start(bf16[128,768]{1,0:T(8,128)(2,1)S(1)} %get-tuple-element.165), channel_id=1, source_target_pairs={{0,8},{4,12},{8,0},{12,4},{16,24},{20,28},{24,16},{28,20},{1,9},{5... | collective-permute-start | bytes 589832 | tf_op jit(solution)/shard_map/ppermute | solution.py:544
  130.6 6.7 %collective-permute-start.39 = (bf16[128,768]{1,0:T(8,128)(2,1)S(1)}, bf16[128,768]{1,0:T(8,128)(2,1)S(1)}, u32[]{:S(2)}, u32[]{:S(2)}) collective-permute-start(bf16[128,768]{1,0:T(8,128)(2,1)S(1)} %get-tuple-element.166), channel_id=1, source_target_pairs={{0,16},{4,20},{8,24},{12,28},{16,0},{20,4},{24,8},{28,12},{1,17},{... | collective-permute-start | bytes 589832 | tf_op jit(solution)/shard_map/ppermute | solution.py:544
  131.2 9.6 %collective-permute-start.40 = (bf16[128,768]{1,0:T(8,128)(2,1)S(1)}, bf16[128,768]{1,0:T(8,128)(2,1)S(1)}, u32[]{:S(2)}, u32[]{:S(2)}) collective-permute-start(bf16[128,768]{1,0:T(8,128)(2,1)S(1)} %get-tuple-element.167), channel_id=1, source_target_pairs={{0,24},{4,28},{8,16},{12,20},{16,8},{20,12},{24,0},{28,4},{1,25},{... | collective-permute-start | bytes 589832 | tf_op jit(solution)/shard_map/ppermute | solution.py:544
  133.9 7.6 %collective-permute-start.43 = (bf16[144,576]{1,0:T(8,128)(2,1)S(1)}, bf16[144,576]{1,0:T(8,128)(2,1)S(1)}, u32[]{:S(2)}, u32[]{:S(2)}) collective-permute-start(bf16[144,576]{1,0:T(8,128)(2,1)S(1)} %get-tuple-element.172), channel_id=1, source_target_pairs={{0,1},{1,0},{2,3},{3,2},{4,5},{5,4},{6,7},{7,6},{8,9},{9,8},{10,11... | collective-permute-start | bytes 497672 | tf_op jit(solution)/shard_map/ppermute | solution.py:547
  135.7 15.6 %collective-permute-start.50 = (bf16[192,768]{1,0:T(8,128)(2,1)S(1)}, bf16[192,768]{1,0:T(8,128)(2,1)S(1)}, u32[]{:S(2)}, u32[]{:S(2)}) collective-permute-start(bf16[192,768]{1,0:T(8,128)(2,1)S(1)} %gate_kernel.9), channel_id=1, source_target_pairs={{0,1},{1,0},{2,3},{3,2},{4,5},{5,4},{6,7},{7,6},{8,9},{9,8},{10,11... | collective-permute-start | bytes 884744 | tf_op jit(solution)/shard_map/ppermute | solution.py:547
  141.6 13.4 %collective-permute-start.45 = (bf16[144,576]{1,0:T(8,128)(2,1)S(1)}, bf16[144,576]{1,0:T(8,128)(2,1)S(1)}, u32[]{:S(2)}, u32[]{:S(2)}) collective-permute-start(bf16[144,576]{1,0:T(8,128)(2,1)S(1)} %sum_kernel.5.refs_1_.refs_3_), channel_id=1, source_target_pairs={{0,2},{1,3},{2,0},{3,1},{4,6},{5,7},{6,4},{7,5},{8,10},{9,11},{10,... | collective-permute-start | bytes 497672 | tf_op jit(solution)/shard_map/ppermute | solution.py:547
  142.0 12.9 %collective-permute-start.44 = (bf16[144,576]{1,0:T(8,128)(2,1)S(1)}, bf16[144,576]{1,0:T(8,128)(2,1)S(1)}, u32[]{:S(2)}, u32[]{:S(2)}) collective-permute-start(bf16[144,576]{1,0:T(8,128)(2,1)S(1)} %gate_kernel.8), channel_id=1, source_target_pairs={{0,1},{1,0},{2,3},{3,2},{4,5},{5,4},{6,7},{7,6},{8,9},{9,8},{10,11... | collective-permute-start | bytes 497672 | tf_op jit(solution)/shard_map/ppermute | solution.py:547
  151.4 10.6 %collective-permute-start.53 = (bf16[192,768]{1,0:T(8,128)(2,1)S(1)}, bf16[192,768]{1,0:T(8,128)(2,1)S(1)}, u32[]{:S(2)}, u32[]{:S(2)}) collective-permute-start(bf16[192,768]{1,0:T(8,128)(2,1)S(1)} %sum_kernel.7.refs_0_), channel_id=1, source_target_pairs={{0,24},{4,28},{8,16},{12,20},{16,8},{20,12},{24,0},{28,4},{1,25},{... | collective-permute-start | bytes 884744 | tf_op jit(solution)/shard_map/ppermute | solution.py:544
  152.1 12.8 %collective-permute-start.52 = (bf16[192,768]{1,0:T(8,128)(2,1)S(1)}, bf16[192,768]{1,0:T(8,128)(2,1)S(1)}, u32[]{:S(2)}, u32[]{:S(2)}) collective-permute-start(bf16[192,768]{1,0:T(8,128)(2,1)S(1)} %sum_kernel.7.refs_0_), channel_id=1, source_target_pairs={{0,16},{4,20},{8,24},{12,28},{16,0},{20,4},{24,8},{28,12},{1,17},{... | collective-permute-start | bytes 884744 | tf_op jit(solution)/shard_map/ppermute | solution.py:544
  153.5 12.7 %collective-permute-start.51 = (bf16[192,768]{1,0:T(8,128)(2,1)S(1)}, bf16[192,768]{1,0:T(8,128)(2,1)S(1)}, u32[]{:S(2)}, u32[]{:S(2)}) collective-permute-start(bf16[192,768]{1,0:T(8,128)(2,1)S(1)} %sum_kernel.7.refs_0_), channel_id=1, source_target_pairs={{0,8},{4,12},{8,0},{12,4},{16,24},{20,28},{24,16},{28,20},{1,9},{5... | collective-permute-start | bytes 884744 | tf_op jit(solution)/shard_map/ppermute | solution.py:544
  155.0 12.1 %collective-permute-start.48 = (bf16[144,576]{1,0:T(8,128)(2,1)S(1)}, bf16[144,576]{1,0:T(8,128)(2,1)S(1)}, u32[]{:S(2)}, u32[]{:S(2)}) collective-permute-start(bf16[144,576]{1,0:T(8,128)(2,1)S(1)} %sum_kernel.6.g0.refs_3_), channel_id=1, source_target_pairs={{0,24},{4,28},{8,16},{12,20},{16,8},{20,12},{24,0},{28,4},{1,25},{... | collective-permute-start | bytes 497672 | tf_op jit(solution)/shard_map/ppermute | solution.py:544
  155.7 13.1 %collective-permute-start.47 = (bf16[144,576]{1,0:T(8,128)(2,1)S(1)}, bf16[144,576]{1,0:T(8,128)(2,1)S(1)}, u32[]{:S(2)}, u32[]{:S(2)}) collective-permute-start(bf16[144,576]{1,0:T(8,128)(2,1)S(1)} %sum_kernel.6.g0.refs_3_), channel_id=1, source_target_pairs={{0,16},{4,20},{8,24},{12,28},{16,0},{20,4},{24,8},{28,12},{1,17},{... | collective-permute-start | bytes 497672 | tf_op jit(solution)/shard_map/ppermute | solution.py:544
  161.9 8.3 %collective-permute-start.46 = (bf16[144,576]{1,0:T(8,128)(2,1)S(1)}, bf16[144,576]{1,0:T(8,128)(2,1)S(1)}, u32[]{:S(2)}, u32[]{:S(2)}) collective-permute-start(bf16[144,576]{1,0:T(8,128)(2,1)S(1)} %sum_kernel.6.g0.refs_3_), channel_id=1, source_target_pairs={{0,8},{4,12},{8,0},{12,4},{16,24},{20,28},{24,16},{28,20},{1,9},{5... | collective-permute-start | bytes 497672 | tf_op jit(solution)/shard_map/ppermute | solution.py:544
  166.3 4.1 %collective-permute-start.54 = (bf16[4,192,768]{2,1,0:T(8,128)(2,1)S(1)}, bf16[4,192,768]{2,1,0:T(8,128)(2,1)S(1)}, u32[]{:S(2)}, u32[]{:S(2)}) collective-permute-start(bf16[4,192,768]{2,1,0:T(8,128)(2,1)S(1)} %stack_kernel.5.refs_1_), channel_id=1, source_target_pairs={{0,4},{4,0},{8,12},{12,8},{16,20},{20,16},{24,28},{28,24},{1,5},{5... | collective-permute-start | bytes 3538952 | tf_op jit(solution)/shard_map/ppermute | solution.py:541
  170.3 3.2 %collective-permute-start.49 = (bf16[4,144,576]{2,1,0:T(8,128)(2,1)S(1)}, bf16[4,144,576]{2,1,0:T(8,128)(2,1)S(1)}, u32[]{:S(2)}, u32[]{:S(2)}) collective-permute-start(bf16[4,144,576]{2,1,0:T(8,128)(2,1)S(1)} %stack_kernel.4.refs_1_), channel_id=1, source_target_pairs={{0,4},{4,0},{8,12},{12,8},{16,20},{20,16},{24,28},{28,24},{1,5},{5... | collective-permute-start | bytes 1990664 | tf_op jit(solution)/shard_map/ppermute | solution.py:541
  (16 other events, 50.5 us)

commit v4 on v3

--- a/solution.py
+++ b/solution.py
@@ -72,7 +72,7 @@
     half = bq.shape[0]
     piece, ocol = bo.shape
     hc = width // PARTS
-    fc = hid.shape[1] // PARTS
+    fc = hid.shape[0] // PARTS
     load_q = pltpu.make_async_copy(wqkv.at[at(idx[1] * half, half, 32)], bq, sem.at[0])
     load_o = pltpu.make_async_copy(
         wout.at[at(idx[0] * piece, piece, 16), at(idx[1] * ocol, ocol, 128)], bo, sem.at[1]
@@ -106,11 +106,12 @@
 
     fold_piece(put, lambda g, col, n: bo[g * third : (g + 1) * third, col : col + n], ocol)
     load_q.wait()
+    units = hid[...].reshape(1, hid.shape[0])
     for j in range(PARTS):
 
         @pl.when(idx[0] == j)
         def _(j=j):
-            pay[half + 2 : half + 3, 2 * hc :] = hid[:, j * fc : (j + 1) * fc]
+            pay[half + 2 : half + 3, 2 * hc :] = units[:, j * fc : (j + 1) * fc]
             for s in range(3):
                 pay[:half, s * hc : (s + 1) * hc] = bq[
                     :, s * width + j * hc : s * width + (j + 1) * hc
@@ -475,9 +476,10 @@
             gvec[n : n + 1, :] = v
         else:
             ggain[n - 6 : n - 5, :] = v
+    units = []
     for j in range(parts):
         k = j ^ c
-        ghid[:, j * hc : (j + 1) * hc] = mine[k, half:base, :].astype(F32)[2:3, 2 * hc :]
+        units.append(mine[k, half:base, :].astype(F32)[2:3, 2 * hc :])
         for src, who in ((mine, core), (other, 1 - core)):
             v = src[k, :half, :].astype(F32)
             for s in range(3):
@@ -490,6 +492,7 @@
             for g, v in enumerate((w[:third, :cols], w[third:, :cols], last)):
                 row = j * piece + g * third
                 gout[row : row + third, at(who * cols, cols, 128)] = v
+    ghid[...] = jnp.concatenate(units, axis=1).reshape(ghid.shape)
 
 
 def call(kernel, out, *args, idx=None, scratch=(), hbm=(), after=(), limit=VMEM_BYTES):
@@ -555,7 +558,7 @@
     def relay_shard(v, after=None):
         near, far = swap_shard(v, 1), swap_shard(v, 2)
         if after is not None:
-            far = gate(far, after())
+            far = gate(far, after(near))
         return [v, near, far, swap_shard(far, 1)]
 
     def trade_part(slots):
@@ -604,7 +607,7 @@
             w_out,
             vec_bias,
             ln_gain,
-            hidden_bias.reshape(1, hid_own),
+            hidden_bias,
             seq_lengths,
             idx=idx,
             hbm=range(7),
@@ -614,13 +617,13 @@
                 ((piece, ocol), BF),
                 (vec_bias.shape, BF),
                 (ln_gain.shape, BF),
-                ((1, hid_own), BF),
+                ((hid_own,), BF),
                 (seq_lengths.shape, jnp.int32),
                 pltpu.SemaphoreType.DMA((7,)),
             ],
         )
         xs = spread_part(xp)
-        got1 = relay_shard(pay1, lambda: [xs[3]])
+        got1 = relay_shard(pay1, lambda near: [xs[3]])
         (pay2,) = call(
             pack2_kernel,
             [((half + fc // CORES, width), BF)],
@@ -660,7 +663,7 @@
             for k, x in enumerate(xs)
         ]
         mix = trade_part([a[2] for a in att])
-        got2 = relay_shard(pay2, lambda: mix[1:])
+        got2 = relay_shard(pay2, lambda near: mix[1:] + [near])
         (mine_o,) = call(
             join_kernel, [((PARTS,) + pay_o.shape, BF)], pair_o, far_o, after=[att[3][2]]
         )
@@ -837,7 +840,7 @@
             swap_core(give2),
             osum,
             idx=idx,
-            after=[got_a, dxp[0]],
+            after=[got_a, near_a, dxp[0]],
         )
         low_b, got_b = relay_sum(far_b, send_b, dxp_got[1:])
         near_b = swap_shard(gate(near_b, [low_b]), 1)
@@ -856,7 +859,7 @@
                 (w_out.shape, F32),
                 ((6, wsh), F32),
                 ((2, wsh), F32),
-                ((1, hid_own), F32),
+                ((hid_own,), F32),
             ],
             *done2,
             idx=idx,
@@ -871,7 +874,7 @@
             gw_down,
             g_vec,
             g_gain,
-            g_hidden.reshape(hid_own),
+            g_hidden,
         )
 
     return body

time: 177 us -> 171 us (0.966)
  waiting for transfers between devices: 71.9 us -> 69.2 us
    ppermute x12, waiting for transfers between devices: 28.5 us -> 17.8 us  [swap_shard(): return lax.ppermute(v, 'shard', xor_perm(shards, k))]
    ppermute x35, waiting for transfers between devices: 40 us -> 47.6 us  [swap_part(): return lax.ppermute(v, 'rep', xor_perm(reps, CORES * k))]
  transfers between devices with their start and end apart: 55 -> 55, of which waited for: 32 -> 29; matrix products, arithmetic and copies ran while one was open for 0% -> 0% of each run, Pallas kernels for 16% -> 17%
where the time goes in v4:
time: 171 us
  waiting for transfers between devices  69.2 us (40%)
  starting transfers between devices  60.1 us (35%)
  Pallas kernels  38.3 us (22%)
    ppermute x35, waiting for transfers between devices, swap_part(): return lax.ppermute(v, 'rep', xor_perm(reps, CORES * k))  47.6 us
    ppermute x35, starting transfers between devices, swap_part(): return lax.ppermute(v, 'rep', xor_perm(reps, CORES * k))  42.2 us
    pallas_call x42, Pallas kernels, call(): pl.pallas_call(run if drop else kernel, out_shape=shapes, in_specs=specs,...  38.3 us
    ppermute x12, waiting for transfers between devices, swap_shard(): return lax.ppermute(v, 'shard', xor_perm(shards, k))  17.8 us
    ppermute x12, starting transfers between devices, swap_shard(): return lax.ppermute(v, 'shard', xor_perm(shards, k))  17.4 us
    ppermute x8, waiting for transfers between devices, swap_core(): return lax.ppermute(v, 'rep', xor_perm(reps, 1))  3.79 us
  transfers between devices with their start and end apart: 55, of which 29 were waited for; matrix products, arithmetic and copies ran while one was open for 0% of the time, Pallas kernels for 17%

profile of v4, /device:TPU:0, one launch (start us, length us, event | category | flops | bytes accessed | tf_op | source)
XLA Modules:
  0.0 170.8 jit_solution(12608232815223887661)
XLA Ops:
  1.3 2.7 %pack_kernel.1 = (bf16[144,768]{1,0:T(8,128)(2,1)}, bf16[144,576]{1,0:T(8,128)(2,1)}) custom-call(s32[3]{0:T(128)} %pad_add_fusion.idx.refs_0_, bf16[128,768]{1,0:T(8,128)(2,1)} %tok.3, bf16[192,2304]{1,0:T(8,128)(2,1)} %wqkv.1, bf16[192,768]{1,0:T(8,128)(2,1)} %wout.1, bf16[6,192]{1,0:T(8,128)(2,1)} %vec_in.1, bf16[2,192]{1,0:T(2,128)(2,1)} %gain_in.1, ...), custom_call_target="tpu_custom_call" | custom-call | flops 11000000512 | bytes 100000 | tf_op jit(solution)/shard_map/pack_kernel/pallas_call | solution.py:514
  3.9 4.0 %collective-permute-start.2 = (bf16[144,768]{1,0:T(8,128)(2,1)}, bf16[144,768]{1,0:T(8,128)(2,1)S(1)}, u32[]{:S(2)}, u32[]{:S(2)}) collective-permute-start(bf16[144,768]{1,0:T(8,128)(2,1)} %get-tuple-element.96.refs_3_.x.x0.refs_1_), channel_id=1, source_target_pairs={{0,24},{4,28},{8,16},{12,20},{16,8},{20,12},{24,0},{28,4},{1,25},{... | collective-permute-start | bytes 663560 | tf_op jit(solution)/shard_map/ppermute | solution.py:547
  7.9 2.6 %collective-permute-start.1 = (bf16[144,576]{1,0:T(8,128)(2,1)}, bf16[144,576]{1,0:T(8,128)(2,1)S(1)}, u32[]{:S(2)}, u32[]{:S(2)}) collective-permute-start(bf16[144,576]{1,0:T(8,128)(2,1)} %get-tuple-element.97.g0), channel_id=1, source_target_pairs={{0,2},{1,3},{2,0},{3,1},{4,6},{5,7},{6,4},{7,5},{8,10},{9,11},{10,... | collective-permute-start | bytes 497672 | tf_op jit(solution)/shard_map/ppermute | solution.py:550
  10.5 1.6 collective-permute-start
  12.1 7.1 %collective-permute-done.1.refs_0_ = bf16[144,576]{1,0:T(8,128)(2,1)S(1)} collective-permute-done((bf16[144,576]{1,0:T(8,128)(2,1)}, bf16[144,576]{1,0:T(8,128)(2,1)S(1)}, u32[]{:S(2)}, u32[]{:S(2)}) %collective-permute-start.1) | collective-permute-done | bytes 165920 | tf_op jit(solution)/shard_map/ppermute | solution.py:550
  21.0 3.8 %collective-permute-done.3.g3.refs_1_ = bf16[144,576]{1,0:T(8,128)(2,1)S(1)} collective-permute-done((bf16[144,576]{1,0:T(8,128)(2,1)S(1)}, bf16[144,576]{1,0:T(8,128)(2,1)S(1)}, u32[]{:S(2)}, u32[]{:S(2)}) %collective-permute-start.3) | collective-permute-done | bytes 165920 | tf_op jit(solution)/shard_map/ppermute | solution.py:550
  28.0 2.8 %collective-permute-start.14 = (bf16[192,768]{1,0:T(8,128)(2,1)S(1)}, bf16[192,768]{1,0:T(8,128)(2,1)S(1)}, u32[]{:S(2)}, u32[]{:S(2)}) collective-permute-start(bf16[192,768]{1,0:T(8,128)(2,1)S(1)} %gate_kernel.6.refs_3_.refs_0_), channel_id=1, source_target_pairs={{0,2},{1,3},{2,0},{3,1},{4,6},{5,7},{6,4},{7,5},{8,10},{9,11},{10,... | collective-permute-start | bytes 884744 | tf_op jit(solution)/shard_map/ppermute | solution.py:550
  30.8 1.7 %collective-permute-start.13 = (bf16[192,768]{1,0:T(8,128)(2,1)S(1)}, bf16[192,768]{1,0:T(8,128)(2,1)S(1)}, u32[]{:S(2)}, u32[]{:S(2)}) collective-permute-start(bf16[192,768]{1,0:T(8,128)(2,1)S(1)} %gate_kernel.6.refs_3_.refs_0_), channel_id=1, source_target_pairs={{0,1},{1,0},{2,3},{3,2},{4,5},{5,4},{6,7},{7,6},{8,9},{9,8},{10,11... | collective-permute-start | bytes 884744 | tf_op jit(solution)/shard_map/ppermute | solution.py:550
  34.9 2.5 %collective-permute-start.9 = (bf16[128,192]{1,0:T(8,128)(2,1)S(1)}, bf16[128,192]{1,0:T(8,128)(2,1)S(1)}, u32[]{:S(2)}, u32[]{:S(2)}) collective-permute-start(bf16[128,192]{1,0:T(8,128)(2,1)S(1)} %get-tuple-element.104.refs_2_), channel_id=1, source_target_pairs={{0,24},{4,28},{8,16},{12,20},{16,8},{20,12},{24,0},{28,4},{1,25},{... | collective-permute-start | bytes 147464 | tf_op jit(solution)/shard_map/ppermute | solution.py:547
  39.8 3.8 %collective-permute-done.11.refs_1_ = bf16[2,4,48,384]{3,2,1,0:T(8,128)(2,1)S(1)} collective-permute-done((bf16[2,4,48,384]{3,2,1,0:T(8,128)(2,1)S(1)}, bf16[2,4,48,384]{3,2,1,0:T(8,128)(2,1)S(1)}, u32[]{:S(2)}, u32[]{:S(2)}) %collective-permute-start.11) | collective-permute-done | bytes 294944 | tf_op jit(solution)/shard_map/ppermute | solution.py:547
  43.6 1.5 collective-permute-start.7
  46.3 1.6 collective-permute-done.7.m1.refs_1_.refs_2_
  48.9 1.1 out_kernel.1
  50.0 1.5 collective-permute-start.18
  51.6 1.5 collective-permute-start.17
  53.6 2.2 %collective-permute-done.15.refs_3_ = bf16[192,768]{1,0:T(8,128)(2,1)S(1)} collective-permute-done((bf16[192,768]{1,0:T(8,128)(2,1)S(1)}, bf16[192,768]{1,0:T(8,128)(2,1)S(1)}, u32[]{:S(2)}, u32[]{:S(2)}) %collective-permute-start.15) | collective-permute-done | bytes 294944 | tf_op jit(solution)/shard_map/ppermute | solution.py:550
  55.8 3.0 %collective-permute-done.18.refs_6_.y.refs_12_ = bf16[128,768]{1,0:T(8,128)(2,1)S(1)} collective-permute-done((bf16[128,768]{1,0:T(8,128)(2,1)S(1)}, bf16[128,768]{1,0:T(8,128)(2,1)S(1)}, u32[]{:S(2)}, u32[]{:S(2)}) %collective-permute-start.18) | collective-permute-done | bytes 196640 | tf_op jit(solution)/shard_map/ppermute | solution.py:547
  58.9 2.3 %collective-permute-done.17.refs_5_.y.refs_11_ = bf16[128,768]{1,0:T(8,128)(2,1)S(1)} collective-permute-done((bf16[128,768]{1,0:T(8,128)(2,1)S(1)}, bf16[128,768]{1,0:T(8,128)(2,1)S(1)}, u32[]{:S(2)}, u32[]{:S(2)}) %collective-permute-start.17) | collective-permute-done | bytes 196640 | tf_op jit(solution)/shard_map/ppermute | solution.py:547
  61.3 2.8 %collective-permute-done.19.other = bf16[4,192,768]{2,1,0:T(8,128)(2,1)S(1)} collective-permute-done((bf16[4,192,768]{2,1,0:T(8,128)(2,1)S(1)}, bf16[4,192,768]{2,1,0:T(8,128)(2,1)S(1)}, u32[]{:S(2)}, u32[]{:S(2)}) %collective-permute-start.19) | collective-permute-done | bytes 1179680 | tf_op jit(solution)/shard_map/ppermute | solution.py:544
  65.6 1.3 collective-permute-start.22
  67.6 1.1 collective-permute-start.21
  69.5 1.2 collective-permute-start.20
  71.4 3.0 %collective-permute-done.22.r3 = bf16[128,768]{1,0:T(8,128)(2,1)S(1)} collective-permute-done((bf16[128,768]{1,0:T(8,128)(2,1)S(1)}, bf16[128,768]{1,0:T(8,128)(2,1)S(1)}, u32[]{:S(2)}, u32[]{:S(2)}) %collective-permute-start.22) | collective-permute-done | bytes 196640 | tf_op jit(solution)/shard_map/ppermute | solution.py:547
  74.3 3.4 %collective-permute-done.21.r2 = bf16[128,768]{1,0:T(8,128)(2,1)S(1)} collective-permute-done((bf16[128,768]{1,0:T(8,128)(2,1)S(1)}, bf16[128,768]{1,0:T(8,128)(2,1)S(1)}, u32[]{:S(2)}, u32[]{:S(2)}) %collective-permute-start.21) | collective-permute-done | bytes 196640 | tf_op jit(solution)/shard_map/ppermute | solution.py:547
  77.7 1.2 ln2_kernel.1
  78.9 1.3 collective-permute-start.25
  81.2 1.2 collective-permute-start.23
  82.4 5.2 %collective-permute-done.25.d.refs_8_ = bf16[128,768]{1,0:T(8,128)(2,1)S(1)} collective-permute-done((bf16[128,768]{1,0:T(8,128)(2,1)S(1)}, bf16[128,768]{1,0:T(8,128)(2,1)S(1)}, u32[]{:S(2)}, u32[]{:S(2)}) %collective-permute-start.25) | collective-permute-done | bytes 196640 | tf_op jit(solution)/shard_map/ppermute | solution.py:547
  88.5 1.3 collective-permute-start.28
  89.9 1.4 collective-permute-done.24.d.refs_7_
  94.1 1.1 collective-permute-done.28.refs_17_.refs_3_.refs_5_
  95.2 2.1 %ffw_kernel.1 = (bf16[4,192,768]{2,1,0:T(8,128)(2,1)S(1)}, bf16[4,192,768]{2,1,0:T(8,128)(2,1)S(1)}, f32[8,768]{1,0:T(8,128)S(1)}) custom-call(s32[3]{0:T(128)S(1)} %copy-done.13, bf16[128,768]{1,0:T(8,128)(2,1)S(1)} %get-tuple-element.131.refs_1_, bf16[128,768]{1,0:T(8,128)(2,1)S(1)} %get-tuple-element.132.refs_2_, ...), custom_call_target="tpu_custom_call" | custom-call | flops 11000000512 | bytes 100000 | tf_op jit(solution)/shard_map/ffw_kernel/pallas_call | solution.py:514
  98.1 1.2 collective-permute-start.26
  101.0 1.3 collective-permute-start.35
  102.3 2.4 %collective-permute-done.27.refs_4_ = bf16[128,768]{1,0:T(8,128)(2,1)S(1)} collective-permute-done((bf16[128,768]{1,0:T(8,128)(2,1)S(1)}, bf16[128,768]{1,0:T(8,128)(2,1)S(1)}, u32[]{:S(2)}, u32[]{:S(2)}) %collective-permute-start.27) | collective-permute-done | bytes 196640 | tf_op jit(solution)/shard_map/ppermute | solution.py:547
  105.1 1.3 ln1b_kernel.1
  106.5 1.4 collective-permute-start.31
  108.9 1.3 collective-permute-start.33
  111.3 1.4 collective-permute-done.32.d
  112.7 1.1 attb_kernel.6.refs_7_.refs_2_
  114.1 1.1 attb_kernel.7.refs_2_.refs_8_.refs_3_
  115.3 2.9 %collective-permute-start.42 = (bf16[192,768]{1,0:T(8,128)(2,1)S(1)}, bf16[192,768]{1,0:T(8,128)(2,1)S(1)}, u32[]{:S(2)}, u32[]{:S(2)}) collective-permute-start(bf16[192,768]{1,0:T(8,128)(2,1)S(1)} %sum_kernel.4.refs_13_.refs_1_), channel_id=1, source_target_pairs={{0,2},{1,3},{2,0},{3,1},{4,6},{5,7},{6,4},{7,5},{8,10},{9,11},{10,... | collective-permute-start | bytes 884744 | tf_op jit(solution)/shard_map/ppermute | solution.py:550
  119.7 1.3 collective-permute-start.34
  121.6 1.1 attb_kernel.4.refs_5_.refs_0_
  122.7 1.7 %collective-permute-start.37 = (bf16[4,48,384]{2,1,0:T(8,128)(2,1)S(1)}, bf16[4,48,384]{2,1,0:T(8,128)(2,1)S(1)}, u32[]{:S(2)}, u32[]{:S(2)}) collective-permute-start(bf16[4,48,384]{2,1,0:T(8,128)(2,1)S(1)} %get-tuple-element.163), channel_id=1, source_target_pairs={{0,24},{4,28},{8,16},{12,20},{16,8},{20,12},{24,0},{28,4},{1,25},{... | collective-permute-start | bytes 442376 | tf_op jit(solution)/shard_map/ppermute | solution.py:547
  124.5 1.1 attb_kernel.5.refs_6_.refs_1_
  125.7 1.5 qw_kernel.1
  127.3 1.9 %collective-permute-done.36.refs_6_ = bf16[4,48,384]{2,1,0:T(8,128)(2,1)S(1)} collective-permute-done((bf16[4,48,384]{2,1,0:T(8,128)(2,1)S(1)}, bf16[4,48,384]{2,1,0:T(8,128)(2,1)S(1)}, u32[]{:S(2)}, u32[]{:S(2)}) %collective-permute-start.36) | collective-permute-done | bytes 147488 | tf_op jit(solution)/shard_map/ppermute | solution.py:547
  129.2 1.4 dx_kernel.1
  130.6 1.2 collective-permute-start.38
  132.7 1.5 collective-permute-start.40
  135.0 1.3 collective-permute-start.44
  136.3 1.8 %collective-permute-done.38.refs_2_ = bf16[128,768]{1,0:T(8,128)(2,1)S(1)} collective-permute-done((bf16[128,768]{1,0:T(8,128)(2,1)S(1)}, bf16[128,768]{1,0:T(8,128)(2,1)S(1)}, u32[]{:S(2)}, u32[]{:S(2)}) %collective-permute-start.38) | collective-permute-done | bytes 196640 | tf_op jit(solution)/shard_map/ppermute | solution.py:547
  138.1 3.6 %collective-permute-done.39.refs_3_ = bf16[128,768]{1,0:T(8,128)(2,1)S(1)} collective-permute-done((bf16[128,768]{1,0:T(8,128)(2,1)S(1)}, bf16[128,768]{1,0:T(8,128)(2,1)S(1)}, u32[]{:S(2)}, u32[]{:S(2)}) %collective-permute-start.39) | collective-permute-done | bytes 196640 | tf_op jit(solution)/shard_map/ppermute | solution.py:547
  143.3 1.6 collective-permute-start.53
  145.5 1.3 collective-permute-start.51
  146.8 3.0 %collective-permute-done.45.refs_1_.refs_5_ = bf16[144,576]{1,0:T(8,128)(2,1)S(1)} collective-permute-done((bf16[144,576]{1,0:T(8,128)(2,1)S(1)}, bf16[144,576]{1,0:T(8,128)(2,1)S(1)}, u32[]{:S(2)}, u32[]{:S(2)}) %collective-permute-start.45) | collective-permute-done | bytes 165920 | tf_op jit(solution)/shard_map/ppermute | solution.py:550
  149.8 1.7 collective-permute-done.46.refs_2_.refs_4_
  151.5 1.3 collective-permute-start.49
  155.1 4.5 %collective-permute-done.52.refs_2_ = bf16[192,768]{1,0:T(8,128)(2,1)S(1)} collective-permute-done((bf16[192,768]{1,0:T(8,128)(2,1)S(1)}, bf16[192,768]{1,0:T(8,128)(2,1)S(1)}, u32[]{:S(2)}, u32[]{:S(2)}) %collective-permute-start.52) | collective-permute-done | bytes 294944 | tf_op jit(solution)/shard_map/ppermute | solution.py:547
  159.9 3.4 %collective-permute-done.49.g3 = bf16[144,576]{1,0:T(8,128)(2,1)S(1)} collective-permute-done((bf16[144,576]{1,0:T(8,128)(2,1)S(1)}, bf16[144,576]{1,0:T(8,128)(2,1)S(1)}, u32[]{:S(2)}, u32[]{:S(2)}) %collective-permute-start.49) | collective-permute-done | bytes 165920 | tf_op jit(solution)/shard_map/ppermute | solution.py:547
  163.4 1.8 %collective-permute-done.48.g2 = bf16[144,576]{1,0:T(8,128)(2,1)S(1)} collective-permute-done((bf16[144,576]{1,0:T(8,128)(2,1)S(1)}, bf16[144,576]{1,0:T(8,128)(2,1)S(1)}, u32[]{:S(2)}, u32[]{:S(2)}) %collective-permute-start.48) | collective-permute-done | bytes 165920 | tf_op jit(solution)/shard_map/ppermute | solution.py:547
  165.4 3.1 %fin1_kernel.1 = (f32[192,3072]{1,0:T(8,128)}, f32[768,768]{1,0:T(8,128)}, f32[8,128]{1,0:T(8,128)S(1)}) custom-call(s32[3]{0:T(128)S(1)} %copy-done.13, bf16[4,192,768]{2,1,0:T(8,128)(2,1)S(1)} %stack_kernel.5.refs_1_, bf16[4,192,768]{2,1,0:T(8,128)(2,1)S(1)} %collective-permute-done.54.refs_2_, bf16[144,576]{1,0:T(8,128)(2,1)S(1)} %sum_kernel.6.g0.refs_3_), custom_call_target="tpu_custom_call" | custom-call | flops 11000000512 | bytes 100000 | tf_op jit(solution)/shard_map/fin1_kernel/pallas_call | solution.py:514
  168.5 2.3 %fin2_kernel.1 = (f32[192,2304]{1,0:T(8,128)}, f32[192,768]{1,0:T(8,128)}, f32[6,192]{1,0:T(8,128)}, f32[2,192]{1,0:T(2,128)}, f32[768]{0:T(1024)}) custom-call(s32[3]{0:T(128)S(1)} %copy-done.13, bf16[4,144,576]{2,1,0:T(8,128)(2,1)S(1)} %stack_kernel.4.refs_1_, bf16[4,144,576]{2,1,0:T(8,128)(2,1)S(1)} %collective-permute-done.50.refs_2_, ...), custom_call_target="tpu_custom_call" | custom-call | flops 11000000512 | bytes 100000 | tf_op jit(solution)/shard_map/fin2_kernel/pallas_call | solution.py:514
  (147 shorter events, 35.5 us)
Async XLA Ops:
  3.9 15.2 %collective-permute-start.2 = (bf16[144,768]{1,0:T(8,128)(2,1)}, bf16[144,768]{1,0:T(8,128)(2,1)S(1)}, u32[]{:S(2)}, u32[]{:S(2)}) collective-permute-start(bf16[144,768]{1,0:T(8,128)(2,1)} %get-tuple-element.96.refs_3_.x.x0.refs_1_), channel_id=1, source_target_pairs={{0,24},{4,28},{8,16},{12,20},{16,8},{20,12},{24,0},{28,4},{1,25},{... | collective-permute-start | bytes 663560 | tf_op jit(solution)/shard_map/ppermute | solution.py:547
  7.9 11.3 %collective-permute-start.1 = (bf16[144,576]{1,0:T(8,128)(2,1)}, bf16[144,576]{1,0:T(8,128)(2,1)S(1)}, u32[]{:S(2)}, u32[]{:S(2)}) collective-permute-start(bf16[144,576]{1,0:T(8,128)(2,1)} %get-tuple-element.97.g0), channel_id=1, source_target_pairs={{0,2},{1,3},{2,0},{3,1},{4,6},{5,7},{6,4},{7,5},{8,10},{9,11},{10,... | collective-permute-start | bytes 497672 | tf_op jit(solution)/shard_map/ppermute | solution.py:550
  10.5 10.5 %collective-permute-start = (bf16[144,576]{1,0:T(8,128)(2,1)}, bf16[144,576]{1,0:T(8,128)(2,1)S(1)}, u32[]{:S(2)}, u32[]{:S(2)}) collective-permute-start(bf16[144,576]{1,0:T(8,128)(2,1)} %get-tuple-element.97.g0), channel_id=1, source_target_pairs={{0,1},{1,0},{2,3},{3,2},{4,5},{5,4},{6,7},{7,6},{8,9},{9,8},{10,11... | collective-permute-start | bytes 497672 | tf_op jit(solution)/shard_map/ppermute | solution.py:550
  19.2 14.7 %copy-start = (bf16[144,768]{1,0:T(8,128)(2,1)}, bf16[144,768]{1,0:T(8,128)(2,1)S(1)}, u32[]{:S(2)}) copy-start(bf16[144,768]{1,0:T(8,128)(2,1)S(1)} %collective-permute-done.2.refs_1_.refs_4_.x) | copy-start | bytes 663556
  19.2 7.3 %copy-start.13 = (s32[3]{0:T(128)S(1)}, s32[3]{0:T(128)}, u32[]{:S(2)}) copy-start(s32[3]{0:T(128)} %pad_add_fusion.idx.refs_0_) | copy-start | bytes 40
  19.2 7.3 %copy-start.14 = (bf16[192,3072]{1,0:T(8,128)(2,1)S(1)}, bf16[192,3072]{1,0:T(8,128)(2,1)}, u32[]{:S(2)}) copy-start(bf16[192,3072]{1,0:T(8,128)(2,1)} %refs_1_.1) | copy-start | bytes 3538948
  19.2 7.3 %copy-start.15 = (bf16[768,768]{1,0:T(8,128)(2,1)S(1)}, bf16[768,768]{1,0:T(8,128)(2,1)}, u32[]{:S(2)}) copy-start(bf16[768,768]{1,0:T(8,128)(2,1)} %refs_2_.1) | copy-start | bytes 3538948
  19.2 5.6 %collective-permute-start.3 = (bf16[144,576]{1,0:T(8,128)(2,1)S(1)}, bf16[144,576]{1,0:T(8,128)(2,1)S(1)}, u32[]{:S(2)}, u32[]{:S(2)}) collective-permute-start(bf16[144,576]{1,0:T(8,128)(2,1)S(1)} %gate_kernel.5.g2), channel_id=1, source_target_pairs={{0,1},{1,0},{2,3},{3,2},{4,5},{5,4},{6,7},{7,6},{8,9},{9,8},{10,11... | collective-permute-start | bytes 497672 | tf_op jit(solution)/shard_map/ppermute | solution.py:550
  20.0 7.5 %collective-permute-start.6 = (bf16[144,768]{1,0:T(8,128)(2,1)}, bf16[144,768]{1,0:T(8,128)(2,1)S(1)}, u32[]{:S(2)}, u32[]{:S(2)}) collective-permute-start(bf16[144,768]{1,0:T(8,128)(2,1)} %get-tuple-element.96.refs_3_.x.x0.refs_1_), channel_id=1, source_target_pairs={{0,16},{4,20},{8,24},{12,28},{16,0},{20,4},{24,8},{28,12},{1,17},{... | collective-permute-start | bytes 663560 | tf_op jit(solution)/shard_map/ppermute | solution.py:547
  20.5 7.5 %collective-permute-start.5 = (bf16[144,768]{1,0:T(8,128)(2,1)}, bf16[144,768]{1,0:T(8,128)(2,1)S(1)}, u32[]{:S(2)}, u32[]{:S(2)}) collective-permute-start(bf16[144,768]{1,0:T(8,128)(2,1)} %get-tuple-element.96.refs_3_.x.x0.refs_1_), channel_id=1, source_target_pairs={{0,8},{4,12},{8,0},{12,4},{16,24},{20,28},{24,16},{28,20},{1,9},{5... | collective-permute-start | bytes 663560 | tf_op jit(solution)/shard_map/ppermute | solution.py:547
  25.9 6.7 %collective-permute-start.10 = (bf16[4,48,384]{2,1,0:T(8,128)(2,1)S(1)}, bf16[4,48,384]{2,1,0:T(8,128)(2,1)S(1)}, u32[]{:S(2)}, u32[]{:S(2)}) collective-permute-start(bf16[4,48,384]{2,1,0:T(8,128)(2,1)S(1)} %get-tuple-element.105), channel_id=1, source_target_pairs={{0,8},{4,12},{8,0},{12,4},{16,24},{20,28},{24,16},{28,20},{1,9},{5... | collective-permute-start | bytes 442376 | tf_op jit(solution)/shard_map/ppermute | solution.py:547
  26.5 6.7 %collective-permute-start.4 = (bf16[4,112,576]{2,1,0:T(8,128)(2,1)S(1)}, bf16[4,112,576]{2,1,0:T(8,128)(2,1)S(1)}, u32[]{:S(2)}, u32[]{:S(2)}) collective-permute-start(bf16[4,112,576]{2,1,0:T(8,128)(2,1)S(1)} %get-tuple-element.98.refs_1_), channel_id=1, source_target_pairs={{0,4},{4,0},{8,12},{12,8},{16,20},{20,16},{24,28},{28,24},{1,5},{5... | collective-permute-start | bytes 1548296 | tf_op jit(solution)/shard_map/ppermute | solution.py:544
  27.5 9.9 %copy-start.3 = (bf16[144,768]{1,0:T(8,128)(2,1)}, bf16[144,768]{1,0:T(8,128)(2,1)S(1)}, u32[]{:S(2)}) copy-start(bf16[144,768]{1,0:T(8,128)(2,1)S(1)} %collective-permute-done.6.refs_3_.x) | copy-start | bytes 663556
  28.0 10.9 %copy-start.5 = (bf16[144,768]{1,0:T(8,128)(2,1)}, bf16[144,768]{1,0:T(8,128)(2,1)S(1)}, u32[]{:S(2)}) copy-start(bf16[144,768]{1,0:T(8,128)(2,1)S(1)} %collective-permute-done.5.refs_2_.x) | copy-start | bytes 663556
  28.0 17.2 %collective-permute-start.14 = (bf16[192,768]{1,0:T(8,128)(2,1)S(1)}, bf16[192,768]{1,0:T(8,128)(2,1)S(1)}, u32[]{:S(2)}, u32[]{:S(2)}) collective-permute-start(bf16[192,768]{1,0:T(8,128)(2,1)S(1)} %gate_kernel.6.refs_3_.refs_0_), channel_id=1, source_target_pairs={{0,2},{1,3},{2,0},{3,1},{4,6},{5,7},{6,4},{7,5},{8,10},{9,11},{10,... | collective-permute-start | bytes 884744 | tf_op jit(solution)/shard_map/ppermute | solution.py:550
  30.8 15.4 %collective-permute-start.13 = (bf16[192,768]{1,0:T(8,128)(2,1)S(1)}, bf16[192,768]{1,0:T(8,128)(2,1)S(1)}, u32[]{:S(2)}, u32[]{:S(2)}) collective-permute-start(bf16[192,768]{1,0:T(8,128)(2,1)S(1)} %gate_kernel.6.refs_3_.refs_0_), channel_id=1, source_target_pairs={{0,1},{1,0},{2,3},{3,2},{4,5},{5,4},{6,7},{7,6},{8,9},{9,8},{10,11... | collective-permute-start | bytes 884744 | tf_op jit(solution)/shard_map/ppermute | solution.py:550
  32.6 11.0 %collective-permute-start.11 = (bf16[2,4,48,384]{3,2,1,0:T(8,128)(2,1)S(1)}, bf16[2,4,48,384]{3,2,1,0:T(8,128)(2,1)S(1)}, u32[]{:S(2)}, u32[]{:S(2)}) collective-permute-start(bf16[2,4,48,384]{3,2,1,0:T(8,128)(2,1)S(1)} %pad_maximum_fusion.refs_0_), channel_id=1, source_target_pairs={{0,16},{4,20},{8,24},{12,28},{16,0},{20,4},{24,8},{28,12},{1,17},{... | collective-permute-start | bytes 884744 | tf_op jit(solution)/shard_map/ppermute | solution.py:547
  33.9 11.4 %copy-start.21 = (bf16[768,576]{1,0:T(8,128)(2,1)}, bf16[768,576]{1,0:T(8,128)(2,1)S(1)}, u32[]{:S(2)}) copy-start(bf16[768,576]{1,0:T(8,128)(2,1)S(1)} %get-tuple-element.99.wq.refs_4_) | copy-start | bytes 2654212
  34.9 11.4 %collective-permute-start.9 = (bf16[128,192]{1,0:T(8,128)(2,1)S(1)}, bf16[128,192]{1,0:T(8,128)(2,1)S(1)}, u32[]{:S(2)}, u32[]{:S(2)}) collective-permute-start(bf16[128,192]{1,0:T(8,128)(2,1)S(1)} %get-tuple-element.104.refs_2_), channel_id=1, source_target_pairs={{0,24},{4,28},{8,16},{12,20},{16,8},{20,12},{24,0},{28,4},{1,25},{... | collective-permute-start | bytes 147464 | tf_op jit(solution)/shard_map/ppermute | solution.py:547
  38.3 8.0 %collective-permute-start.8 = (bf16[128,192]{1,0:T(8,128)(2,1)S(1)}, bf16[128,192]{1,0:T(8,128)(2,1)S(1)}, u32[]{:S(2)}, u32[]{:S(2)}) collective-permute-start(bf16[128,192]{1,0:T(8,128)(2,1)S(1)} %get-tuple-element.103), channel_id=1, source_target_pairs={{0,16},{4,20},{8,24},{12,28},{16,0},{20,4},{24,8},{28,12},{1,17},{... | collective-permute-start | bytes 147464 | tf_op jit(solution)/shard_map/ppermute | solution.py:547
  43.6 4.3 %collective-permute-start.7 = (bf16[128,192]{1,0:T(8,128)(2,1)S(1)}, bf16[128,192]{1,0:T(8,128)(2,1)S(1)}, u32[]{:S(2)}, u32[]{:S(2)}) collective-permute-start(bf16[128,192]{1,0:T(8,128)(2,1)S(1)} %get-tuple-element.102), channel_id=1, source_target_pairs={{0,8},{4,12},{8,0},{12,4},{16,24},{20,28},{24,16},{28,20},{1,9},{5... | collective-permute-start | bytes 147464 | tf_op jit(solution)/shard_map/ppermute | solution.py:547
  45.2 3.0 %collective-permute-start.12 = (bf16[4,4,48,384]{3,2,1,0:T(8,128)(2,1)S(1)}, bf16[4,4,48,384]{3,2,1,0:T(8,128)(2,1)S(1)}, u32[]{:S(2)}, u32[]{:S(2)}) collective-permute-start(bf16[4,4,48,384]{3,2,1,0:T(8,128)(2,1)S(1)} %join_kernel.1.mine), channel_id=1, source_target_pairs={{0,4},{4,0},{8,12},{12,8},{16,20},{20,16},{24,28},{28,24},{1,5},{5... | collective-permute-start | bytes 1769480 | tf_op jit(solution)/shard_map/ppermute | solution.py:544
  47.9 7.9 %collective-permute-start.15 = (bf16[192,768]{1,0:T(8,128)(2,1)S(1)}, bf16[192,768]{1,0:T(8,128)(2,1)S(1)}, u32[]{:S(2)}, u32[]{:S(2)}) collective-permute-start(bf16[192,768]{1,0:T(8,128)(2,1)S(1)} %gate_kernel.7.refs_2_), channel_id=1, source_target_pairs={{0,1},{1,0},{2,3},{3,2},{4,5},{5,4},{6,7},{7,6},{8,9},{9,8},{10,11... | collective-permute-start | bytes 884744 | tf_op jit(solution)/shard_map/ppermute | solution.py:550
  50.0 8.8 %collective-permute-start.18 = (bf16[128,768]{1,0:T(8,128)(2,1)S(1)}, bf16[128,768]{1,0:T(8,128)(2,1)S(1)}, u32[]{:S(2)}, u32[]{:S(2)}) collective-permute-start(bf16[128,768]{1,0:T(8,128)(2,1)S(1)} %get-tuple-element.108.y.refs_9_), channel_id=1, source_target_pairs={{0,24},{4,28},{8,16},{12,20},{16,8},{20,12},{24,0},{28,4},{1,25},{... | collective-permute-start | bytes 589832 | tf_op jit(solution)/shard_map/ppermute | solution.py:547
  51.6 9.6 %collective-permute-start.17 = (bf16[128,768]{1,0:T(8,128)(2,1)S(1)}, bf16[128,768]{1,0:T(8,128)(2,1)S(1)}, u32[]{:S(2)}, u32[]{:S(2)}) collective-permute-start(bf16[128,768]{1,0:T(8,128)(2,1)S(1)} %get-tuple-element.108.y.refs_9_), channel_id=1, source_target_pairs={{0,16},{4,20},{8,24},{12,28},{16,0},{20,4},{24,8},{28,12},{1,17},{... | collective-permute-start | bytes 589832 | tf_op jit(solution)/shard_map/ppermute | solution.py:547
  53.1 8.1 %collective-permute-start.16 = (bf16[128,768]{1,0:T(8,128)(2,1)S(1)}, bf16[128,768]{1,0:T(8,128)(2,1)S(1)}, u32[]{:S(2)}, u32[]{:S(2)}) collective-permute-start(bf16[128,768]{1,0:T(8,128)(2,1)S(1)} %get-tuple-element.108.y.refs_9_), channel_id=1, source_target_pairs={{0,8},{4,12},{8,0},{12,4},{16,24},{20,28},{24,16},{28,20},{1,9},{5... | collective-permute-start | bytes 589832 | tf_op jit(solution)/shard_map/ppermute | solution.py:547
  61.3 2.9 %collective-permute-start.19 = (bf16[4,192,768]{2,1,0:T(8,128)(2,1)S(1)}, bf16[4,192,768]{2,1,0:T(8,128)(2,1)S(1)}, u32[]{:S(2)}, u32[]{:S(2)}) collective-permute-start(bf16[4,192,768]{2,1,0:T(8,128)(2,1)S(1)} %stack_kernel.3.mine), channel_id=1, source_target_pairs={{0,4},{4,0},{8,12},{12,8},{16,20},{20,16},{24,28},{28,24},{1,5},{5... | collective-permute-start | bytes 3538952 | tf_op jit(solution)/shard_map/ppermute | solution.py:544
  65.6 8.8 %collective-permute-start.22 = (bf16[128,768]{1,0:T(8,128)(2,1)S(1)}, bf16[128,768]{1,0:T(8,128)(2,1)S(1)}, u32[]{:S(2)}, u32[]{:S(2)}) collective-permute-start(bf16[128,768]{1,0:T(8,128)(2,1)S(1)} %get-tuple-element.114), channel_id=1, source_target_pairs={{0,24},{4,28},{8,16},{12,20},{16,8},{20,12},{24,0},{28,4},{1,25},{... | collective-permute-start | bytes 589832 | tf_op jit(solution)/shard_map/ppermute | solution.py:547
  67.6 10.1 %collective-permute-start.21 = (bf16[128,768]{1,0:T(8,128)(2,1)S(1)}, bf16[128,768]{1,0:T(8,128)(2,1)S(1)}, u32[]{:S(2)}, u32[]{:S(2)}) collective-permute-start(bf16[128,768]{1,0:T(8,128)(2,1)S(1)} %get-tuple-element.113), channel_id=1, source_target_pairs={{0,16},{4,20},{8,24},{12,28},{16,0},{20,4},{24,8},{28,12},{1,17},{... | collective-permute-start | bytes 589832 | tf_op jit(solution)/shard_map/ppermute | solution.py:547
  69.4 8.3 %copy-start.19 = (bf16[128,768]{1,0:T(8,128)(2,1)S(1)}, bf16[128,768]{1,0:T(8,128)(2,1)}, u32[]{:S(2)}) copy-start(bf16[128,768]{1,0:T(8,128)(2,1)} %cot.1) | copy-start | bytes 589828
  69.5 8.3 %collective-permute-start.20 = (bf16[128,768]{1,0:T(8,128)(2,1)S(1)}, bf16[128,768]{1,0:T(8,128)(2,1)S(1)}, u32[]{:S(2)}, u32[]{:S(2)}) collective-permute-start(bf16[128,768]{1,0:T(8,128)(2,1)S(1)} %get-tuple-element.112), channel_id=1, source_target_pairs={{0,8},{4,12},{8,0},{12,4},{16,24},{20,28},{24,16},{28,20},{1,9},{5... | collective-permute-start | bytes 589832 | tf_op jit(solution)/shard_map/ppermute | solution.py:547
  78.9 8.7 %collective-permute-start.25 = (bf16[128,768]{1,0:T(8,128)(2,1)S(1)}, bf16[128,768]{1,0:T(8,128)(2,1)S(1)}, u32[]{:S(2)}, u32[]{:S(2)}) collective-permute-start(bf16[128,768]{1,0:T(8,128)(2,1)S(1)} %get-tuple-element.117.refs_0_.refs_5_), channel_id=1, source_target_pairs={{0,24},{4,28},{8,16},{12,20},{16,8},{20,12},{24,0},{28,4},{1,25},{... | collective-permute-start | bytes 589832 | tf_op jit(solution)/shard_map/ppermute | solution.py:547
  80.2 11.1 %collective-permute-start.24 = (bf16[128,768]{1,0:T(8,128)(2,1)S(1)}, bf16[128,768]{1,0:T(8,128)(2,1)S(1)}, u32[]{:S(2)}, u32[]{:S(2)}) collective-permute-start(bf16[128,768]{1,0:T(8,128)(2,1)S(1)} %get-tuple-element.117.refs_0_.refs_5_), channel_id=1, source_target_pairs={{0,16},{4,20},{8,24},{12,28},{16,0},{20,4},{24,8},{28,12},{1,17},{... | collective-permute-start | bytes 589832 | tf_op jit(solution)/shard_map/ppermute | solution.py:547
  81.2 11.0 %collective-permute-start.23 = (bf16[128,768]{1,0:T(8,128)(2,1)S(1)}, bf16[128,768]{1,0:T(8,128)(2,1)S(1)}, u32[]{:S(2)}, u32[]{:S(2)}) collective-permute-start(bf16[128,768]{1,0:T(8,128)(2,1)S(1)} %get-tuple-element.117.refs_0_.refs_5_), channel_id=1, source_target_pairs={{0,8},{4,12},{8,0},{12,4},{16,24},{20,28},{24,16},{28,20},{1,9},{5... | collective-permute-start | bytes 589832 | tf_op jit(solution)/shard_map/ppermute | solution.py:547
  88.5 6.6 %collective-permute-start.28 = (bf16[128,768]{1,0:T(8,128)(2,1)S(1)}, bf16[128,768]{1,0:T(8,128)(2,1)S(1)}, u32[]{:S(2)}, u32[]{:S(2)}) collective-permute-start(bf16[128,768]{1,0:T(8,128)(2,1)S(1)} %get-tuple-element.128), channel_id=1, source_target_pairs={{0,24},{4,28},{8,16},{12,20},{16,8},{20,12},{24,0},{28,4},{1,25},{... | collective-permute-start | bytes 589832 | tf_op jit(solution)/shard_map/ppermute | solution.py:547
  97.3 2.9 %collective-permute-start.29 = (bf16[4,192,768]{2,1,0:T(8,128)(2,1)S(1)}, bf16[4,192,768]{2,1,0:T(8,128)(2,1)S(1)}, u32[]{:S(2)}, u32[]{:S(2)}) collective-permute-start(bf16[4,192,768]{2,1,0:T(8,128)(2,1)S(1)} %get-tuple-element.137), channel_id=1, source_target_pairs={{0,4},{4,0},{8,12},{12,8},{16,20},{20,16},{24,28},{28,24},{1,5},{5... | collective-permute-start | bytes 3538952 | tf_op jit(solution)/shard_map/ppermute | solution.py:544
  97.4 7.3 %collective-permute-start.27 = (bf16[128,768]{1,0:T(8,128)(2,1)S(1)}, bf16[128,768]{1,0:T(8,128)(2,1)S(1)}, u32[]{:S(2)}, u32[]{:S(2)}) collective-permute-start(bf16[128,768]{1,0:T(8,128)(2,1)S(1)} %get-tuple-element.127), channel_id=1, source_target_pairs={{0,16},{4,20},{8,24},{12,28},{16,0},{20,4},{24,8},{28,12},{1,17},{... | collective-permute-start | bytes 589832 | tf_op jit(solution)/shard_map/ppermute | solution.py:547
  98.1 7.0 %collective-permute-start.26 = (bf16[128,768]{1,0:T(8,128)(2,1)S(1)}, bf16[128,768]{1,0:T(8,128)(2,1)S(1)}, u32[]{:S(2)}, u32[]{:S(2)}) collective-permute-start(bf16[128,768]{1,0:T(8,128)(2,1)S(1)} %get-tuple-element.126), channel_id=1, source_target_pairs={{0,8},{4,12},{8,0},{12,4},{16,24},{20,28},{24,16},{28,20},{1,9},{5... | collective-permute-start | bytes 589832 | tf_op jit(solution)/shard_map/ppermute | solution.py:547
  101.0 14.2 %collective-permute-start.35 = (bf16[192,768]{1,0:T(8,128)(2,1)S(1)}, bf16[192,768]{1,0:T(8,128)(2,1)S(1)}, u32[]{:S(2)}, u32[]{:S(2)}) collective-permute-start(bf16[192,768]{1,0:T(8,128)(2,1)S(1)} %get-tuple-element.138.refs_10_), channel_id=1, source_target_pairs={{0,1},{1,0},{2,3},{3,2},{4,5},{5,4},{6,7},{7,6},{8,9},{9,8},{10,11... | collective-permute-start | bytes 884744 | tf_op jit(solution)/shard_map/ppermute | solution.py:550
  106.5 16.3 %collective-permute-start.31 = (bf16[128,192]{1,0:T(8,128)(2,1)S(1)}, bf16[128,192]{1,0:T(8,128)(2,1)S(1)}, u32[]{:S(2)}, u32[]{:S(2)}) collective-permute-start(bf16[128,192]{1,0:T(8,128)(2,1)S(1)} %get-tuple-element.148), channel_id=1, source_target_pairs={{0,8},{4,12},{8,0},{12,4},{16,24},{20,28},{24,16},{28,20},{1,9},{5... | collective-permute-start | bytes 147464 | tf_op jit(solution)/shard_map/ppermute | solution.py:547
  107.9 4.9 %collective-permute-start.32 = (bf16[128,192]{1,0:T(8,128)(2,1)S(1)}, bf16[128,192]{1,0:T(8,128)(2,1)S(1)}, u32[]{:S(2)}, u32[]{:S(2)}) collective-permute-start(bf16[128,192]{1,0:T(8,128)(2,1)S(1)} %get-tuple-element.151), channel_id=1, source_target_pairs={{0,16},{4,20},{8,24},{12,28},{16,0},{20,4},{24,8},{28,12},{1,17},{... | collective-permute-start | bytes 147464 | tf_op jit(solution)/shard_map/ppermute | solution.py:547
  108.9 5.2 %collective-permute-start.33 = (bf16[128,192]{1,0:T(8,128)(2,1)S(1)}, bf16[128,192]{1,0:T(8,128)(2,1)S(1)}, u32[]{:S(2)}, u32[]{:S(2)}) collective-permute-start(bf16[128,192]{1,0:T(8,128)(2,1)S(1)} %get-tuple-element.154), channel_id=1, source_target_pairs={{0,24},{4,28},{8,16},{12,20},{16,8},{20,12},{24,0},{28,4},{1,25},{... | collective-permute-start | bytes 147464 | tf_op jit(solution)/shard_map/ppermute | solution.py:547
  111.3 7.7 %collective-permute-start.30 = (bf16[4,192,384]{2,1,0:T(8,128)(2,1)S(1)}, bf16[4,192,384]{2,1,0:T(8,128)(2,1)S(1)}, u32[]{:S(2)}, u32[]{:S(2)}) collective-permute-start(bf16[4,192,384]{2,1,0:T(8,128)(2,1)S(1)} %get-tuple-element.146), channel_id=1, source_target_pairs={{0,4},{4,0},{8,12},{12,8},{16,20},{20,16},{24,28},{28,24},{1,5},{5... | collective-permute-start | bytes 1769480 | tf_op jit(solution)/shard_map/ppermute | solution.py:544
  115.3 19.0 %collective-permute-start.42 = (bf16[192,768]{1,0:T(8,128)(2,1)S(1)}, bf16[192,768]{1,0:T(8,128)(2,1)S(1)}, u32[]{:S(2)}, u32[]{:S(2)}) collective-permute-start(bf16[192,768]{1,0:T(8,128)(2,1)S(1)} %sum_kernel.4.refs_13_.refs_1_), channel_id=1, source_target_pairs={{0,2},{1,3},{2,0},{3,1},{4,6},{5,7},{6,4},{7,5},{8,10},{9,11},{10,... | collective-permute-start | bytes 884744 | tf_op jit(solution)/shard_map/ppermute | solution.py:550
  118.2 14.6 %collective-permute-start.43 = (bf16[192,768]{1,0:T(8,128)(2,1)S(1)}, bf16[192,768]{1,0:T(8,128)(2,1)S(1)}, u32[]{:S(2)}, u32[]{:S(2)}) collective-permute-start(bf16[192,768]{1,0:T(8,128)(2,1)S(1)} %gate_kernel.8), channel_id=1, source_target_pairs={{0,1},{1,0},{2,3},{3,2},{4,5},{5,4},{6,7},{7,6},{8,9},{9,8},{10,11... | collective-permute-start | bytes 884744 | tf_op jit(solution)/shard_map/ppermute | solution.py:550
  119.7 5.9 %collective-permute-start.34 = (bf16[4,48,384]{2,1,0:T(8,128)(2,1)S(1)}, bf16[4,48,384]{2,1,0:T(8,128)(2,1)S(1)}, u32[]{:S(2)}, u32[]{:S(2)}) collective-permute-start(bf16[4,48,384]{2,1,0:T(8,128)(2,1)S(1)} %get-tuple-element.159), channel_id=1, source_target_pairs={{0,8},{4,12},{8,0},{12,4},{16,24},{20,28},{24,16},{28,20},{1,9},{5... | collective-permute-start | bytes 442376 | tf_op jit(solution)/shard_map/ppermute | solution.py:547
  121.0 8.2 %collective-permute-start.36 = (bf16[4,48,384]{2,1,0:T(8,128)(2,1)S(1)}, bf16[4,48,384]{2,1,0:T(8,128)(2,1)S(1)}, u32[]{:S(2)}, u32[]{:S(2)}) collective-permute-start(bf16[4,48,384]{2,1,0:T(8,128)(2,1)S(1)} %get-tuple-element.162), channel_id=1, source_target_pairs={{0,16},{4,20},{8,24},{12,28},{16,0},{20,4},{24,8},{28,12},{1,17},{... | collective-permute-start | bytes 442376 | tf_op jit(solution)/shard_map/ppermute | solution.py:547
  122.7 6.5 %collective-permute-start.37 = (bf16[4,48,384]{2,1,0:T(8,128)(2,1)S(1)}, bf16[4,48,384]{2,1,0:T(8,128)(2,1)S(1)}, u32[]{:S(2)}, u32[]{:S(2)}) collective-permute-start(bf16[4,48,384]{2,1,0:T(8,128)(2,1)S(1)} %get-tuple-element.163), channel_id=1, source_target_pairs={{0,24},{4,28},{8,16},{12,20},{16,8},{20,12},{24,0},{28,4},{1,25},{... | collective-permute-start | bytes 442376 | tf_op jit(solution)/shard_map/ppermute | solution.py:547
  127.2 7.1 %collective-permute-start.41 = (bf16[4,112,576]{2,1,0:T(8,128)(2,1)S(1)}, bf16[4,112,576]{2,1,0:T(8,128)(2,1)S(1)}, u32[]{:S(2)}, u32[]{:S(2)}) collective-permute-start(bf16[4,112,576]{2,1,0:T(8,128)(2,1)S(1)} %get-tuple-element.161.refs_5_), channel_id=1, source_target_pairs={{0,4},{4,0},{8,12},{12,8},{16,20},{20,16},{24,28},{28,24},{1,5},{5... | collective-permute-start | bytes 1548296 | tf_op jit(solution)/shard_map/ppermute | solution.py:544
  130.6 7.5 %collective-permute-start.38 = (bf16[128,768]{1,0:T(8,128)(2,1)S(1)}, bf16[128,768]{1,0:T(8,128)(2,1)S(1)}, u32[]{:S(2)}, u32[]{:S(2)}) collective-permute-start(bf16[128,768]{1,0:T(8,128)(2,1)S(1)} %get-tuple-element.165), channel_id=1, source_target_pairs={{0,8},{4,12},{8,0},{12,4},{16,24},{20,28},{24,16},{28,20},{1,9},{5... | collective-permute-start | bytes 589832 | tf_op jit(solution)/shard_map/ppermute | solution.py:547
  131.8 9.9 %collective-permute-start.39 = (bf16[128,768]{1,0:T(8,128)(2,1)S(1)}, bf16[128,768]{1,0:T(8,128)(2,1)S(1)}, u32[]{:S(2)}, u32[]{:S(2)}) collective-permute-start(bf16[128,768]{1,0:T(8,128)(2,1)S(1)} %get-tuple-element.166), channel_id=1, source_target_pairs={{0,16},{4,20},{8,24},{12,28},{16,0},{20,4},{24,8},{28,12},{1,17},{... | collective-permute-start | bytes 589832 | tf_op jit(solution)/shard_map/ppermute | solution.py:547
  132.7 9.0 %collective-permute-start.40 = (bf16[128,768]{1,0:T(8,128)(2,1)S(1)}, bf16[128,768]{1,0:T(8,128)(2,1)S(1)}, u32[]{:S(2)}, u32[]{:S(2)}) collective-permute-start(bf16[128,768]{1,0:T(8,128)(2,1)S(1)} %get-tuple-element.167), channel_id=1, source_target_pairs={{0,24},{4,28},{8,16},{12,20},{16,8},{20,12},{24,0},{28,4},{1,25},{... | collective-permute-start | bytes 589832 | tf_op jit(solution)/shard_map/ppermute | solution.py:547
  135.0 6.7 %collective-permute-start.44 = (bf16[144,576]{1,0:T(8,128)(2,1)S(1)}, bf16[144,576]{1,0:T(8,128)(2,1)S(1)}, u32[]{:S(2)}, u32[]{:S(2)}) collective-permute-start(bf16[144,576]{1,0:T(8,128)(2,1)S(1)} %get-tuple-element.173), channel_id=1, source_target_pairs={{0,1},{1,0},{2,3},{3,2},{4,5},{5,4},{6,7},{7,6},{8,9},{9,8},{10,11... | collective-permute-start | bytes 497672 | tf_op jit(solution)/shard_map/ppermute | solution.py:550
  141.8 9.7 %collective-permute-start.46 = (bf16[144,576]{1,0:T(8,128)(2,1)S(1)}, bf16[144,576]{1,0:T(8,128)(2,1)S(1)}, u32[]{:S(2)}, u32[]{:S(2)}) collective-permute-start(bf16[144,576]{1,0:T(8,128)(2,1)S(1)} %sum_kernel.5.refs_1_.refs_3_), channel_id=1, source_target_pairs={{0,2},{1,3},{2,0},{3,1},{4,6},{5,7},{6,4},{7,5},{8,10},{9,11},{10,... | collective-permute-start | bytes 497672 | tf_op jit(solution)/shard_map/ppermute | solution.py:550
  142.2 7.6 %collective-permute-start.45 = (bf16[144,576]{1,0:T(8,128)(2,1)S(1)}, bf16[144,576]{1,0:T(8,128)(2,1)S(1)}, u32[]{:S(2)}, u32[]{:S(2)}) collective-permute-start(bf16[144,576]{1,0:T(8,128)(2,1)S(1)} %gate_kernel.9), channel_id=1, source_target_pairs={{0,1},{1,0},{2,3},{3,2},{4,5},{5,4},{6,7},{7,6},{8,9},{9,8},{10,11... | collective-permute-start | bytes 497672 | tf_op jit(solution)/shard_map/ppermute | solution.py:550
  143.3 10.9 %collective-permute-start.53 = (bf16[192,768]{1,0:T(8,128)(2,1)S(1)}, bf16[192,768]{1,0:T(8,128)(2,1)S(1)}, u32[]{:S(2)}, u32[]{:S(2)}) collective-permute-start(bf16[192,768]{1,0:T(8,128)(2,1)S(1)} %sum_kernel.7.refs_0_), channel_id=1, source_target_pairs={{0,24},{4,28},{8,16},{12,20},{16,8},{20,12},{24,0},{28,4},{1,25},{... | collective-permute-start | bytes 884744 | tf_op jit(solution)/shard_map/ppermute | solution.py:547
  144.8 14.7 %collective-permute-start.52 = (bf16[192,768]{1,0:T(8,128)(2,1)S(1)}, bf16[192,768]{1,0:T(8,128)(2,1)S(1)}, u32[]{:S(2)}, u32[]{:S(2)}) collective-permute-start(bf16[192,768]{1,0:T(8,128)(2,1)S(1)} %sum_kernel.7.refs_0_), channel_id=1, source_target_pairs={{0,16},{4,20},{8,24},{12,28},{16,0},{20,4},{24,8},{28,12},{1,17},{... | collective-permute-start | bytes 884744 | tf_op jit(solution)/shard_map/ppermute | solution.py:547
  145.5 14.1 %collective-permute-start.51 = (bf16[192,768]{1,0:T(8,128)(2,1)S(1)}, bf16[192,768]{1,0:T(8,128)(2,1)S(1)}, u32[]{:S(2)}, u32[]{:S(2)}) collective-permute-start(bf16[192,768]{1,0:T(8,128)(2,1)S(1)} %sum_kernel.7.refs_0_), channel_id=1, source_target_pairs={{0,8},{4,12},{8,0},{12,4},{16,24},{20,28},{24,16},{28,20},{1,9},{5... | collective-permute-start | bytes 884744 | tf_op jit(solution)/shard_map/ppermute | solution.py:547
  151.5 11.9 %collective-permute-start.49 = (bf16[144,576]{1,0:T(8,128)(2,1)S(1)}, bf16[144,576]{1,0:T(8,128)(2,1)S(1)}, u32[]{:S(2)}, u32[]{:S(2)}) collective-permute-start(bf16[144,576]{1,0:T(8,128)(2,1)S(1)} %sum_kernel.6.g0.refs_3_), channel_id=1, source_target_pairs={{0,24},{4,28},{8,16},{12,20},{16,8},{20,12},{24,0},{28,4},{1,25},{... | collective-permute-start | bytes 497672 | tf_op jit(solution)/shard_map/ppermute | solution.py:547
  152.9 12.4 %collective-permute-start.48 = (bf16[144,576]{1,0:T(8,128)(2,1)S(1)}, bf16[144,576]{1,0:T(8,128)(2,1)S(1)}, u32[]{:S(2)}, u32[]{:S(2)}) collective-permute-start(bf16[144,576]{1,0:T(8,128)(2,1)S(1)} %sum_kernel.6.g0.refs_3_), channel_id=1, source_target_pairs={{0,16},{4,20},{8,24},{12,28},{16,0},{20,4},{24,8},{28,12},{1,17},{... | collective-permute-start | bytes 497672 | tf_op jit(solution)/shard_map/ppermute | solution.py:547
  154.2 11.0 %collective-permute-start.47 = (bf16[144,576]{1,0:T(8,128)(2,1)S(1)}, bf16[144,576]{1,0:T(8,128)(2,1)S(1)}, u32[]{:S(2)}, u32[]{:S(2)}) collective-permute-start(bf16[144,576]{1,0:T(8,128)(2,1)S(1)} %sum_kernel.6.g0.refs_3_), channel_id=1, source_target_pairs={{0,8},{4,12},{8,0},{12,4},{16,24},{20,28},{24,16},{28,20},{1,9},{5... | collective-permute-start | bytes 497672 | tf_op jit(solution)/shard_map/ppermute | solution.py:547
  159.8 5.6 %collective-permute-start.54 = (bf16[4,192,768]{2,1,0:T(8,128)(2,1)S(1)}, bf16[4,192,768]{2,1,0:T(8,128)(2,1)S(1)}, u32[]{:S(2)}, u32[]{:S(2)}) collective-permute-start(bf16[4,192,768]{2,1,0:T(8,128)(2,1)S(1)} %stack_kernel.5.refs_1_), channel_id=1, source_target_pairs={{0,4},{4,0},{8,12},{12,8},{16,20},{20,16},{24,28},{28,24},{1,5},{5... | collective-permute-start | bytes 3538952 | tf_op jit(solution)/shard_map/ppermute | solution.py:544
  159.9 8.6 %copy-start.2 = (f32[128,768]{1,0:T(8,128)}, f32[128,768]{1,0:T(8,128)S(1)}, u32[]{:S(2)}) copy-start(f32[128,768]{1,0:T(8,128)S(1)} %add_add_fusion.refs_4_) | copy-start | bytes 1179652
  165.3 3.2 %collective-permute-start.50 = (bf16[4,144,576]{2,1,0:T(8,128)(2,1)S(1)}, bf16[4,144,576]{2,1,0:T(8,128)(2,1)S(1)}, u32[]{:S(2)}, u32[]{:S(2)}) collective-permute-start(bf16[4,144,576]{2,1,0:T(8,128)(2,1)S(1)} %stack_kernel.4.refs_1_), channel_id=1, source_target_pairs={{0,4},{4,0},{8,12},{12,8},{16,20},{20,16},{24,28},{28,24},{1,5},{5... | collective-permute-start | bytes 1990664 | tf_op jit(solution)/shard_map/ppermute | solution.py:544
  (16 other events, 46.7 us)

commit v5 on v4

--- a/solution.py
+++ b/solution.py
@@ -680,7 +680,7 @@
         )
         ys = spread_part(y1low)
         (mine2,) = call(
-            stack_kernel, [((shards,) + pay2.shape, BF)], *got2, after=ys[1:]
+            stack_kernel, [((shards,) + pay2.shape, BF)], *got2, after=[ys[3]]
         )
         wu, wd = call(
             w2_kernel,

time: 171 us -> 168 us (0.982)
  waiting for transfers between devices: 69.2 us -> 64.9 us
    ppermute x35, waiting for transfers between devices: 47.6 us -> 44.2 us  [swap_part(): return lax.ppermute(v, 'rep', xor_perm(reps, CORES * k))]
  transfers between devices with their start and end apart: 55 -> 55, of which waited for: 29 -> 30; matrix products, arithmetic and copies ran while one was open for 0% -> 0% of each run, Pallas kernels for 17% -> 18%
where the time goes in v5:
time: 168 us
  waiting for transfers between devices  64.9 us (39%)
  starting transfers between devices  61.3 us (36%)
  Pallas kernels  38.3 us (23%)
    ppermute x35, waiting for transfers between devices, swap_part(): return lax.ppermute(v, 'rep', xor_perm(reps, CORES * k))  44.2 us
    ppermute x35, starting transfers between devices, swap_part(): return lax.ppermute(v, 'rep', xor_perm(reps, CORES * k))  42.8 us
    pallas_call x42, Pallas kernels, call(): pl.pallas_call(run if drop else kernel, out_shape=shapes, in_specs=specs,...  38.3 us
    ppermute x12, waiting for transfers between devices, swap_shard(): return lax.ppermute(v, 'shard', xor_perm(shards, k))  18.7 us
    ppermute x12, starting transfers between devices, swap_shard(): return lax.ppermute(v, 'shard', xor_perm(shards, k))  17.9 us
  transfers between devices with their start and end apart: 55, of which 30 were waited for; matrix products, arithmetic and copies ran while one was open for 0% of the time, Pallas kernels for 18%

profile of v5, /device:TPU:0, one launch (start us, length us, event | category | flops | bytes accessed | tf_op | source)
XLA Modules:
  0.0 167.7 jit_solution(15779320653693610956)
XLA Ops:
  1.3 2.7 %pack_kernel.1 = (bf16[144,768]{1,0:T(8,128)(2,1)}, bf16[144,576]{1,0:T(8,128)(2,1)}) custom-call(s32[3]{0:T(128)} %pad_add_fusion.idx.refs_0_, bf16[128,768]{1,0:T(8,128)(2,1)} %tok.3, bf16[192,2304]{1,0:T(8,128)(2,1)} %wqkv.1, bf16[192,768]{1,0:T(8,128)(2,1)} %wout.1, bf16[6,192]{1,0:T(8,128)(2,1)} %vec_in.1, bf16[2,192]{1,0:T(2,128)(2,1)} %gain_in.1, ...), custom_call_target="tpu_custom_call" | custom-call | flops 11000000512 | bytes 100000 | tf_op jit(solution)/shard_map/pack_kernel/pallas_call | solution.py:514
  3.9 4.0 %collective-permute-start.2 = (bf16[144,768]{1,0:T(8,128)(2,1)}, bf16[144,768]{1,0:T(8,128)(2,1)S(1)}, u32[]{:S(2)}, u32[]{:S(2)}) collective-permute-start(bf16[144,768]{1,0:T(8,128)(2,1)} %get-tuple-element.96.refs_3_.x.x0.refs_1_), channel_id=1, source_target_pairs={{0,24},{4,28},{8,16},{12,20},{16,8},{20,12},{24,0},{28,4},{1,25},{... | collective-permute-start | bytes 663560 | tf_op jit(solution)/shard_map/ppermute | solution.py:547
  7.9 2.6 %collective-permute-start.1 = (bf16[144,576]{1,0:T(8,128)(2,1)}, bf16[144,576]{1,0:T(8,128)(2,1)S(1)}, u32[]{:S(2)}, u32[]{:S(2)}) collective-permute-start(bf16[144,576]{1,0:T(8,128)(2,1)} %get-tuple-element.97.g0), channel_id=1, source_target_pairs={{0,2},{1,3},{2,0},{3,1},{4,6},{5,7},{6,4},{7,5},{8,10},{9,11},{10,... | collective-permute-start | bytes 497672 | tf_op jit(solution)/shard_map/ppermute | solution.py:550
  10.5 1.6 collective-permute-start
  12.1 7.1 %collective-permute-done.1.refs_0_ = bf16[144,576]{1,0:T(8,128)(2,1)S(1)} collective-permute-done((bf16[144,576]{1,0:T(8,128)(2,1)}, bf16[144,576]{1,0:T(8,128)(2,1)S(1)}, u32[]{:S(2)}, u32[]{:S(2)}) %collective-permute-start.1) | collective-permute-done | bytes 165920 | tf_op jit(solution)/shard_map/ppermute | solution.py:550
  21.0 3.8 %collective-permute-done.3.g3.refs_1_ = bf16[144,576]{1,0:T(8,128)(2,1)S(1)} collective-permute-done((bf16[144,576]{1,0:T(8,128)(2,1)S(1)}, bf16[144,576]{1,0:T(8,128)(2,1)S(1)}, u32[]{:S(2)}, u32[]{:S(2)}) %collective-permute-start.3) | collective-permute-done | bytes 165920 | tf_op jit(solution)/shard_map/ppermute | solution.py:550
  28.0 2.8 %collective-permute-start.14 = (bf16[192,768]{1,0:T(8,128)(2,1)S(1)}, bf16[192,768]{1,0:T(8,128)(2,1)S(1)}, u32[]{:S(2)}, u32[]{:S(2)}) collective-permute-start(bf16[192,768]{1,0:T(8,128)(2,1)S(1)} %gate_kernel.6.refs_3_.refs_0_), channel_id=1, source_target_pairs={{0,2},{1,3},{2,0},{3,1},{4,6},{5,7},{6,4},{7,5},{8,10},{9,11},{10,... | collective-permute-start | bytes 884744 | tf_op jit(solution)/shard_map/ppermute | solution.py:550
  30.8 1.7 %collective-permute-start.13 = (bf16[192,768]{1,0:T(8,128)(2,1)S(1)}, bf16[192,768]{1,0:T(8,128)(2,1)S(1)}, u32[]{:S(2)}, u32[]{:S(2)}) collective-permute-start(bf16[192,768]{1,0:T(8,128)(2,1)S(1)} %gate_kernel.6.refs_3_.refs_0_), channel_id=1, source_target_pairs={{0,1},{1,0},{2,3},{3,2},{4,5},{5,4},{6,7},{7,6},{8,9},{9,8},{10,11... | collective-permute-start | bytes 884744 | tf_op jit(solution)/shard_map/ppermute | solution.py:550
  34.9 2.5 %collective-permute-start.9 = (bf16[128,192]{1,0:T(8,128)(2,1)S(1)}, bf16[128,192]{1,0:T(8,128)(2,1)S(1)}, u32[]{:S(2)}, u32[]{:S(2)}) collective-permute-start(bf16[128,192]{1,0:T(8,128)(2,1)S(1)} %get-tuple-element.104.refs_2_), channel_id=1, source_target_pairs={{0,24},{4,28},{8,16},{12,20},{16,8},{20,12},{24,0},{28,4},{1,25},{... | collective-permute-start | bytes 147464 | tf_op jit(solution)/shard_map/ppermute | solution.py:547
  39.8 3.8 %collective-permute-done.11.refs_1_ = bf16[2,4,48,384]{3,2,1,0:T(8,128)(2,1)S(1)} collective-permute-done((bf16[2,4,48,384]{3,2,1,0:T(8,128)(2,1)S(1)}, bf16[2,4,48,384]{3,2,1,0:T(8,128)(2,1)S(1)}, u32[]{:S(2)}, u32[]{:S(2)}) %collective-permute-start.11) | collective-permute-done | bytes 294944 | tf_op jit(solution)/shard_map/ppermute | solution.py:547
  43.6 1.5 collective-permute-start.7
  46.3 1.6 collective-permute-done.7.m1.refs_1_.refs_2_
  48.9 1.1 out_kernel.1
  50.0 1.5 collective-permute-start.16
  51.6 4.2 %collective-permute-done.15.refs_3_ = bf16[192,768]{1,0:T(8,128)(2,1)S(1)} collective-permute-done((bf16[192,768]{1,0:T(8,128)(2,1)S(1)}, bf16[192,768]{1,0:T(8,128)(2,1)S(1)}, u32[]{:S(2)}, u32[]{:S(2)}) %collective-permute-start.15) | collective-permute-done | bytes 294944 | tf_op jit(solution)/shard_map/ppermute | solution.py:550
  55.8 1.2 collective-permute-done.16.refs_4_.y.refs_12_
  57.8 1.2 collective-permute-start.18
  58.9 1.1 collective-permute-done.17.other
  61.4 1.2 collective-permute-start.22
  62.6 1.9 %collective-permute-done.20.y.refs_11_ = bf16[128,768]{1,0:T(8,128)(2,1)S(1)} collective-permute-done((bf16[128,768]{1,0:T(8,128)(2,1)S(1)}, bf16[128,768]{1,0:T(8,128)(2,1)S(1)}, u32[]{:S(2)}, u32[]{:S(2)}) %collective-permute-start.20) | collective-permute-done | bytes 196640 | tf_op jit(solution)/shard_map/ppermute | solution.py:547
  66.5 1.2 collective-permute-start.19
  68.4 1.9 %collective-permute-done.22.r3 = bf16[128,768]{1,0:T(8,128)(2,1)S(1)} collective-permute-done((bf16[128,768]{1,0:T(8,128)(2,1)S(1)}, bf16[128,768]{1,0:T(8,128)(2,1)S(1)}, u32[]{:S(2)}, u32[]{:S(2)}) %collective-permute-start.22) | collective-permute-done | bytes 196640 | tf_op jit(solution)/shard_map/ppermute | solution.py:547
  70.3 3.8 %collective-permute-done.21.r2 = bf16[128,768]{1,0:T(8,128)(2,1)S(1)} collective-permute-done((bf16[128,768]{1,0:T(8,128)(2,1)S(1)}, bf16[128,768]{1,0:T(8,128)(2,1)S(1)}, u32[]{:S(2)}, u32[]{:S(2)}) %collective-permute-start.21) | collective-permute-done | bytes 196640 | tf_op jit(solution)/shard_map/ppermute | solution.py:547
  74.1 1.2 ln2_kernel.1
  75.3 1.2 collective-permute-start.25
  76.5 1.4 collective-permute-start.24
  78.8 5.2 %collective-permute-done.25.d.refs_8_ = bf16[128,768]{1,0:T(8,128)(2,1)S(1)} collective-permute-done((bf16[128,768]{1,0:T(8,128)(2,1)S(1)}, bf16[128,768]{1,0:T(8,128)(2,1)S(1)}, u32[]{:S(2)}, u32[]{:S(2)}) %collective-permute-start.25) | collective-permute-done | bytes 196640 | tf_op jit(solution)/shard_map/ppermute | solution.py:547
  84.9 1.3 collective-permute-start.28
  86.2 1.3 collective-permute-done.24.d.refs_7_
  90.4 1.2 collective-permute-done.28.refs_17_.refs_3_.refs_5_
  91.6 2.1 %ffw_kernel.1 = (bf16[4,192,768]{2,1,0:T(8,128)(2,1)S(1)}, bf16[4,192,768]{2,1,0:T(8,128)(2,1)S(1)}, f32[8,768]{1,0:T(8,128)S(1)}) custom-call(s32[3]{0:T(128)S(1)} %copy-done.13, bf16[128,768]{1,0:T(8,128)(2,1)S(1)} %get-tuple-element.131.refs_1_, bf16[128,768]{1,0:T(8,128)(2,1)S(1)} %get-tuple-element.132.refs_2_, ...), custom_call_target="tpu_custom_call" | custom-call | flops 11000000512 | bytes 100000 | tf_op jit(solution)/shard_map/ffw_kernel/pallas_call | solution.py:514
  94.5 1.2 collective-permute-start.26
  97.4 1.5 collective-permute-start.35
  98.9 2.2 %collective-permute-done.27.refs_4_ = bf16[128,768]{1,0:T(8,128)(2,1)S(1)} collective-permute-done((bf16[128,768]{1,0:T(8,128)(2,1)S(1)}, bf16[128,768]{1,0:T(8,128)(2,1)S(1)}, u32[]{:S(2)}, u32[]{:S(2)}) %collective-permute-start.27) | collective-permute-done | bytes 196640 | tf_op jit(solution)/shard_map/ppermute | solution.py:547
  101.5 1.3 ln1b_kernel.1
  102.8 1.4 collective-permute-start.31
  104.2 1.4 collective-permute-start.32
  107.7 1.5 collective-permute-done.32.d
  109.2 1.1 attb_kernel.6.refs_7_.refs_2_
  110.8 1.1 attb_kernel.7.refs_2_.refs_8_.refs_3_
  112.0 3.2 %collective-permute-start.42 = (bf16[192,768]{1,0:T(8,128)(2,1)S(1)}, bf16[192,768]{1,0:T(8,128)(2,1)S(1)}, u32[]{:S(2)}, u32[]{:S(2)}) collective-permute-start(bf16[192,768]{1,0:T(8,128)(2,1)S(1)} %sum_kernel.4.refs_13_.refs_1_), channel_id=1, source_target_pairs={{0,2},{1,3},{2,0},{3,1},{4,6},{5,7},{6,4},{7,5},{8,10},{9,11},{10,... | collective-permute-start | bytes 884744 | tf_op jit(solution)/shard_map/ppermute | solution.py:550
  118.0 1.1 attb_kernel.4.refs_5_.refs_0_
  119.1 2.4 %collective-permute-start.37 = (bf16[4,48,384]{2,1,0:T(8,128)(2,1)S(1)}, bf16[4,48,384]{2,1,0:T(8,128)(2,1)S(1)}, u32[]{:S(2)}, u32[]{:S(2)}) collective-permute-start(bf16[4,48,384]{2,1,0:T(8,128)(2,1)S(1)} %get-tuple-element.163), channel_id=1, source_target_pairs={{0,24},{4,28},{8,16},{12,20},{16,8},{20,12},{24,0},{28,4},{1,25},{... | collective-permute-start | bytes 442376 | tf_op jit(solution)/shard_map/ppermute | solution.py:547
  121.5 1.1 attb_kernel.5.refs_6_.refs_1_
  123.3 1.5 qw_kernel.1
  125.7 1.4 dx_kernel.1
  127.0 1.4 collective-permute-start.38
  128.4 1.2 collective-permute-start.39
  129.7 1.1 collective-permute-start.40
  131.5 1.3 collective-permute-start.44
  132.8 2.1 %collective-permute-done.38.refs_2_ = bf16[128,768]{1,0:T(8,128)(2,1)S(1)} collective-permute-done((bf16[128,768]{1,0:T(8,128)(2,1)S(1)}, bf16[128,768]{1,0:T(8,128)(2,1)S(1)}, u32[]{:S(2)}, u32[]{:S(2)}) %collective-permute-start.38) | collective-permute-done | bytes 196640 | tf_op jit(solution)/shard_map/ppermute | solution.py:547
  134.9 3.1 %collective-permute-done.39.refs_3_ = bf16[128,768]{1,0:T(8,128)(2,1)S(1)} collective-permute-done((bf16[128,768]{1,0:T(8,128)(2,1)S(1)}, bf16[128,768]{1,0:T(8,128)(2,1)S(1)}, u32[]{:S(2)}, u32[]{:S(2)}) %collective-permute-start.39) | collective-permute-done | bytes 196640 | tf_op jit(solution)/shard_map/ppermute | solution.py:547
  139.6 1.4 collective-permute-start.53
  141.0 1.6 collective-permute-start.52
  143.2 2.3 %collective-permute-done.45.refs_1_.refs_5_ = bf16[144,576]{1,0:T(8,128)(2,1)S(1)} collective-permute-done((bf16[144,576]{1,0:T(8,128)(2,1)S(1)}, bf16[144,576]{1,0:T(8,128)(2,1)S(1)}, u32[]{:S(2)}, u32[]{:S(2)}) %collective-permute-start.45) | collective-permute-done | bytes 165920 | tf_op jit(solution)/shard_map/ppermute | solution.py:550
  145.4 1.2 collective-permute-done.46.refs_2_.refs_4_
  146.7 2.6 %collective-permute-start.49 = (bf16[144,576]{1,0:T(8,128)(2,1)S(1)}, bf16[144,576]{1,0:T(8,128)(2,1)S(1)}, u32[]{:S(2)}, u32[]{:S(2)}) collective-permute-start(bf16[144,576]{1,0:T(8,128)(2,1)S(1)} %sum_kernel.6.g0.refs_3_), channel_id=1, source_target_pairs={{0,24},{4,28},{8,16},{12,20},{16,8},{20,12},{24,0},{28,4},{1,25},{... | collective-permute-start | bytes 497672 | tf_op jit(solution)/shard_map/ppermute | solution.py:547
  149.9 1.5 collective-permute-start.47
  151.4 4.6 %collective-permute-done.52.refs_2_ = bf16[192,768]{1,0:T(8,128)(2,1)S(1)} collective-permute-done((bf16[192,768]{1,0:T(8,128)(2,1)S(1)}, bf16[192,768]{1,0:T(8,128)(2,1)S(1)}, u32[]{:S(2)}, u32[]{:S(2)}) %collective-permute-start.52) | collective-permute-done | bytes 294944 | tf_op jit(solution)/shard_map/ppermute | solution.py:547
  157.0 1.6 collective-permute-done.49.g3
  158.7 1.8 %collective-permute-done.48.g2 = bf16[144,576]{1,0:T(8,128)(2,1)S(1)} collective-permute-done((bf16[144,576]{1,0:T(8,128)(2,1)S(1)}, bf16[144,576]{1,0:T(8,128)(2,1)S(1)}, u32[]{:S(2)}, u32[]{:S(2)}) %collective-permute-start.48) | collective-permute-done | bytes 165920 | tf_op jit(solution)/shard_map/ppermute | solution.py:547
  160.4 1.6 collective-permute-done.47.g1
  162.2 3.1 %fin1_kernel.1 = (f32[192,3072]{1,0:T(8,128)}, f32[768,768]{1,0:T(8,128)}, f32[8,128]{1,0:T(8,128)S(1)}) custom-call(s32[3]{0:T(128)S(1)} %copy-done.13, bf16[4,192,768]{2,1,0:T(8,128)(2,1)S(1)} %stack_kernel.5.refs_1_, bf16[4,192,768]{2,1,0:T(8,128)(2,1)S(1)} %collective-permute-done.54.refs_2_, bf16[144,576]{1,0:T(8,128)(2,1)S(1)} %sum_kernel.6.g0.refs_3_), custom_call_target="tpu_custom_call" | custom-call | flops 11000000512 | bytes 100000 | tf_op jit(solution)/shard_map/fin1_kernel/pallas_call | solution.py:514
  165.4 2.3 %fin2_kernel.1 = (f32[192,2304]{1,0:T(8,128)}, f32[192,768]{1,0:T(8,128)}, f32[6,192]{1,0:T(8,128)}, f32[2,192]{1,0:T(2,128)}, f32[768]{0:T(1024)}) custom-call(s32[3]{0:T(128)S(1)} %copy-done.13, bf16[4,144,576]{2,1,0:T(8,128)(2,1)S(1)} %stack_kernel.4.refs_1_, bf16[4,144,576]{2,1,0:T(8,128)(2,1)S(1)} %collective-permute-done.50.refs_2_, ...), custom_call_target="tpu_custom_call" | custom-call | flops 11000000512 | bytes 100000 | tf_op jit(solution)/shard_map/fin2_kernel/pallas_call | solution.py:514
  (147 shorter events, 35.9 us)
Async XLA Ops:
  3.9 15.2 %collective-permute-start.2 = (bf16[144,768]{1,0:T(8,128)(2,1)}, bf16[144,768]{1,0:T(8,128)(2,1)S(1)}, u32[]{:S(2)}, u32[]{:S(2)}) collective-permute-start(bf16[144,768]{1,0:T(8,128)(2,1)} %get-tuple-element.96.refs_3_.x.x0.refs_1_), channel_id=1, source_target_pairs={{0,24},{4,28},{8,16},{12,20},{16,8},{20,12},{24,0},{28,4},{1,25},{... | collective-permute-start | bytes 663560 | tf_op jit(solution)/shard_map/ppermute | solution.py:547
  7.9 11.3 %collective-permute-start.1 = (bf16[144,576]{1,0:T(8,128)(2,1)}, bf16[144,576]{1,0:T(8,128)(2,1)S(1)}, u32[]{:S(2)}, u32[]{:S(2)}) collective-permute-start(bf16[144,576]{1,0:T(8,128)(2,1)} %get-tuple-element.97.g0), channel_id=1, source_target_pairs={{0,2},{1,3},{2,0},{3,1},{4,6},{5,7},{6,4},{7,5},{8,10},{9,11},{10,... | collective-permute-start | bytes 497672 | tf_op jit(solution)/shard_map/ppermute | solution.py:550
  10.5 10.5 %collective-permute-start = (bf16[144,576]{1,0:T(8,128)(2,1)}, bf16[144,576]{1,0:T(8,128)(2,1)S(1)}, u32[]{:S(2)}, u32[]{:S(2)}) collective-permute-start(bf16[144,576]{1,0:T(8,128)(2,1)} %get-tuple-element.97.g0), channel_id=1, source_target_pairs={{0,1},{1,0},{2,3},{3,2},{4,5},{5,4},{6,7},{7,6},{8,9},{9,8},{10,11... | collective-permute-start | bytes 497672 | tf_op jit(solution)/shard_map/ppermute | solution.py:550
  19.2 14.7 %copy-start = (bf16[144,768]{1,0:T(8,128)(2,1)}, bf16[144,768]{1,0:T(8,128)(2,1)S(1)}, u32[]{:S(2)}) copy-start(bf16[144,768]{1,0:T(8,128)(2,1)S(1)} %collective-permute-done.2.refs_1_.refs_4_.x) | copy-start | bytes 663556
  19.2 7.3 %copy-start.13 = (s32[3]{0:T(128)S(1)}, s32[3]{0:T(128)}, u32[]{:S(2)}) copy-start(s32[3]{0:T(128)} %pad_add_fusion.idx.refs_0_) | copy-start | bytes 40
  19.2 7.3 %copy-start.14 = (bf16[192,3072]{1,0:T(8,128)(2,1)S(1)}, bf16[192,3072]{1,0:T(8,128)(2,1)}, u32[]{:S(2)}) copy-start(bf16[192,3072]{1,0:T(8,128)(2,1)} %refs_1_.1) | copy-start | bytes 3538948
  19.2 7.3 %copy-start.15 = (bf16[768,768]{1,0:T(8,128)(2,1)S(1)}, bf16[768,768]{1,0:T(8,128)(2,1)}, u32[]{:S(2)}) copy-start(bf16[768,768]{1,0:T(8,128)(2,1)} %refs_2_.1) | copy-start | bytes 3538948
  19.2 5.6 %collective-permute-start.3 = (bf16[144,576]{1,0:T(8,128)(2,1)S(1)}, bf16[144,576]{1,0:T(8,128)(2,1)S(1)}, u32[]{:S(2)}, u32[]{:S(2)}) collective-permute-start(bf16[144,576]{1,0:T(8,128)(2,1)S(1)} %gate_kernel.5.g2), channel_id=1, source_target_pairs={{0,1},{1,0},{2,3},{3,2},{4,5},{5,4},{6,7},{7,6},{8,9},{9,8},{10,11... | collective-permute-start | bytes 497672 | tf_op jit(solution)/shard_map/ppermute | solution.py:550
  20.0 7.5 %collective-permute-start.6 = (bf16[144,768]{1,0:T(8,128)(2,1)}, bf16[144,768]{1,0:T(8,128)(2,1)S(1)}, u32[]{:S(2)}, u32[]{:S(2)}) collective-permute-start(bf16[144,768]{1,0:T(8,128)(2,1)} %get-tuple-element.96.refs_3_.x.x0.refs_1_), channel_id=1, source_target_pairs={{0,16},{4,20},{8,24},{12,28},{16,0},{20,4},{24,8},{28,12},{1,17},{... | collective-permute-start | bytes 663560 | tf_op jit(solution)/shard_map/ppermute | solution.py:547
  20.5 7.5 %collective-permute-start.5 = (bf16[144,768]{1,0:T(8,128)(2,1)}, bf16[144,768]{1,0:T(8,128)(2,1)S(1)}, u32[]{:S(2)}, u32[]{:S(2)}) collective-permute-start(bf16[144,768]{1,0:T(8,128)(2,1)} %get-tuple-element.96.refs_3_.x.x0.refs_1_), channel_id=1, source_target_pairs={{0,8},{4,12},{8,0},{12,4},{16,24},{20,28},{24,16},{28,20},{1,9},{5... | collective-permute-start | bytes 663560 | tf_op jit(solution)/shard_map/ppermute | solution.py:547
  25.9 6.7 %collective-permute-start.10 = (bf16[4,48,384]{2,1,0:T(8,128)(2,1)S(1)}, bf16[4,48,384]{2,1,0:T(8,128)(2,1)S(1)}, u32[]{:S(2)}, u32[]{:S(2)}) collective-permute-start(bf16[4,48,384]{2,1,0:T(8,128)(2,1)S(1)} %get-tuple-element.105), channel_id=1, source_target_pairs={{0,8},{4,12},{8,0},{12,4},{16,24},{20,28},{24,16},{28,20},{1,9},{5... | collective-permute-start | bytes 442376 | tf_op jit(solution)/shard_map/ppermute | solution.py:547
  26.5 6.7 %collective-permute-start.4 = (bf16[4,112,576]{2,1,0:T(8,128)(2,1)S(1)}, bf16[4,112,576]{2,1,0:T(8,128)(2,1)S(1)}, u32[]{:S(2)}, u32[]{:S(2)}) collective-permute-start(bf16[4,112,576]{2,1,0:T(8,128)(2,1)S(1)} %get-tuple-element.98.refs_1_), channel_id=1, source_target_pairs={{0,4},{4,0},{8,12},{12,8},{16,20},{20,16},{24,28},{28,24},{1,5},{5... | collective-permute-start | bytes 1548296 | tf_op jit(solution)/shard_map/ppermute | solution.py:544
  27.5 9.9 %copy-start.3 = (bf16[144,768]{1,0:T(8,128)(2,1)}, bf16[144,768]{1,0:T(8,128)(2,1)S(1)}, u32[]{:S(2)}) copy-start(bf16[144,768]{1,0:T(8,128)(2,1)S(1)} %collective-permute-done.6.refs_3_.x) | copy-start | bytes 663556
  28.0 10.9 %copy-start.5 = (bf16[144,768]{1,0:T(8,128)(2,1)}, bf16[144,768]{1,0:T(8,128)(2,1)S(1)}, u32[]{:S(2)}) copy-start(bf16[144,768]{1,0:T(8,128)(2,1)S(1)} %collective-permute-done.5.refs_2_.x) | copy-start | bytes 663556
  28.0 17.2 %collective-permute-start.14 = (bf16[192,768]{1,0:T(8,128)(2,1)S(1)}, bf16[192,768]{1,0:T(8,128)(2,1)S(1)}, u32[]{:S(2)}, u32[]{:S(2)}) collective-permute-start(bf16[192,768]{1,0:T(8,128)(2,1)S(1)} %gate_kernel.6.refs_3_.refs_0_), channel_id=1, source_target_pairs={{0,2},{1,3},{2,0},{3,1},{4,6},{5,7},{6,4},{7,5},{8,10},{9,11},{10,... | collective-permute-start | bytes 884744 | tf_op jit(solution)/shard_map/ppermute | solution.py:550
  30.8 15.4 %collective-permute-start.13 = (bf16[192,768]{1,0:T(8,128)(2,1)S(1)}, bf16[192,768]{1,0:T(8,128)(2,1)S(1)}, u32[]{:S(2)}, u32[]{:S(2)}) collective-permute-start(bf16[192,768]{1,0:T(8,128)(2,1)S(1)} %gate_kernel.6.refs_3_.refs_0_), channel_id=1, source_target_pairs={{0,1},{1,0},{2,3},{3,2},{4,5},{5,4},{6,7},{7,6},{8,9},{9,8},{10,11... | collective-permute-start | bytes 884744 | tf_op jit(solution)/shard_map/ppermute | solution.py:550
  32.6 11.0 %collective-permute-start.11 = (bf16[2,4,48,384]{3,2,1,0:T(8,128)(2,1)S(1)}, bf16[2,4,48,384]{3,2,1,0:T(8,128)(2,1)S(1)}, u32[]{:S(2)}, u32[]{:S(2)}) collective-permute-start(bf16[2,4,48,384]{3,2,1,0:T(8,128)(2,1)S(1)} %pad_maximum_fusion.refs_0_), channel_id=1, source_target_pairs={{0,16},{4,20},{8,24},{12,28},{16,0},{20,4},{24,8},{28,12},{1,17},{... | collective-permute-start | bytes 884744 | tf_op jit(solution)/shard_map/ppermute | solution.py:547
  33.9 11.4 %copy-start.21 = (bf16[768,576]{1,0:T(8,128)(2,1)}, bf16[768,576]{1,0:T(8,128)(2,1)S(1)}, u32[]{:S(2)}) copy-start(bf16[768,576]{1,0:T(8,128)(2,1)S(1)} %get-tuple-element.99.wq.refs_4_) | copy-start | bytes 2654212
  34.9 11.4 %collective-permute-start.9 = (bf16[128,192]{1,0:T(8,128)(2,1)S(1)}, bf16[128,192]{1,0:T(8,128)(2,1)S(1)}, u32[]{:S(2)}, u32[]{:S(2)}) collective-permute-start(bf16[128,192]{1,0:T(8,128)(2,1)S(1)} %get-tuple-element.104.refs_2_), channel_id=1, source_target_pairs={{0,24},{4,28},{8,16},{12,20},{16,8},{20,12},{24,0},{28,4},{1,25},{... | collective-permute-start | bytes 147464 | tf_op jit(solution)/shard_map/ppermute | solution.py:547
  38.3 8.0 %collective-permute-start.8 = (bf16[128,192]{1,0:T(8,128)(2,1)S(1)}, bf16[128,192]{1,0:T(8,128)(2,1)S(1)}, u32[]{:S(2)}, u32[]{:S(2)}) collective-permute-start(bf16[128,192]{1,0:T(8,128)(2,1)S(1)} %get-tuple-element.103), channel_id=1, source_target_pairs={{0,16},{4,20},{8,24},{12,28},{16,0},{20,4},{24,8},{28,12},{1,17},{... | collective-permute-start | bytes 147464 | tf_op jit(solution)/shard_map/ppermute | solution.py:547
  43.6 4.3 %collective-permute-start.7 = (bf16[128,192]{1,0:T(8,128)(2,1)S(1)}, bf16[128,192]{1,0:T(8,128)(2,1)S(1)}, u32[]{:S(2)}, u32[]{:S(2)}) collective-permute-start(bf16[128,192]{1,0:T(8,128)(2,1)S(1)} %get-tuple-element.102), channel_id=1, source_target_pairs={{0,8},{4,12},{8,0},{12,4},{16,24},{20,28},{24,16},{28,20},{1,9},{5... | collective-permute-start | bytes 147464 | tf_op jit(solution)/shard_map/ppermute | solution.py:547
  45.2 3.0 %collective-permute-start.12 = (bf16[4,4,48,384]{3,2,1,0:T(8,128)(2,1)S(1)}, bf16[4,4,48,384]{3,2,1,0:T(8,128)(2,1)S(1)}, u32[]{:S(2)}, u32[]{:S(2)}) collective-permute-start(bf16[4,4,48,384]{3,2,1,0:T(8,128)(2,1)S(1)} %join_kernel.1.mine), channel_id=1, source_target_pairs={{0,4},{4,0},{8,12},{12,8},{16,20},{20,16},{24,28},{28,24},{1,5},{5... | collective-permute-start | bytes 1769480 | tf_op jit(solution)/shard_map/ppermute | solution.py:544
  47.9 7.9 %collective-permute-start.15 = (bf16[192,768]{1,0:T(8,128)(2,1)S(1)}, bf16[192,768]{1,0:T(8,128)(2,1)S(1)}, u32[]{:S(2)}, u32[]{:S(2)}) collective-permute-start(bf16[192,768]{1,0:T(8,128)(2,1)S(1)} %gate_kernel.7.refs_2_), channel_id=1, source_target_pairs={{0,1},{1,0},{2,3},{3,2},{4,5},{5,4},{6,7},{7,6},{8,9},{9,8},{10,11... | collective-permute-start | bytes 884744 | tf_op jit(solution)/shard_map/ppermute | solution.py:550
  50.0 7.0 %collective-permute-start.16 = (bf16[128,768]{1,0:T(8,128)(2,1)S(1)}, bf16[128,768]{1,0:T(8,128)(2,1)S(1)}, u32[]{:S(2)}, u32[]{:S(2)}) collective-permute-start(bf16[128,768]{1,0:T(8,128)(2,1)S(1)} %get-tuple-element.108.y.refs_9_), channel_id=1, source_target_pairs={{0,24},{4,28},{8,16},{12,20},{16,8},{20,12},{24,0},{28,4},{1,25},{... | collective-permute-start | bytes 589832 | tf_op jit(solution)/shard_map/ppermute | solution.py:547
  57.1 2.9 %collective-permute-start.17 = (bf16[4,192,768]{2,1,0:T(8,128)(2,1)S(1)}, bf16[4,192,768]{2,1,0:T(8,128)(2,1)S(1)}, u32[]{:S(2)}, u32[]{:S(2)}) collective-permute-start(bf16[4,192,768]{2,1,0:T(8,128)(2,1)S(1)} %stack_kernel.3.mine), channel_id=1, source_target_pairs={{0,4},{4,0},{8,12},{12,8},{16,20},{20,16},{24,28},{28,24},{1,5},{5... | collective-permute-start | bytes 3538952 | tf_op jit(solution)/shard_map/ppermute | solution.py:544
  57.2 7.3 %collective-permute-start.20 = (bf16[128,768]{1,0:T(8,128)(2,1)S(1)}, bf16[128,768]{1,0:T(8,128)(2,1)S(1)}, u32[]{:S(2)}, u32[]{:S(2)}) collective-permute-start(bf16[128,768]{1,0:T(8,128)(2,1)S(1)} %get-tuple-element.108.y.refs_9_), channel_id=1, source_target_pairs={{0,16},{4,20},{8,24},{12,28},{16,0},{20,4},{24,8},{28,12},{1,17},{... | collective-permute-start | bytes 589832 | tf_op jit(solution)/shard_map/ppermute | solution.py:547
  57.8 8.0 %collective-permute-start.18 = (bf16[128,768]{1,0:T(8,128)(2,1)S(1)}, bf16[128,768]{1,0:T(8,128)(2,1)S(1)}, u32[]{:S(2)}, u32[]{:S(2)}) collective-permute-start(bf16[128,768]{1,0:T(8,128)(2,1)S(1)} %get-tuple-element.108.y.refs_9_), channel_id=1, source_target_pairs={{0,8},{4,12},{8,0},{12,4},{16,24},{20,28},{24,16},{28,20},{1,9},{5... | collective-permute-start | bytes 589832 | tf_op jit(solution)/shard_map/ppermute | solution.py:547
  61.4 8.9 %collective-permute-start.22 = (bf16[128,768]{1,0:T(8,128)(2,1)S(1)}, bf16[128,768]{1,0:T(8,128)(2,1)S(1)}, u32[]{:S(2)}, u32[]{:S(2)}) collective-permute-start(bf16[128,768]{1,0:T(8,128)(2,1)S(1)} %get-tuple-element.114), channel_id=1, source_target_pairs={{0,24},{4,28},{8,16},{12,20},{16,8},{20,12},{24,0},{28,4},{1,25},{... | collective-permute-start | bytes 589832 | tf_op jit(solution)/shard_map/ppermute | solution.py:547
  65.2 8.9 %collective-permute-start.21 = (bf16[128,768]{1,0:T(8,128)(2,1)S(1)}, bf16[128,768]{1,0:T(8,128)(2,1)S(1)}, u32[]{:S(2)}, u32[]{:S(2)}) collective-permute-start(bf16[128,768]{1,0:T(8,128)(2,1)S(1)} %get-tuple-element.113), channel_id=1, source_target_pairs={{0,16},{4,20},{8,24},{12,28},{16,0},{20,4},{24,8},{28,12},{1,17},{... | collective-permute-start | bytes 589832 | tf_op jit(solution)/shard_map/ppermute | solution.py:547
  66.5 7.6 %copy-start.19 = (bf16[128,768]{1,0:T(8,128)(2,1)S(1)}, bf16[128,768]{1,0:T(8,128)(2,1)}, u32[]{:S(2)}) copy-start(bf16[128,768]{1,0:T(8,128)(2,1)} %cot.1) | copy-start | bytes 589828
  66.5 7.6 %collective-permute-start.19 = (bf16[128,768]{1,0:T(8,128)(2,1)S(1)}, bf16[128,768]{1,0:T(8,128)(2,1)S(1)}, u32[]{:S(2)}, u32[]{:S(2)}) collective-permute-start(bf16[128,768]{1,0:T(8,128)(2,1)S(1)} %get-tuple-element.112), channel_id=1, source_target_pairs={{0,8},{4,12},{8,0},{12,4},{16,24},{20,28},{24,16},{28,20},{1,9},{5... | collective-permute-start | bytes 589832 | tf_op jit(solution)/shard_map/ppermute | solution.py:547
  75.3 8.7 %collective-permute-start.25 = (bf16[128,768]{1,0:T(8,128)(2,1)S(1)}, bf16[128,768]{1,0:T(8,128)(2,1)S(1)}, u32[]{:S(2)}, u32[]{:S(2)}) collective-permute-start(bf16[128,768]{1,0:T(8,128)(2,1)S(1)} %get-tuple-element.117.refs_0_.refs_5_), channel_id=1, source_target_pairs={{0,24},{4,28},{8,16},{12,20},{16,8},{20,12},{24,0},{28,4},{1,25},{... | collective-permute-start | bytes 589832 | tf_op jit(solution)/shard_map/ppermute | solution.py:547
  76.5 11.1 %collective-permute-start.24 = (bf16[128,768]{1,0:T(8,128)(2,1)S(1)}, bf16[128,768]{1,0:T(8,128)(2,1)S(1)}, u32[]{:S(2)}, u32[]{:S(2)}) collective-permute-start(bf16[128,768]{1,0:T(8,128)(2,1)S(1)} %get-tuple-element.117.refs_0_.refs_5_), channel_id=1, source_target_pairs={{0,16},{4,20},{8,24},{12,28},{16,0},{20,4},{24,8},{28,12},{1,17},{... | collective-permute-start | bytes 589832 | tf_op jit(solution)/shard_map/ppermute | solution.py:547
  77.9 10.6 %collective-permute-start.23 = (bf16[128,768]{1,0:T(8,128)(2,1)S(1)}, bf16[128,768]{1,0:T(8,128)(2,1)S(1)}, u32[]{:S(2)}, u32[]{:S(2)}) collective-permute-start(bf16[128,768]{1,0:T(8,128)(2,1)S(1)} %get-tuple-element.117.refs_0_.refs_5_), channel_id=1, source_target_pairs={{0,8},{4,12},{8,0},{12,4},{16,24},{20,28},{24,16},{28,20},{1,9},{5... | collective-permute-start | bytes 589832 | tf_op jit(solution)/shard_map/ppermute | solution.py:547
  84.9 6.6 %collective-permute-start.28 = (bf16[128,768]{1,0:T(8,128)(2,1)S(1)}, bf16[128,768]{1,0:T(8,128)(2,1)S(1)}, u32[]{:S(2)}, u32[]{:S(2)}) collective-permute-start(bf16[128,768]{1,0:T(8,128)(2,1)S(1)} %get-tuple-element.128), channel_id=1, source_target_pairs={{0,24},{4,28},{8,16},{12,20},{16,8},{20,12},{24,0},{28,4},{1,25},{... | collective-permute-start | bytes 589832 | tf_op jit(solution)/shard_map/ppermute | solution.py:547
  93.7 2.9 %collective-permute-start.29 = (bf16[4,192,768]{2,1,0:T(8,128)(2,1)S(1)}, bf16[4,192,768]{2,1,0:T(8,128)(2,1)S(1)}, u32[]{:S(2)}, u32[]{:S(2)}) collective-permute-start(bf16[4,192,768]{2,1,0:T(8,128)(2,1)S(1)} %get-tuple-element.137), channel_id=1, source_target_pairs={{0,4},{4,0},{8,12},{12,8},{16,20},{20,16},{24,28},{28,24},{1,5},{5... | collective-permute-start | bytes 3538952 | tf_op jit(solution)/shard_map/ppermute | solution.py:544
  93.8 7.3 %collective-permute-start.27 = (bf16[128,768]{1,0:T(8,128)(2,1)S(1)}, bf16[128,768]{1,0:T(8,128)(2,1)S(1)}, u32[]{:S(2)}, u32[]{:S(2)}) collective-permute-start(bf16[128,768]{1,0:T(8,128)(2,1)S(1)} %get-tuple-element.127), channel_id=1, source_target_pairs={{0,16},{4,20},{8,24},{12,28},{16,0},{20,4},{24,8},{28,12},{1,17},{... | collective-permute-start | bytes 589832 | tf_op jit(solution)/shard_map/ppermute | solution.py:547
  94.5 7.0 %collective-permute-start.26 = (bf16[128,768]{1,0:T(8,128)(2,1)S(1)}, bf16[128,768]{1,0:T(8,128)(2,1)S(1)}, u32[]{:S(2)}, u32[]{:S(2)}) collective-permute-start(bf16[128,768]{1,0:T(8,128)(2,1)S(1)} %get-tuple-element.126), channel_id=1, source_target_pairs={{0,8},{4,12},{8,0},{12,4},{16,24},{20,28},{24,16},{28,20},{1,9},{5... | collective-permute-start | bytes 589832 | tf_op jit(solution)/shard_map/ppermute | solution.py:547
  97.4 14.5 %collective-permute-start.35 = (bf16[192,768]{1,0:T(8,128)(2,1)S(1)}, bf16[192,768]{1,0:T(8,128)(2,1)S(1)}, u32[]{:S(2)}, u32[]{:S(2)}) collective-permute-start(bf16[192,768]{1,0:T(8,128)(2,1)S(1)} %get-tuple-element.138.refs_10_), channel_id=1, source_target_pairs={{0,1},{1,0},{2,3},{3,2},{4,5},{5,4},{6,7},{7,6},{8,9},{9,8},{10,11... | collective-permute-start | bytes 884744 | tf_op jit(solution)/shard_map/ppermute | solution.py:550
  102.8 16.3 %collective-permute-start.31 = (bf16[128,192]{1,0:T(8,128)(2,1)S(1)}, bf16[128,192]{1,0:T(8,128)(2,1)S(1)}, u32[]{:S(2)}, u32[]{:S(2)}) collective-permute-start(bf16[128,192]{1,0:T(8,128)(2,1)S(1)} %get-tuple-element.148), channel_id=1, source_target_pairs={{0,8},{4,12},{8,0},{12,4},{16,24},{20,28},{24,16},{28,20},{1,9},{5... | collective-permute-start | bytes 147464 | tf_op jit(solution)/shard_map/ppermute | solution.py:547
  104.2 5.0 %collective-permute-start.32 = (bf16[128,192]{1,0:T(8,128)(2,1)S(1)}, bf16[128,192]{1,0:T(8,128)(2,1)S(1)}, u32[]{:S(2)}, u32[]{:S(2)}) collective-permute-start(bf16[128,192]{1,0:T(8,128)(2,1)S(1)} %get-tuple-element.151), channel_id=1, source_target_pairs={{0,16},{4,20},{8,24},{12,28},{16,0},{20,4},{24,8},{28,12},{1,17},{... | collective-permute-start | bytes 147464 | tf_op jit(solution)/shard_map/ppermute | solution.py:547
  105.6 5.2 %collective-permute-start.33 = (bf16[128,192]{1,0:T(8,128)(2,1)S(1)}, bf16[128,192]{1,0:T(8,128)(2,1)S(1)}, u32[]{:S(2)}, u32[]{:S(2)}) collective-permute-start(bf16[128,192]{1,0:T(8,128)(2,1)S(1)} %get-tuple-element.154), channel_id=1, source_target_pairs={{0,24},{4,28},{8,16},{12,20},{16,8},{20,12},{24,0},{28,4},{1,25},{... | collective-permute-start | bytes 147464 | tf_op jit(solution)/shard_map/ppermute | solution.py:547
  107.6 8.5 %collective-permute-start.30 = (bf16[4,192,384]{2,1,0:T(8,128)(2,1)S(1)}, bf16[4,192,384]{2,1,0:T(8,128)(2,1)S(1)}, u32[]{:S(2)}, u32[]{:S(2)}) collective-permute-start(bf16[4,192,384]{2,1,0:T(8,128)(2,1)S(1)} %get-tuple-element.146), channel_id=1, source_target_pairs={{0,4},{4,0},{8,12},{12,8},{16,20},{20,16},{24,28},{28,24},{1,5},{5... | collective-permute-start | bytes 1769480 | tf_op jit(solution)/shard_map/ppermute | solution.py:544
  112.0 18.7 %collective-permute-start.42 = (bf16[192,768]{1,0:T(8,128)(2,1)S(1)}, bf16[192,768]{1,0:T(8,128)(2,1)S(1)}, u32[]{:S(2)}, u32[]{:S(2)}) collective-permute-start(bf16[192,768]{1,0:T(8,128)(2,1)S(1)} %sum_kernel.4.refs_13_.refs_1_), channel_id=1, source_target_pairs={{0,2},{1,3},{2,0},{3,1},{4,6},{5,7},{6,4},{7,5},{8,10},{9,11},{10,... | collective-permute-start | bytes 884744 | tf_op jit(solution)/shard_map/ppermute | solution.py:550
  115.2 14.4 %collective-permute-start.43 = (bf16[192,768]{1,0:T(8,128)(2,1)S(1)}, bf16[192,768]{1,0:T(8,128)(2,1)S(1)}, u32[]{:S(2)}, u32[]{:S(2)}) collective-permute-start(bf16[192,768]{1,0:T(8,128)(2,1)S(1)} %gate_kernel.8), channel_id=1, source_target_pairs={{0,1},{1,0},{2,3},{3,2},{4,5},{5,4},{6,7},{7,6},{8,9},{9,8},{10,11... | collective-permute-start | bytes 884744 | tf_op jit(solution)/shard_map/ppermute | solution.py:550
  116.8 6.5 %collective-permute-start.34 = (bf16[4,48,384]{2,1,0:T(8,128)(2,1)S(1)}, bf16[4,48,384]{2,1,0:T(8,128)(2,1)S(1)}, u32[]{:S(2)}, u32[]{:S(2)}) collective-permute-start(bf16[4,48,384]{2,1,0:T(8,128)(2,1)S(1)} %get-tuple-element.159), channel_id=1, source_target_pairs={{0,8},{4,12},{8,0},{12,4},{16,24},{20,28},{24,16},{28,20},{1,9},{5... | collective-permute-start | bytes 442376 | tf_op jit(solution)/shard_map/ppermute | solution.py:547
  117.3 8.3 %collective-permute-start.36 = (bf16[4,48,384]{2,1,0:T(8,128)(2,1)S(1)}, bf16[4,48,384]{2,1,0:T(8,128)(2,1)S(1)}, u32[]{:S(2)}, u32[]{:S(2)}) collective-permute-start(bf16[4,48,384]{2,1,0:T(8,128)(2,1)S(1)} %get-tuple-element.162), channel_id=1, source_target_pairs={{0,16},{4,20},{8,24},{12,28},{16,0},{20,4},{24,8},{28,12},{1,17},{... | collective-permute-start | bytes 442376 | tf_op jit(solution)/shard_map/ppermute | solution.py:547
  119.1 6.5 %collective-permute-start.37 = (bf16[4,48,384]{2,1,0:T(8,128)(2,1)S(1)}, bf16[4,48,384]{2,1,0:T(8,128)(2,1)S(1)}, u32[]{:S(2)}, u32[]{:S(2)}) collective-permute-start(bf16[4,48,384]{2,1,0:T(8,128)(2,1)S(1)} %get-tuple-element.163), channel_id=1, source_target_pairs={{0,24},{4,28},{8,16},{12,20},{16,8},{20,12},{24,0},{28,4},{1,25},{... | collective-permute-start | bytes 442376 | tf_op jit(solution)/shard_map/ppermute | solution.py:547
  124.8 5.9 %collective-permute-start.41 = (bf16[4,112,576]{2,1,0:T(8,128)(2,1)S(1)}, bf16[4,112,576]{2,1,0:T(8,128)(2,1)S(1)}, u32[]{:S(2)}, u32[]{:S(2)}) collective-permute-start(bf16[4,112,576]{2,1,0:T(8,128)(2,1)S(1)} %get-tuple-element.161.refs_5_), channel_id=1, source_target_pairs={{0,4},{4,0},{8,12},{12,8},{16,20},{20,16},{24,28},{28,24},{1,5},{5... | collective-permute-start | bytes 1548296 | tf_op jit(solution)/shard_map/ppermute | solution.py:544
  127.0 7.9 %collective-permute-start.38 = (bf16[128,768]{1,0:T(8,128)(2,1)S(1)}, bf16[128,768]{1,0:T(8,128)(2,1)S(1)}, u32[]{:S(2)}, u32[]{:S(2)}) collective-permute-start(bf16[128,768]{1,0:T(8,128)(2,1)S(1)} %get-tuple-element.165), channel_id=1, source_target_pairs={{0,8},{4,12},{8,0},{12,4},{16,24},{20,28},{24,16},{28,20},{1,9},{5... | collective-permute-start | bytes 589832 | tf_op jit(solution)/shard_map/ppermute | solution.py:547
  128.4 9.6 %collective-permute-start.39 = (bf16[128,768]{1,0:T(8,128)(2,1)S(1)}, bf16[128,768]{1,0:T(8,128)(2,1)S(1)}, u32[]{:S(2)}, u32[]{:S(2)}) collective-permute-start(bf16[128,768]{1,0:T(8,128)(2,1)S(1)} %get-tuple-element.166), channel_id=1, source_target_pairs={{0,16},{4,20},{8,24},{12,28},{16,0},{20,4},{24,8},{28,12},{1,17},{... | collective-permute-start | bytes 589832 | tf_op jit(solution)/shard_map/ppermute | solution.py:547
  129.7 8.4 %collective-permute-start.40 = (bf16[128,768]{1,0:T(8,128)(2,1)S(1)}, bf16[128,768]{1,0:T(8,128)(2,1)S(1)}, u32[]{:S(2)}, u32[]{:S(2)}) collective-permute-start(bf16[128,768]{1,0:T(8,128)(2,1)S(1)} %get-tuple-element.167), channel_id=1, source_target_pairs={{0,24},{4,28},{8,16},{12,20},{16,8},{20,12},{24,0},{28,4},{1,25},{... | collective-permute-start | bytes 589832 | tf_op jit(solution)/shard_map/ppermute | solution.py:547
  131.5 6.6 %collective-permute-start.44 = (bf16[144,576]{1,0:T(8,128)(2,1)S(1)}, bf16[144,576]{1,0:T(8,128)(2,1)S(1)}, u32[]{:S(2)}, u32[]{:S(2)}) collective-permute-start(bf16[144,576]{1,0:T(8,128)(2,1)S(1)} %get-tuple-element.173), channel_id=1, source_target_pairs={{0,1},{1,0},{2,3},{3,2},{4,5},{5,4},{6,7},{7,6},{8,9},{9,8},{10,11... | collective-permute-start | bytes 497672 | tf_op jit(solution)/shard_map/ppermute | solution.py:550
  138.1 8.5 %collective-permute-start.46 = (bf16[144,576]{1,0:T(8,128)(2,1)S(1)}, bf16[144,576]{1,0:T(8,128)(2,1)S(1)}, u32[]{:S(2)}, u32[]{:S(2)}) collective-permute-start(bf16[144,576]{1,0:T(8,128)(2,1)S(1)} %sum_kernel.5.refs_1_.refs_3_), channel_id=1, source_target_pairs={{0,2},{1,3},{2,0},{3,1},{4,6},{5,7},{6,4},{7,5},{8,10},{9,11},{10,... | collective-permute-start | bytes 497672 | tf_op jit(solution)/shard_map/ppermute | solution.py:550
  138.9 6.6 %collective-permute-start.45 = (bf16[144,576]{1,0:T(8,128)(2,1)S(1)}, bf16[144,576]{1,0:T(8,128)(2,1)S(1)}, u32[]{:S(2)}, u32[]{:S(2)}) collective-permute-start(bf16[144,576]{1,0:T(8,128)(2,1)S(1)} %gate_kernel.9), channel_id=1, source_target_pairs={{0,1},{1,0},{2,3},{3,2},{4,5},{5,4},{6,7},{7,6},{8,9},{9,8},{10,11... | collective-permute-start | bytes 497672 | tf_op jit(solution)/shard_map/ppermute | solution.py:550
  139.6 10.3 %collective-permute-start.53 = (bf16[192,768]{1,0:T(8,128)(2,1)S(1)}, bf16[192,768]{1,0:T(8,128)(2,1)S(1)}, u32[]{:S(2)}, u32[]{:S(2)}) collective-permute-start(bf16[192,768]{1,0:T(8,128)(2,1)S(1)} %sum_kernel.7.refs_0_), channel_id=1, source_target_pairs={{0,24},{4,28},{8,16},{12,20},{16,8},{20,12},{24,0},{28,4},{1,25},{... | collective-permute-start | bytes 884744 | tf_op jit(solution)/shard_map/ppermute | solution.py:547
  141.0 15.0 %collective-permute-start.52 = (bf16[192,768]{1,0:T(8,128)(2,1)S(1)}, bf16[192,768]{1,0:T(8,128)(2,1)S(1)}, u32[]{:S(2)}, u32[]{:S(2)}) collective-permute-start(bf16[192,768]{1,0:T(8,128)(2,1)S(1)} %sum_kernel.7.refs_0_), channel_id=1, source_target_pairs={{0,16},{4,20},{8,24},{12,28},{16,0},{20,4},{24,8},{28,12},{1,17},{... | collective-permute-start | bytes 884744 | tf_op jit(solution)/shard_map/ppermute | solution.py:547
  142.6 14.1 %collective-permute-start.51 = (bf16[192,768]{1,0:T(8,128)(2,1)S(1)}, bf16[192,768]{1,0:T(8,128)(2,1)S(1)}, u32[]{:S(2)}, u32[]{:S(2)}) collective-permute-start(bf16[192,768]{1,0:T(8,128)(2,1)S(1)} %sum_kernel.7.refs_0_), channel_id=1, source_target_pairs={{0,8},{4,12},{8,0},{12,4},{16,24},{20,28},{24,16},{28,20},{1,9},{5... | collective-permute-start | bytes 884744 | tf_op jit(solution)/shard_map/ppermute | solution.py:547
  146.7 12.0 %collective-permute-start.49 = (bf16[144,576]{1,0:T(8,128)(2,1)S(1)}, bf16[144,576]{1,0:T(8,128)(2,1)S(1)}, u32[]{:S(2)}, u32[]{:S(2)}) collective-permute-start(bf16[144,576]{1,0:T(8,128)(2,1)S(1)} %sum_kernel.6.g0.refs_3_), channel_id=1, source_target_pairs={{0,24},{4,28},{8,16},{12,20},{16,8},{20,12},{24,0},{28,4},{1,25},{... | collective-permute-start | bytes 497672 | tf_op jit(solution)/shard_map/ppermute | solution.py:547
  149.3 11.2 %collective-permute-start.48 = (bf16[144,576]{1,0:T(8,128)(2,1)S(1)}, bf16[144,576]{1,0:T(8,128)(2,1)S(1)}, u32[]{:S(2)}, u32[]{:S(2)}) collective-permute-start(bf16[144,576]{1,0:T(8,128)(2,1)S(1)} %sum_kernel.6.g0.refs_3_), channel_id=1, source_target_pairs={{0,16},{4,20},{8,24},{12,28},{16,0},{20,4},{24,8},{28,12},{1,17},{... | collective-permute-start | bytes 497672 | tf_op jit(solution)/shard_map/ppermute | solution.py:547
  149.9 12.2 %collective-permute-start.47 = (bf16[144,576]{1,0:T(8,128)(2,1)S(1)}, bf16[144,576]{1,0:T(8,128)(2,1)S(1)}, u32[]{:S(2)}, u32[]{:S(2)}) collective-permute-start(bf16[144,576]{1,0:T(8,128)(2,1)S(1)} %sum_kernel.6.g0.refs_3_), channel_id=1, source_target_pairs={{0,8},{4,12},{8,0},{12,4},{16,24},{20,28},{24,16},{28,20},{1,9},{5... | collective-permute-start | bytes 497672 | tf_op jit(solution)/shard_map/ppermute | solution.py:547
  156.8 5.4 %collective-permute-start.54 = (bf16[4,192,768]{2,1,0:T(8,128)(2,1)S(1)}, bf16[4,192,768]{2,1,0:T(8,128)(2,1)S(1)}, u32[]{:S(2)}, u32[]{:S(2)}) collective-permute-start(bf16[4,192,768]{2,1,0:T(8,128)(2,1)S(1)} %stack_kernel.5.refs_1_), channel_id=1, source_target_pairs={{0,4},{4,0},{8,12},{12,8},{16,20},{20,16},{24,28},{28,24},{1,5},{5... | collective-permute-start | bytes 3538952 | tf_op jit(solution)/shard_map/ppermute | solution.py:544
  157.0 8.4 %copy-start.2 = (f32[128,768]{1,0:T(8,128)}, f32[128,768]{1,0:T(8,128)S(1)}, u32[]{:S(2)}) copy-start(f32[128,768]{1,0:T(8,128)S(1)} %add_add_fusion.refs_4_) | copy-start | bytes 1179652
  162.2 3.2 %collective-permute-start.50 = (bf16[4,144,576]{2,1,0:T(8,128)(2,1)S(1)}, bf16[4,144,576]{2,1,0:T(8,128)(2,1)S(1)}, u32[]{:S(2)}, u32[]{:S(2)}) collective-permute-start(bf16[4,144,576]{2,1,0:T(8,128)(2,1)S(1)} %stack_kernel.4.refs_1_), channel_id=1, source_target_pairs={{0,4},{4,0},{8,12},{12,8},{16,20},{20,16},{24,28},{28,24},{1,5},{5... | collective-permute-start | bytes 1990664 | tf_op jit(solution)/shard_map/ppermute | solution.py:544
  (16 other events, 47.8 us)

commit v6 on v5

--- a/solution.py
+++ b/solution.py
@@ -842,7 +842,7 @@
             idx=idx,
             after=[got_a, near_a, dxp[0]],
         )
-        low_b, got_b = relay_sum(far_b, send_b, dxp_got[1:])
+        low_b, got_b = relay_sum(far_b, send_b, [dxp_got[3]])
         near_b = swap_shard(gate(near_b, [low_b]), 1)
         piece1 = join(own_a, near_a, got_a, [low_b])
         done1 = spread_piece(piece1, [got_b, near_b])

time: 168 us -> 167 us (level)
  waiting for transfers between devices: 64.9 us -> 61.5 us
    ppermute x35, waiting for transfers between devices: 44.2 us -> 39.9 us  [swap_part(): return lax.ppermute(v, 'rep', xor_perm(reps, CORES * k))]
  transfers between devices with their start and end apart: 55 -> 55, of which waited for: 30 -> 28; matrix products, arithmetic and copies ran while one was open for 0% -> 0% of each run, Pallas kernels for 18% -> 18%
where the time goes in v6:
time: 167 us; the launch traced here: 166 us
  starting transfers between devices  62.8 us (38%)
  waiting for transfers between devices  61.5 us (37%)
  Pallas kernels  38.3 us (23%)
    ppermute x35, starting transfers between devices, swap_part(): return lax.ppermute(v, 'rep', xor_perm(reps, CORES * k))  44.4 us
    ppermute x35, waiting for transfers between devices, swap_part(): return lax.ppermute(v, 'rep', xor_perm(reps, CORES * k))  39.9 us
    pallas_call x42, Pallas kernels, call(): pl.pallas_call(run if drop else kernel, out_shape=shapes, in_specs=specs,...  38.3 us
    ppermute x12, waiting for transfers between devices, swap_shard(): return lax.ppermute(v, 'shard', xor_perm(shards, k))  19.5 us
    ppermute x12, starting transfers between devices, swap_shard(): return lax.ppermute(v, 'shard', xor_perm(shards, k))  18 us
  transfers between devices with their start and end apart: 55, of which 28 were waited for; matrix products, arithmetic and copies ran while one was open for 0% of the time, Pallas kernels for 18%

profile of v6, /device:TPU:0, one launch (start us, length us, event | category | flops | bytes accessed | tf_op | source)
XLA Modules:
  0.0 165.8 jit_solution(3166798526293488880)
XLA Ops:
  1.3 2.7 %pack_kernel.1 = (bf16[144,768]{1,0:T(8,128)(2,1)}, bf16[144,576]{1,0:T(8,128)(2,1)}) custom-call(s32[3]{0:T(128)} %pad_add_fusion.idx.refs_0_, bf16[128,768]{1,0:T(8,128)(2,1)} %tok.3, bf16[192,2304]{1,0:T(8,128)(2,1)} %wqkv.1, bf16[192,768]{1,0:T(8,128)(2,1)} %wout.1, bf16[6,192]{1,0:T(8,128)(2,1)} %vec_in.1, bf16[2,192]{1,0:T(2,128)(2,1)} %gain_in.1, ...), custom_call_target="tpu_custom_call" | custom-call | flops 11000000512 | bytes 100000 | tf_op jit(solution)/shard_map/pack_kernel/pallas_call | solution.py:514
  3.9 4.0 %collective-permute-start.2 = (bf16[144,768]{1,0:T(8,128)(2,1)}, bf16[144,768]{1,0:T(8,128)(2,1)S(1)}, u32[]{:S(2)}, u32[]{:S(2)}) collective-permute-start(bf16[144,768]{1,0:T(8,128)(2,1)} %get-tuple-element.96.refs_3_.x.x0.refs_1_), channel_id=1, source_target_pairs={{0,24},{4,28},{8,16},{12,20},{16,8},{20,12},{24,0},{28,4},{1,25},{... | collective-permute-start | bytes 663560 | tf_op jit(solution)/shard_map/ppermute | solution.py:547
  7.9 2.6 %collective-permute-start.1 = (bf16[144,576]{1,0:T(8,128)(2,1)}, bf16[144,576]{1,0:T(8,128)(2,1)S(1)}, u32[]{:S(2)}, u32[]{:S(2)}) collective-permute-start(bf16[144,576]{1,0:T(8,128)(2,1)} %get-tuple-element.97.g0), channel_id=1, source_target_pairs={{0,2},{1,3},{2,0},{3,1},{4,6},{5,7},{6,4},{7,5},{8,10},{9,11},{10,... | collective-permute-start | bytes 497672 | tf_op jit(solution)/shard_map/ppermute | solution.py:550
  10.5 1.6 collective-permute-start
  12.1 7.1 %collective-permute-done.1.refs_0_ = bf16[144,576]{1,0:T(8,128)(2,1)S(1)} collective-permute-done((bf16[144,576]{1,0:T(8,128)(2,1)}, bf16[144,576]{1,0:T(8,128)(2,1)S(1)}, u32[]{:S(2)}, u32[]{:S(2)}) %collective-permute-start.1) | collective-permute-done | bytes 165920 | tf_op jit(solution)/shard_map/ppermute | solution.py:550
  21.0 3.8 %collective-permute-done.3.g3.refs_1_ = bf16[144,576]{1,0:T(8,128)(2,1)S(1)} collective-permute-done((bf16[144,576]{1,0:T(8,128)(2,1)S(1)}, bf16[144,576]{1,0:T(8,128)(2,1)S(1)}, u32[]{:S(2)}, u32[]{:S(2)}) %collective-permute-start.3) | collective-permute-done | bytes 165920 | tf_op jit(solution)/shard_map/ppermute | solution.py:550
  26.5 1.0 pack2_kernel.1.refs_0_
  28.0 2.8 %collective-permute-start.14 = (bf16[192,768]{1,0:T(8,128)(2,1)S(1)}, bf16[192,768]{1,0:T(8,128)(2,1)S(1)}, u32[]{:S(2)}, u32[]{:S(2)}) collective-permute-start(bf16[192,768]{1,0:T(8,128)(2,1)S(1)} %gate_kernel.6.refs_3_.refs_0_), channel_id=1, source_target_pairs={{0,2},{1,3},{2,0},{3,1},{4,6},{5,7},{6,4},{7,5},{8,10},{9,11},{10,... | collective-permute-start | bytes 884744 | tf_op jit(solution)/shard_map/ppermute | solution.py:550
  30.8 1.7 %collective-permute-start.13 = (bf16[192,768]{1,0:T(8,128)(2,1)S(1)}, bf16[192,768]{1,0:T(8,128)(2,1)S(1)}, u32[]{:S(2)}, u32[]{:S(2)}) collective-permute-start(bf16[192,768]{1,0:T(8,128)(2,1)S(1)} %gate_kernel.6.refs_3_.refs_0_), channel_id=1, source_target_pairs={{0,1},{1,0},{2,3},{3,2},{4,5},{5,4},{6,7},{7,6},{8,9},{9,8},{10,11... | collective-permute-start | bytes 884744 | tf_op jit(solution)/shard_map/ppermute | solution.py:550
  34.9 2.5 %collective-permute-start.9 = (bf16[128,192]{1,0:T(8,128)(2,1)S(1)}, bf16[128,192]{1,0:T(8,128)(2,1)S(1)}, u32[]{:S(2)}, u32[]{:S(2)}) collective-permute-start(bf16[128,192]{1,0:T(8,128)(2,1)S(1)} %get-tuple-element.104.refs_2_), channel_id=1, source_target_pairs={{0,24},{4,28},{8,16},{12,20},{16,8},{20,12},{24,0},{28,4},{1,25},{... | collective-permute-start | bytes 147464 | tf_op jit(solution)/shard_map/ppermute | solution.py:547
  39.8 3.8 %collective-permute-done.11.refs_1_ = bf16[2,4,48,384]{3,2,1,0:T(8,128)(2,1)S(1)} collective-permute-done((bf16[2,4,48,384]{3,2,1,0:T(8,128)(2,1)S(1)}, bf16[2,4,48,384]{3,2,1,0:T(8,128)(2,1)S(1)}, u32[]{:S(2)}, u32[]{:S(2)}) %collective-permute-start.11) | collective-permute-done | bytes 294944 | tf_op jit(solution)/shard_map/ppermute | solution.py:547
  43.6 1.5 collective-permute-start.7
  46.3 1.6 collective-permute-done.7.m1.refs_1_.refs_2_
  48.9 1.1 out_kernel.1
  50.0 1.5 collective-permute-start.16
  51.6 4.2 %collective-permute-done.15.refs_3_ = bf16[192,768]{1,0:T(8,128)(2,1)S(1)} collective-permute-done((bf16[192,768]{1,0:T(8,128)(2,1)S(1)}, bf16[192,768]{1,0:T(8,128)(2,1)S(1)}, u32[]{:S(2)}, u32[]{:S(2)}) %collective-permute-start.15) | collective-permute-done | bytes 294944 | tf_op jit(solution)/shard_map/ppermute | solution.py:550
  55.8 1.2 collective-permute-done.16.refs_4_.y.refs_12_
  57.8 1.2 collective-permute-start.18
  58.9 1.1 collective-permute-done.17.other
  61.4 1.2 collective-permute-start.22
  62.6 1.9 %collective-permute-done.20.y.refs_11_ = bf16[128,768]{1,0:T(8,128)(2,1)S(1)} collective-permute-done((bf16[128,768]{1,0:T(8,128)(2,1)S(1)}, bf16[128,768]{1,0:T(8,128)(2,1)S(1)}, u32[]{:S(2)}, u32[]{:S(2)}) %collective-permute-start.20) | collective-permute-done | bytes 196640 | tf_op jit(solution)/shard_map/ppermute | solution.py:547
  66.5 1.2 collective-permute-start.19
  68.4 2.0 %collective-permute-done.22.r3 = bf16[128,768]{1,0:T(8,128)(2,1)S(1)} collective-permute-done((bf16[128,768]{1,0:T(8,128)(2,1)S(1)}, bf16[128,768]{1,0:T(8,128)(2,1)S(1)}, u32[]{:S(2)}, u32[]{:S(2)}) %collective-permute-start.22) | collective-permute-done | bytes 196640 | tf_op jit(solution)/shard_map/ppermute | solution.py:547
  70.4 3.7 %collective-permute-done.21.r2 = bf16[128,768]{1,0:T(8,128)(2,1)S(1)} collective-permute-done((bf16[128,768]{1,0:T(8,128)(2,1)S(1)}, bf16[128,768]{1,0:T(8,128)(2,1)S(1)}, u32[]{:S(2)}, u32[]{:S(2)}) %collective-permute-start.21) | collective-permute-done | bytes 196640 | tf_op jit(solution)/shard_map/ppermute | solution.py:547
  74.1 1.2 ln2_kernel.1
  75.3 1.2 collective-permute-start.25
  76.5 1.4 collective-permute-start.24
  78.8 5.2 %collective-permute-done.25.d.refs_8_ = bf16[128,768]{1,0:T(8,128)(2,1)S(1)} collective-permute-done((bf16[128,768]{1,0:T(8,128)(2,1)S(1)}, bf16[128,768]{1,0:T(8,128)(2,1)S(1)}, u32[]{:S(2)}, u32[]{:S(2)}) %collective-permute-start.25) | collective-permute-done | bytes 196640 | tf_op jit(solution)/shard_map/ppermute | solution.py:547
  84.9 1.3 collective-permute-start.28
  86.2 1.3 collective-permute-done.24.d.refs_7_
  88.5 0.9 ffb_kernel.4
  90.4 1.2 collective-permute-done.28.refs_17_.refs_3_.refs_5_
  91.6 2.1 %ffw_kernel.1 = (bf16[4,192,768]{2,1,0:T(8,128)(2,1)S(1)}, bf16[4,192,768]{2,1,0:T(8,128)(2,1)S(1)}, f32[8,768]{1,0:T(8,128)S(1)}) custom-call(s32[3]{0:T(128)S(1)} %copy-done.13, bf16[128,768]{1,0:T(8,128)(2,1)S(1)} %get-tuple-element.131.refs_1_, bf16[128,768]{1,0:T(8,128)(2,1)S(1)} %get-tuple-element.132.refs_2_, ...), custom_call_target="tpu_custom_call" | custom-call | flops 11000000512 | bytes 100000 | tf_op jit(solution)/shard_map/ffw_kernel/pallas_call | solution.py:514
  94.5 1.2 collective-permute-start.26
  95.6 1.0 collective-permute-done.29.refs_2_
  97.4 1.4 collective-permute-start.35
  98.9 2.2 %collective-permute-done.27.refs_4_ = bf16[128,768]{1,0:T(8,128)(2,1)S(1)} collective-permute-done((bf16[128,768]{1,0:T(8,128)(2,1)S(1)}, bf16[128,768]{1,0:T(8,128)(2,1)S(1)}, u32[]{:S(2)}, u32[]{:S(2)}) %collective-permute-start.27) | collective-permute-done | bytes 196640 | tf_op jit(solution)/shard_map/ppermute | solution.py:547
  101.4 1.3 ln1b_kernel.1
  102.8 1.4 collective-permute-start.31
  104.2 1.4 collective-permute-start.32
  106.5 1.1 outw_kernel.1
  107.7 1.5 collective-permute-done.32.d
  109.2 1.1 attb_kernel.6.refs_7_.refs_2_
  110.8 1.1 attb_kernel.7.refs_2_.refs_8_.refs_3_
  112.0 3.3 %collective-permute-start.42 = (bf16[192,768]{1,0:T(8,128)(2,1)S(1)}, bf16[192,768]{1,0:T(8,128)(2,1)S(1)}, u32[]{:S(2)}, u32[]{:S(2)}) collective-permute-start(bf16[192,768]{1,0:T(8,128)(2,1)S(1)} %sum_kernel.4.refs_13_.refs_1_), channel_id=1, source_target_pairs={{0,2},{1,3},{2,0},{3,1},{4,6},{5,7},{6,4},{7,5},{8,10},{9,11},{10,... | collective-permute-start | bytes 884744 | tf_op jit(solution)/shard_map/ppermute | solution.py:550
  118.0 1.1 attb_kernel.4.refs_5_.refs_0_
  119.1 2.4 %collective-permute-start.37 = (bf16[4,48,384]{2,1,0:T(8,128)(2,1)S(1)}, bf16[4,48,384]{2,1,0:T(8,128)(2,1)S(1)}, u32[]{:S(2)}, u32[]{:S(2)}) collective-permute-start(bf16[4,48,384]{2,1,0:T(8,128)(2,1)S(1)} %get-tuple-element.163), channel_id=1, source_target_pairs={{0,24},{4,28},{8,16},{12,20},{16,8},{20,12},{24,0},{28,4},{1,25},{... | collective-permute-start | bytes 442376 | tf_op jit(solution)/shard_map/ppermute | solution.py:547
  121.5 1.1 attb_kernel.5.refs_6_.refs_1_
  123.3 1.5 qw_kernel.1
  125.7 1.4 dx_kernel.1
  127.0 2.0 %collective-permute-start.40 = (bf16[128,768]{1,0:T(8,128)(2,1)S(1)}, bf16[128,768]{1,0:T(8,128)(2,1)S(1)}, u32[]{:S(2)}, u32[]{:S(2)}) collective-permute-start(bf16[128,768]{1,0:T(8,128)(2,1)S(1)} %get-tuple-element.167), channel_id=1, source_target_pairs={{0,24},{4,28},{8,16},{12,20},{16,8},{20,12},{24,0},{28,4},{1,25},{... | collective-permute-start | bytes 589832 | tf_op jit(solution)/shard_map/ppermute | solution.py:547
  129.9 1.3 collective-permute-start.44
  131.7 1.1 collective-permute-start.39
  132.7 3.1 %collective-permute-done.40.refs_2_ = bf16[128,768]{1,0:T(8,128)(2,1)S(1)} collective-permute-done((bf16[128,768]{1,0:T(8,128)(2,1)S(1)}, bf16[128,768]{1,0:T(8,128)(2,1)S(1)}, u32[]{:S(2)}, u32[]{:S(2)}) %collective-permute-start.40) | collective-permute-done | bytes 196640 | tf_op jit(solution)/shard_map/ppermute | solution.py:547
  137.4 2.4 %collective-permute-start.53 = (bf16[192,768]{1,0:T(8,128)(2,1)S(1)}, bf16[192,768]{1,0:T(8,128)(2,1)S(1)}, u32[]{:S(2)}, u32[]{:S(2)}) collective-permute-start(bf16[192,768]{1,0:T(8,128)(2,1)S(1)} %sum_kernel.7.refs_0_), channel_id=1, source_target_pairs={{0,24},{4,28},{8,16},{12,20},{16,8},{20,12},{24,0},{28,4},{1,25},{... | collective-permute-start | bytes 884744 | tf_op jit(solution)/shard_map/ppermute | solution.py:547
  139.8 3.9 %collective-permute-done.45.refs_1_.refs_5_ = bf16[144,576]{1,0:T(8,128)(2,1)S(1)} collective-permute-done((bf16[144,576]{1,0:T(8,128)(2,1)S(1)}, bf16[144,576]{1,0:T(8,128)(2,1)S(1)}, u32[]{:S(2)}, u32[]{:S(2)}) %collective-permute-start.45) | collective-permute-done | bytes 165920 | tf_op jit(solution)/shard_map/ppermute | solution.py:550
  144.9 1.2 collective-permute-start.51
  146.2 2.5 %collective-permute-start.49 = (bf16[144,576]{1,0:T(8,128)(2,1)S(1)}, bf16[144,576]{1,0:T(8,128)(2,1)S(1)}, u32[]{:S(2)}, u32[]{:S(2)}) collective-permute-start(bf16[144,576]{1,0:T(8,128)(2,1)S(1)} %sum_kernel.6.g0.refs_3_), channel_id=1, source_target_pairs={{0,24},{4,28},{8,16},{12,20},{16,8},{20,12},{24,0},{28,4},{1,25},{... | collective-permute-start | bytes 497672 | tf_op jit(solution)/shard_map/ppermute | solution.py:547
  148.7 4.7 %collective-permute-done.52.refs_2_ = bf16[192,768]{1,0:T(8,128)(2,1)S(1)} collective-permute-done((bf16[192,768]{1,0:T(8,128)(2,1)S(1)}, bf16[192,768]{1,0:T(8,128)(2,1)S(1)}, u32[]{:S(2)}, u32[]{:S(2)}) %collective-permute-start.52) | collective-permute-done | bytes 294944 | tf_op jit(solution)/shard_map/ppermute | solution.py:547
  153.4 1.3 collective-permute-start.48
  154.7 1.7 %collective-permute-start.47 = (bf16[144,576]{1,0:T(8,128)(2,1)S(1)}, bf16[144,576]{1,0:T(8,128)(2,1)S(1)}, u32[]{:S(2)}, u32[]{:S(2)}) collective-permute-start(bf16[144,576]{1,0:T(8,128)(2,1)S(1)} %sum_kernel.6.g0.refs_3_), channel_id=1, source_target_pairs={{0,8},{4,12},{8,0},{12,4},{16,24},{20,28},{24,16},{28,20},{1,9},{5... | collective-permute-start | bytes 497672 | tf_op jit(solution)/shard_map/ppermute | solution.py:547
  156.8 2.9 %collective-permute-done.48.g2 = bf16[144,576]{1,0:T(8,128)(2,1)S(1)} collective-permute-done((bf16[144,576]{1,0:T(8,128)(2,1)S(1)}, bf16[144,576]{1,0:T(8,128)(2,1)S(1)}, u32[]{:S(2)}, u32[]{:S(2)}) %collective-permute-start.48) | collective-permute-done | bytes 165920 | tf_op jit(solution)/shard_map/ppermute | solution.py:547
  160.4 3.1 %fin1_kernel.1 = (f32[192,3072]{1,0:T(8,128)}, f32[768,768]{1,0:T(8,128)}, f32[8,128]{1,0:T(8,128)S(1)}) custom-call(s32[3]{0:T(128)S(1)} %copy-done.13, bf16[4,192,768]{2,1,0:T(8,128)(2,1)S(1)} %stack_kernel.5.refs_1_, bf16[4,192,768]{2,1,0:T(8,128)(2,1)S(1)} %collective-permute-done.54.refs_2_, bf16[144,576]{1,0:T(8,128)(2,1)S(1)} %sum_kernel.6.g0.refs_3_), custom_call_target="tpu_custom_call" | custom-call | flops 11000000512 | bytes 100000 | tf_op jit(solution)/shard_map/fin1_kernel/pallas_call | solution.py:514
  163.5 2.3 %fin2_kernel.1 = (f32[192,2304]{1,0:T(8,128)}, f32[192,768]{1,0:T(8,128)}, f32[6,192]{1,0:T(8,128)}, f32[2,192]{1,0:T(2,128)}, f32[768]{0:T(1024)}) custom-call(s32[3]{0:T(128)S(1)} %copy-done.13, bf16[4,144,576]{2,1,0:T(8,128)(2,1)S(1)} %stack_kernel.4.refs_1_, bf16[4,144,576]{2,1,0:T(8,128)(2,1)S(1)} %collective-permute-done.50.refs_2_, ...), custom_call_target="tpu_custom_call" | custom-call | flops 11000000512 | bytes 100000 | tf_op jit(solution)/shard_map/fin2_kernel/pallas_call | solution.py:514
  (147 shorter events, 32.4 us)
Async XLA Ops:
  3.9 15.2 %collective-permute-start.2 = (bf16[144,768]{1,0:T(8,128)(2,1)}, bf16[144,768]{1,0:T(8,128)(2,1)S(1)}, u32[]{:S(2)}, u32[]{:S(2)}) collective-permute-start(bf16[144,768]{1,0:T(8,128)(2,1)} %get-tuple-element.96.refs_3_.x.x0.refs_1_), channel_id=1, source_target_pairs={{0,24},{4,28},{8,16},{12,20},{16,8},{20,12},{24,0},{28,4},{1,25},{... | collective-permute-start | bytes 663560 | tf_op jit(solution)/shard_map/ppermute | solution.py:547
  7.9 11.3 %collective-permute-start.1 = (bf16[144,576]{1,0:T(8,128)(2,1)}, bf16[144,576]{1,0:T(8,128)(2,1)S(1)}, u32[]{:S(2)}, u32[]{:S(2)}) collective-permute-start(bf16[144,576]{1,0:T(8,128)(2,1)} %get-tuple-element.97.g0), channel_id=1, source_target_pairs={{0,2},{1,3},{2,0},{3,1},{4,6},{5,7},{6,4},{7,5},{8,10},{9,11},{10,... | collective-permute-start | bytes 497672 | tf_op jit(solution)/shard_map/ppermute | solution.py:550
  10.5 10.5 %collective-permute-start = (bf16[144,576]{1,0:T(8,128)(2,1)}, bf16[144,576]{1,0:T(8,128)(2,1)S(1)}, u32[]{:S(2)}, u32[]{:S(2)}) collective-permute-start(bf16[144,576]{1,0:T(8,128)(2,1)} %get-tuple-element.97.g0), channel_id=1, source_target_pairs={{0,1},{1,0},{2,3},{3,2},{4,5},{5,4},{6,7},{7,6},{8,9},{9,8},{10,11... | collective-permute-start | bytes 497672 | tf_op jit(solution)/shard_map/ppermute | solution.py:550
  19.2 14.7 %copy-start = (bf16[144,768]{1,0:T(8,128)(2,1)}, bf16[144,768]{1,0:T(8,128)(2,1)S(1)}, u32[]{:S(2)}) copy-start(bf16[144,768]{1,0:T(8,128)(2,1)S(1)} %collective-permute-done.2.refs_1_.refs_4_.x) | copy-start | bytes 663556
  19.2 7.3 %copy-start.13 = (s32[3]{0:T(128)S(1)}, s32[3]{0:T(128)}, u32[]{:S(2)}) copy-start(s32[3]{0:T(128)} %pad_add_fusion.idx.refs_0_) | copy-start | bytes 40
  19.2 7.3 %copy-start.14 = (bf16[192,3072]{1,0:T(8,128)(2,1)S(1)}, bf16[192,3072]{1,0:T(8,128)(2,1)}, u32[]{:S(2)}) copy-start(bf16[192,3072]{1,0:T(8,128)(2,1)} %refs_1_.1) | copy-start | bytes 3538948
  19.2 7.3 %copy-start.15 = (bf16[768,768]{1,0:T(8,128)(2,1)S(1)}, bf16[768,768]{1,0:T(8,128)(2,1)}, u32[]{:S(2)}) copy-start(bf16[768,768]{1,0:T(8,128)(2,1)} %refs_2_.1) | copy-start | bytes 3538948
  19.2 7.3 %copy-start.16 = (bf16[144,768]{1,0:T(8,128)(2,1)S(1)}, bf16[144,768]{1,0:T(8,128)(2,1)}, u32[]{:S(2)}) copy-start(bf16[144,768]{1,0:T(8,128)(2,1)} %get-tuple-element.96.refs_3_.x.x0.refs_1_) | copy-start | bytes 663556
  19.2 5.6 %collective-permute-start.3 = (bf16[144,576]{1,0:T(8,128)(2,1)S(1)}, bf16[144,576]{1,0:T(8,128)(2,1)S(1)}, u32[]{:S(2)}, u32[]{:S(2)}) collective-permute-start(bf16[144,576]{1,0:T(8,128)(2,1)S(1)} %gate_kernel.5.g2), channel_id=1, source_target_pairs={{0,1},{1,0},{2,3},{3,2},{4,5},{5,4},{6,7},{7,6},{8,9},{9,8},{10,11... | collective-permute-start | bytes 497672 | tf_op jit(solution)/shard_map/ppermute | solution.py:550
  20.0 7.5 %collective-permute-start.6 = (bf16[144,768]{1,0:T(8,128)(2,1)}, bf16[144,768]{1,0:T(8,128)(2,1)S(1)}, u32[]{:S(2)}, u32[]{:S(2)}) collective-permute-start(bf16[144,768]{1,0:T(8,128)(2,1)} %get-tuple-element.96.refs_3_.x.x0.refs_1_), channel_id=1, source_target_pairs={{0,16},{4,20},{8,24},{12,28},{16,0},{20,4},{24,8},{28,12},{1,17},{... | collective-permute-start | bytes 663560 | tf_op jit(solution)/shard_map/ppermute | solution.py:547
  20.5 7.5 %collective-permute-start.5 = (bf16[144,768]{1,0:T(8,128)(2,1)}, bf16[144,768]{1,0:T(8,128)(2,1)S(1)}, u32[]{:S(2)}, u32[]{:S(2)}) collective-permute-start(bf16[144,768]{1,0:T(8,128)(2,1)} %get-tuple-element.96.refs_3_.x.x0.refs_1_), channel_id=1, source_target_pairs={{0,8},{4,12},{8,0},{12,4},{16,24},{20,28},{24,16},{28,20},{1,9},{5... | collective-permute-start | bytes 663560 | tf_op jit(solution)/shard_map/ppermute | solution.py:547
  25.9 6.7 %collective-permute-start.10 = (bf16[4,48,384]{2,1,0:T(8,128)(2,1)S(1)}, bf16[4,48,384]{2,1,0:T(8,128)(2,1)S(1)}, u32[]{:S(2)}, u32[]{:S(2)}) collective-permute-start(bf16[4,48,384]{2,1,0:T(8,128)(2,1)S(1)} %get-tuple-element.105), channel_id=1, source_target_pairs={{0,8},{4,12},{8,0},{12,4},{16,24},{20,28},{24,16},{28,20},{1,9},{5... | collective-permute-start | bytes 442376 | tf_op jit(solution)/shard_map/ppermute | solution.py:547
  26.5 6.7 %collective-permute-start.4 = (bf16[4,112,576]{2,1,0:T(8,128)(2,1)S(1)}, bf16[4,112,576]{2,1,0:T(8,128)(2,1)S(1)}, u32[]{:S(2)}, u32[]{:S(2)}) collective-permute-start(bf16[4,112,576]{2,1,0:T(8,128)(2,1)S(1)} %get-tuple-element.98.refs_1_), channel_id=1, source_target_pairs={{0,4},{4,0},{8,12},{12,8},{16,20},{20,16},{24,28},{28,24},{1,5},{5... | collective-permute-start | bytes 1548296 | tf_op jit(solution)/shard_map/ppermute | solution.py:544
  27.5 9.9 %copy-start.3 = (bf16[144,768]{1,0:T(8,128)(2,1)}, bf16[144,768]{1,0:T(8,128)(2,1)S(1)}, u32[]{:S(2)}) copy-start(bf16[144,768]{1,0:T(8,128)(2,1)S(1)} %collective-permute-done.6.refs_3_.x) | copy-start | bytes 663556
  28.0 10.9 %copy-start.5 = (bf16[144,768]{1,0:T(8,128)(2,1)}, bf16[144,768]{1,0:T(8,128)(2,1)S(1)}, u32[]{:S(2)}) copy-start(bf16[144,768]{1,0:T(8,128)(2,1)S(1)} %collective-permute-done.5.refs_2_.x) | copy-start | bytes 663556
  28.0 17.2 %collective-permute-start.14 = (bf16[192,768]{1,0:T(8,128)(2,1)S(1)}, bf16[192,768]{1,0:T(8,128)(2,1)S(1)}, u32[]{:S(2)}, u32[]{:S(2)}) collective-permute-start(bf16[192,768]{1,0:T(8,128)(2,1)S(1)} %gate_kernel.6.refs_3_.refs_0_), channel_id=1, source_target_pairs={{0,2},{1,3},{2,0},{3,1},{4,6},{5,7},{6,4},{7,5},{8,10},{9,11},{10,... | collective-permute-start | bytes 884744 | tf_op jit(solution)/shard_map/ppermute | solution.py:550
  30.8 15.4 %collective-permute-start.13 = (bf16[192,768]{1,0:T(8,128)(2,1)S(1)}, bf16[192,768]{1,0:T(8,128)(2,1)S(1)}, u32[]{:S(2)}, u32[]{:S(2)}) collective-permute-start(bf16[192,768]{1,0:T(8,128)(2,1)S(1)} %gate_kernel.6.refs_3_.refs_0_), channel_id=1, source_target_pairs={{0,1},{1,0},{2,3},{3,2},{4,5},{5,4},{6,7},{7,6},{8,9},{9,8},{10,11... | collective-permute-start | bytes 884744 | tf_op jit(solution)/shard_map/ppermute | solution.py:550
  32.6 11.0 %collective-permute-start.11 = (bf16[2,4,48,384]{3,2,1,0:T(8,128)(2,1)S(1)}, bf16[2,4,48,384]{3,2,1,0:T(8,128)(2,1)S(1)}, u32[]{:S(2)}, u32[]{:S(2)}) collective-permute-start(bf16[2,4,48,384]{3,2,1,0:T(8,128)(2,1)S(1)} %pad_maximum_fusion.refs_0_), channel_id=1, source_target_pairs={{0,16},{4,20},{8,24},{12,28},{16,0},{20,4},{24,8},{28,12},{1,17},{... | collective-permute-start | bytes 884744 | tf_op jit(solution)/shard_map/ppermute | solution.py:547
  33.9 11.4 %copy-start.21 = (bf16[768,576]{1,0:T(8,128)(2,1)}, bf16[768,576]{1,0:T(8,128)(2,1)S(1)}, u32[]{:S(2)}) copy-start(bf16[768,576]{1,0:T(8,128)(2,1)S(1)} %get-tuple-element.99.wq.refs_4_) | copy-start | bytes 2654212
  34.9 11.4 %collective-permute-start.9 = (bf16[128,192]{1,0:T(8,128)(2,1)S(1)}, bf16[128,192]{1,0:T(8,128)(2,1)S(1)}, u32[]{:S(2)}, u32[]{:S(2)}) collective-permute-start(bf16[128,192]{1,0:T(8,128)(2,1)S(1)} %get-tuple-element.104.refs_2_), channel_id=1, source_target_pairs={{0,24},{4,28},{8,16},{12,20},{16,8},{20,12},{24,0},{28,4},{1,25},{... | collective-permute-start | bytes 147464 | tf_op jit(solution)/shard_map/ppermute | solution.py:547
  38.3 8.0 %collective-permute-start.8 = (bf16[128,192]{1,0:T(8,128)(2,1)S(1)}, bf16[128,192]{1,0:T(8,128)(2,1)S(1)}, u32[]{:S(2)}, u32[]{:S(2)}) collective-permute-start(bf16[128,192]{1,0:T(8,128)(2,1)S(1)} %get-tuple-element.103), channel_id=1, source_target_pairs={{0,16},{4,20},{8,24},{12,28},{16,0},{20,4},{24,8},{28,12},{1,17},{... | collective-permute-start | bytes 147464 | tf_op jit(solution)/shard_map/ppermute | solution.py:547
  43.6 4.3 %collective-permute-start.7 = (bf16[128,192]{1,0:T(8,128)(2,1)S(1)}, bf16[128,192]{1,0:T(8,128)(2,1)S(1)}, u32[]{:S(2)}, u32[]{:S(2)}) collective-permute-start(bf16[128,192]{1,0:T(8,128)(2,1)S(1)} %get-tuple-element.102), channel_id=1, source_target_pairs={{0,8},{4,12},{8,0},{12,4},{16,24},{20,28},{24,16},{28,20},{1,9},{5... | collective-permute-start | bytes 147464 | tf_op jit(solution)/shard_map/ppermute | solution.py:547
  45.2 3.0 %collective-permute-start.12 = (bf16[4,4,48,384]{3,2,1,0:T(8,128)(2,1)S(1)}, bf16[4,4,48,384]{3,2,1,0:T(8,128)(2,1)S(1)}, u32[]{:S(2)}, u32[]{:S(2)}) collective-permute-start(bf16[4,4,48,384]{3,2,1,0:T(8,128)(2,1)S(1)} %join_kernel.1.mine), channel_id=1, source_target_pairs={{0,4},{4,0},{8,12},{12,8},{16,20},{20,16},{24,28},{28,24},{1,5},{5... | collective-permute-start | bytes 1769480 | tf_op jit(solution)/shard_map/ppermute | solution.py:544
  47.9 7.9 %collective-permute-start.15 = (bf16[192,768]{1,0:T(8,128)(2,1)S(1)}, bf16[192,768]{1,0:T(8,128)(2,1)S(1)}, u32[]{:S(2)}, u32[]{:S(2)}) collective-permute-start(bf16[192,768]{1,0:T(8,128)(2,1)S(1)} %gate_kernel.7.refs_2_), channel_id=1, source_target_pairs={{0,1},{1,0},{2,3},{3,2},{4,5},{5,4},{6,7},{7,6},{8,9},{9,8},{10,11... | collective-permute-start | bytes 884744 | tf_op jit(solution)/shard_map/ppermute | solution.py:550
  50.0 7.0 %collective-permute-start.16 = (bf16[128,768]{1,0:T(8,128)(2,1)S(1)}, bf16[128,768]{1,0:T(8,128)(2,1)S(1)}, u32[]{:S(2)}, u32[]{:S(2)}) collective-permute-start(bf16[128,768]{1,0:T(8,128)(2,1)S(1)} %get-tuple-element.108.y.refs_9_), channel_id=1, source_target_pairs={{0,24},{4,28},{8,16},{12,20},{16,8},{20,12},{24,0},{28,4},{1,25},{... | collective-permute-start | bytes 589832 | tf_op jit(solution)/shard_map/ppermute | solution.py:547
  57.1 2.9 %collective-permute-start.17 = (bf16[4,192,768]{2,1,0:T(8,128)(2,1)S(1)}, bf16[4,192,768]{2,1,0:T(8,128)(2,1)S(1)}, u32[]{:S(2)}, u32[]{:S(2)}) collective-permute-start(bf16[4,192,768]{2,1,0:T(8,128)(2,1)S(1)} %stack_kernel.3.mine), channel_id=1, source_target_pairs={{0,4},{4,0},{8,12},{12,8},{16,20},{20,16},{24,28},{28,24},{1,5},{5... | collective-permute-start | bytes 3538952 | tf_op jit(solution)/shard_map/ppermute | solution.py:544
  57.2 7.3 %collective-permute-start.20 = (bf16[128,768]{1,0:T(8,128)(2,1)S(1)}, bf16[128,768]{1,0:T(8,128)(2,1)S(1)}, u32[]{:S(2)}, u32[]{:S(2)}) collective-permute-start(bf16[128,768]{1,0:T(8,128)(2,1)S(1)} %get-tuple-element.108.y.refs_9_), channel_id=1, source_target_pairs={{0,16},{4,20},{8,24},{12,28},{16,0},{20,4},{24,8},{28,12},{1,17},{... | collective-permute-start | bytes 589832 | tf_op jit(solution)/shard_map/ppermute | solution.py:547
  57.8 8.0 %collective-permute-start.18 = (bf16[128,768]{1,0:T(8,128)(2,1)S(1)}, bf16[128,768]{1,0:T(8,128)(2,1)S(1)}, u32[]{:S(2)}, u32[]{:S(2)}) collective-permute-start(bf16[128,768]{1,0:T(8,128)(2,1)S(1)} %get-tuple-element.108.y.refs_9_), channel_id=1, source_target_pairs={{0,8},{4,12},{8,0},{12,4},{16,24},{20,28},{24,16},{28,20},{1,9},{5... | collective-permute-start | bytes 589832 | tf_op jit(solution)/shard_map/ppermute | solution.py:547
  61.4 9.0 %collective-permute-start.22 = (bf16[128,768]{1,0:T(8,128)(2,1)S(1)}, bf16[128,768]{1,0:T(8,128)(2,1)S(1)}, u32[]{:S(2)}, u32[]{:S(2)}) collective-permute-start(bf16[128,768]{1,0:T(8,128)(2,1)S(1)} %get-tuple-element.114), channel_id=1, source_target_pairs={{0,24},{4,28},{8,16},{12,20},{16,8},{20,12},{24,0},{28,4},{1,25},{... | collective-permute-start | bytes 589832 | tf_op jit(solution)/shard_map/ppermute | solution.py:547
  65.2 8.9 %collective-permute-start.21 = (bf16[128,768]{1,0:T(8,128)(2,1)S(1)}, bf16[128,768]{1,0:T(8,128)(2,1)S(1)}, u32[]{:S(2)}, u32[]{:S(2)}) collective-permute-start(bf16[128,768]{1,0:T(8,128)(2,1)S(1)} %get-tuple-element.113), channel_id=1, source_target_pairs={{0,16},{4,20},{8,24},{12,28},{16,0},{20,4},{24,8},{28,12},{1,17},{... | collective-permute-start | bytes 589832 | tf_op jit(solution)/shard_map/ppermute | solution.py:547
  66.5 7.7 %copy-start.19 = (bf16[128,768]{1,0:T(8,128)(2,1)S(1)}, bf16[128,768]{1,0:T(8,128)(2,1)}, u32[]{:S(2)}) copy-start(bf16[128,768]{1,0:T(8,128)(2,1)} %cot.1) | copy-start | bytes 589828
  66.5 7.6 %collective-permute-start.19 = (bf16[128,768]{1,0:T(8,128)(2,1)S(1)}, bf16[128,768]{1,0:T(8,128)(2,1)S(1)}, u32[]{:S(2)}, u32[]{:S(2)}) collective-permute-start(bf16[128,768]{1,0:T(8,128)(2,1)S(1)} %get-tuple-element.112), channel_id=1, source_target_pairs={{0,8},{4,12},{8,0},{12,4},{16,24},{20,28},{24,16},{28,20},{1,9},{5... | collective-permute-start | bytes 589832 | tf_op jit(solution)/shard_map/ppermute | solution.py:547
  75.3 8.7 %collective-permute-start.25 = (bf16[128,768]{1,0:T(8,128)(2,1)S(1)}, bf16[128,768]{1,0:T(8,128)(2,1)S(1)}, u32[]{:S(2)}, u32[]{:S(2)}) collective-permute-start(bf16[128,768]{1,0:T(8,128)(2,1)S(1)} %get-tuple-element.117.refs_0_.refs_5_), channel_id=1, source_target_pairs={{0,24},{4,28},{8,16},{12,20},{16,8},{20,12},{24,0},{28,4},{1,25},{... | collective-permute-start | bytes 589832 | tf_op jit(solution)/shard_map/ppermute | solution.py:547
  76.5 11.0 %collective-permute-start.24 = (bf16[128,768]{1,0:T(8,128)(2,1)S(1)}, bf16[128,768]{1,0:T(8,128)(2,1)S(1)}, u32[]{:S(2)}, u32[]{:S(2)}) collective-permute-start(bf16[128,768]{1,0:T(8,128)(2,1)S(1)} %get-tuple-element.117.refs_0_.refs_5_), channel_id=1, source_target_pairs={{0,16},{4,20},{8,24},{12,28},{16,0},{20,4},{24,8},{28,12},{1,17},{... | collective-permute-start | bytes 589832 | tf_op jit(solution)/shard_map/ppermute | solution.py:547
  77.9 10.6 %collective-permute-start.23 = (bf16[128,768]{1,0:T(8,128)(2,1)S(1)}, bf16[128,768]{1,0:T(8,128)(2,1)S(1)}, u32[]{:S(2)}, u32[]{:S(2)}) collective-permute-start(bf16[128,768]{1,0:T(8,128)(2,1)S(1)} %get-tuple-element.117.refs_0_.refs_5_), channel_id=1, source_target_pairs={{0,8},{4,12},{8,0},{12,4},{16,24},{20,28},{24,16},{28,20},{1,9},{5... | collective-permute-start | bytes 589832 | tf_op jit(solution)/shard_map/ppermute | solution.py:547
  84.9 6.6 %collective-permute-start.28 = (bf16[128,768]{1,0:T(8,128)(2,1)S(1)}, bf16[128,768]{1,0:T(8,128)(2,1)S(1)}, u32[]{:S(2)}, u32[]{:S(2)}) collective-permute-start(bf16[128,768]{1,0:T(8,128)(2,1)S(1)} %get-tuple-element.128), channel_id=1, source_target_pairs={{0,24},{4,28},{8,16},{12,20},{16,8},{20,12},{24,0},{28,4},{1,25},{... | collective-permute-start | bytes 589832 | tf_op jit(solution)/shard_map/ppermute | solution.py:547
  93.7 2.9 %collective-permute-start.29 = (bf16[4,192,768]{2,1,0:T(8,128)(2,1)S(1)}, bf16[4,192,768]{2,1,0:T(8,128)(2,1)S(1)}, u32[]{:S(2)}, u32[]{:S(2)}) collective-permute-start(bf16[4,192,768]{2,1,0:T(8,128)(2,1)S(1)} %get-tuple-element.137), channel_id=1, source_target_pairs={{0,4},{4,0},{8,12},{12,8},{16,20},{20,16},{24,28},{28,24},{1,5},{5... | collective-permute-start | bytes 3538952 | tf_op jit(solution)/shard_map/ppermute | solution.py:544
  93.8 7.3 %collective-permute-start.27 = (bf16[128,768]{1,0:T(8,128)(2,1)S(1)}, bf16[128,768]{1,0:T(8,128)(2,1)S(1)}, u32[]{:S(2)}, u32[]{:S(2)}) collective-permute-start(bf16[128,768]{1,0:T(8,128)(2,1)S(1)} %get-tuple-element.127), channel_id=1, source_target_pairs={{0,16},{4,20},{8,24},{12,28},{16,0},{20,4},{24,8},{28,12},{1,17},{... | collective-permute-start | bytes 589832 | tf_op jit(solution)/shard_map/ppermute | solution.py:547
  94.5 7.0 %collective-permute-start.26 = (bf16[128,768]{1,0:T(8,128)(2,1)S(1)}, bf16[128,768]{1,0:T(8,128)(2,1)S(1)}, u32[]{:S(2)}, u32[]{:S(2)}) collective-permute-start(bf16[128,768]{1,0:T(8,128)(2,1)S(1)} %get-tuple-element.126), channel_id=1, source_target_pairs={{0,8},{4,12},{8,0},{12,4},{16,24},{20,28},{24,16},{28,20},{1,9},{5... | collective-permute-start | bytes 589832 | tf_op jit(solution)/shard_map/ppermute | solution.py:547
  97.4 14.5 %collective-permute-start.35 = (bf16[192,768]{1,0:T(8,128)(2,1)S(1)}, bf16[192,768]{1,0:T(8,128)(2,1)S(1)}, u32[]{:S(2)}, u32[]{:S(2)}) collective-permute-start(bf16[192,768]{1,0:T(8,128)(2,1)S(1)} %get-tuple-element.138.refs_10_), channel_id=1, source_target_pairs={{0,1},{1,0},{2,3},{3,2},{4,5},{5,4},{6,7},{7,6},{8,9},{9,8},{10,11... | collective-permute-start | bytes 884744 | tf_op jit(solution)/shard_map/ppermute | solution.py:550
  102.8 16.3 %collective-permute-start.31 = (bf16[128,192]{1,0:T(8,128)(2,1)S(1)}, bf16[128,192]{1,0:T(8,128)(2,1)S(1)}, u32[]{:S(2)}, u32[]{:S(2)}) collective-permute-start(bf16[128,192]{1,0:T(8,128)(2,1)S(1)} %get-tuple-element.148), channel_id=1, source_target_pairs={{0,8},{4,12},{8,0},{12,4},{16,24},{20,28},{24,16},{28,20},{1,9},{5... | collective-permute-start | bytes 147464 | tf_op jit(solution)/shard_map/ppermute | solution.py:547
  104.2 5.0 %collective-permute-start.32 = (bf16[128,192]{1,0:T(8,128)(2,1)S(1)}, bf16[128,192]{1,0:T(8,128)(2,1)S(1)}, u32[]{:S(2)}, u32[]{:S(2)}) collective-permute-start(bf16[128,192]{1,0:T(8,128)(2,1)S(1)} %get-tuple-element.151), channel_id=1, source_target_pairs={{0,16},{4,20},{8,24},{12,28},{16,0},{20,4},{24,8},{28,12},{1,17},{... | collective-permute-start | bytes 147464 | tf_op jit(solution)/shard_map/ppermute | solution.py:547
  105.6 5.2 %collective-permute-start.33 = (bf16[128,192]{1,0:T(8,128)(2,1)S(1)}, bf16[128,192]{1,0:T(8,128)(2,1)S(1)}, u32[]{:S(2)}, u32[]{:S(2)}) collective-permute-start(bf16[128,192]{1,0:T(8,128)(2,1)S(1)} %get-tuple-element.154), channel_id=1, source_target_pairs={{0,24},{4,28},{8,16},{12,20},{16,8},{20,12},{24,0},{28,4},{1,25},{... | collective-permute-start | bytes 147464 | tf_op jit(solution)/shard_map/ppermute | solution.py:547
  107.6 8.5 %collective-permute-start.30 = (bf16[4,192,384]{2,1,0:T(8,128)(2,1)S(1)}, bf16[4,192,384]{2,1,0:T(8,128)(2,1)S(1)}, u32[]{:S(2)}, u32[]{:S(2)}) collective-permute-start(bf16[4,192,384]{2,1,0:T(8,128)(2,1)S(1)} %get-tuple-element.146), channel_id=1, source_target_pairs={{0,4},{4,0},{8,12},{12,8},{16,20},{20,16},{24,28},{28,24},{1,5},{5... | collective-permute-start | bytes 1769480 | tf_op jit(solution)/shard_map/ppermute | solution.py:544
  112.0 17.1 %collective-permute-start.42 = (bf16[192,768]{1,0:T(8,128)(2,1)S(1)}, bf16[192,768]{1,0:T(8,128)(2,1)S(1)}, u32[]{:S(2)}, u32[]{:S(2)}) collective-permute-start(bf16[192,768]{1,0:T(8,128)(2,1)S(1)} %sum_kernel.4.refs_13_.refs_1_), channel_id=1, source_target_pairs={{0,2},{1,3},{2,0},{3,1},{4,6},{5,7},{6,4},{7,5},{8,10},{9,11},{10,... | collective-permute-start | bytes 884744 | tf_op jit(solution)/shard_map/ppermute | solution.py:550
  115.2 13.8 %collective-permute-start.43 = (bf16[192,768]{1,0:T(8,128)(2,1)S(1)}, bf16[192,768]{1,0:T(8,128)(2,1)S(1)}, u32[]{:S(2)}, u32[]{:S(2)}) collective-permute-start(bf16[192,768]{1,0:T(8,128)(2,1)S(1)} %gate_kernel.8), channel_id=1, source_target_pairs={{0,1},{1,0},{2,3},{3,2},{4,5},{5,4},{6,7},{7,6},{8,9},{9,8},{10,11... | collective-permute-start | bytes 884744 | tf_op jit(solution)/shard_map/ppermute | solution.py:550
  116.8 6.5 %collective-permute-start.34 = (bf16[4,48,384]{2,1,0:T(8,128)(2,1)S(1)}, bf16[4,48,384]{2,1,0:T(8,128)(2,1)S(1)}, u32[]{:S(2)}, u32[]{:S(2)}) collective-permute-start(bf16[4,48,384]{2,1,0:T(8,128)(2,1)S(1)} %get-tuple-element.159), channel_id=1, source_target_pairs={{0,8},{4,12},{8,0},{12,4},{16,24},{20,28},{24,16},{28,20},{1,9},{5... | collective-permute-start | bytes 442376 | tf_op jit(solution)/shard_map/ppermute | solution.py:547
  117.3 8.3 %collective-permute-start.36 = (bf16[4,48,384]{2,1,0:T(8,128)(2,1)S(1)}, bf16[4,48,384]{2,1,0:T(8,128)(2,1)S(1)}, u32[]{:S(2)}, u32[]{:S(2)}) collective-permute-start(bf16[4,48,384]{2,1,0:T(8,128)(2,1)S(1)} %get-tuple-element.162), channel_id=1, source_target_pairs={{0,16},{4,20},{8,24},{12,28},{16,0},{20,4},{24,8},{28,12},{1,17},{... | collective-permute-start | bytes 442376 | tf_op jit(solution)/shard_map/ppermute | solution.py:547
  119.1 6.5 %collective-permute-start.37 = (bf16[4,48,384]{2,1,0:T(8,128)(2,1)S(1)}, bf16[4,48,384]{2,1,0:T(8,128)(2,1)S(1)}, u32[]{:S(2)}, u32[]{:S(2)}) collective-permute-start(bf16[4,48,384]{2,1,0:T(8,128)(2,1)S(1)} %get-tuple-element.163), channel_id=1, source_target_pairs={{0,24},{4,28},{8,16},{12,20},{16,8},{20,12},{24,0},{28,4},{1,25},{... | collective-permute-start | bytes 442376 | tf_op jit(solution)/shard_map/ppermute | solution.py:547
  124.8 4.3 %collective-permute-start.41 = (bf16[4,112,576]{2,1,0:T(8,128)(2,1)S(1)}, bf16[4,112,576]{2,1,0:T(8,128)(2,1)S(1)}, u32[]{:S(2)}, u32[]{:S(2)}) collective-permute-start(bf16[4,112,576]{2,1,0:T(8,128)(2,1)S(1)} %get-tuple-element.161.refs_5_), channel_id=1, source_target_pairs={{0,4},{4,0},{8,12},{12,8},{16,20},{20,16},{24,28},{28,24},{1,5},{5... | collective-permute-start | bytes 1548296 | tf_op jit(solution)/shard_map/ppermute | solution.py:544
  127.0 8.8 %collective-permute-start.40 = (bf16[128,768]{1,0:T(8,128)(2,1)S(1)}, bf16[128,768]{1,0:T(8,128)(2,1)S(1)}, u32[]{:S(2)}, u32[]{:S(2)}) collective-permute-start(bf16[128,768]{1,0:T(8,128)(2,1)S(1)} %get-tuple-element.167), channel_id=1, source_target_pairs={{0,24},{4,28},{8,16},{12,20},{16,8},{20,12},{24,0},{28,4},{1,25},{... | collective-permute-start | bytes 589832 | tf_op jit(solution)/shard_map/ppermute | solution.py:547
  129.9 5.9 %collective-permute-start.44 = (bf16[144,576]{1,0:T(8,128)(2,1)S(1)}, bf16[144,576]{1,0:T(8,128)(2,1)S(1)}, u32[]{:S(2)}, u32[]{:S(2)}) collective-permute-start(bf16[144,576]{1,0:T(8,128)(2,1)S(1)} %get-tuple-element.173), channel_id=1, source_target_pairs={{0,1},{1,0},{2,3},{3,2},{4,5},{5,4},{6,7},{7,6},{8,9},{9,8},{10,11... | collective-permute-start | bytes 497672 | tf_op jit(solution)/shard_map/ppermute | solution.py:550
  131.1 25.3 %collective-permute-start.38 = (bf16[128,768]{1,0:T(8,128)(2,1)S(1)}, bf16[128,768]{1,0:T(8,128)(2,1)S(1)}, u32[]{:S(2)}, u32[]{:S(2)}) collective-permute-start(bf16[128,768]{1,0:T(8,128)(2,1)S(1)} %get-tuple-element.165), channel_id=1, source_target_pairs={{0,8},{4,12},{8,0},{12,4},{16,24},{20,28},{24,16},{28,20},{1,9},{5... | collective-permute-start | bytes 589832 | tf_op jit(solution)/shard_map/ppermute | solution.py:547
  131.7 24.9 %collective-permute-start.39 = (bf16[128,768]{1,0:T(8,128)(2,1)S(1)}, bf16[128,768]{1,0:T(8,128)(2,1)S(1)}, u32[]{:S(2)}, u32[]{:S(2)}) collective-permute-start(bf16[128,768]{1,0:T(8,128)(2,1)S(1)} %get-tuple-element.166), channel_id=1, source_target_pairs={{0,16},{4,20},{8,24},{12,28},{16,0},{20,4},{24,8},{28,12},{1,17},{... | collective-permute-start | bytes 589832 | tf_op jit(solution)/shard_map/ppermute | solution.py:547
  135.9 9.0 %collective-permute-start.46 = (bf16[144,576]{1,0:T(8,128)(2,1)S(1)}, bf16[144,576]{1,0:T(8,128)(2,1)S(1)}, u32[]{:S(2)}, u32[]{:S(2)}) collective-permute-start(bf16[144,576]{1,0:T(8,128)(2,1)S(1)} %sum_kernel.5.refs_1_.refs_3_), channel_id=1, source_target_pairs={{0,2},{1,3},{2,0},{3,1},{4,6},{5,7},{6,4},{7,5},{8,10},{9,11},{10,... | collective-permute-start | bytes 497672 | tf_op jit(solution)/shard_map/ppermute | solution.py:550
  136.6 7.1 %collective-permute-start.45 = (bf16[144,576]{1,0:T(8,128)(2,1)S(1)}, bf16[144,576]{1,0:T(8,128)(2,1)S(1)}, u32[]{:S(2)}, u32[]{:S(2)}) collective-permute-start(bf16[144,576]{1,0:T(8,128)(2,1)S(1)} %gate_kernel.9), channel_id=1, source_target_pairs={{0,1},{1,0},{2,3},{3,2},{4,5},{5,4},{6,7},{7,6},{8,9},{9,8},{10,11... | collective-permute-start | bytes 497672 | tf_op jit(solution)/shard_map/ppermute | solution.py:550
  137.4 8.8 %collective-permute-start.53 = (bf16[192,768]{1,0:T(8,128)(2,1)S(1)}, bf16[192,768]{1,0:T(8,128)(2,1)S(1)}, u32[]{:S(2)}, u32[]{:S(2)}) collective-permute-start(bf16[192,768]{1,0:T(8,128)(2,1)S(1)} %sum_kernel.7.refs_0_), channel_id=1, source_target_pairs={{0,24},{4,28},{8,16},{12,20},{16,8},{20,12},{24,0},{28,4},{1,25},{... | collective-permute-start | bytes 884744 | tf_op jit(solution)/shard_map/ppermute | solution.py:547
  143.7 9.7 %collective-permute-start.52 = (bf16[192,768]{1,0:T(8,128)(2,1)S(1)}, bf16[192,768]{1,0:T(8,128)(2,1)S(1)}, u32[]{:S(2)}, u32[]{:S(2)}) collective-permute-start(bf16[192,768]{1,0:T(8,128)(2,1)S(1)} %sum_kernel.7.refs_0_), channel_id=1, source_target_pairs={{0,16},{4,20},{8,24},{12,28},{16,0},{20,4},{24,8},{28,12},{1,17},{... | collective-permute-start | bytes 884744 | tf_op jit(solution)/shard_map/ppermute | solution.py:547
  144.9 9.8 %collective-permute-start.51 = (bf16[192,768]{1,0:T(8,128)(2,1)S(1)}, bf16[192,768]{1,0:T(8,128)(2,1)S(1)}, u32[]{:S(2)}, u32[]{:S(2)}) collective-permute-start(bf16[192,768]{1,0:T(8,128)(2,1)S(1)} %sum_kernel.7.refs_0_), channel_id=1, source_target_pairs={{0,8},{4,12},{8,0},{12,4},{16,24},{20,28},{24,16},{28,20},{1,9},{5... | collective-permute-start | bytes 884744 | tf_op jit(solution)/shard_map/ppermute | solution.py:547
  146.2 10.6 %collective-permute-start.49 = (bf16[144,576]{1,0:T(8,128)(2,1)S(1)}, bf16[144,576]{1,0:T(8,128)(2,1)S(1)}, u32[]{:S(2)}, u32[]{:S(2)}) collective-permute-start(bf16[144,576]{1,0:T(8,128)(2,1)S(1)} %sum_kernel.6.g0.refs_3_), channel_id=1, source_target_pairs={{0,24},{4,28},{8,16},{12,20},{16,8},{20,12},{24,0},{28,4},{1,25},{... | collective-permute-start | bytes 497672 | tf_op jit(solution)/shard_map/ppermute | solution.py:547
  153.4 6.3 %collective-permute-start.48 = (bf16[144,576]{1,0:T(8,128)(2,1)S(1)}, bf16[144,576]{1,0:T(8,128)(2,1)S(1)}, u32[]{:S(2)}, u32[]{:S(2)}) collective-permute-start(bf16[144,576]{1,0:T(8,128)(2,1)S(1)} %sum_kernel.6.g0.refs_3_), channel_id=1, source_target_pairs={{0,16},{4,20},{8,24},{12,28},{16,0},{20,4},{24,8},{28,12},{1,17},{... | collective-permute-start | bytes 497672 | tf_op jit(solution)/shard_map/ppermute | solution.py:547
  154.7 5.5 %collective-permute-start.47 = (bf16[144,576]{1,0:T(8,128)(2,1)S(1)}, bf16[144,576]{1,0:T(8,128)(2,1)S(1)}, u32[]{:S(2)}, u32[]{:S(2)}) collective-permute-start(bf16[144,576]{1,0:T(8,128)(2,1)S(1)} %sum_kernel.6.g0.refs_3_), channel_id=1, source_target_pairs={{0,8},{4,12},{8,0},{12,4},{16,24},{20,28},{24,16},{28,20},{1,9},{5... | collective-permute-start | bytes 497672 | tf_op jit(solution)/shard_map/ppermute | solution.py:547
  156.4 3.9 %collective-permute-start.54 = (bf16[4,192,768]{2,1,0:T(8,128)(2,1)S(1)}, bf16[4,192,768]{2,1,0:T(8,128)(2,1)S(1)}, u32[]{:S(2)}, u32[]{:S(2)}) collective-permute-start(bf16[4,192,768]{2,1,0:T(8,128)(2,1)S(1)} %stack_kernel.5.refs_1_), channel_id=1, source_target_pairs={{0,4},{4,0},{8,12},{12,8},{16,20},{20,16},{24,28},{28,24},{1,5},{5... | collective-permute-start | bytes 3538952 | tf_op jit(solution)/shard_map/ppermute | solution.py:544
  160.3 3.2 %collective-permute-start.50 = (bf16[4,144,576]{2,1,0:T(8,128)(2,1)S(1)}, bf16[4,144,576]{2,1,0:T(8,128)(2,1)S(1)}, u32[]{:S(2)}, u32[]{:S(2)}) collective-permute-start(bf16[4,144,576]{2,1,0:T(8,128)(2,1)S(1)} %stack_kernel.4.refs_1_), channel_id=1, source_target_pairs={{0,4},{4,0},{8,12},{12,8},{16,20},{20,16},{24,28},{28,24},{1,5},{5... | collective-permute-start | bytes 1990664 | tf_op jit(solution)/shard_map/ppermute | solution.py:544
  (16 other events, 47.4 us)
